TPU v7x, 32 devices: a whole 2x2x4 slice. The times are simulated.
32 devices in a mesh: dp: 4 (over z), expert: 8 (over y, x, core).
Axes of the slice: x: 2, y: 2, z: 4, core: 2. Of those that a mesh axis runs over, the one named last changes fastest.
Arguments:
- tokens: bfloat16 [32, 256, 1152], P(('dp', 'expert')), may hold values from -6 to 6
- lengths: int32 [32], P(('dp', 'expert')), may hold values from 128 to 256, as said below
- routes: int32 [32, 256], P(('dp', 'expert')), may hold values from 0 to 7, as said below
- slot_index: int32 [32, 256], P(('dp', 'expert')), may hold values from 0 to 64, as said below
- mixer_norm: bfloat16 [1152], P('expert'), may hold values from 0.5 to 1.5
- in_weight: bfloat16 [1152, 4608], P(None, 'expert'), may hold values from -0.1875 to 0.1875
- conv_weight: bfloat16 [4, 2304], P(None, 'expert'), may hold values from -3 to 3
- conv_bias: bfloat16 [2304], P('expert'), may hold values from -3 to 3
- scan_weight: bfloat16 [2304, 104], P('expert'), may hold values from -0.125 to 0.125
- step_weight: bfloat16 [72, 2304], P(None, 'expert'), may hold values from -0.75 to 0.75
- step_bias: bfloat16 [2304], P('expert'), may hold values from -6 to -1
- decay_log: bfloat16 [2304, 16], P('expert'), may hold values from -1 to 2.796875
- skip_gain: bfloat16 [2304], P('expert'), may hold values from 0.5 to 1.5
- out_weight: bfloat16 [2304, 1152], P('expert'), may hold values from -0.25 to 0.25
- moe_norm: bfloat16 [1152], P('expert'), may hold values from 0.5 to 1.5
- router_weight: bfloat16 [1152, 8], P('expert'), may hold values from -0.09375 to 0.09375
- up_weight: bfloat16 [8, 1152, 3072], P('expert'), may hold values from -0.1875 to 0.1875
- down_weight: bfloat16 [8, 3072, 1152], P('expert'), may hold values from -0.875 to 0.875
- cotangent: bfloat16 [32, 256, 1152], P(('dp', 'expert')), may hold values from -6 to 6
Outputs:
- layer_out: bfloat16 [32, 256, 1152], P(('dp', 'expert'))
- tokens_grad: float32 [32, 256, 1152], P(('dp', 'expert'))
- mixer_norm_grad: float32 [1152], P('expert')
- in_weight_grad: float32 [1152, 4608], P(None, 'expert')
- conv_weight_grad: float32 [4, 2304], P(None, 'expert')
- conv_bias_grad: float32 [2304], P('expert')
- scan_weight_grad: float32 [2304, 104], P('expert')
- step_weight_grad: float32 [72, 2304], P(None, 'expert')
- step_bias_grad: float32 [2304], P('expert')
- decay_log_grad: float32 [2304, 16], P('expert')
- skip_gain_grad: float32 [2304], P('expert')
- out_weight_grad: float32 [2304, 1152], P('expert')
- moe_norm_grad: float32 [1152], P('expert')
- router_weight_grad: float32 [1152, 8], P('expert')
- up_weight_grad: float32 [8, 1152, 3072], P('expert')
- down_weight_grad: float32 [8, 3072, 1152], P('expert')
Inputs may be any that keep to these rules, and one draw needn't show every extreme that they name: `lengths`: each device holds one sequence of this many real tokens followed by padding; some device's sequence fills all 256 rows. Padding rows carry routes too. `slot_index`: within one device, the kept tokens of one route have slots 0, 1, 2, ... in order of position; 64 marks a dropped token or a padding row; on every device some expert fills all 64 slots and drops further tokens.
All inputs are finite; a program needn't handle non-finite values.
Results may differ from a plain program's by a relative error of at most 0.019.
Values may be sent and summed in bfloat16 or wider, within the bound.
A program may use at most 768 MiB of HBM per device.

v0:
```python
from functools import partial

import jax
import jax.numpy as jnp
from jax import lax
from jax.sharding import PartitionSpec as P

CAP = 64
SCAN_BLOCK = 16


def product(left, right):
    return jnp.dot(left, right, preferred_element_type=jnp.float32)


def contract_rows(left, right):
    return lax.dot_general(
        left, right, (((0,), (0,)), ((), ())), preferred_element_type=jnp.float32
    )


def times_transpose(left, right):
    return lax.dot_general(
        left, right, (((1,), (1,)), ((), ())), preferred_element_type=jnp.float32
    )


def gelu_exact(values):
    return jax.nn.gelu(values, approximate=False)


def rms_scale(values, gain_vec):
    return values * lax.rsqrt(jnp.mean(values * values, -1, keepdims=True) + 1e-05) * gain_vec


def conv_front(x_inner, conv_kernel, conv_offset):
    length = x_inner.shape[0]
    tap_count = conv_kernel.shape[0]
    padded = jnp.pad(x_inner, ((tap_count - 1, 0), (0, 0)))
    summed = conv_offset + conv_kernel[0] * padded[0:length]
    for offset in range(1, tap_count):
        summed = summed + conv_kernel[offset] * padded[offset : offset + length]
    return jax.nn.silu(summed)


def block_scan(u_act, step_size, b_mat, c_mat, a_mat):
    length, channels = u_act.shape
    blocks = length // SCAN_BLOCK

    def arrange(values):
        return values.reshape(blocks, SCAN_BLOCK, values.shape[1]).transpose(1, 0, 2)

    seq_u, seq_step, seq_b, seq_c = (
        arrange(u_act),
        arrange(step_size),
        arrange(b_mat),
        arrange(c_mat),
    )

    def advance(carry_state, u_now, step_now, b_now):
        return (
            jnp.exp(step_now[:, :, None] * a_mat[None]) * carry_state
            + (step_now * u_now)[:, :, None] * b_now[:, None, :]
        )

    def local_step(carry_state, inputs):
        return (advance(carry_state, inputs[0], inputs[1], inputs[2]), None)

    zeros_state = jnp.zeros((blocks, channels, a_mat.shape[1]), jnp.float32)
    block_ends, _ = lax.scan(local_step, zeros_state, (seq_u, seq_step, seq_b))
    block_decay = jnp.exp(jnp.sum(seq_step, 0)[:, :, None] * a_mat[None])

    def combine(earlier, later):
        return (earlier[0] * later[0], later[0] * earlier[1] + later[1])

    _, carried = lax.associative_scan(combine, (block_decay, block_ends))
    starts = jnp.concatenate([zeros_state[:1], carried[:-1]], 0)

    def out_step(carry_state, inputs):
        carry_state = advance(carry_state, inputs[0], inputs[1], inputs[2])
        return (carry_state, jnp.sum(carry_state * inputs[3][:, None, :], 2))

    _, scanned = lax.scan(out_step, starts, (seq_u, seq_step, seq_b, seq_c))
    return scanned.transpose(1, 0, 2).reshape(length, channels)


def mixer_tail(step_proj, u_act, b_mat, c_mat, gate_in, step_bias, decay_log, skip_gain):
    step_size = jax.nn.softplus(step_proj + step_bias)
    scanned = block_scan(u_act, step_size, b_mat, c_mat, -jnp.exp(decay_log))
    return (scanned + skip_gain * u_act) * jax.nn.silu(gate_in)


def spread_copies(buffer, experts, split_count):
    slots_each = buffer.shape[0] // experts
    model_width = buffer.shape[1]
    widened = jnp.broadcast_to(
        buffer.reshape(experts, 1, slots_each, model_width),
        (experts, split_count, slots_each, model_width),
    )
    return widened.reshape(experts * split_count, slots_each, model_width)


def expert_forward(received, up_local, down_local, keep_pre):
    pieces, row_count, model_width = received.shape
    flat_rows = received.reshape(pieces * row_count, model_width)
    hidden_pre = product(flat_rows, up_local)
    activated = gelu_exact(hidden_pre).astype(jnp.bfloat16)
    partial_out = (
        product(activated, down_local).astype(jnp.bfloat16).reshape(pieces, row_count, model_width)
    )
    returned = lax.all_to_all(partial_out, "expert", split_axis=0, concat_axis=0, tiled=True)
    return (returned, received, hidden_pre.reshape(pieces, row_count, hidden_pre.shape[1]))


def shards(
    tokens,
    lengths,
    routes,
    slot_index,
    mixer_norm,
    in_weight,
    conv_weight,
    conv_bias,
    scan_weight,
    step_weight,
    step_bias,
    decay_log,
    skip_gain,
    out_weight,
    moe_norm,
    router_weight,
    up_weight,
    down_weight,
    cotangent,
):
    gathered = (
        lax.all_gather(mixer_norm, "expert", axis=0, tiled=True),
        lax.all_gather(in_weight, "expert", axis=1, tiled=True),
        lax.all_gather(conv_weight, "expert", axis=1, tiled=True),
        lax.all_gather(conv_bias, "expert", axis=0, tiled=True),
        lax.all_gather(scan_weight, "expert", axis=0, tiled=True),
        lax.all_gather(step_weight, "expert", axis=1, tiled=True),
        lax.all_gather(step_bias, "expert", axis=0, tiled=True),
        lax.all_gather(decay_log, "expert", axis=0, tiled=True),
        lax.all_gather(skip_gain, "expert", axis=0, tiled=True),
        lax.all_gather(out_weight, "expert", axis=0, tiled=True),
        lax.all_gather(moe_norm, "expert", axis=0, tiled=True),
        lax.all_gather(router_weight, "expert", axis=0, tiled=True),
    )
    (
        norm_first,
        in_full,
        conv_full,
        cbias_full,
        xproj_full,
        dtproj_full,
        dbias_full,
        alog_full,
        skip_full,
        out_full,
        norm_second,
        router_full,
    ) = gathered
    f32 = jnp.float32
    bf16 = jnp.bfloat16
    model_width = tokens.shape[2]
    row_total = tokens.shape[1]
    inner_width = out_full.shape[0]
    dt_rank = dtproj_full.shape[0]
    state_size = alog_full.shape[1]
    experts = router_full.shape[1]
    pieces = lax.axis_size("expert")
    split_count = pieces // experts
    up_local = up_weight[0]
    down_local = down_weight[0]
    tokens_f = tokens[0].astype(f32)
    live_rows = (jnp.arange(row_total, dtype=jnp.int32) < lengths[0]).astype(f32)[:, None]
    normed, norm_back_first = jax.vjp(rms_scale, tokens_f, norm_first.astype(f32))
    normed_low = normed.astype(bf16)
    projected_in = product(normed_low, in_full)
    u_act, conv_back = jax.vjp(
        conv_front, projected_in[:, :inner_width], conv_full.astype(f32), cbias_full.astype(f32)
    )
    u_low = u_act.astype(bf16)
    projected_x = product(u_low, xproj_full)
    dt_low = projected_x[:, :dt_rank].astype(bf16)
    step_proj = product(dt_low, dtproj_full)
    gated_out, tail_back = jax.vjp(
        mixer_tail,
        step_proj,
        u_act,
        projected_x[:, dt_rank : dt_rank + state_size],
        projected_x[:, dt_rank + state_size :],
        projected_in[:, inner_width:],
        dbias_full.astype(f32),
        alog_full.astype(f32),
        skip_full.astype(f32),
    )
    gated_low = gated_out.astype(bf16)
    mid_tokens = tokens_f + product(gated_low, out_full)
    normed_two, norm_back_second = jax.vjp(rms_scale, mid_tokens, norm_second.astype(f32))
    normed_two_low = normed_two.astype(bf16)
    logits = product(normed_two_low, router_full)
    router_probs = jax.nn.softmax(logits, -1)
    chosen = (routes[0][:, None] == jnp.arange(experts, dtype=jnp.int32)[None, :]).astype(f32)
    gate_value = jnp.sum(router_probs * chosen, 1)
    columns = jnp.arange(experts * CAP, dtype=jnp.int32)[None, :]
    dispatch = (
        (routes[0][:, None] == columns // CAP) & (slot_index[0][:, None] == columns % CAP)
    ).astype(bf16)
    wide_columns = jnp.arange(pieces * CAP, dtype=jnp.int32)[None, :]
    collect = (
        (routes[0][:, None] == wide_columns // (split_count * CAP))
        & (slot_index[0][:, None] == wide_columns % CAP)
    ).astype(bf16)
    send_rows = spread_copies(
        contract_rows(dispatch, normed_two_low).astype(bf16), experts, split_count
    )
    forward_pieces = partial(
        expert_forward, up_local=up_local, down_local=down_local, keep_pre=True
    )
    results = forward_pieces(
        lax.all_to_all(send_rows, "expert", split_axis=0, concat_axis=0, tiled=True)
    )
    returned = results[0]
    received_rows = results[1]
    expert_sum = product(collect, returned.reshape(-1, model_width))
    layer_out = (live_rows * (mid_tokens + gate_value[:, None] * expert_sum)).astype(bf16)
    grad_out = cotangent[0].astype(f32) * live_rows
    grad_gate = jnp.sum(grad_out * expert_sum, 1)
    grad_rows_low = (gate_value[:, None] * grad_out).astype(bf16)
    send_grads = spread_copies(
        contract_rows(dispatch, grad_rows_low).astype(bf16), experts, split_count
    )
    got_grads = lax.all_to_all(send_grads, "expert", split_axis=0, concat_axis=0, tiled=True)
    grads_flat = got_grads.reshape(-1, model_width)
    rows_flat = received_rows.reshape(-1, model_width)
    hidden_pre = results[2].reshape(rows_flat.shape[0], -1)
    activated, gelu_back = jax.vjp(gelu_exact, hidden_pre)
    act_low = activated.astype(bf16)
    grad_act = times_transpose(grads_flat, down_local)
    grad_pre = gelu_back(grad_act)[0].astype(bf16)
    grad_up = contract_rows(rows_flat, grad_pre)
    grad_down = contract_rows(act_low, grads_flat)
    grad_rows_in = times_transpose(grad_pre, up_local).astype(bf16).reshape(pieces, -1, model_width)
    back_rows = lax.all_to_all(grad_rows_in, "expert", split_axis=0, concat_axis=0, tiled=True)
    grad_normed_two = product(collect, back_rows.reshape(-1, model_width))
    grad_logits = (
        router_probs * (chosen * grad_gate[:, None] - (gate_value * grad_gate)[:, None])
    ).astype(bf16)
    grad_router = contract_rows(normed_two_low, grad_logits)
    grad_normed_two = grad_normed_two + times_transpose(grad_logits, router_full)
    grad_mid_norm, grad_norm_second = norm_back_second(grad_normed_two)
    grad_mid = grad_mid_norm + grad_out
    grad_mix_low = grad_mid.astype(bf16)
    grad_outw = contract_rows(gated_low, grad_mix_low)
    grad_gated = times_transpose(grad_mix_low, out_full)
    grad_step, grad_u_scan, grad_b, grad_c, grad_gate_in, grad_dbias, grad_alog, grad_skip = (
        tail_back(grad_gated)
    )
    grad_step_low = grad_step.astype(bf16)
    grad_dtw = contract_rows(dt_low, grad_step_low)
    grad_dt_part = times_transpose(grad_step_low, dtproj_full)
    grad_projx_low = jnp.concatenate([grad_dt_part, grad_b, grad_c], 1).astype(bf16)
    grad_xw = contract_rows(u_low, grad_projx_low)
    grad_u = grad_u_scan + times_transpose(grad_projx_low, xproj_full)
    grad_xin, grad_convw, grad_convb = conv_back(grad_u)
    grad_in_low = jnp.concatenate([grad_xin, grad_gate_in], 1).astype(bf16)
    grad_inw = contract_rows(normed_low, grad_in_low)
    grad_normed = times_transpose(grad_in_low, in_full)
    grad_tokens_norm, grad_norm_first = norm_back_first(grad_normed)
    tokens_grad = (grad_mid + grad_tokens_norm)[None]
    shares = (
        lax.psum_scatter(
            grad_norm_first.astype(jnp.bfloat16), "expert", scatter_dimension=0, tiled=True
        ).astype(jnp.float32),
        lax.psum_scatter(
            grad_inw.astype(jnp.bfloat16), "expert", scatter_dimension=1, tiled=True
        ).astype(jnp.float32),
        lax.psum_scatter(
            grad_convw.astype(jnp.bfloat16), "expert", scatter_dimension=1, tiled=True
        ).astype(jnp.float32),
        lax.psum_scatter(
            grad_convb.astype(jnp.bfloat16), "expert", scatter_dimension=0, tiled=True
        ).astype(jnp.float32),
        lax.psum_scatter(
            grad_xw.astype(jnp.bfloat16), "expert", scatter_dimension=0, tiled=True
        ).astype(jnp.float32),
        lax.psum_scatter(
            grad_dtw.astype(jnp.bfloat16), "expert", scatter_dimension=1, tiled=True
        ).astype(jnp.float32),
        lax.psum_scatter(
            grad_dbias.astype(jnp.bfloat16), "expert", scatter_dimension=0, tiled=True
        ).astype(jnp.float32),
        lax.psum_scatter(
            grad_alog.astype(jnp.bfloat16), "expert", scatter_dimension=0, tiled=True
        ).astype(jnp.float32),
        lax.psum_scatter(
            grad_skip.astype(jnp.bfloat16), "expert", scatter_dimension=0, tiled=True
        ).astype(jnp.float32),
        lax.psum_scatter(
            grad_outw.astype(jnp.bfloat16), "expert", scatter_dimension=0, tiled=True
        ).astype(jnp.float32),
        lax.psum_scatter(
            grad_norm_second.astype(jnp.bfloat16), "expert", scatter_dimension=0, tiled=True
        ).astype(jnp.float32),
        lax.psum_scatter(
            grad_router.astype(jnp.bfloat16), "expert", scatter_dimension=0, tiled=True
        ).astype(jnp.float32),
    )
    totals = (
        lax.psum(shares[0].astype(jnp.bfloat16), "dp").astype(jnp.float32),
        lax.psum(shares[1].astype(jnp.bfloat16), "dp").astype(jnp.float32),
        lax.psum(shares[2].astype(jnp.bfloat16), "dp").astype(jnp.float32),
        lax.psum(shares[3].astype(jnp.bfloat16), "dp").astype(jnp.float32),
        lax.psum(shares[4].astype(jnp.bfloat16), "dp").astype(jnp.float32),
        lax.psum(shares[5].astype(jnp.bfloat16), "dp").astype(jnp.float32),
        lax.psum(shares[6].astype(jnp.bfloat16), "dp").astype(jnp.float32),
        lax.psum(shares[7].astype(jnp.bfloat16), "dp").astype(jnp.float32),
        lax.psum(shares[8].astype(jnp.bfloat16), "dp").astype(jnp.float32),
        lax.psum(shares[9].astype(jnp.bfloat16), "dp").astype(jnp.float32),
        lax.psum(shares[10].astype(jnp.bfloat16), "dp").astype(jnp.float32),
        lax.psum(shares[11].astype(jnp.bfloat16), "dp").astype(jnp.float32),
        lax.psum(grad_up.astype(jnp.bfloat16), "dp").astype(jnp.float32),
        lax.psum(grad_down.astype(jnp.bfloat16), "dp").astype(jnp.float32),
    )
    return (
        layer_out[None],
        tokens_grad,
        totals[0],
        totals[1],
        totals[2],
        totals[3],
        totals[4],
        totals[5],
        totals[6],
        totals[7],
        totals[8],
        totals[9],
        totals[10],
        totals[11],
        totals[12][None],
        totals[13][None],
    )


def solution(mesh):
    in_specs = (
        P(("dp", "expert"), None, None),
        P(("dp", "expert")),
        P(("dp", "expert"), None),
        P(("dp", "expert"), None),
        P("expert"),
        P(None, "expert"),
        P(None, "expert"),
        P("expert"),
        P("expert", None),
        P(None, "expert"),
        P("expert"),
        P("expert", None),
        P("expert"),
        P("expert", None),
        P("expert"),
        P("expert", None),
        P("expert", None, None),
        P("expert", None, None),
        P(("dp", "expert"), None, None),
    )
    out_specs = (
        P(("dp", "expert"), None, None),
        P(("dp", "expert"), None, None),
        P("expert"),
        P(None, "expert"),
        P(None, "expert"),
        P("expert"),
        P("expert", None),
        P(None, "expert"),
        P("expert"),
        P("expert", None),
        P("expert"),
        P("expert", None),
        P("expert"),
        P("expert", None),
        P("expert", None, None),
        P("expert", None, None),
    )
    return jax.shard_map(shards, mesh=mesh, in_specs=in_specs, out_specs=out_specs, check_vma=False)
```

profile of v0, /device:TPU:9, one launch (start us, length us, event | category | flops | bytes accessed | tf_op | source)
XLA Modules:
  0.0 2010.9 jit_solution(18006519856308187381)
XLA Ops:
  16.3 22.6 %all-reduce.57 = (bf16[1152]{0:T(1024)(128)(2,1)S(1)}, bf16[2304]{0:T(1024)(128)(2,1)S(1)}, bf16[2304]{0:T(1024)(128)(2,1)S(1)}, bf16[2304]{0:T(1024)(128)(2,1)S(1)}, bf16[1152]{0:T(1024)(128)(2,1)}) all-reduce(bf16[1152]{0:T(1024)(128)(2,1)S(1)} %dynamic-update-slice.1, ...), channel_id=1, replica_groups=mesh['dp'=4,'expert'=8] {'expert'}, use_global_device_ids=true, to_apply=%add.47 | all-reduce | flops 9216 | bytes 36864
  40.3 10.5 all-gather
  51.5 14.5 all_gather.40
  66.6 11.1 all-gather.1
  78.9 9.4 all-gather.2
  112.1 12.7 broadcast.381.clone
  124.8 12.7 broadcast.381.clone.1
  140.9 119.5 %while.96 = (s32[]{:T(128)}, f32[16,2304,16]{1,2,0:T(8,128)S(1)}, f32[16,16,2304,1]{2,1,3,0:T(8,128)}, f32[16,16,2304,16]{2,3,1,0:T(8,128)}, f32[16,16,2304,16]{...) while((s32[]{:T(128)}, f32[16,2304,16]{1,2,0:T(8,128)S(1)}, ...), condition=%wide.region_2.3_spmd.clone, body=%wide.region_1.2_spmd.clone.sunk | while | flops 4202499 | bytes 13881496 | solution.py:70
  300.6 12.7 broadcast.381
  313.4 12.7 broadcast.381.clone.2
  326.1 12.7 broadcast.381.clone.3
  344.3 165.4 %while.95 = (s32[]{:T(128)}, f32[16,2304,16]{1,2,0:T(8,128)S(1)}, f32[16,16,2304]{2,1,0:T(8,128)}, f32[16,16,2304,1]{2,1,3,0:T(8,128)}, f32[16,16,2304,16]{2,3,1...) while((s32[]{:T(128)}, f32[16,2304,16]{1,2,0:T(8,128)S(1)}, ...), condition=%wide.region_6.7_spmd, body=%wide.region_4.6_spmd.sunk | while | flops 4165634 | bytes 16710817 | solution.py:83
  528.3 19.9 all-gather.3
  555.1 20.1 multiply_convert_fusion
  590.8 12.9 add_convert_fusion
  605.3 8.3 fusion.25
  621.5 9.7 all-to-all-done.3
  650.9 160.7 %while.97 = (s32[]{:T(128)}, f32[2304,16]{0,1:T(8,128)S(1)}, f32[16,2304,16]{1,2,0:T(8,128)S(1)}, f32[16,16,2304]{2,1,0:T(8,128)}, f32[16,16,2304]{2,1,0:T(8,128...) while((s32[]{:T(128)}, f32[2304,16]{0,1:T(8,128)S(1)}, ...), condition=%wide.region_19.20_spmd.clone, body=%wide.region_13.19_spmd.clone.sunk | while | flops 9510404 | bytes 19922728 | solution.py:83
  879.4 139.3 %while.98 = (s32[]{:T(128)}, f32[2304,16]{0,1:T(8,128)S(1)}, f32[16,2304,16]{1,2,0:T(8,128)S(1)}, f32[16,16,2304]{2,1,0:T(8,128)}, f32[16,16,2304]{2,1,0:T(8,128...) while((s32[]{:T(128)}, f32[2304,16]{0,1:T(8,128)S(1)}, ...), condition=%wide.region_25.26_spmd.clone, body=%wide.region_20.25_spmd.clone.sunk | while | flops 6561540 | bytes 16978120 | solution.py:70
  1054.8 9.6 multiply_reduce_fusion.13
  1095.8 9.5 fusion.8
  1105.3 8.4 fusion.46
  1113.7 23.1 %all-reduce.56 = (bf16[1152]{0:T(1024)(128)(2,1)S(1)}, bf16[2304]{0:T(1024)(128)(2,1)S(1)}, bf16[2304]{0:T(1024)(128)(2,1)S(1)}, bf16[2304]{0:T(1024)(128)(2,1)S(1)}, bf16[1152]{0:T(1024)(128)(2,1)S(1)}) all-reduce(bf16[1152]{0:T(1024)(128)(2,1)S(1)} %get-tuple-element.974, ...), channel_id=2, replica_groups=mesh['dp'=4,'expert'=8] {'expert'}, use_global_device_ids=true, to_apply=%region_29.30.clone | all-reduce | flops 9216 | bytes 36864
  1142.8 32.5 %reduce-scatter.26.cloned.1.call-done = bf16[288,16]{1,0:T(8,128)(2,1)} async-done(((bf16[2304,16]{1,0:T(8,128)(2,1)}), bf16[288,16]{1,0:T(8,128)(2,1)}) %reduce-scatter.26.cloned.1.call-update) | async-done | bytes 9232
  1176.8 35.8 %reduce-scatter.24.cloned.1.call-done = bf16[288,72]{1,0:T(8,128)(2,1)} async-done(((bf16[2304,72]{1,0:T(8,128)(2,1)}), bf16[288,72]{1,0:T(8,128)(2,1)}) %reduce-scatter.24.cloned.1.call-update) | async-done | bytes 41488
  1214.2 35.9 %reduce-scatter.18.cloned.1.call-done = bf16[288,104]{1,0:T(8,128)(2,1)} async-done(((bf16[2304,104]{1,0:T(8,128)(2,1)}), bf16[288,104]{1,0:T(8,128)(2,1)}) %reduce-scatter.18.cloned.1.call-update) | async-done | bytes 59920 | tf_op jit(solution)/shard_map/reduce_scatter | solution.py:286
  1250.2 9.1 fusion.7
  1259.3 51.7 %reduce-scatter.20.cloned.1.call-done = bf16[288,1152]{1,0:T(8,128)(2,1)} async-done(((bf16[2304,1152]{1,0:T(8,128)(2,1)}), bf16[288,1152]{1,0:T(8,128)(2,1)}) %reduce-scatter.20.cloned.1.call-update) | async-done | bytes 663568 | tf_op jit(solution)/shard_map/reduce_scatter | solution.py:301
  1311.0 86.7 %reduce-scatter.16.cloned.1.call-done = bf16[1152,576]{0,1:T(8,128)(2,1)} async-done(((bf16[1152,4608]{0,1:T(8,128)(2,1)}), bf16[1152,576]{0,1:T(8,128)(2,1)}) %reduce-scatter.16.cloned.1.call-update) | async-done | bytes 1327120 | tf_op jit(solution)/shard_map/reduce_scatter | solution.py:277
  1400.3 36.2 %all-reduce.63.cloned.1.call-done = (bf16[144]{0:T(256)(128)(2,1)}, bf16[4,288]{1,0:T(4,128)(2,1)}, bf16[288]{0:T(512)(128)(2,1)}, bf16[288,104]{1,0:T(8,128)(2,...) async-done(((bf16[144]{0:T(256)(128)(2,1)}, ...) | async-done | bytes 117520 | tf_op jit(solution)/shard_map/psum | solution.py:312
  1449.6 535.3 %all-reduce.65.cloned.1.call-done = (bf16[1152,576]{0,1:T(8,128)(2,1)}, bf16[288,1152]{1,0:T(8,128)(2,1)}, bf16[1,1152,3072]{2,1,0:T(8,128)(2,1)}, bf16[1,3072,1152]{2,1,0:T(8,128)(2,1)}) async-done(((bf16[1152,576]{0,1:T(8,128)(2,1)}, bf16[288,1152]{1,0:T(8,128)(2,1)}, bf16[1,1152,3072]{2,1,0:T(8,128)(2,1)}, bf16[1,3072,1152]{2,1,0:T(8,128)(2,1)}), (bf16[1152,576]{0,1:T(8,128)(2,1)}, ...) | async-done | bytes 16146448 | tf_op jit(solution)/shard_map/psum | solution.py:313
  1984.8 10.3 broadcast_in_dim.144
  (1064 shorter events, 902.2 us)
Async XLA Ops:
  7.2 31.7 %copy-start.39 = (bf16[1,256,1152]{2,1,0:T(8,128)(2,1)S(1)}, bf16[1,256,1152]{2,1,0:T(8,128)(2,1)}, u32[]{:S(2)}) copy-start(bf16[1,256,1152]{2,1,0:T(8,128)(2,1)} %param.27) | copy-start | bytes 1769476
  7.2 33.1 %copy-start.134 = (bf16[4,288]{1,0:T(4,128)(2,1)S(1)}, bf16[4,288]{1,0:T(4,128)(2,1)}, u32[]{:S(2)}) copy-start(bf16[4,288]{1,0:T(4,128)(2,1)} %param.33) | copy-start | bytes 6916
  7.2 44.3 %copy-start.99 = (bf16[288,104]{1,0:T(8,128)(2,1)S(1)}, bf16[288,104]{1,0:T(8,128)(2,1)}, u32[]{:S(2)}) copy-start(bf16[288,104]{1,0:T(8,128)(2,1)} %param.35) | copy-start | bytes 179716
  7.2 59.4 %copy-start.100 = (bf16[72,288]{1,0:T(8,128)(2,1)S(1)}, bf16[72,288]{1,0:T(8,128)(2,1)}, u32[]{:S(2)}) copy-start(bf16[72,288]{1,0:T(8,128)(2,1)} %param.36) | copy-start | bytes 124420
  7.2 82.7 %all-gather.7.cloned.1.call-start = ((), (), s32[]{:S(2)}) async-start(), calls=%async_computation.11 | async-start | bytes 11943936 | tf_op jit(solution)/shard_map/all_gather | solution.py:138
  8.0 509.0 %all-gather.9.cloned.1.call-start = ((), (), s32[]{:S(2)}) async-start(), calls=%async_computation.12 | async-start | bytes 5971968 | tf_op jit(solution)/shard_map/all_gather | solution.py:146
  38.9 51.1 %copy-start.94 = (f32[1152]{0:T(1024)}, f32[1152]{0:T(1024)S(1)}, u32[]{:S(2)}) copy-start(f32[1152]{0:T(1024)S(1)} %convert_element_type.203) | copy-start | bytes 13828
  39.1 49.4 %copy-start.129 = (f32[256]{0:T(256)}, f32[256]{0:T(256)S(1)}, u32[]{:S(2)}) copy-start(f32[256]{0:T(256)S(1)} %fusion.50) | copy-start | bytes 3076
  88.6 171.7 %copy-start.71 = (f32[2304,16]{0,1:T(8,128)}, f32[2304,16]{0,1:T(8,128)S(1)}, u32[]{:S(2)}) copy-start(f32[2304,16]{0,1:T(8,128)S(1)} %get-tuple-element.1204) | copy-start | bytes 442372
  106.9 153.4 %copy-start.69 = (f32[16,2304]{1,0:T(8,128)}, f32[16,2304]{1,0:T(8,128)S(1)}, u32[]{:S(2)}) copy-start(f32[16,2304]{1,0:T(8,128)S(1)} %fusion.98) | copy-start | bytes 442372
  260.3 23.4 %copy-start = (f32[16,2304,16]{1,2,0:T(8,128)}, f32[16,2304,16]{1,2,0:T(8,128)S(1)}, u32[]{:S(2)}) copy-start(f32[16,2304,16]{1,2,0:T(8,128)S(1)} %get-tuple-element.794) | copy-start | bytes 7077892
  522.9 26.4 %copy-start.24 = (bf16[256,1152]{1,0:T(8,128)(2,1)}, bf16[256,1152]{1,0:T(8,128)(2,1)S(1)}, u32[]{:S(2)}) copy-start(bf16[256,1152]{1,0:T(8,128)(2,1)S(1)} %multiply_convert_fusion.3) | copy-start | bytes 1769476
  522.9 26.5 %copy-start.52 = (bf16[1,256,1152]{2,1,0:T(8,128)(2,1)S(1)}, bf16[1,256,1152]{2,1,0:T(8,128)(2,1)}, u32[]{:S(2)}) copy-start(bf16[1,256,1152]{2,1,0:T(8,128)(2,1)} %param.45) | copy-start | bytes 1769476
  524.7 26.5 %all-to-all-start = ((bf16[8,64,1152]{2,1,0:T(8,128)(2,1)}), bf16[8,64,1152]{2,1,0:T(8,128)(2,1)S(1)}, u32[]{:S(2)}, u32[]{:S(2)}) async-start(bf16[8,64,1152]{2,1,0:T(8,128)(2,1)} %bitcast.35), calls=%async_computation | async-start | bytes 2359296 | tf_op jit(solution)/shard_map/all_to_all | solution.py:223
  549.3 83.8 %copy-start.117 = (f32[256]{0:T(256)}, f32[256]{0:T(256)S(1)}, u32[]{:S(2)}) copy-start(f32[256]{0:T(256)S(1)} %get-tuple-element.1215) | copy-start | bytes 3076
  549.4 83.8 %copy-start.122 = (f32[256]{0:T(256)}, f32[256]{0:T(256)S(1)}, u32[]{:S(2)}) copy-start(f32[256]{0:T(256)S(1)} %fusion.84) | copy-start | bytes 3076
  551.2 24.0 %copy-start.76 = (bf16[8,64,1152]{2,1,0:T(8,128)(2,1)}, bf16[8,64,1152]{2,1,0:T(8,128)(2,1)S(1)}, u32[]{:S(2)}) copy-start(bf16[8,64,1152]{2,1,0:T(8,128)(2,1)S(1)} %all-to-all-done) | copy-start | bytes 3538948
  551.2 34.0 %all-to-all-start.2 = ((bf16[8,64,1152]{2,1,0:T(8,128)(2,1)}), bf16[8,64,1152]{2,1,0:T(8,128)(2,1)S(1)}, u32[]{:S(2)}, u32[]{:S(2)}) async-start(bf16[8,64,1152]{2,1,0:T(8,128)(2,1)} %bitcast.350), calls=%async_computation.2 | async-start | bytes 2359296 | tf_op jit(solution)/shard_map/all_to_all | solution.py:235
  586.2 27.4 %all-to-all-start.1 = ((bf16[8,64,1152]{2,1,0:T(8,128)(2,1)}), bf16[8,64,1152]{2,1,0:T(8,128)(2,1)S(1)}, u32[]{:S(2)}, u32[]{:S(2)}) async-start(bf16[8,64,1152]{2,1,0:T(8,128)(2,1)} %bitcast.39), calls=%async_computation.1 | async-start | bytes 2359296 | tf_op jit(solution)/shard_map/all_to_all | solution.py:111
  613.6 17.6 all-to-all-start.3
  617.9 522.0 %reduce-scatter.22.cloned.1.call-start = ((), (), s32[]{:S(2)}) async-start(), calls=%async_computation.16 | async-start | bytes 663552
  621.5 12.8 copy-start.120
  621.5 12.8 copy-start.127
  1054.7 11.0 copy-start.25
  1065.7 75.7 %reduce-scatter.28.cloned.1.call-start = ((), (), s32[]{:S(2)}) async-start(), calls=%async_computation.19 | async-start | bytes 331776
  1066.9 108.4 %reduce-scatter.26.cloned.1.call-start = ((), (), s32[]{:S(2)}) async-start(), calls=%async_computation.18 | async-start | bytes 663552
  1070.9 141.8 %reduce-scatter.24.cloned.1.call-start = ((), (), s32[]{:S(2)}) async-start(), calls=%async_computation.17 | async-start | bytes 663552
  1075.1 175.1 %reduce-scatter.18.cloned.1.call-start = ((), (), s32[]{:S(2)}) async-start(), calls=%async_computation.14 | async-start | bytes 663552 | tf_op jit(solution)/shard_map/reduce_scatter | solution.py:286
  1077.2 233.7 %reduce-scatter.20.cloned.1.call-start = ((), (), s32[]{:S(2)}) async-start(), calls=%async_computation.15 | async-start | bytes 5971968 | tf_op jit(solution)/shard_map/reduce_scatter | solution.py:301
  1083.2 314.5 %reduce-scatter.16.cloned.1.call-start = ((), (), s32[]{:S(2)}) async-start(), calls=%async_computation.13 | async-start | bytes 11943936 | tf_op jit(solution)/shard_map/reduce_scatter | solution.py:277
  1094.4 342.1 %all-reduce.63.cloned.1.call-start = ((), (), s32[]{:S(2)}) async-start(), calls=%async_computation.20 | async-start | bytes 305152 | tf_op jit(solution)/shard_map/psum | solution.py:312
  1250.2 734.7 %all-reduce.65.cloned.1.call-start = ((), (), s32[]{:S(2)}) async-start(), calls=%async_computation.21 | async-start | bytes 32292864 | tf_op jit(solution)/shard_map/psum | solution.py:313
  (153 other events, 542.5 us)
Sparse Core Ops, SparseCore 0:
  9.9 69.7 all-gather.6
  81.7 41.3 all-gather.8
  1065.8 36.1 reduce-scatter.21
  1104.9 32.9 reduce-scatter.27
  1140.9 34.3 reduce-scatter.25
  1178.2 34.3 reduce-scatter.23
  1215.8 34.3 reduce-scatter.17
  1253.6 57.3 reduce-scatter.19
  1315.5 82.1 reduce-scatter.15
  1402.2 34.3 all-reduce.62
  1440.0 544.7 all-reduce.64
where the time goes:
time: 2030 us; the launch traced here: 2010 us
  waiting for transfers between devices  825 us (41%)
  other arithmetic  535 us (26%)
  local copies, waits for them, and re-layouts  365 us (18%)
  matrix products  135 us (7%)
  blocking collectives  111 us (5%)
    psum x1, waiting for transfers between devices, shards(): lax.psum(shares[1].astype(jnp.bfloat16), 'dp').astype(jnp.float32)  535 us
    dynamic_update_slice x64, other arithmetic, block_scan(): block_ends, _ = lax.scan(local_step, zeros_state, (seq_u, seq_step, seq_b))  151 us
    reduce_sum x32, other arithmetic, advance(): (step_now * u_now)[:, :, None] * b_now[:, None, :]  151 us
    reduce_scatter x1, waiting for transfers between devices, shards(): lax.psum_scatter(grad_inw.astype(jnp.bfloat16), 'expert', scatter_dimensi...  86.7 us
    another operation x19, local copies, waits for them, and re-layouts  79.3 us
    unnamed x15, waiting for transfers between devices  69.8 us
    pad x23, local copies, waits for them, and re-layouts, block_scan(): _, carried = lax.associative_scan(combine, (block_decay, block_ends))  66.5 us
    dynamic_update_slice x32, other arithmetic, block_scan(): _, scanned = lax.scan(out_step, starts, (seq_u, seq_step, seq_b, seq_c))  56.1 us
  transfers between devices with their start and end apart: 15, of which 8 were waited for; matrix products, arithmetic and copies ran while one was open for 28% of the time, Pallas kernels for 0%

commit v1 on v0

v1 whole, which is shorter than its diff:
```python
from functools import partial

import jax
import jax.numpy as jnp
from jax import lax
from jax.experimental import pallas as pl
from jax.experimental.pallas import tpu as pltpu
from jax.sharding import PartitionSpec as P

CAP = 64
BLOCK = 16
LOG2E = 1.4426950408889634
F32 = jnp.float32
BF16 = jnp.bfloat16
VMEM_LIMIT = 56 * 1024 * 1024


def product(left, right):
    return jnp.dot(left, right, preferred_element_type=F32)


def contract_rows(left, right):
    return lax.dot_general(left, right, (((0,), (0,)), ((), ())), preferred_element_type=F32)


def times_transpose(left, right):
    return lax.dot_general(left, right, (((1,), (1,)), ((), ())), preferred_element_type=F32)


def exact_product(left, right):
    return jnp.dot(left, right, preferred_element_type=F32, precision=lax.Precision.HIGHEST)


def iota(shape, axis):
    return lax.broadcasted_iota(jnp.int32, shape, axis)


def sigmoid(values):
    return 1.0 / (1.0 + jnp.exp(-values))


def softplus(values):
    return jnp.maximum(values, 0.0) + jnp.log1p(jnp.exp(-jnp.abs(values)))


def shift_rows(values, offset):
    rows = values.shape[0]
    if offset == 0:
        return values
    rolled = pltpu.roll(values, offset % rows, 0)
    row = iota(values.shape, 0)
    keep = row >= offset if offset > 0 else row < rows + offset
    return jnp.where(keep, rolled, 0.0)


def two_parts(values):
    high = values.astype(BF16)
    low = (values - high.astype(F32)).astype(BF16)
    return high, low


def spread_rows(proj_block, first, state):
    rows, width = proj_block.shape
    big = rows * state
    pick = (iota((big, rows), 0) // state == iota((big, rows), 1)).astype(F32)
    copied = exact_product(pick, proj_block)
    lane = iota((big, width), 1)
    own = lane == first + iota((big, width), 0) % state
    column = jnp.sum(jnp.where(own, copied, 0.0), axis=1, keepdims=True)
    return jnp.broadcast_to(column, (big, 128))


def diagonal_blocks(proj_block, first, state):
    rows, width = proj_block.shape
    big = rows * state
    place = (iota((width, big), 0) == first + iota((width, big), 1) % state).astype(BF16)
    own = iota((rows, big), 0) == iota((rows, big), 1) // state
    parts = [
        jnp.where(own, product(part, place), 0.0).astype(BF16) for part in two_parts(proj_block)
    ]
    return jnp.concatenate(parts, 0)


def front_kernel(
    tokens_ref, gain_ref, wx_ref, wg_ref, conv_ref, bias_ref, scanw_ref,
    normed_ref, xin_ref, u_ref, gate_ref, proj_ref,
):
    step = pl.program_id(0)

    @pl.when(step == 0)
    def _():
        values = tokens_ref[...].astype(F32)
        scale = lax.rsqrt(jnp.mean(values * values, -1, keepdims=True) + 1e-05)
        normed_ref[...] = (values * scale * gain_ref[...]).astype(BF16)
        proj_ref[...] = jnp.zeros_like(proj_ref)

    normed = normed_ref[...]
    x_inner = times_transpose(normed, wx_ref[...])
    gate_ref[...] = times_transpose(normed, wg_ref[...])
    xin_ref[...] = x_inner
    taps = conv_ref.shape[0]
    summed = bias_ref[...] + conv_ref[taps - 1 : taps, :] * x_inner
    for back in range(1, taps):
        tap = taps - 1 - back
        summed = summed + conv_ref[tap : tap + 1, :] * shift_rows(x_inner, back)
    u_act = summed * sigmoid(summed)
    u_ref[...] = u_act
    proj_ref[...] += product(u_act.astype(BF16), scanw_ref[...])


def front(tokens, gain, in_t, conv, bias, scan_w, tile):
    rows, width = tokens.shape
    channels = scan_w.shape[0]
    cols = scan_w.shape[1]
    steps = channels // tile
    return pl.pallas_call(
        front_kernel,
        grid=(steps,),
        in_specs=[
            pl.BlockSpec((rows, width), lambda i: (0, 0)),
            pl.BlockSpec((1, width), lambda i: (0, 0)),
            pl.BlockSpec((tile, width), lambda i: (i, 0)),
            pl.BlockSpec((tile, width), lambda i: (i + steps, 0)),
            pl.BlockSpec((conv.shape[0], tile), lambda i: (0, i)),
            pl.BlockSpec((1, tile), lambda i: (0, i)),
            pl.BlockSpec((tile, cols), lambda i: (i, 0)),
        ],
        out_specs=[
            pl.BlockSpec((rows, width), lambda i: (0, 0)),
            pl.BlockSpec((rows, tile), lambda i: (0, i)),
            pl.BlockSpec((rows, tile), lambda i: (0, i)),
            pl.BlockSpec((rows, tile), lambda i: (0, i)),
            pl.BlockSpec((rows, cols), lambda i: (0, 0)),
        ],
        out_shape=[
            jax.ShapeDtypeStruct((rows, width), BF16),
            jax.ShapeDtypeStruct((rows, channels), F32),
            jax.ShapeDtypeStruct((rows, channels), F32),
            jax.ShapeDtypeStruct((rows, channels), F32),
            jax.ShapeDtypeStruct((rows, cols), F32),
        ],
        compiler_params=pltpu.CompilerParams(vmem_limit_bytes=VMEM_LIMIT),
        name="mixer_front",
    )(tokens, gain, in_t, in_t, conv, bias, scan_w)


def scan_kernel(
    proj_ref, stepw_ref, dbias_ref, decay_ref, skip_ref, u_ref, gate_ref, outw_ref, tokens_ref,
    step_ref, mixed_ref, gated_ref, hist_ref, mid_ref,
    b_wide, c_blocks, du, scanned,
):
    tile_id = pl.program_id(0)
    rank = stepw_ref.shape[0]
    state = decay_ref.shape[0]
    rows = u_ref.shape[0]
    blocks = rows // BLOCK
    big = BLOCK * state

    @pl.when(tile_id == 0)
    def _():
        mid_ref[...] = tokens_ref[...].astype(F32)

        def build(block, carry):
            part = proj_ref[pl.ds(pl.multiple_of(block * BLOCK, BLOCK), BLOCK), :]
            b_wide[pl.ds(pl.multiple_of(block * big, big), big), :] = spread_rows(part, rank, state)
            c_blocks[pl.ds(pl.multiple_of(block * 2 * BLOCK, 2 * BLOCK), 2 * BLOCK), :] = (
                diagonal_blocks(part, rank + state, state)
            )
            return carry

        lax.fori_loop(0, blocks, build, 0)

    u_act = u_ref[...]
    step_size = softplus(
        product(proj_ref[:, :rank].astype(BF16), stepw_ref[...]) + dbias_ref[...]
    )
    step_ref[...] = step_size
    du[...] = step_size * u_act
    decay = decay_ref[...] * LOG2E
    tile = u_act.shape[1]
    hist_ref[0:state, :] = jnp.zeros((state, tile), BF16)

    def run_block(block, held):
        base = pl.multiple_of(block * BLOCK, BLOCK)
        steps_now = step_ref[pl.ds(base, BLOCK), :]
        du_now = du[pl.ds(base, BLOCK), :]
        wide_base = pl.multiple_of(block * big, big)
        for t in range(BLOCK):
            b_now = b_wide[pl.ds(wide_base + t * state, state), :]
            fade = jnp.exp2(steps_now[t : t + 1, :] * decay)
            fresh = du_now[t : t + 1, :] * jnp.concatenate([b_now] * (tile // 128), 1)
            held = fade * held + fresh
            hist_ref[pl.ds(wide_base + (t + 1) * state, state), :] = held.astype(BF16)
        weights = c_blocks[pl.ds(pl.multiple_of(block * 2 * BLOCK, 2 * BLOCK), 2 * BLOCK), :]
        both = product(weights, hist_ref[pl.ds(wide_base + state, big), :])
        scanned[pl.ds(base, BLOCK), :] = both[:BLOCK] + both[BLOCK:]
        return held

    lax.fori_loop(0, blocks, run_block, jnp.zeros((state, tile), F32))
    mixed = scanned[...] + skip_ref[...] * u_act
    mixed_ref[...] = mixed
    gate_in = gate_ref[...]
    gated = (mixed * (gate_in * sigmoid(gate_in))).astype(BF16)
    gated_ref[...] = gated
    mid_ref[...] += product(gated, outw_ref[...])


def scan_forward(proj, step_w, dbias, decay, skip, u_act, gate_in, out_w, tokens, tile):
    rows, channels = u_act.shape
    width = tokens.shape[1]
    cols = proj.shape[1]
    rank, state = step_w.shape[0], decay.shape[0]
    steps = channels // tile
    hist_rows = (rows + 1) * state
    column = lambda i: (0, i)
    fixed = lambda i: (0, 0)
    return pl.pallas_call(
        scan_kernel,
        grid=(steps,),
        in_specs=[
            pl.BlockSpec((rows, cols), fixed),
            pl.BlockSpec((rank, tile), column),
            pl.BlockSpec((1, tile), column),
            pl.BlockSpec((state, tile), column),
            pl.BlockSpec((1, tile), column),
            pl.BlockSpec((rows, tile), column),
            pl.BlockSpec((rows, tile), column),
            pl.BlockSpec((tile, width), lambda i: (i, 0)),
            pl.BlockSpec((rows, width), fixed),
        ],
        out_specs=[
            pl.BlockSpec((rows, tile), column),
            pl.BlockSpec((rows, tile), column),
            pl.BlockSpec((rows, tile), column),
            pl.BlockSpec((hist_rows, tile), column),
            pl.BlockSpec((rows, width), fixed),
        ],
        out_shape=[
            jax.ShapeDtypeStruct((rows, channels), F32),
            jax.ShapeDtypeStruct((rows, channels), F32),
            jax.ShapeDtypeStruct((rows, channels), BF16),
            jax.ShapeDtypeStruct((hist_rows, channels), BF16),
            jax.ShapeDtypeStruct((rows, width), F32),
        ],
        scratch_shapes=[
            pltpu.VMEM((rows * state, 128), F32),
            pltpu.VMEM((rows * 2, BLOCK * state), BF16),
            pltpu.VMEM((rows, tile), F32),
            pltpu.VMEM((rows, tile), F32),
        ],
        compiler_params=pltpu.CompilerParams(vmem_limit_bytes=VMEM_LIMIT),
        name="scan_forward",
    )(proj, step_w, dbias, decay, skip, u_act, gate_in, out_w, tokens)


def scan_back_kernel(
    proj_ref, stepw_ref, dbias_ref, decay_ref, skip_ref, u_ref, gate_ref, outw_ref, gradmix_ref,
    step_ref, mixed_ref, hist_ref,
    gradu_ref, gradgate_ref, gradstepw_ref, gradbias_ref, gradskip_ref, gradlog_ref, gradproj_ref,
    c_wide, b_blocks, b_sums, c_sums, gy, du, g_hist, w_hist, grad_du, grad_step,
):
    tile_id = pl.program_id(0)
    cols, rank = proj_ref.shape[1], stepw_ref.shape[0]
    state = decay_ref.shape[0]
    rows, tile = u_ref.shape
    blocks = rows // BLOCK
    big = BLOCK * state

    @pl.when(tile_id == 0)
    def _():
        gradproj_ref[...] = jnp.zeros_like(gradproj_ref)
        b_sums[...] = jnp.zeros_like(b_sums)
        c_sums[...] = jnp.zeros_like(c_sums)

        def build(block, carry):
            part = proj_ref[pl.ds(pl.multiple_of(block * BLOCK, BLOCK), BLOCK), :]
            c_wide[pl.ds(pl.multiple_of(block * big, big), big), :] = spread_rows(
                part, rank + state, state
            )
            b_blocks[pl.ds(pl.multiple_of(block * 2 * BLOCK, 2 * BLOCK), 2 * BLOCK), :] = (
                diagonal_blocks(part, rank, state)
            )
            return carry

        lax.fori_loop(0, blocks, build, 0)

    grad_gated = times_transpose(gradmix_ref[...], outw_ref[...])
    gate_in = gate_ref[...]
    gate_sig = sigmoid(gate_in)
    grad_mixed = grad_gated * (gate_in * gate_sig)
    gradgate_ref[...] = (
        grad_gated * mixed_ref[...] * (gate_sig * (1.0 + gate_in * (1.0 - gate_sig)))
    ).astype(BF16)
    u_act = u_ref[...]
    step_size = step_ref[...]
    gy[...] = grad_mixed
    du[...] = step_size * u_act
    gradskip_ref[...] = jnp.sum(grad_mixed * u_act, 0, keepdims=True)
    rate = decay_ref[...]
    decay = rate * LOG2E
    sums = (iota((BLOCK, big), 0) == iota((BLOCK, big), 1) // state).astype(BF16)

    def run_block(turn, carry):
        carried, log_sum = carry
        block = blocks - 1 - turn
        base = pl.multiple_of(block * BLOCK, BLOCK)
        wide_base = pl.multiple_of(block * big, big)
        steps_now = step_ref[pl.ds(base, BLOCK), :]
        gy_now = gy[pl.ds(base, BLOCK), :]
        for t in range(BLOCK - 1, -1, -1):
            c_now = c_wide[pl.ds(wide_base + t * state, state), :]
            step_now = steps_now[t : t + 1, :]
            fade = jnp.exp2(step_now * decay)
            grad = gy_now[t : t + 1, :] * jnp.concatenate([c_now] * (tile // 128), 1) + carried
            g_hist[t * state : (t + 1) * state, :] = grad.astype(BF16)
            carried = fade * grad
            before = hist_ref[pl.ds(wide_base + t * state, state), :].astype(F32)
            weighted = carried * before * rate
            w_hist[t * state : (t + 1) * state, :] = weighted.astype(BF16)
            log_sum = log_sum + weighted * step_now
        grads = g_hist[...]
        both = product(
            b_blocks[pl.ds(pl.multiple_of(block * 2 * BLOCK, 2 * BLOCK), 2 * BLOCK), :], grads
        )
        grad_du[pl.ds(base, BLOCK), :] = both[:BLOCK] + both[BLOCK:]
        grad_step[pl.ds(base, BLOCK), :] = product(sums, w_hist[...])
        b_sums[pl.ds(base, BLOCK), :] += times_transpose(
            du[pl.ds(base, BLOCK), :].astype(BF16), grads
        )
        c_sums[pl.ds(base, BLOCK), :] += times_transpose(
            gy_now.astype(BF16), hist_ref[pl.ds(wide_base + state, big), :]
        )
        return carried, log_sum

    zeros = jnp.zeros((state, tile), F32)
    _, log_sum = lax.fori_loop(0, blocks, run_block, (zeros, zeros))
    gradlog_ref[...] = log_sum
    full_du = grad_du[...]
    gradu_ref[...] = full_du * step_size + skip_ref[...] * gy[...]
    grad_size = grad_step[...] + full_du * u_act
    grad_pre = grad_size * (1.0 - jnp.exp(-step_size))
    gradbias_ref[...] = jnp.sum(grad_pre, 0, keepdims=True)
    grad_low = grad_pre.astype(BF16)
    gradstepw_ref[...] = contract_rows(proj_ref[:, :rank].astype(BF16), grad_low)
    gradproj_ref[:, :rank] += times_transpose(grad_low, stepw_ref[...])

    @pl.when(tile_id == pl.num_programs(0) - 1)
    def _():
        own = iota((rows, big), 0) % BLOCK == iota((rows, big), 1) // state
        lane = iota((big, cols), 1)
        slot = iota((big, cols), 0) % state
        total = gradproj_ref[...]
        for sums_ref, first in ((b_sums, rank), (c_sums, rank + state)):
            place = (lane == first + slot).astype(F32)
            total = total + exact_product(jnp.where(own, sums_ref[...], 0.0), place)
        gradproj_ref[...] = total


def scan_backward(
    proj, step_w, dbias, decay, skip, u_act, gate_in, out_w, grad_mix, step_size, mixed, hist, tile
):
    rows, channels = u_act.shape
    width = grad_mix.shape[1]
    cols = proj.shape[1]
    rank, state = step_w.shape[0], decay.shape[0]
    steps = channels // tile
    big = BLOCK * state
    column = lambda i: (0, i)
    fixed = lambda i: (0, 0)
    return pl.pallas_call(
        scan_back_kernel,
        grid=(steps,),
        in_specs=[
            pl.BlockSpec((rows, cols), fixed),
            pl.BlockSpec((rank, tile), column),
            pl.BlockSpec((1, tile), column),
            pl.BlockSpec((state, tile), column),
            pl.BlockSpec((1, tile), column),
            pl.BlockSpec((rows, tile), column),
            pl.BlockSpec((rows, tile), column),
            pl.BlockSpec((tile, width), lambda i: (i, 0)),
            pl.BlockSpec((rows, width), fixed),
            pl.BlockSpec((rows, tile), column),
            pl.BlockSpec((rows, tile), column),
            pl.BlockSpec((hist.shape[0], tile), column),
        ],
        out_specs=[
            pl.BlockSpec((rows, tile), column),
            pl.BlockSpec((rows, tile), column),
            pl.BlockSpec((rank, tile), column),
            pl.BlockSpec((1, tile), column),
            pl.BlockSpec((1, tile), column),
            pl.BlockSpec((state, tile), column),
            pl.BlockSpec((rows, cols), fixed),
        ],
        out_shape=[
            jax.ShapeDtypeStruct((rows, channels), F32),
            jax.ShapeDtypeStruct((rows, channels), BF16),
            jax.ShapeDtypeStruct((rank, channels), F32),
            jax.ShapeDtypeStruct((1, channels), F32),
            jax.ShapeDtypeStruct((1, channels), F32),
            jax.ShapeDtypeStruct((state, channels), F32),
            jax.ShapeDtypeStruct((rows, cols), F32),
        ],
        scratch_shapes=[
            pltpu.VMEM((rows * state, 128), F32),
            pltpu.VMEM((rows * 2, big), BF16),
            pltpu.VMEM((rows, big), F32),
            pltpu.VMEM((rows, big), F32),
            pltpu.VMEM((rows, tile), F32),
            pltpu.VMEM((rows, tile), F32),
            pltpu.VMEM((big, tile), BF16),
            pltpu.VMEM((big, tile), BF16),
            pltpu.VMEM((rows, tile), F32),
            pltpu.VMEM((rows, tile), F32),
        ],
        compiler_params=pltpu.CompilerParams(vmem_limit_bytes=VMEM_LIMIT),
        name="scan_backward",
    )(proj, step_w, dbias, decay, skip, u_act, gate_in, out_w, grad_mix, step_size, mixed, hist)


def back_kernel(
    gradproj_ref, scanw_ref, gradu_ref, xin_ref, conv_ref, bias_ref, gradgate_ref, wx_ref, wg_ref,
    u_ref, tokens_ref, gain_ref, gradmid_ref,
    gradx_ref, gradconv_ref, gradbias_ref, gradscanw_ref, gradtok_ref, gradgain_ref,
    total,
):
    tile_id = pl.program_id(0)

    @pl.when(tile_id == 0)
    def _():
        total[...] = jnp.zeros_like(total)

    grad_proj = gradproj_ref[...].astype(BF16)
    grad_u = gradu_ref[...] + times_transpose(grad_proj, scanw_ref[...])
    gradscanw_ref[...] = contract_rows(u_ref[...].astype(BF16), grad_proj)
    x_inner = xin_ref[...]
    taps = conv_ref.shape[0]
    shifted = [shift_rows(x_inner, taps - 1 - tap) for tap in range(taps)]
    summed = bias_ref[...]
    for tap in range(taps):
        summed = summed + conv_ref[tap : tap + 1, :] * shifted[tap]
    sig = sigmoid(summed)
    grad_sum = grad_u * (sig * (1.0 + summed * (1.0 - sig)))
    gradbias_ref[...] = jnp.sum(grad_sum, 0, keepdims=True)
    grad_x = jnp.zeros_like(x_inner)
    for tap in range(taps):
        gradconv_ref[tap : tap + 1, :] = jnp.sum(grad_sum * shifted[tap], 0, keepdims=True)
        grad_x = grad_x + conv_ref[tap : tap + 1, :] * shift_rows(grad_sum, tap + 1 - taps)
    grad_x = grad_x.astype(BF16)
    gradx_ref[...] = grad_x
    total[...] += product(grad_x, wx_ref[...]) + product(gradgate_ref[...], wg_ref[...])

    @pl.when(tile_id == pl.num_programs(0) - 1)
    def _():
        values = tokens_ref[...].astype(F32)
        scale = lax.rsqrt(jnp.mean(values * values, -1, keepdims=True) + 1e-05)
        unit = values * scale
        grad = total[...]
        gradgain_ref[...] = jnp.sum(grad * unit, 0, keepdims=True)
        inner = grad * gain_ref[...]
        gradtok_ref[...] = gradmid_ref[...] + scale * (
            inner - unit * jnp.mean(inner * unit, -1, keepdims=True)
        )


def mixer_back(
    grad_proj, scan_w, grad_u, x_inner, conv, bias, grad_gate, in_t, u_act, tokens, gain, grad_mid,
    tile,
):
    rows, channels = u_act.shape
    width = tokens.shape[1]
    cols = scan_w.shape[1]
    taps = conv.shape[0]
    steps = channels // tile
    column = lambda i: (0, i)
    fixed = lambda i: (0, 0)
    return pl.pallas_call(
        back_kernel,
        grid=(steps,),
        in_specs=[
            pl.BlockSpec((rows, cols), fixed),
            pl.BlockSpec((tile, cols), lambda i: (i, 0)),
            pl.BlockSpec((rows, tile), column),
            pl.BlockSpec((rows, tile), column),
            pl.BlockSpec((taps, tile), column),
            pl.BlockSpec((1, tile), column),
            pl.BlockSpec((rows, tile), column),
            pl.BlockSpec((tile, width), lambda i: (i, 0)),
            pl.BlockSpec((tile, width), lambda i: (i + steps, 0)),
            pl.BlockSpec((rows, tile), column),
            pl.BlockSpec((rows, width), fixed),
            pl.BlockSpec((1, width), fixed),
            pl.BlockSpec((rows, width), fixed),
        ],
        out_specs=[
            pl.BlockSpec((rows, tile), column),
            pl.BlockSpec((taps, tile), column),
            pl.BlockSpec((1, tile), column),
            pl.BlockSpec((tile, cols), lambda i: (i, 0)),
            pl.BlockSpec((rows, width), fixed),
            pl.BlockSpec((1, width), fixed),
        ],
        out_shape=[
            jax.ShapeDtypeStruct((rows, channels), BF16),
            jax.ShapeDtypeStruct((taps, channels), F32),
            jax.ShapeDtypeStruct((1, channels), F32),
            jax.ShapeDtypeStruct((channels, cols), F32),
            jax.ShapeDtypeStruct((rows, width), F32),
            jax.ShapeDtypeStruct((1, width), F32),
        ],
        scratch_shapes=[pltpu.VMEM((rows, width), F32)],
        compiler_params=pltpu.CompilerParams(vmem_limit_bytes=VMEM_LIMIT),
        name="mixer_back",
    )(
        grad_proj, scan_w, grad_u, x_inner, conv, bias, grad_gate, in_t, in_t, u_act, tokens, gain,
        grad_mid,
    )


def gelu_parts(values):
    weight = jnp.exp(values * values * -0.5)
    scaled = jnp.abs(values) * 0.7071067811865476
    ratio = 1.0 / (1.0 + 0.3275911 * scaled)
    series = 1.061405429 * ratio - 1.453152027
    series = series * ratio + 1.421413741
    series = series * ratio - 0.284496736
    series = series * ratio + 0.254829592
    tail = (0.5 * ratio) * series * weight
    below = jnp.where(values >= 0.0, 1.0 - tail, tail)
    return values * below, below + values * weight * 0.3989422804014327


def router_kernel(
    mid_ref, gain_ref, router_ref, routes_col_ref, routes_row_ref, slots_row_ref, live_ref, cot_ref,
    send_ref, normed_ref, probs_ref,
):
    mid = mid_ref[...]
    rows = mid.shape[0]
    experts = router_ref.shape[1]
    scale = lax.rsqrt(jnp.mean(mid * mid, -1, keepdims=True) + 1e-05)
    normed = (mid * scale * gain_ref[...]).astype(BF16)
    normed_ref[...] = normed
    logits = product(normed, router_ref[...])
    weights = jnp.exp(logits - jnp.max(logits, -1, keepdims=True))
    probs = weights / jnp.sum(weights, -1, keepdims=True)
    probs_ref[...] = probs
    chosen = (routes_col_ref[...] == iota((rows, experts), 1)).astype(F32)
    gate = jnp.sum(probs * chosen, 1, keepdims=True)
    grads = (gate * (cot_ref[...].astype(F32) * live_ref[...])).astype(BF16)
    slot = iota((experts * CAP, rows), 0)
    dispatch = (
        (routes_row_ref[...] == slot // CAP) & (slots_row_ref[...] == slot % CAP)
    ).astype(BF16)
    width = mid.shape[1]
    send_ref[:, :CAP, :] = product(dispatch, normed).astype(BF16).reshape(experts, CAP, width)
    send_ref[:, CAP:, :] = product(dispatch, grads).astype(BF16).reshape(experts, CAP, width)


def router_step(mid, gain, router, routes_col, routes_row, slots_row, live, cotangent):
    rows, width = mid.shape
    experts = router.shape[1]
    return pl.pallas_call(
        router_kernel,
        out_shape=[
            jax.ShapeDtypeStruct((experts, 2 * CAP, width), BF16),
            jax.ShapeDtypeStruct((rows, width), BF16),
            jax.ShapeDtypeStruct((rows, experts), F32),
        ],
        compiler_params=pltpu.CompilerParams(vmem_limit_bytes=VMEM_LIMIT),
        name="router_step",
    )(mid, gain, router, routes_col, routes_row, slots_row, live, cotangent)


def expert_kernel(got_ref, up_ref, down_ref, back_ref, out_sum, in_sum):
    step = pl.program_id(0)
    pieces, double, width = got_ref.shape
    rows = got_ref[:, :CAP, :].reshape(pieces * CAP, width)
    grads = got_ref[:, CAP:, :].reshape(pieces * CAP, width)

    @pl.when(step == 0)
    def _():
        out_sum[...] = jnp.zeros_like(out_sum)
        in_sum[...] = jnp.zeros_like(in_sum)

    activated, slope = gelu_parts(product(rows, up_ref[...]))
    out_sum[...] += product(activated.astype(BF16), down_ref[...])
    grad_pre = (times_transpose(grads, down_ref[...]) * slope).astype(BF16)
    in_sum[...] += times_transpose(grad_pre, up_ref[...])

    @pl.when(step == pl.num_programs(0) - 1)
    def _():
        back_ref[:, :CAP, :] = out_sum[...].astype(BF16).reshape(pieces, CAP, width)
        back_ref[:, CAP:, :] = in_sum[...].astype(BF16).reshape(pieces, CAP, width)


def expert_step(got, up, down, tile):
    pieces, double, width = got.shape
    hidden = up.shape[1]
    fixed = lambda i: (0, 0, 0)
    return pl.pallas_call(
        expert_kernel,
        grid=(hidden // tile,),
        in_specs=[
            pl.BlockSpec(got.shape, fixed),
            pl.BlockSpec((width, tile), lambda i: (0, i)),
            pl.BlockSpec((tile, width), lambda i: (i, 0)),
        ],
        out_specs=pl.BlockSpec(got.shape, fixed),
        out_shape=jax.ShapeDtypeStruct(got.shape, BF16),
        scratch_shapes=[pltpu.VMEM((pieces * CAP, width), F32)] * 2,
        compiler_params=pltpu.CompilerParams(vmem_limit_bytes=VMEM_LIMIT),
        name="expert_step",
    )(got, up, down)


def expert_grads_kernel(chunks, all_ref, up_ref, down_ref, gup_ref, gdown_ref, rows_t):
    chunk = pl.program_id(1)
    groups, pieces, double, width = all_ref.shape
    count = groups * pieces * CAP
    rows = all_ref[:, :, :CAP, :].reshape(count, width)
    grads = all_ref[:, :, CAP:, :].reshape(count, width)

    @pl.when((pl.program_id(0) == 0) | (chunks > 1))
    def _():
        rows_t[...] = rows.T

    activated, slope = gelu_parts(product(rows, up_ref[...]))
    grad_pre = (times_transpose(grads, down_ref[...]) * slope).astype(BF16)
    grad_up = product(rows_t[...], grad_pre)
    grad_down = contract_rows(activated.astype(BF16), grads)

    @pl.when(chunk == 0)
    def _():
        gup_ref[...] = grad_up
        gdown_ref[...] = grad_down

    if chunks > 1:

        @pl.when(chunk > 0)
        def _():
            gup_ref[...] += grad_up
            gdown_ref[...] += grad_down


def expert_grads(gathered, up, down, tile):
    groups, pieces, double, width = gathered.shape
    hidden = up.shape[1]
    together = max(1, min(groups, 32 // pieces))
    chunks = groups // together
    return pl.pallas_call(
        partial(expert_grads_kernel, chunks),
        grid=(hidden // tile, chunks),
        in_specs=[
            pl.BlockSpec((together, pieces, double, width), lambda i, j: (j, 0, 0, 0)),
            pl.BlockSpec((width, tile), lambda i, j: (0, i)),
            pl.BlockSpec((tile, width), lambda i, j: (i, 0)),
        ],
        out_specs=[
            pl.BlockSpec((width, tile), lambda i, j: (0, i)),
            pl.BlockSpec((tile, width), lambda i, j: (i, 0)),
        ],
        out_shape=[
            jax.ShapeDtypeStruct((width, hidden), F32),
            jax.ShapeDtypeStruct((hidden, width), F32),
        ],
        scratch_shapes=[pltpu.VMEM((width, together * pieces * CAP), BF16)],
        compiler_params=pltpu.CompilerParams(vmem_limit_bytes=VMEM_LIMIT),
        name="expert_grads",
    )(gathered, up, down)


def combine_kernel(
    mid_ref, gain_ref, router_ref, routes_ref, slots_ref, live_ref, cot_ref, probs_ref, normed_ref,
    back_ref, out_ref, gradmid_ref, gradmix_ref, gradrouter_ref, gradgain_ref,
):
    mid = mid_ref[...]
    rows, width = mid.shape
    experts = router_ref.shape[1]
    routes = routes_ref[...]
    chosen = (routes == iota((rows, experts), 1)).astype(F32)
    probs = probs_ref[...]
    gate = jnp.sum(probs * chosen, 1, keepdims=True)
    live = live_ref[...]
    slot = iota((rows, experts * CAP), 1)
    collect = ((routes == slot // CAP) & (slots_ref[...] == slot % CAP)).astype(BF16)
    expert_sum = product(collect, back_ref[:, :CAP, :].reshape(experts * CAP, width))
    out_ref[...] = (live * (mid + gate * expert_sum)).astype(BF16)
    grad_out = cot_ref[...].astype(F32) * live
    grad_gate = jnp.sum(grad_out * expert_sum, 1, keepdims=True)
    grad_logits = (probs * (chosen * grad_gate - gate * grad_gate)).astype(BF16)
    gradrouter_ref[...] = contract_rows(normed_ref[...], grad_logits)
    grad = product(collect, back_ref[:, CAP:, :].reshape(experts * CAP, width))
    grad = grad + times_transpose(grad_logits, router_ref[...])
    scale = lax.rsqrt(jnp.mean(mid * mid, -1, keepdims=True) + 1e-05)
    unit = mid * scale
    gradgain_ref[...] = jnp.sum(grad * unit, 0, keepdims=True)
    inner = grad * gain_ref[...]
    grad_mid = grad_out + scale * (inner - unit * jnp.mean(inner * unit, -1, keepdims=True))
    gradmid_ref[...] = grad_mid
    gradmix_ref[...] = grad_mid.astype(BF16)


def combine_step(mid, gain, router, routes, slots, live, cotangent, probs, normed, back):
    rows, width = mid.shape
    return pl.pallas_call(
        combine_kernel,
        out_shape=[
            jax.ShapeDtypeStruct((rows, width), BF16),
            jax.ShapeDtypeStruct((rows, width), F32),
            jax.ShapeDtypeStruct((rows, width), BF16),
            jax.ShapeDtypeStruct(router.shape, F32),
            jax.ShapeDtypeStruct((1, width), F32),
        ],
        compiler_params=pltpu.CompilerParams(vmem_limit_bytes=VMEM_LIMIT),
        name="combine_step",
    )(mid, gain, router, routes, slots, live, cotangent, probs, normed, back)


def gather(value):
    return lax.all_gather(value, "expert", axis=0, tiled=True)


def exchange(value):
    return lax.all_to_all(value, "expert", split_axis=0, concat_axis=0, tiled=True)


def shards(
    tokens, lengths, routes, slot_index, mixer_norm, in_weight, conv_weight, conv_bias,
    scan_weight, step_weight, step_bias, decay_log, skip_gain, out_weight, moe_norm, router_weight,
    up_weight, down_weight, cotangent,
):
    devices = lax.axis_size("expert")
    rows, width = tokens.shape[1:]
    part = out_weight.shape[0]
    channels = part * devices
    cols = scan_weight.shape[1]
    rank, state, taps = step_weight.shape[0], decay_log.shape[1], conv_weight.shape[0]
    experts = router_weight.shape[1]
    split = devices // experts
    slice_w = width // devices
    tile = 768

    in_t = gather(in_weight.T)
    by_column = jnp.concatenate(
        [step_weight, decay_log.T, conv_weight, conv_bias[None], step_bias[None], skip_gain[None]], 0
    )
    by_width = jnp.concatenate([mixer_norm[:, None], moe_norm[:, None], router_weight], 1)
    small = jnp.concatenate(
        [by_column.reshape(-1), scan_weight.reshape(-1), by_width.reshape(-1)]
    )
    small = gather(small[None])
    first = by_column.size
    second = first + scan_weight.size
    columns = (
        small[:, :first].reshape(devices, by_column.shape[0], part)
        .transpose(1, 0, 2).reshape(by_column.shape[0], channels)
    )
    scan_full = small[:, first:second].reshape(channels, cols)
    widths = small[:, second:].reshape(width, experts + 2)
    out_full = gather(out_weight)
    step_full = columns[:rank]
    rest = columns[rank:].astype(F32)
    rate = -jnp.exp(rest[:state])
    conv_full = rest[state : state + taps]
    bias_full, dbias_full, skip_full = (
        rest[state + taps + k : state + taps + k + 1] for k in range(3)
    )
    gain_first = widths[:, 0].astype(F32)[None]
    gain_second = widths[:, 1].astype(F32)[None]
    router = widths[:, 2:]
    up, down = up_weight[0], down_weight[0]
    live = (jnp.arange(rows, dtype=jnp.int32) < lengths[0]).astype(F32)[:, None]
    routes_col, slots_col = routes[0][:, None], slot_index[0][:, None]

    normed_low, x_inner, u_act, gate_in, proj = front(
        tokens[0], gain_first, in_t, conv_full, bias_full, scan_full, tile
    )
    step_size, mixed, gated, hist, mid = scan_forward(
        proj, step_full, dbias_full, rate, skip_full, u_act, gate_in, out_full, tokens[0], tile
    )
    send, normed_two, probs = router_step(
        mid, gain_second, router, routes_col, routes, slot_index, live, cotangent[0]
    )
    wide = jnp.broadcast_to(send[:, None], (experts, split) + send.shape[1:])
    got = exchange(wide.reshape(devices, 2 * CAP, width))
    everyone = lax.all_gather(got, "dp")
    pieces_back = exchange(expert_step(got, up, down, min(512, up.shape[1] // 3)))
    pieces_back = pieces_back.reshape(experts, split, 2 * CAP, width)
    back = pieces_back[:, 0]
    if split > 1:
        back = jnp.sum(pieces_back.astype(F32), 1).astype(BF16)
    layer_out, grad_mid, grad_mix, grad_router, grad_gain_second = combine_step(
        mid, gain_second, router, routes_col, slots_col, live, cotangent[0], probs, normed_two, back
    )
    grad_u, grad_gate, grad_step_w, grad_dbias, grad_skip, grad_log, grad_proj = scan_backward(
        proj, step_full, dbias_full, rate, skip_full, u_act, gate_in, out_full, grad_mix, step_size,
        mixed, hist, tile,
    )
    grad_x, grad_conv, grad_bias, grad_scan_w, tokens_grad, grad_gain_first = mixer_back(
        grad_proj, scan_full, grad_u, x_inner, conv_full, bias_full, grad_gate, in_t, u_act,
        tokens[0], gain_first, grad_mid, tile,
    )

    grad_in = jnp.concatenate([grad_x, grad_gate], 1)
    grad_in_parts = exchange(grad_in.reshape(rows, devices, 2 * part).transpose(1, 0, 2))
    normed_all = gather(normed_low)
    grad_in_w = contract_rows(normed_all, grad_in_parts.reshape(devices * rows, 2 * part))
    gated_parts = exchange(gated.reshape(rows, devices, part).transpose(1, 0, 2))
    grad_mix_all = gather(grad_mix)
    grad_out_w = contract_rows(gated_parts.reshape(devices * rows, part), grad_mix_all)

    grad_columns = jnp.concatenate(
        [grad_step_w, grad_log, grad_conv, grad_bias, grad_dbias, grad_skip], 0
    ).astype(BF16)
    count = grad_columns.shape[0]
    grad_columns = grad_columns.reshape(count, devices, part).transpose(1, 0, 2)
    grad_widths = jnp.concatenate([grad_gain_first.T, grad_gain_second.T, grad_router], 1)
    grad_small = jnp.concatenate(
        [
            grad_columns.reshape(devices, -1),
            grad_scan_w.astype(BF16).reshape(devices, -1),
            grad_widths.astype(BF16).reshape(devices, -1),
        ],
        1,
    )
    grad_small = jnp.sum(exchange(grad_small).astype(F32), 0)
    flat = jnp.concatenate(
        [grad_in_w.astype(BF16).reshape(-1), grad_out_w.astype(BF16).reshape(-1), grad_small.astype(BF16)]
    )
    flat = lax.psum(flat, "dp").astype(F32)
    grad_up, grad_down = expert_grads(everyone, up, down, min(256, up.shape[1]))

    in_size = in_weight.size
    out_size = in_size + out_weight.size
    in_total = flat[:in_size].reshape(in_weight.shape)
    out_total = flat[in_size:out_size].reshape(out_weight.shape)
    tail = flat[out_size:]
    columns_total = tail[:first].reshape(by_column.shape)
    scan_total = tail[first:second].reshape(scan_weight.shape)
    widths_total = tail[second:].reshape(slice_w, experts + 2)
    return (
        layer_out[None],
        tokens_grad[None],
        widths_total[:, 0],
        in_total,
        columns_total[rank + state : rank + state + taps],
        columns_total[rank + state + taps],
        scan_total,
        columns_total[:rank],
        columns_total[rank + state + taps + 1],
        columns_total[rank : rank + state].T,
        columns_total[rank + state + taps + 2],
        out_total,
        widths_total[:, 1],
        widths_total[:, 2:],
        grad_up[None],
        grad_down[None],
    )


def solution(mesh):
    in_specs = (
        P(("dp", "expert"), None, None),
        P(("dp", "expert")),
        P(("dp", "expert"), None),
        P(("dp", "expert"), None),
        P("expert"),
        P(None, "expert"),
        P(None, "expert"),
        P("expert"),
        P("expert", None),
        P(None, "expert"),
        P("expert"),
        P("expert", None),
        P("expert"),
        P("expert", None),
        P("expert"),
        P("expert", None),
        P("expert", None, None),
        P("expert", None, None),
        P(("dp", "expert"), None, None),
    )
    out_specs = (
        P(("dp", "expert"), None, None),
        P(("dp", "expert"), None, None),
        P("expert"),
        P(None, "expert"),
        P(None, "expert"),
        P("expert"),
        P("expert", None),
        P(None, "expert"),
        P("expert"),
        P("expert", None),
        P("expert"),
        P("expert", None),
        P("expert"),
        P("expert", None),
        P("expert", None, None),
        P("expert", None, None),
    )
    return jax.shard_map(shards, mesh=mesh, in_specs=in_specs, out_specs=out_specs, check_vma=False)
```

time: 2030 us -> 812 us (0.40)
  other arithmetic: 535 us -> 22.6 us
  waiting for transfers between devices: 825 us -> 343 us
  local copies, waits for them, and re-layouts: 365 us -> 73.5 us
  Pallas kernels: 0 us -> 243 us
  matrix products: 135 us -> 10.6 us
  blocking collectives: 111 us -> 55.3 us
    psum x2 -> x1, waiting for transfers between devices: 571 us -> 87.2 us  [shards(): flat = lax.psum(flat, 'dp').astype(F32)]
    pallas_call x0 -> x8, Pallas kernels: none -> 243 us  [the longest x1 98.4 us: expert_grads(): pl.pallas_call(partial(expert_grads_kernel, chunks), grid=(hidden // tile...]
    dynamic_update_slice x96 -> x0, other arithmetic: 208 us -> none  [the longest x64 151 us: block_scan(): block_ends, _ = lax.scan(local_step, zeros_state, (seq_u, seq_step, seq_b))]
    all_gather x2 -> x5, waiting for transfers between devices: 0.02 us -> 207 us  [the longest x1 145 us: shards(): everyone = lax.all_gather(got, 'dp')]
    reduce_sum x86 -> x1, other arithmetic: 186 us -> 3.36 us  [shards(): grad_small = jnp.sum(exchange(grad_small).astype(F32), 0)]
    reduce_scatter x3 -> x0, waiting for transfers between devices: 174 us -> none  [the longest x1 86.7 us: shards(): lax.psum_scatter(grad_inw.astype(jnp.bfloat16), 'expert', scatter_dimensi...]
    mul x128 -> x0, local copies, waits for them, and re-layouts: 96.7 us -> none  [the longest x80 55.7 us: advance(): (step_now * u_now)[:, :, None] * b_now[:, None, :]]
    dot_general x16 -> x0, matrix products: 96.7 us -> none  [the longest x7 48.7 us: times_transpose(): lax.dot_general(left, right, (((1,), (1,)), ((), ())), preferred_element_...]
  transfers between devices with their start and end apart: 15 -> 10, of which waited for: 8 -> 7; matrix products, arithmetic and copies ran while one was open for 28% -> 11% of each run, Pallas kernels for 0% -> 18%
where the time goes in v1:
time: 812 us; the launch traced here: 798 us
  waiting for transfers between devices  343 us (42%)
  Pallas kernels  243 us (30%)
  local copies, waits for them, and re-layouts  73.5 us (9%)
  blocking collectives  55.3 us (7%)
  starting transfers between devices  34.9 us (4%)
  other arithmetic  22.6 us (3%)
  between operations  15.7 us (2%)
  matrix products  10.6 us (1%)
    all_gather x1, waiting for transfers between devices, shards(): everyone = lax.all_gather(got, 'dp')  145 us
    pallas_call x1, Pallas kernels, expert_grads(): pl.pallas_call(partial(expert_grads_kernel, chunks), grid=(hidden // tile...  98.4 us
    psum x1, waiting for transfers between devices, shards(): flat = lax.psum(flat, 'dp').astype(F32)  87.2 us
    all_gather x4, waiting for transfers between devices, gather(): return lax.all_gather(value, 'expert', axis=0, tiled=True)  62.1 us
    pallas_call x1, Pallas kernels, scan_backward(): pl.pallas_call(scan_back_kernel, grid=(steps,), in_specs=[pl.BlockSpec((r...  49.5 us
    all_to_all x4, waiting for transfers between devices, exchange(): lax.all_to_all(value, 'expert', split_axis=0, concat_axis=0, tiled=True)  46.5 us
    all_to_all x4, starting transfers between devices, exchange(): lax.all_to_all(value, 'expert', split_axis=0, concat_axis=0, tiled=True)  34.7 us
    all_to_all x1, blocking collectives, exchange(): lax.all_to_all(value, 'expert', split_axis=0, concat_axis=0, tiled=True)  33 us
  transfers between devices with their start and end apart: 10, of which 7 were waited for; matrix products, arithmetic and copies ran while one was open for 11% of the time, Pallas kernels for 18%

profile of v1, /device:TPU:9, one launch (start us, length us, event | category | flops | bytes accessed | tf_op | source)
XLA Modules:
  0.0 798.2 jit_solution(5446424328201400789)
XLA Ops:
  15.8 22.3 %all-gather.2 = bf16[8,1,58752]{2,1,0:T(2,128)(2,1)S(1)} all-gather(bf16[1,1,58752]{2,1,0:T(2,128)(2,1)S(1)} %reshape.226), channel_id=2, replica_groups=mesh['dp'=4,'expert'=8] {'expert'}, dimensions={0}, use_global_device_ids=true | all-gather | bytes 1057536 | tf_op jit(solution)/shard_map/all_gather | solution.py:721
  44.6 36.6 %all-gather.9.cloned.1.call-done.wx_ref.wg_ref = bf16[4608,1152]{1,0:T(8,128)(2,1)} async-done(((bf16[576,1152]{1,0:T(8,128)(2,1)}), bf16[4608,1152]{1,0:T(8,128)(2,1)}) %all-gather.9.cloned.1.call-update) | async-done | bytes 10616848 | tf_op jit(solution)/shard_map/all_gather | solution.py:721
  81.2 10.8 %mixer_front.1 = (bf16[256,1152]{1,0:T(8,128)(2,1)}, f32[256,2304]{1,0:T(8,128)}, f32[256,2304]{1,0:T(8,128)}, f32[256,2304]{1,0:T(8,128)}, f32[256,104]{1,0:T(8,128)}) custom-call(bf16[256,1152]{1,0:T(8,128)(2,1)} %bitcast.46, f32[1,1152]{1,0:T(1,128)} %reshape.222.gain_ref, bf16[4608,1152]{1,0:T(8,128)(2,1)} %all-gather.9.cloned.1.call-done.wx_ref.wg_ref, ...), custom_call_target="tpu_custom_call" | custom-call | tf_op jit(solution)/shard_map/mixer_front/pallas_call | solution.py:116
  99.0 25.5 %all-gather.11.cloned.1.call-done.outw_ref = bf16[2304,1152]{1,0:T(8,128)(2,1)} async-done(((bf16[288,1152]{1,0:T(8,128)(2,1)}), bf16[2304,1152]{1,0:T(8,128)(2,1)}) %all-gather.11.cloned.1.call-update) | async-done | bytes 5308432 | tf_op jit(solution)/shard_map/all_gather | solution.py:721
  124.5 32.9 %scan_forward.1 = (f32[256,2304]{1,0:T(8,128)}, f32[256,2304]{1,0:T(8,128)}, bf16[256,2304]{1,0:T(8,128)(2,1)}, bf16[4112,2304]{1,0:T(8,128)(2,1)}, f32[256,1152]{1,0:T(8,128)}) custom-call(f32[256,104]{1,0:T(8,128)} %get-tuple-element.49.proj_ref, bf16[72,2304]{1,0:T(8,128)(2,1)} %slice.188.stepw_ref, f32[1,2304]{1,0:T(1,128)} %slice.190.dbias_ref, ...), custom_call_target="tpu_custom_call" | custom-call | tf_op jit(solution)/shard_map/scan_forward/pallas_call | solution.py:217
  157.4 4.4 router_step.1
  161.8 33.0 %all_to_all.29.got_ref = bf16[8,128,1152]{2,1,0:T(8,128)(2,1)} all-to-all(bf16[8,128,1152]{2,1,0:T(8,128)(2,1)} %get-tuple-element.55), channel_id=1, replica_groups=mesh['dp'=4,'expert'=8] {'expert'}, dimensions={0} | all-to-all | bytes 4718592 | tf_op jit(solution)/shard_map/all_to_all | solution.py:725
  194.8 26.8 %expert_step.1 = bf16[8,128,1152]{2,1,0:T(8,128)(2,1)} custom-call(bf16[8,128,1152]{2,1,0:T(8,128)(2,1)} %all_to_all.29.got_ref, bf16[1152,3072]{1,0:T(8,128)(2,1)} %bitcast.40, bf16[3072,1152]{1,0:T(8,128)(2,1)} %bitcast.42), custom_call_target="tpu_custom_call" | custom-call | tf_op jit(solution)/shard_map/expert_step/pallas_call | solution.py:601
  221.6 5.0 all-to-all-start.1
  227.5 25.1 %all-to-all-done.1.back_ref = bf16[8,128,1152]{2,1,0:T(8,128)(2,1)S(1)} async-done(((bf16[8,128,1152]{2,1,0:T(8,128)(2,1)}), bf16[8,128,1152]{2,1,0:T(8,128)(2,1)S(1)}, u32[]{:S(2)}, u32[]{:S(2)}) %all-to-all-start.1) | async-done | bytes 2359328 | tf_op jit(solution)/shard_map/all_to_all | solution.py:725
  254.0 6.1 combine_step.1
  261.6 7.0 all-to-all-start.3
  268.6 49.5 %scan_backward.1 = (f32[256,2304]{1,0:T(8,128)}, bf16[256,2304]{1,0:T(8,128)(2,1)}, f32[72,2304]{1,0:T(8,128)}, f32[1,2304]{1,0:T(1,128)}, f32[1,2304]{1,0:T(1,1...) custom-call(f32[256,104]{1,0:T(8,128)} %get-tuple-element.49.proj_ref, bf16[72,2304]{1,0:T(8,128)(2,1)} %slice.188.stepw_ref, ...), custom_call_target="tpu_custom_call" | custom-call | tf_op jit(solution)/shard_map/scan_backward/pallas_call | solution.py:370
  318.2 13.9 %mixer_back.1 = (bf16[256,2304]{1,0:T(8,128)(2,1)}, f32[4,2304]{1,0:T(4,128)}, f32[1,2304]{1,0:T(1,128)}, f32[2304,104]{1,0:T(8,128)}, f32[256,1152]{1,0:T(8,128)}, /*index=5*/f32[1,1152]{1,0:T(1,128)}) custom-call(f32[256,104]{1,0:T(8,128)} %get-tuple-element.61.gradproj_ref, bf16[2304,104]{1,0:T(8,128)(2,1)} %reshape.212.scanw_ref, ...), custom_call_target="tpu_custom_call" | custom-call | tf_op jit(solution)/shard_map/mixer_back/pallas_call | solution.py:478
  338.7 3.4 dynamic-update-slice
  342.1 3.7 dynamic-update-slice.1
  347.7 2.6 reduce.22
  352.2 15.4 %all-to-all-start.4 = ((bf16[8,2,29376]{2,1,0:T(2,128)(2,1)}), bf16[8,2,29376]{2,1,0:T(2,128)(2,1)}, u32[]{:S(2)}, u32[]{:S(2)}) async-start(bf16[8,2,29376]{2,1,0:T(2,128)(2,1)} %reshape.239), calls=%async_computation.4 | async-start | bytes 1884160 | tf_op jit(solution)/shard_map/all_to_all | solution.py:725
  369.0 2.4 copy.133
  371.4 6.8 all-to-all-done.4
  378.2 7.3 all-to-all-start.2
  386.7 6.8 reshape.240
  393.6 3.4 reduce_sum.12
  396.9 14.6 %all-to-all-done.2 = bf16[8,256,576]{1,2,0:T(8,128)(2,1)S(1)} async-done(((bf16[8,256,576]{1,2,0:T(8,128)(2,1)}), bf16[8,256,576]{1,2,0:T(8,128)(2,1)S(1)}, u32[]{:S(2)}, u32[]{:S(2)}) %all-to-all-start.2) | async-done | bytes 2359328 | tf_op jit(solution)/shard_map/all_to_all | solution.py:725
  413.2 6.3 convolution_convert_fusion
  422.2 4.4 convolution_convert_fusion.1
  427.3 11.6 %pad_maximum_fusion.1 = bf16[1054080]{0:T(1024)(128)(2,1)} fusion(bf16[58752]{0:T(1024)(128)(2,1)S(1)} %reduce_sum.12, bf16[331776]{0:T(1024)(128)(2,1)S(1)} %reshape.218, bf16[663552]{0:T(1024)(128)(2,1)S(1)} %reshape.215), kind=kLoop, calls=%fused_computation.3 | loop fusion | flops 6324480 | bytes 4216320 | tf_op jit(solution)/shard_map/concatenate | solution.py:828
  439.4 87.2 %all-reduce.2.cloned.1.call-done = bf16[1054080]{0:T(1024)(128)(2,1)} async-done(((bf16[1054080]{0:T(1024)(128)(2,1)}), bf16[1054080]{0:T(1024)(128)(2,1)}) %all-reduce.2.cloned.1.call-update) | async-done | bytes 2108176 | tf_op jit(solution)/shard_map/psum | solution.py:831
  526.7 3.0 slice.230
  529.7 3.1 slice.200
  547.6 145.0 %all-gather.17.cloned.1.call-done = bf16[32,128,1152]{2,1,0:T(8,128)(2,1)} async-done(((bf16[8,128,1152]{2,1,0:T(8,128)(2,1)}), bf16[32,128,1152]{2,1,0:T(8,128)(2,1)}) %all-gather.17.cloned.1.call-update) | async-done | bytes 9437200 | tf_op jit(solution)/shard_map/all_gather | solution.py:787
  692.6 98.4 %expert_grads.1 = (f32[1152,3072]{1,0:T(8,128)}, f32[3072,1152]{1,0:T(8,128)}) custom-call(bf16[4,8,128,1152]{3,2,1,0:T(8,128)(2,1)} %bitcast.45, bf16[1152,3072]{1,0:T(8,128)(2,1)} %bitcast.41, bf16[3072,1152]{1,0:T(8,128)(2,1)} %bitcast.43), custom_call_target="tpu_custom_call" | custom-call | tf_op jit(solution)/shard_map/expert_grads/pallas_call | solution.py:651
  (145 shorter events, 58.4 us)
Async XLA Ops:
  7.2 7.1 copy-start.16
  7.2 7.1 copy-start.17
  7.2 7.1 copy-start.15
  7.2 74.0 %all-gather.9.cloned.1.call-start = ((), (), s32[]{:S(2)}) async-start(), calls=%async_computation.5 | async-start | bytes 11943936 | tf_op jit(solution)/shard_map/all_gather | solution.py:721
  7.9 116.6 %all-gather.11.cloned.1.call-start = ((), (), s32[]{:S(2)}) async-start(), calls=%async_computation.6 | async-start | bytes 5971968 | tf_op jit(solution)/shard_map/all_gather | solution.py:721
  8.7 404.5 %all-gather.13.cloned.1.call-start = ((), (), s32[]{:S(2)}) async-start(), calls=%async_computation.7 | async-start | bytes 5308416 | tf_op jit(solution)/shard_map/all_gather | solution.py:721
  92.0 5.6 copy-start.13
  221.6 5.0 copy-start.14
  221.6 31.0 %all-to-all-start.1 = ((bf16[8,128,1152]{2,1,0:T(8,128)(2,1)}), bf16[8,128,1152]{2,1,0:T(8,128)(2,1)S(1)}, u32[]{:S(2)}, u32[]{:S(2)}) async-start(bf16[8,128,1152]{2,1,0:T(8,128)(2,1)} %expert_step.1), calls=%async_computation.1 | async-start | bytes 4718592 | tf_op jit(solution)/shard_map/all_to_all | solution.py:725
  226.6 195.5 %all-gather.15.cloned.1.call-start = ((), (), s32[]{:S(2)}) async-start(), calls=%async_computation.8 | async-start | bytes 5308416 | tf_op jit(solution)/shard_map/all_gather | solution.py:721
  252.6 1.4 copy-start
  254.0 6.2 copy-start.4
  261.6 90.6 %all-to-all-start.3 = ((bf16[8,256,288]{1,2,0:T(8,128)(2,1)}), bf16[8,256,288]{1,2,0:T(8,128)(2,1)S(1)}, u32[]{:S(2)}, u32[]{:S(2)}) async-start(bf16[8,256,288]{1,2,0:T(8,128)(2,1)} %bitcast.15), calls=%async_computation.3 | async-start | bytes 2359296 | tf_op jit(solution)/shard_map/all_to_all | solution.py:725
  318.1 14.9 %copy-start.12 = (f32[1,1152]{1,0:T(1,128)S(1)}, f32[1,1152]{1,0:T(1,128)}, u32[]{:S(2)}) copy-start(f32[1,1152]{1,0:T(1,128)} %get-tuple-element.78) | copy-start | bytes 13828
  318.1 15.2 %copy-start.6 = (f32[1152,8]{1,0:T(8,128)S(1)}, f32[1152,8]{1,0:T(8,128)}, u32[]{:S(2)}) copy-start(f32[1152,8]{1,0:T(8,128)} %get-tuple-element.79) | copy-start | bytes 110596
  332.0 1.9 copy-start.10
  332.0 1.9 copy-start.11
  332.0 2.2 copy-start.8
  332.0 2.3 copy-start.9
  332.1 2.4 copy-start.5
  333.4 1.9 copy-start.7
  347.7 19.9 %copy-start.1 = (bf16[256,2304]{1,0:T(8,128)(2,1)S(1)}, bf16[256,2304]{1,0:T(8,128)(2,1)}, u32[]{:S(2)}) copy-start(bf16[256,2304]{1,0:T(8,128)(2,1)} %get-tuple-element.64.gradgate_ref) | copy-start | bytes 3538948
  352.2 15.4 %copy-start.2 = (bf16[8,256,288]{1,2,0:T(8,128)(2,1)}, bf16[8,256,288]{1,2,0:T(8,128)(2,1)S(1)}, u32[]{:S(2)}) copy-start(bf16[8,256,288]{1,2,0:T(8,128)(2,1)S(1)} %all-to-all-done.3) | copy-start | bytes 3538948
  352.2 26.0 %all-to-all-start.4 = ((bf16[8,2,29376]{2,1,0:T(2,128)(2,1)}), bf16[8,2,29376]{2,1,0:T(2,128)(2,1)}, u32[]{:S(2)}, u32[]{:S(2)}) async-start(bf16[8,2,29376]{2,1,0:T(2,128)(2,1)} %reshape.239), calls=%async_computation.4 | async-start | bytes 1884160 | tf_op jit(solution)/shard_map/all_to_all | solution.py:725
  378.2 7.3 copy-start.3
  378.2 33.3 %all-to-all-start.2 = ((bf16[8,256,576]{1,2,0:T(8,128)(2,1)}), bf16[8,256,576]{1,2,0:T(8,128)(2,1)S(1)}, u32[]{:S(2)}, u32[]{:S(2)}) async-start(bf16[8,256,576]{1,2,0:T(8,128)(2,1)} %bitcast.13), calls=%async_computation.2 | async-start | bytes 4718592 | tf_op jit(solution)/shard_map/all_to_all | solution.py:725
  385.5 141.2 %all-reduce.2.cloned.1.call-start = ((), (), s32[]{:S(2)}) async-start(), calls=%async_computation.9 | async-start | bytes 4218880 | tf_op jit(solution)/shard_map/psum | solution.py:831
  438.9 253.7 %all-gather.17.cloned.1.call-start = ((), (), s32[]{:S(2)}) async-start(), calls=%async_computation.10 | async-start | bytes 11796480 | tf_op jit(solution)/shard_map/all_gather | solution.py:787
Sparse Core Ops, SparseCore 0:
  9.9 71.2 all-gather.8
  83.1 41.3 all-gather.10
  126.4 39.0 all-gather.12
  260.3 52.3 all-gather.14
  439.0 87.6 all-reduce.1
  528.1 164.4 all-gather.16

commit v2 on v1

--- a/solution.py
+++ b/solution.py
@@ -41,6 +41,12 @@
 
 def softplus(values):
     return jnp.maximum(values, 0.0) + jnp.log1p(jnp.exp(-jnp.abs(values)))
+
+
+def split_lanes(out_ref, value):
+    parts, _, width = out_ref.shape
+    for part in range(parts):
+        out_ref[part] = value[:, part * width : (part + 1) * width]
 
 
 def shift_rows(values, offset):
@@ -144,32 +150,29 @@
     )(tokens, gain, in_t, in_t, conv, bias, scan_w)
 
 
-def scan_kernel(
-    proj_ref, stepw_ref, dbias_ref, decay_ref, skip_ref, u_ref, gate_ref, outw_ref, tokens_ref,
-    step_ref, mixed_ref, gated_ref, hist_ref, mid_ref,
-    b_wide, c_blocks, du, scanned,
+def scan_prepare(proj_ref, b_wide, c_blocks, b_first, c_first, state):
+    blocks = proj_ref.shape[0] // BLOCK
+    big = BLOCK * state
+
+    def build(block, carry):
+        part = proj_ref[pl.ds(pl.multiple_of(block * BLOCK, BLOCK), BLOCK), :]
+        b_wide[pl.ds(pl.multiple_of(block * big, big), big), :] = spread_rows(part, b_first, state)
+        c_blocks[pl.ds(pl.multiple_of(block * 2 * BLOCK, 2 * BLOCK), 2 * BLOCK), :] = (
+            diagonal_blocks(part, c_first, state)
+        )
+        return carry
+
+    lax.fori_loop(0, blocks, build, 0)
+
+
+def scan_tile(
+    proj_ref, stepw_ref, dbias_ref, decay_ref, skip_ref, u_ref, gate_ref, step_ref, mixed_ref,
+    hist_ref, b_wide, c_blocks, du, scanned, between,
 ):
-    tile_id = pl.program_id(0)
-    rank = stepw_ref.shape[0]
-    state = decay_ref.shape[0]
-    rows = u_ref.shape[0]
+    rank, state = stepw_ref.shape[0], decay_ref.shape[0]
+    rows, tile = u_ref.shape
     blocks = rows // BLOCK
     big = BLOCK * state
-
-    @pl.when(tile_id == 0)
-    def _():
-        mid_ref[...] = tokens_ref[...].astype(F32)
-
-        def build(block, carry):
-            part = proj_ref[pl.ds(pl.multiple_of(block * BLOCK, BLOCK), BLOCK), :]
-            b_wide[pl.ds(pl.multiple_of(block * big, big), big), :] = spread_rows(part, rank, state)
-            c_blocks[pl.ds(pl.multiple_of(block * 2 * BLOCK, 2 * BLOCK), 2 * BLOCK), :] = (
-                diagonal_blocks(part, rank + state, state)
-            )
-            return carry
-
-        lax.fori_loop(0, blocks, build, 0)
-
     u_act = u_ref[...]
     step_size = softplus(
         product(proj_ref[:, :rank].astype(BF16), stepw_ref[...]) + dbias_ref[...]
@@ -177,7 +180,6 @@
     step_ref[...] = step_size
     du[...] = step_size * u_act
     decay = decay_ref[...] * LOG2E
-    tile = u_act.shape[1]
     hist_ref[0:state, :] = jnp.zeros((state, tile), BF16)
 
     def run_block(block, held):
@@ -196,11 +198,33 @@
         scanned[pl.ds(base, BLOCK), :] = both[:BLOCK] + both[BLOCK:]
         return held
 
-    lax.fori_loop(0, blocks, run_block, jnp.zeros((state, tile), F32))
+    held = jnp.zeros((state, tile), F32)
+    held = lax.fori_loop(0, blocks // 2, run_block, held)
+    between(0)
+    lax.fori_loop(blocks // 2, blocks, run_block, held)
+    between(1)
     mixed = scanned[...] + skip_ref[...] * u_act
     mixed_ref[...] = mixed
     gate_in = gate_ref[...]
-    gated = (mixed * (gate_in * sigmoid(gate_in))).astype(BF16)
+    return (mixed * (gate_in * sigmoid(gate_in))).astype(BF16)
+
+
+def scan_kernel(
+    proj_ref, stepw_ref, dbias_ref, decay_ref, skip_ref, u_ref, gate_ref, outw_ref, tokens_ref,
+    step_ref, mixed_ref, gated_ref, hist_ref, mid_ref,
+    b_wide, c_blocks, du, scanned,
+):
+    rank, state = stepw_ref.shape[0], decay_ref.shape[0]
+
+    @pl.when(pl.program_id(0) == 0)
+    def _():
+        mid_ref[...] = tokens_ref[...].astype(F32)
+        scan_prepare(proj_ref, b_wide, c_blocks, rank, rank + state, state)
+
+    gated = scan_tile(
+        proj_ref, stepw_ref, dbias_ref, decay_ref, skip_ref, u_ref, gate_ref, step_ref, mixed_ref,
+        hist_ref, b_wide, c_blocks, du, scanned, lambda half: None,
+    )
     gated_ref[...] = gated
     mid_ref[...] += product(gated, outw_ref[...])
 
@@ -253,10 +277,14 @@
     )(proj, step_w, dbias, decay, skip, u_act, gate_in, out_w, tokens)
 
 
-def scan_back_kernel(
-    proj_ref, stepw_ref, dbias_ref, decay_ref, skip_ref, u_ref, gate_ref, outw_ref, gradmix_ref,
+def scan_back_kernel(*refs, between=lambda half: None):
+    scan_back_tile(between, *refs)
+
+
+def scan_back_tile(
+    between, proj_ref, stepw_ref, dbias_ref, decay_ref, skip_ref, u_ref, gate_ref, outw_ref, gradmix_ref,
     step_ref, mixed_ref, hist_ref,
-    gradu_ref, gradgate_ref, gradstepw_ref, gradbias_ref, gradskip_ref, gradlog_ref, gradproj_ref,
+    gradu_ref, gradgate_ref, pack_ref, gradproj_ref,
     c_wide, b_blocks, b_sums, c_sums, gy, du, g_hist, w_hist, grad_du, grad_step,
 ):
     tile_id = pl.program_id(0)
@@ -271,31 +299,21 @@
         gradproj_ref[...] = jnp.zeros_like(gradproj_ref)
         b_sums[...] = jnp.zeros_like(b_sums)
         c_sums[...] = jnp.zeros_like(c_sums)
-
-        def build(block, carry):
-            part = proj_ref[pl.ds(pl.multiple_of(block * BLOCK, BLOCK), BLOCK), :]
-            c_wide[pl.ds(pl.multiple_of(block * big, big), big), :] = spread_rows(
-                part, rank + state, state
-            )
-            b_blocks[pl.ds(pl.multiple_of(block * 2 * BLOCK, 2 * BLOCK), 2 * BLOCK), :] = (
-                diagonal_blocks(part, rank, state)
-            )
-            return carry
-
-        lax.fori_loop(0, blocks, build, 0)
+        scan_prepare(proj_ref, c_wide, b_blocks, rank + state, rank, state)
 
     grad_gated = times_transpose(gradmix_ref[...], outw_ref[...])
     gate_in = gate_ref[...]
     gate_sig = sigmoid(gate_in)
     grad_mixed = grad_gated * (gate_in * gate_sig)
-    gradgate_ref[...] = (
-        grad_gated * mixed_ref[...] * (gate_sig * (1.0 + gate_in * (1.0 - gate_sig)))
-    ).astype(BF16)
+    split_lanes(
+        gradgate_ref,
+        (grad_gated * mixed_ref[...] * (gate_sig * (1.0 + gate_in * (1.0 - gate_sig)))).astype(BF16),
+    )
     u_act = u_ref[...]
     step_size = step_ref[...]
     gy[...] = grad_mixed
     du[...] = step_size * u_act
-    gradskip_ref[...] = jnp.sum(grad_mixed * u_act, 0, keepdims=True)
+    grad_skip = jnp.sum(grad_mixed * u_act, 0, keepdims=True)
     rate = decay_ref[...]
     decay = rate * LOG2E
     sums = (iota((BLOCK, big), 0) == iota((BLOCK, big), 1) // state).astype(BF16)
@@ -333,15 +351,20 @@
         return carried, log_sum
 
     zeros = jnp.zeros((state, tile), F32)
-    _, log_sum = lax.fori_loop(0, blocks, run_block, (zeros, zeros))
-    gradlog_ref[...] = log_sum
+    held = lax.fori_loop(0, blocks // 2, run_block, (zeros, zeros))
+    between(0)
+    _, log_sum = lax.fori_loop(blocks // 2, blocks, run_block, held)
+    between(1)
     full_du = grad_du[...]
     gradu_ref[...] = full_du * step_size + skip_ref[...] * gy[...]
     grad_size = grad_step[...] + full_du * u_act
     grad_pre = grad_size * (1.0 - jnp.exp(-step_size))
-    gradbias_ref[...] = jnp.sum(grad_pre, 0, keepdims=True)
     grad_low = grad_pre.astype(BF16)
-    gradstepw_ref[...] = contract_rows(proj_ref[:, :rank].astype(BF16), grad_low)
+    grad_step_w = contract_rows(proj_ref[:, :rank].astype(BF16), grad_low)
+    packed = jnp.concatenate(
+        [grad_step_w, log_sum, jnp.sum(grad_pre, 0, keepdims=True), grad_skip, zeros[:6]], 0
+    )
+    split_lanes(pack_ref, packed.astype(BF16))
     gradproj_ref[:, :rank] += times_transpose(grad_low, stepw_ref[...])
 
     @pl.when(tile_id == pl.num_programs(0) - 1)
@@ -357,9 +380,13 @@
 
 
 def scan_backward(
-    proj, step_w, dbias, decay, skip, u_act, gate_in, out_w, grad_mix, step_size, mixed, hist, tile
+    proj, step_w, dbias, decay, skip, u_act, gate_in, out_w, grad_mix, step_size, mixed, hist, tile,
+    devices,
 ):
     rows, channels = u_act.shape
+    gate_parts = tile * devices // (2 * channels)
+    pack_parts = tile * devices // channels
+    pack_rows = step_w.shape[0] + decay.shape[0] + 8
     width = grad_mix.shape[1]
     cols = proj.shape[1]
     rank, state = step_w.shape[0], decay.shape[0]
@@ -386,20 +413,14 @@
         ],
         out_specs=[
             pl.BlockSpec((rows, tile), column),
-            pl.BlockSpec((rows, tile), column),
-            pl.BlockSpec((rank, tile), column),
-            pl.BlockSpec((1, tile), column),
-            pl.BlockSpec((1, tile), column),
-            pl.BlockSpec((state, tile), column),
+            pl.BlockSpec((gate_parts, rows, tile // gate_parts), lambda i: (i, 0, 0)),
+            pl.BlockSpec((pack_parts, pack_rows, tile // pack_parts), lambda i: (i, 0, 0)),
             pl.BlockSpec((rows, cols), fixed),
         ],
         out_shape=[
             jax.ShapeDtypeStruct((rows, channels), F32),
-            jax.ShapeDtypeStruct((rows, channels), BF16),
-            jax.ShapeDtypeStruct((rank, channels), F32),
-            jax.ShapeDtypeStruct((1, channels), F32),
-            jax.ShapeDtypeStruct((1, channels), F32),
-            jax.ShapeDtypeStruct((state, channels), F32),
+            jax.ShapeDtypeStruct((devices // 2, rows, 2 * channels // devices), BF16),
+            jax.ShapeDtypeStruct((devices, pack_rows, channels // devices), BF16),
             jax.ShapeDtypeStruct((rows, cols), F32),
         ],
         scratch_shapes=[
@@ -421,8 +442,8 @@
 
 def back_kernel(
     gradproj_ref, scanw_ref, gradu_ref, xin_ref, conv_ref, bias_ref, gradgate_ref, wx_ref, wg_ref,
-    u_ref, tokens_ref, gain_ref, gradmid_ref,
-    gradx_ref, gradconv_ref, gradbias_ref, gradscanw_ref, gradtok_ref, gradgain_ref,
+    u_ref, tokens_ref, gain_ref, gradmid_ref, widths_ref,
+    gradx_ref, pack_ref, tail_ref, gradtok_ref,
     total,
 ):
     tile_id = pl.program_id(0)
@@ -433,7 +454,7 @@
 
     grad_proj = gradproj_ref[...].astype(BF16)
     grad_u = gradu_ref[...] + times_transpose(grad_proj, scanw_ref[...])
-    gradscanw_ref[...] = contract_rows(u_ref[...].astype(BF16), grad_proj)
+    pieces = [contract_rows(grad_proj, u_ref[...].astype(BF16))]
     x_inner = xin_ref[...]
     taps = conv_ref.shape[0]
     shifted = [shift_rows(x_inner, taps - 1 - tap) for tap in range(taps)]
@@ -442,14 +463,17 @@
         summed = summed + conv_ref[tap : tap + 1, :] * shifted[tap]
     sig = sigmoid(summed)
     grad_sum = grad_u * (sig * (1.0 + summed * (1.0 - sig)))
-    gradbias_ref[...] = jnp.sum(grad_sum, 0, keepdims=True)
     grad_x = jnp.zeros_like(x_inner)
     for tap in range(taps):
-        gradconv_ref[tap : tap + 1, :] = jnp.sum(grad_sum * shifted[tap], 0, keepdims=True)
+        pieces.append(jnp.sum(grad_sum * shifted[tap], 0, keepdims=True))
         grad_x = grad_x + conv_ref[tap : tap + 1, :] * shift_rows(grad_sum, tap + 1 - taps)
+    pieces.append(jnp.sum(grad_sum, 0, keepdims=True))
+    pieces.append(jnp.zeros((pack_ref.shape[1] - grad_proj.shape[1] - taps - 1, x_inner.shape[1]), F32))
+    split_lanes(pack_ref, jnp.concatenate(pieces, 0).astype(BF16))
     grad_x = grad_x.astype(BF16)
-    gradx_ref[...] = grad_x
-    total[...] += product(grad_x, wx_ref[...]) + product(gradgate_ref[...], wg_ref[...])
+    split_lanes(gradx_ref, grad_x)
+    grad_gate = jnp.concatenate([gradgate_ref[k] for k in range(gradgate_ref.shape[0])], 1)
+    total[...] += product(grad_x, wx_ref[...]) + product(grad_gate, wg_ref[...])
 
     @pl.when(tile_id == pl.num_programs(0) - 1)
     def _():
@@ -457,7 +481,11 @@
         scale = lax.rsqrt(jnp.mean(values * values, -1, keepdims=True) + 1e-05)
         unit = values * scale
         grad = total[...]
-        gradgain_ref[...] = jnp.sum(grad * unit, 0, keepdims=True)
+        widths = jnp.concatenate([widths_ref[...], jnp.sum(grad * unit, 0, keepdims=True)], 0)
+        widths = jnp.concatenate(
+            [widths, jnp.zeros((tail_ref.shape[1] - widths.shape[0], widths.shape[1]), F32)], 0
+        )
+        split_lanes(tail_ref, widths.astype(BF16))
         inner = grad * gain_ref[...]
         gradtok_ref[...] = gradmid_ref[...] + scale * (
             inner - unit * jnp.mean(inner * unit, -1, keepdims=True)
@@ -466,9 +494,13 @@
 
 def mixer_back(
     grad_proj, scan_w, grad_u, x_inner, conv, bias, grad_gate, in_t, u_act, tokens, gain, grad_mid,
-    tile,
+    grad_widths, tile, devices,
 ):
     rows, channels = u_act.shape
+    gate_parts = tile * devices // (2 * channels)
+    pack_parts = tile * devices // channels
+    pack_rows = scan_w.shape[1] + 8
+    tail_rows = grad_widths.shape[0] + 7
     width = tokens.shape[1]
     cols = scan_w.shape[1]
     taps = conv.shape[0]
@@ -485,36 +517,33 @@
             pl.BlockSpec((rows, tile), column),
             pl.BlockSpec((taps, tile), column),
             pl.BlockSpec((1, tile), column),
-            pl.BlockSpec((rows, tile), column),
+            pl.BlockSpec((gate_parts, rows, tile // gate_parts), lambda i: (i, 0, 0)),
             pl.BlockSpec((tile, width), lambda i: (i, 0)),
             pl.BlockSpec((tile, width), lambda i: (i + steps, 0)),
             pl.BlockSpec((rows, tile), column),
             pl.BlockSpec((rows, width), fixed),
             pl.BlockSpec((1, width), fixed),
             pl.BlockSpec((rows, width), fixed),
+            pl.BlockSpec(grad_widths.shape, fixed),
         ],
         out_specs=[
-            pl.BlockSpec((rows, tile), column),
-            pl.BlockSpec((taps, tile), column),
-            pl.BlockSpec((1, tile), column),
-            pl.BlockSpec((tile, cols), lambda i: (i, 0)),
+            pl.BlockSpec((gate_parts, rows, tile // gate_parts), lambda i: (i, 0, 0)),
+            pl.BlockSpec((pack_parts, pack_rows, tile // pack_parts), lambda i: (i, 0, 0)),
+            pl.BlockSpec((devices, tail_rows, width // devices), lambda i: (0, 0, 0)),
             pl.BlockSpec((rows, width), fixed),
-            pl.BlockSpec((1, width), fixed),
         ],
         out_shape=[
-            jax.ShapeDtypeStruct((rows, channels), BF16),
-            jax.ShapeDtypeStruct((taps, channels), F32),
-            jax.ShapeDtypeStruct((1, channels), F32),
-            jax.ShapeDtypeStruct((channels, cols), F32),
+            jax.ShapeDtypeStruct((devices // 2, rows, 2 * channels // devices), BF16),
+            jax.ShapeDtypeStruct((devices, pack_rows, channels // devices), BF16),
+            jax.ShapeDtypeStruct((devices, tail_rows, width // devices), BF16),
             jax.ShapeDtypeStruct((rows, width), F32),
-            jax.ShapeDtypeStruct((1, width), F32),
         ],
         scratch_shapes=[pltpu.VMEM((rows, width), F32)],
         compiler_params=pltpu.CompilerParams(vmem_limit_bytes=VMEM_LIMIT),
         name="mixer_back",
     )(
         grad_proj, scan_w, grad_u, x_inner, conv, bias, grad_gate, in_t, in_t, u_act, tokens, gain,
-        grad_mid,
+        grad_mid, grad_widths,
     )
 
 
@@ -533,7 +562,7 @@
 
 def router_kernel(
     mid_ref, gain_ref, router_ref, routes_col_ref, routes_row_ref, slots_row_ref, live_ref, cot_ref,
-    send_ref, normed_ref, probs_ref,
+    sendr_ref, sendg_ref, normed_ref, probs_ref,
 ):
     mid = mid_ref[...]
     rows = mid.shape[0]
@@ -553,8 +582,8 @@
         (routes_row_ref[...] == slot // CAP) & (slots_row_ref[...] == slot % CAP)
     ).astype(BF16)
     width = mid.shape[1]
-    send_ref[:, :CAP, :] = product(dispatch, normed).astype(BF16).reshape(experts, CAP, width)
-    send_ref[:, CAP:, :] = product(dispatch, grads).astype(BF16).reshape(experts, CAP, width)
+    sendr_ref[...] = product(dispatch, normed).astype(BF16).reshape(experts, CAP, width)
+    sendg_ref[...] = product(dispatch, grads).astype(BF16).reshape(experts, CAP, width)
 
 
 def router_step(mid, gain, router, routes_col, routes_row, slots_row, live, cotangent):
@@ -563,7 +592,8 @@
     return pl.pallas_call(
         router_kernel,
         out_shape=[
-            jax.ShapeDtypeStruct((experts, 2 * CAP, width), BF16),
+            jax.ShapeDtypeStruct((experts, CAP, width), BF16),
+            jax.ShapeDtypeStruct((experts, CAP, width), BF16),
             jax.ShapeDtypeStruct((rows, width), BF16),
             jax.ShapeDtypeStruct((rows, experts), F32),
         ],
@@ -572,54 +602,95 @@
     )(mid, gain, router, routes_col, routes_row, slots_row, live, cotangent)
 
 
-def expert_kernel(got_ref, up_ref, down_ref, back_ref, out_sum, in_sum):
+def expert_out_kernel(rows_ref, up_ref, down_ref, out_ref, slope_ref, total):
     step = pl.program_id(0)
-    pieces, double, width = got_ref.shape
-    rows = got_ref[:, :CAP, :].reshape(pieces * CAP, width)
-    grads = got_ref[:, CAP:, :].reshape(pieces * CAP, width)
+    pieces, cap, width = rows_ref.shape
+    rows = rows_ref[...].reshape(pieces * cap, width)
 
     @pl.when(step == 0)
     def _():
-        out_sum[...] = jnp.zeros_like(out_sum)
-        in_sum[...] = jnp.zeros_like(in_sum)
+        total[...] = jnp.zeros_like(total)
 
     activated, slope = gelu_parts(product(rows, up_ref[...]))
-    out_sum[...] += product(activated.astype(BF16), down_ref[...])
-    grad_pre = (times_transpose(grads, down_ref[...]) * slope).astype(BF16)
-    in_sum[...] += times_transpose(grad_pre, up_ref[...])
+    slope_ref[...] = slope.astype(BF16)
+    total[...] += product(activated.astype(BF16), down_ref[...])
 
     @pl.when(step == pl.num_programs(0) - 1)
     def _():
-        back_ref[:, :CAP, :] = out_sum[...].astype(BF16).reshape(pieces, CAP, width)
-        back_ref[:, CAP:, :] = in_sum[...].astype(BF16).reshape(pieces, CAP, width)
-
-
-def expert_step(got, up, down, tile):
-    pieces, double, width = got.shape
+        out_ref[...] = total[...].astype(BF16).reshape(pieces, cap, width)
+
+
+def expert_out(rows, up, down, tile):
+    pieces, cap, width = rows.shape
     hidden = up.shape[1]
     fixed = lambda i: (0, 0, 0)
     return pl.pallas_call(
-        expert_kernel,
+        expert_out_kernel,
         grid=(hidden // tile,),
         in_specs=[
-            pl.BlockSpec(got.shape, fixed),
+            pl.BlockSpec(rows.shape, fixed),
             pl.BlockSpec((width, tile), lambda i: (0, i)),
             pl.BlockSpec((tile, width), lambda i: (i, 0)),
         ],
-        out_specs=pl.BlockSpec(got.shape, fixed),
-        out_shape=jax.ShapeDtypeStruct(got.shape, BF16),
-        scratch_shapes=[pltpu.VMEM((pieces * CAP, width), F32)] * 2,
+        out_specs=[
+            pl.BlockSpec(rows.shape, fixed),
+            pl.BlockSpec((pieces * cap, tile), lambda i: (0, i)),
+        ],
+        out_shape=[
+            jax.ShapeDtypeStruct(rows.shape, BF16),
+            jax.ShapeDtypeStruct((pieces * cap, hidden), BF16),
+        ],
+        scratch_shapes=[pltpu.VMEM((pieces * cap, width), F32)],
         compiler_params=pltpu.CompilerParams(vmem_limit_bytes=VMEM_LIMIT),
-        name="expert_step",
-    )(got, up, down)
-
-
-def expert_grads_kernel(chunks, all_ref, up_ref, down_ref, gup_ref, gdown_ref, rows_t):
+        name="expert_out",
+    )(rows, up, down)
+
+
+def expert_back_kernel(grads_ref, up_ref, down_ref, slope_ref, out_ref, total):
+    step = pl.program_id(0)
+    pieces, cap, width = grads_ref.shape
+    grads = grads_ref[...].reshape(pieces * cap, width)
+
+    @pl.when(step == 0)
+    def _():
+        total[...] = jnp.zeros_like(total)
+
+    slope = slope_ref[...].astype(F32)
+    grad_pre = (times_transpose(grads, down_ref[...]) * slope).astype(BF16)
+    total[...] += times_transpose(grad_pre, up_ref[...])
+
+    @pl.when(step == pl.num_programs(0) - 1)
+    def _():
+        out_ref[...] = total[...].astype(BF16).reshape(pieces, cap, width)
+
+
+def expert_back(grads, up, down, slope, tile):
+    pieces, cap, width = grads.shape
+    hidden = up.shape[1]
+    fixed = lambda i: (0, 0, 0)
+    return pl.pallas_call(
+        expert_back_kernel,
+        grid=(hidden // tile,),
+        in_specs=[
+            pl.BlockSpec(grads.shape, fixed),
+            pl.BlockSpec((width, tile), lambda i: (0, i)),
+            pl.BlockSpec((tile, width), lambda i: (i, 0)),
+            pl.BlockSpec((pieces * cap, tile), lambda i: (0, i)),
+        ],
+        out_specs=pl.BlockSpec(grads.shape, fixed),
+        out_shape=jax.ShapeDtypeStruct(grads.shape, BF16),
+        scratch_shapes=[pltpu.VMEM((pieces * cap, width), F32)],
+        compiler_params=pltpu.CompilerParams(vmem_limit_bytes=VMEM_LIMIT),
+        name="expert_back",
+    )(grads, up, down, slope)
+
+
+def expert_grads_kernel(chunks, rows_ref, grads_ref, up_ref, down_ref, gup_ref, gdown_ref, rows_t):
     chunk = pl.program_id(1)
-    groups, pieces, double, width = all_ref.shape
-    count = groups * pieces * CAP
-    rows = all_ref[:, :, :CAP, :].reshape(count, width)
-    grads = all_ref[:, :, CAP:, :].reshape(count, width)
+    groups, pieces, cap, width = rows_ref.shape
+    count = groups * pieces * cap
+    rows = rows_ref[...].reshape(count, width)
+    grads = grads_ref[...].reshape(count, width)
 
     @pl.when((pl.program_id(0) == 0) | (chunks > 1))
     def _():
@@ -643,16 +714,18 @@
             gdown_ref[...] += grad_down
 
 
-def expert_grads(gathered, up, down, tile):
-    groups, pieces, double, width = gathered.shape
+def expert_grads(rows, grads, up, down, tile):
+    groups, pieces, cap, width = rows.shape
     hidden = up.shape[1]
     together = max(1, min(groups, 32 // pieces))
     chunks = groups // together
+    some = pl.BlockSpec((together, pieces, cap, width), lambda i, j: (j, 0, 0, 0))
     return pl.pallas_call(
         partial(expert_grads_kernel, chunks),
         grid=(hidden // tile, chunks),
         in_specs=[
-            pl.BlockSpec((together, pieces, double, width), lambda i, j: (j, 0, 0, 0)),
+            some,
+            some,
             pl.BlockSpec((width, tile), lambda i, j: (0, i)),
             pl.BlockSpec((tile, width), lambda i, j: (i, 0)),
         ],
@@ -664,15 +737,15 @@
             jax.ShapeDtypeStruct((width, hidden), F32),
             jax.ShapeDtypeStruct((hidden, width), F32),
         ],
-        scratch_shapes=[pltpu.VMEM((width, together * pieces * CAP), BF16)],
+        scratch_shapes=[pltpu.VMEM((width, together * pieces * cap), BF16)],
         compiler_params=pltpu.CompilerParams(vmem_limit_bytes=VMEM_LIMIT),
         name="expert_grads",
-    )(gathered, up, down)
+    )(rows, grads, up, down)
 
 
 def combine_kernel(
     mid_ref, gain_ref, router_ref, routes_ref, slots_ref, live_ref, cot_ref, probs_ref, normed_ref,
-    back_ref, out_ref, gradmid_ref, gradmix_ref, gradrouter_ref, gradgain_ref,
+    backr_ref, backg_ref, out_ref, gradmid_ref, gradmix_ref, widths_ref,
 ):
     mid = mid_ref[...]
     rows, width = mid.shape
@@ -684,24 +757,24 @@
     live = live_ref[...]
     slot = iota((rows, experts * CAP), 1)
     collect = ((routes == slot // CAP) & (slots_ref[...] == slot % CAP)).astype(BF16)
-    expert_sum = product(collect, back_ref[:, :CAP, :].reshape(experts * CAP, width))
+    expert_sum = product(collect, backr_ref[...].reshape(experts * CAP, width))
     out_ref[...] = (live * (mid + gate * expert_sum)).astype(BF16)
     grad_out = cot_ref[...].astype(F32) * live
     grad_gate = jnp.sum(grad_out * expert_sum, 1, keepdims=True)
     grad_logits = (probs * (chosen * grad_gate - gate * grad_gate)).astype(BF16)
-    gradrouter_ref[...] = contract_rows(normed_ref[...], grad_logits)
-    grad = product(collect, back_ref[:, CAP:, :].reshape(experts * CAP, width))
+    grad_router = contract_rows(grad_logits, normed_ref[...])
+    grad = product(collect, backg_ref[...].reshape(experts * CAP, width))
     grad = grad + times_transpose(grad_logits, router_ref[...])
     scale = lax.rsqrt(jnp.mean(mid * mid, -1, keepdims=True) + 1e-05)
     unit = mid * scale
-    gradgain_ref[...] = jnp.sum(grad * unit, 0, keepdims=True)
+    widths_ref[...] = jnp.concatenate([grad_router, jnp.sum(grad * unit, 0, keepdims=True)], 0)
     inner = grad * gain_ref[...]
     grad_mid = grad_out + scale * (inner - unit * jnp.mean(inner * unit, -1, keepdims=True))
     gradmid_ref[...] = grad_mid
     gradmix_ref[...] = grad_mid.astype(BF16)
 
 
-def combine_step(mid, gain, router, routes, slots, live, cotangent, probs, normed, back):
+def combine_step(mid, gain, router, routes, slots, live, cotangent, probs, normed, backr, backg):
     rows, width = mid.shape
     return pl.pallas_call(
         combine_kernel,
@@ -709,12 +782,907 @@
             jax.ShapeDtypeStruct((rows, width), BF16),
             jax.ShapeDtypeStruct((rows, width), F32),
             jax.ShapeDtypeStruct((rows, width), BF16),
-            jax.ShapeDtypeStruct(router.shape, F32),
-            jax.ShapeDtypeStruct((1, width), F32),
+            jax.ShapeDtypeStruct((router.shape[1] + 1, width), F32),
         ],
         compiler_params=pltpu.CompilerParams(vmem_limit_bytes=VMEM_LIMIT),
         name="combine_step",
-    )(mid, gain, router, routes, slots, live, cotangent, probs, normed, back)
+    )(mid, gain, router, routes, slots, live, cotangent, probs, normed, backr, backg)
+
+
+MESH = pl.DeviceIdType.MESH
+
+
+def neighbour(bit):
+    me = lax.axis_index("expert")
+    return me + (1 - 2 * ((me // bit) % 2)) * bit
+
+
+def greet(line=True):
+    devices, copies = lax.axis_size("expert"), lax.axis_size("dp")
+    me, place = lax.axis_index("expert"), lax.axis_index("dp")
+    barrier = pltpu.get_barrier_semaphore()
+    for k in range(1, devices):
+        pl.semaphore_signal(
+            barrier, inc=1, device_id={"expert": (me + k) % devices}, device_id_type=MESH
+        )
+    if line:
+
+        @pl.when(place < copies - 1)
+        def _():
+            pl.semaphore_signal(barrier, inc=1, device_id={"dp": place + 1}, device_id_type=MESH)
+
+        @pl.when(place > 0)
+        def _():
+            pl.semaphore_signal(barrier, inc=1, device_id={"dp": place - 1}, device_id_type=MESH)
+
+    ends = (place == 0) | (place == copies - 1)
+    if line:
+        pl.when(ends)(lambda: pl.semaphore_wait(barrier, devices))
+        pl.when(jnp.logical_not(ends))(lambda: pl.semaphore_wait(barrier, devices + 1))
+    else:
+        pl.semaphore_wait(barrier, devices - 1)
+
+
+class Exchange:
+    def __init__(self, source, target, send_sems, recv_sems, local_sem):
+        devices, me = lax.axis_size("expert"), lax.axis_index("expert")
+        self.copies = []
+        for k in range(1, devices):
+            peer = (me + k) % devices
+            self.copies.append(
+                pltpu.make_async_remote_copy(
+                    source.at[peer], target.at[me], send_sems.at[k], recv_sems.at[k],
+                    device_id={"expert": peer}, device_id_type=MESH,
+                )
+            )
+        self.local = pltpu.make_async_copy(source.at[me], target.at[me], local_sem)
+
+    def start(self):
+        for copy in self.copies:
+            copy.start()
+        self.local.start()
+
+    def wait(self):
+        self.local.wait()
+        for copy in self.copies:
+            copy.wait()
+
+
+class Line:
+    def __init__(self, stage, from_left, from_right, next_left, next_right, send_sems, recv_sems):
+        place = lax.axis_index("dp")
+        last = lax.axis_size("dp") - 1
+        self.right = pltpu.make_async_remote_copy(
+            from_left, next_left, send_sems.at[0], recv_sems.at[0],
+            device_id={"dp": jnp.minimum(place + 1, last)}, device_id_type=MESH,
+        )
+        self.left = pltpu.make_async_remote_copy(
+            from_right, next_right, send_sems.at[1], recv_sems.at[1],
+            device_id={"dp": jnp.maximum(place - 1, 0)}, device_id_type=MESH,
+        )
+        self.send_right = (place >= stage - 1) & (place < last)
+        self.send_left = (last - place >= stage - 1) & (place > 0)
+        self.get_left = place >= stage
+        self.get_right = last - place >= stage
+
+    def start(self):
+        pl.when(self.send_right)(lambda: self.right.start())
+        pl.when(self.send_left)(lambda: self.left.start())
+
+    def wait(self):
+        pl.when(self.send_right)(lambda: self.right.wait_send())
+        pl.when(self.send_left)(lambda: self.left.wait_send())
+        pl.when(self.get_left)(lambda: self.right.wait_recv())
+        pl.when(self.get_right)(lambda: self.left.wait_recv())
+
+
+def expert_layer_kernel(
+    mid_ref, gain_ref, router_ref, routes_col_ref, routes_row_ref, slots_col_ref, slots_row_ref,
+    live_ref, cot_ref, up_hbm, down_hbm,
+    out_ref, gradmid_ref, gradmix_ref, widths_ref, rows_out, grads_out, left_rows, right_rows,
+    up_ref, down_ref, normed_ref, send_r, send_g, got_r, got_g, slope_ref, total, give_r, give_g,
+    back_r, back_g, probs_ref, weight_sems, send_sems, recv_sems, local_sems, line_send, line_recv,
+    out_sems,
+):
+    tile = 512
+    rows, width = mid_ref.shape
+    experts = router_ref.shape[1]
+    hidden = up_ref.shape[1]
+    load_up = pltpu.make_async_copy(up_hbm, up_ref, weight_sems.at[0])
+    load_down = pltpu.make_async_copy(down_hbm, down_ref, weight_sems.at[1])
+    load_up.start()
+    load_down.start()
+    greet()
+
+    ways = [
+        Exchange(source, target, send_sems.at[k], recv_sems.at[k], local_sems.at[k])
+        for k, (source, target) in enumerate(
+            [(send_r, got_r), (send_g, got_g), (give_r, back_r), (give_g, back_g)]
+        )
+    ]
+    mid = mid_ref[...]
+    scale = lax.rsqrt(jnp.mean(mid * mid, -1, keepdims=True) + 1e-05)
+    normed = (mid * scale * gain_ref[...]).astype(BF16)
+    normed_ref[...] = normed
+    slot = iota((experts * CAP, rows), 0)
+    dispatch = (
+        (routes_row_ref[...] == slot // CAP) & (slots_row_ref[...] == slot % CAP)
+    ).astype(BF16)
+    send_r[...] = product(dispatch, normed).astype(BF16).reshape(experts, CAP, width)
+    ways[0].start()
+    logits = product(normed, router_ref[...])
+    weights = jnp.exp(logits - jnp.max(logits, -1, keepdims=True))
+    probs = weights / jnp.sum(weights, -1, keepdims=True)
+    probs_ref[...] = probs
+    chosen = (routes_col_ref[...] == iota((rows, experts), 1)).astype(F32)
+    gate = jnp.sum(probs * chosen, 1, keepdims=True)
+    grads = (gate * (cot_ref[...].astype(F32) * live_ref[...])).astype(BF16)
+    send_g[...] = product(dispatch, grads).astype(BF16).reshape(experts, CAP, width)
+    ways[1].start()
+
+    load_up.wait()
+    load_down.wait()
+    ways[0].wait()
+    line = Line(1, got_r, got_r, left_rows, right_rows, line_send, line_recv)
+    line.start()
+    keep_rows = pltpu.make_async_copy(got_r, rows_out, out_sems.at[0])
+    keep_rows.start()
+    total[...] = jnp.zeros_like(total)
+
+    def forward(step, carry):
+        at = pl.ds(pl.multiple_of(step * tile, tile), tile)
+        inputs = got_r[...].reshape(experts * CAP, width)
+        activated, slope = gelu_parts(product(inputs, up_ref[:, at]))
+        slope_ref[:, at] = slope.astype(BF16)
+        total[...] += product(activated.astype(BF16), down_ref[at, :])
+        return carry
+
+    lax.fori_loop(0, hidden // tile, forward, 0)
+    give_r[...] = total[...].astype(BF16).reshape(experts, CAP, width)
+    ways[2].start()
+    ways[1].wait()
+    keep_grads = pltpu.make_async_copy(got_g, grads_out, out_sems.at[1])
+    keep_grads.start()
+    total[...] = jnp.zeros_like(total)
+
+    def backward(step, carry):
+        at = pl.ds(pl.multiple_of(step * tile, tile), tile)
+        outputs = got_g[...].reshape(experts * CAP, width)
+        slope = slope_ref[:, at].astype(F32)
+        grad_pre = (times_transpose(outputs, down_ref[at, :]) * slope).astype(BF16)
+        total[...] += times_transpose(grad_pre, up_ref[:, at])
+        return carry
+
+    lax.fori_loop(0, hidden // tile, backward, 0)
+    give_g[...] = total[...].astype(BF16).reshape(experts, CAP, width)
+    ways[3].start()
+
+    routes = routes_col_ref[...]
+    chosen = (routes == iota((rows, experts), 1)).astype(F32)
+    probs = probs_ref[...]
+    gate = jnp.sum(probs * chosen, 1, keepdims=True)
+    live = live_ref[...]
+    slot = iota((rows, experts * CAP), 1)
+    collect = ((routes == slot // CAP) & (slots_col_ref[...] == slot % CAP)).astype(BF16)
+    ways[2].wait()
+    expert_sum = product(collect, back_r[...].reshape(experts * CAP, width))
+    mid = mid_ref[...]
+    out_ref[...] = (live * (mid + gate * expert_sum)).astype(BF16)
+    grad_out = cot_ref[...].astype(F32) * live
+    grad_gate = jnp.sum(grad_out * expert_sum, 1, keepdims=True)
+    grad_logits = (probs * (chosen * grad_gate - gate * grad_gate)).astype(BF16)
+    grad_router = contract_rows(grad_logits, normed_ref[...])
+    from_logits = times_transpose(grad_logits, router_ref[...])
+    scale = lax.rsqrt(jnp.mean(mid * mid, -1, keepdims=True) + 1e-05)
+    unit = mid * scale
+    ways[3].wait()
+    grad = product(collect, back_g[...].reshape(experts * CAP, width)) + from_logits
+    widths_ref[...] = jnp.concatenate([grad_router, jnp.sum(grad * unit, 0, keepdims=True)], 0)
+    inner = grad * gain_ref[...]
+    grad_mid = grad_out + scale * (inner - unit * jnp.mean(inner * unit, -1, keepdims=True))
+    gradmid_ref[...] = grad_mid
+    gradmix_ref[...] = grad_mid.astype(BF16)
+    keep_rows.wait()
+    keep_grads.wait()
+    line.wait()
+
+
+def expert_layer(
+    mid, gain, router, routes_col, routes_row, slots_col, slots_row, live, cotangent, up, down
+):
+    rows, width = mid.shape
+    experts = router.shape[1]
+    hidden = up.shape[1]
+    buffer = (experts, CAP, width)
+    here = pl.BlockSpec(memory_space=pltpu.VMEM)
+    far = pl.BlockSpec(memory_space=pl.ANY)
+    slots = jax.ShapeDtypeStruct(buffer, BF16)
+    dma = pltpu.SemaphoreType.DMA
+    return pl.pallas_call(
+        expert_layer_kernel,
+        in_specs=[here] * 9 + [far] * 2,
+        out_specs=[here] * 4 + [far] * 4,
+        out_shape=[
+            jax.ShapeDtypeStruct((rows, width), BF16),
+            jax.ShapeDtypeStruct((rows, width), F32),
+            jax.ShapeDtypeStruct((rows, width), BF16),
+            jax.ShapeDtypeStruct((experts + 1, width), F32),
+        ] + [slots] * 4,
+        scratch_shapes=[
+            pltpu.VMEM(up.shape, BF16),
+            pltpu.VMEM(down.shape, BF16),
+            pltpu.VMEM((rows, width), BF16),
+        ] + [pltpu.VMEM(buffer, BF16)] * 4 + [
+            pltpu.VMEM((experts * CAP, hidden), BF16),
+            pltpu.VMEM((experts * CAP, width), F32),
+        ] + [pltpu.VMEM(buffer, BF16)] * 4 + [
+            pltpu.VMEM((rows, experts), F32),
+            dma((2,)), dma((4, experts)), dma((4, experts)), dma((4,)), dma((2,)), dma((2,)),
+            dma((2,)),
+        ],
+        compiler_params=pltpu.CompilerParams(
+            vmem_limit_bytes=VMEM_LIMIT, collective_id=1, has_side_effects=True
+        ),
+        name="expert_layer",
+    )(mid, gain, router, routes_col, routes_row, slots_col, slots_row, live, cotangent, up, down)
+
+
+class PlaneGather:
+    def __init__(self, source, target, send_sems, recv_sems, local_sem):
+        me = lax.axis_index("expert")
+        core, side, above = neighbour(1), neighbour(2), neighbour(4)
+        far = side + above - me
+        rows = target.shape[1]
+        first, second = pl.ds(0, rows // 2), pl.ds(rows // 2, rows - rows // 2)
+        every = pl.ds(0, rows)
+
+        def send(k, block, owner, part, device):
+            return pltpu.make_async_remote_copy(
+                block, target.at[owner, part], send_sems.at[k], recv_sems.at[k],
+                device_id={"expert": device}, device_id_type=MESH,
+            )
+
+        self.copies = [
+            send(0, source.at[first], me, first, side),
+            send(1, source.at[second], me, second, side),
+            send(2, source.at[first], me, first, above),
+            send(3, source.at[second], me, second, above),
+            send(4, target.at[side, first], side, first, above),
+            send(5, target.at[above, second], above, second, side),
+            send(6, source, me, every, core),
+            send(7, target.at[side], side, every, core),
+            send(8, target.at[above], above, every, core),
+            send(9, target.at[far], far, every, core),
+        ]
+        self.local = pltpu.make_async_copy(source, target.at[me], local_sem)
+
+    def step(self, number):
+        copies = self.copies
+        for k in ((), (0, 3), (1, 2), (4, 5), (6, 7, 8, 9))[number]:
+            copies[k].wait_recv()
+        for k in ((0, 3, 1, 2, 6), (4, 5), (7, 8), (9,), ())[number]:
+            copies[k].start()
+        if number == 0:
+            self.local.start()
+        if number == 4:
+            self.local.wait()
+            for copy in copies:
+                copy.wait_send()
+
+
+class Spread:
+    def __init__(self, source, target, send_sems, recv_sems, local_sem):
+        devices, me = lax.axis_size("expert"), lax.axis_index("expert")
+        self.copies = [
+            pltpu.make_async_remote_copy(
+                source, target.at[me], send_sems.at[k], recv_sems.at[k],
+                device_id={"expert": (me + k) % devices}, device_id_type=MESH,
+            )
+            for k in range(1, devices)
+        ]
+        self.local = pltpu.make_async_copy(source, target.at[me], local_sem)
+
+    start, wait = Exchange.start, Exchange.wait
+
+
+DMA = pltpu.SemaphoreType.DMA
+FAR = pl.BlockSpec(memory_space=pl.ANY)
+
+
+def remote_params(collective_id):
+    return pltpu.CompilerParams(
+        vmem_limit_bytes=VMEM_LIMIT, collective_id=collective_id, has_side_effects=True
+    )
+
+
+def gather_kernel(in_ref, *refs):
+    small = len(refs) // 2 - 3
+    sources, targets = refs[:small], refs[small + 1 : 2 * small + 1]
+    in_full = refs[small]
+    big_send, big_recv, small_send, small_recv, local_sems = refs[2 * small + 1 :]
+    greet(line=False)
+    big = PlaneGather(in_ref, in_full, big_send, big_recv, local_sems.at[small])
+    spreads = [
+        Spread(sources[k], targets[k], small_send.at[k], small_recv.at[k], local_sems.at[k])
+        for k in range(small)
+    ]
+    big.step(0)
+    for spread in spreads:
+        spread.start()
+    for number in range(1, 5):
+        big.step(number)
+    for spread in spreads:
+        spread.wait()
+
+
+def gather_weights(in_t, *small):
+    devices = lax.axis_size("expert")
+    count = len(small)
+    full = [jax.ShapeDtypeStruct((devices,) + v.shape, v.dtype) for v in (in_t,) + small]
+    return pl.pallas_call(
+        gather_kernel,
+        in_specs=[FAR] * (count + 1),
+        out_specs=[FAR] * (count + 1),
+        out_shape=full,
+        scratch_shapes=[
+            DMA((10,)), DMA((10,)), DMA((count, devices)), DMA((count, devices)), DMA((count + 1,)),
+        ],
+        compiler_params=remote_params(2),
+        name="gather_weights",
+    )(in_t, *small)
+
+
+def scan_plane_kernel(
+    proj_ref, stepw_ref, dbias_ref, decay_ref, skip_ref, u_ref, gate_ref, tokens_ref, outw_ref,
+    step_ref, mixed_ref, gated_ref, hist_ref, mid_ref, outw_all,
+    b_wide, c_blocks, du, scanned, gated_all, outw_here, send_sems, recv_sems, local_sems,
+):
+    tile_id = pl.program_id(0)
+    rank, state = stepw_ref.shape[0], decay_ref.shape[0]
+    tile = u_ref.shape[1]
+    gather = PlaneGather(outw_ref, outw_here, send_sems, recv_sems, local_sems.at[0])
+    keep = pltpu.make_async_copy(outw_here, outw_all, local_sems.at[1])
+
+    @pl.when(tile_id == 0)
+    def _():
+        greet(line=False)
+        gather.step(0)
+        scan_prepare(proj_ref, b_wide, c_blocks, rank, rank + state, state)
+
+    def between(half):
+        for turn in range(2):
+
+            @pl.when(tile_id == turn)
+            def _():
+                gather.step(2 * turn + half + 1)
+                if turn + half == 2:
+                    keep.start()
+
+    gated = scan_tile(
+        proj_ref, stepw_ref, dbias_ref, decay_ref, skip_ref, u_ref, gate_ref, step_ref, mixed_ref,
+        hist_ref, b_wide, c_blocks, du, scanned, between,
+    )
+    split_lanes(gated_ref, gated)
+    gated_all[:, pl.ds(pl.multiple_of(tile_id * tile, tile), tile)] = gated
+
+    @pl.when(tile_id == 1)
+    def _():
+        devices, part, width = outw_here.shape
+        weights = outw_here[...].reshape(devices * part, width)
+        mid_ref[...] = tokens_ref[...].astype(F32) + product(gated_all[...], weights)
+        keep.wait()
+
+
+def scan_forward_plane(proj, step_w, dbias, decay, skip, u_act, gate_in, out_w, tokens):
+    rows, channels = u_act.shape
+    width = tokens.shape[1]
+    cols = proj.shape[1]
+    rank, state = step_w.shape[0], decay.shape[0]
+    devices = lax.axis_size("expert")
+    tile = channels // 2
+    part = channels // devices
+    hist_rows = (rows + 1) * state
+    column = lambda i: (0, i)
+    fixed = lambda i: (0, 0)
+    return pl.pallas_call(
+        scan_plane_kernel,
+        grid=(2,),
+        in_specs=[
+            pl.BlockSpec((rows, cols), fixed),
+            pl.BlockSpec((rank, tile), column),
+            pl.BlockSpec((1, tile), column),
+            pl.BlockSpec((state, tile), column),
+            pl.BlockSpec((1, tile), column),
+            pl.BlockSpec((rows, tile), column),
+            pl.BlockSpec((rows, tile), column),
+            pl.BlockSpec((rows, width), fixed),
+            FAR,
+        ],
+        out_specs=[
+            pl.BlockSpec((rows, tile), column),
+            pl.BlockSpec((rows, tile), column),
+            pl.BlockSpec((devices // 2, rows, part), lambda i: (i, 0, 0)),
+            pl.BlockSpec((hist_rows, tile), column),
+            pl.BlockSpec((rows, width), fixed),
+            FAR,
+        ],
+        out_shape=[
+            jax.ShapeDtypeStruct((rows, channels), F32),
+            jax.ShapeDtypeStruct((rows, channels), F32),
+            jax.ShapeDtypeStruct((devices, rows, part), BF16),
+            jax.ShapeDtypeStruct((hist_rows, channels), BF16),
+            jax.ShapeDtypeStruct((rows, width), F32),
+            jax.ShapeDtypeStruct((devices, part, width), BF16),
+        ],
+        scratch_shapes=[
+            pltpu.VMEM((rows * state, 128), F32),
+            pltpu.VMEM((rows * 2, BLOCK * state), BF16),
+            pltpu.VMEM((rows, tile), F32),
+            pltpu.VMEM((rows, tile), F32),
+            pltpu.VMEM((rows, channels), BF16),
+            pltpu.VMEM((devices, part, width), BF16),
+            DMA((10,)), DMA((10,)), DMA((2,)),
+        ],
+        compiler_params=remote_params(3),
+        name="scan_forward_plane",
+    )(proj, step_w, dbias, decay, skip, u_act, gate_in, tokens, out_w)
+
+
+def scan_back_plane_kernel(*refs):
+    inputs, refs = refs[:12], refs[12:]
+    (mix_ref, normed_ref, gated_ref, own_grads, left_rows, right_rows), refs = refs[:6], refs[6:]
+    outputs, refs = refs[:4], refs[4:]
+    (mix_all, normed_all, gated_all, left_grads, right_grads, next_left, next_right), refs = (
+        refs[:7], refs[7:]
+    )
+    scratch, refs = refs[:10], refs[10:]
+    g_send, g_recv, x_send, x_recv, l_send, l_recv, local_sems = refs
+    tile_id = pl.program_id(0)
+    mix = PlaneGather(mix_ref, mix_all, g_send.at[0], g_recv.at[0], local_sems.at[0])
+    normed = PlaneGather(normed_ref, normed_all, g_send.at[1], g_recv.at[1], local_sems.at[1])
+    gated = Exchange(gated_ref, gated_all, x_send, x_recv, local_sems.at[2])
+    line_g = Line(
+        1, own_grads, own_grads, left_grads, right_grads, l_send.at[0], l_recv.at[0]
+    )
+    line_r = Line(
+        2, left_rows, right_rows, next_left, next_right, l_send.at[1], l_recv.at[1]
+    )
+
+    @pl.when(tile_id == 0)
+    def _():
+        greet()
+        line_g.start()
+        line_r.start()
+        mix.step(0)
+        gated.start()
+        normed.step(0)
+
+    def between(half):
+        for turn in range(2):
+
+            @pl.when(tile_id == turn)
+            def _():
+                mix.step(2 * turn + half + 1)
+                normed.step(2 * turn + half + 1)
+                if turn + half == 2:
+                    gated.wait()
+                    line_g.wait()
+                    line_r.wait()
+
+    scan_back_tile(between, *inputs, *outputs, *scratch)
+
+
+def scan_backward_plane(
+    proj, step_w, dbias, decay, skip, u_act, gate_in, out_w, grad_mix, step_size, mixed, hist,
+    normed_low, gated, own_grads, left_rows, right_rows,
+):
+    rows, channels = u_act.shape
+    width = grad_mix.shape[1]
+    cols = proj.shape[1]
+    rank, state = step_w.shape[0], decay.shape[0]
+    devices = lax.axis_size("expert")
+    tile = channels // 2
+    gate_parts, pack_parts = devices // 4, devices // 2
+    pack_rows = rank + state + 8
+    big = BLOCK * state
+    column = lambda i: (0, i)
+    fixed = lambda i: (0, 0)
+    slots = jax.ShapeDtypeStruct(own_grads.shape, BF16)
+    everyone = jax.ShapeDtypeStruct((devices, rows, width), BF16)
+    return pl.pallas_call(
+        scan_back_plane_kernel,
+        grid=(2,),
+        in_specs=[
+            pl.BlockSpec((rows, cols), fixed),
+            pl.BlockSpec((rank, tile), column),
+            pl.BlockSpec((1, tile), column),
+            pl.BlockSpec((state, tile), column),
+            pl.BlockSpec((1, tile), column),
+            pl.BlockSpec((rows, tile), column),
+            pl.BlockSpec((rows, tile), column),
+            pl.BlockSpec((tile, width), lambda i: (i, 0)),
+            pl.BlockSpec((rows, width), fixed),
+            pl.BlockSpec((rows, tile), column),
+            pl.BlockSpec((rows, tile), column),
+            pl.BlockSpec((hist.shape[0], tile), column),
+        ] + [FAR] * 6,
+        out_specs=[
+            pl.BlockSpec((rows, tile), column),
+            pl.BlockSpec((gate_parts, rows, tile // gate_parts), lambda i: (i, 0, 0)),
+            pl.BlockSpec((pack_parts, pack_rows, tile // pack_parts), lambda i: (i, 0, 0)),
+            pl.BlockSpec((rows, cols), fixed),
+        ] + [FAR] * 7,
+        out_shape=[
+            jax.ShapeDtypeStruct((rows, channels), F32),
+            jax.ShapeDtypeStruct((devices // 2, rows, 2 * channels // devices), BF16),
+            jax.ShapeDtypeStruct((devices, pack_rows, channels // devices), BF16),
+            jax.ShapeDtypeStruct((rows, cols), F32),
+            everyone,
+            everyone,
+            jax.ShapeDtypeStruct(gated.shape, BF16),
+        ] + [slots] * 4,
+        scratch_shapes=[
+            pltpu.VMEM((rows * state, 128), F32),
+            pltpu.VMEM((rows * 2, big), BF16),
+            pltpu.VMEM((rows, big), F32),
+            pltpu.VMEM((rows, big), F32),
+            pltpu.VMEM((rows, tile), F32),
+            pltpu.VMEM((rows, tile), F32),
+            pltpu.VMEM((big, tile), BF16),
+            pltpu.VMEM((big, tile), BF16),
+            pltpu.VMEM((rows, tile), F32),
+            pltpu.VMEM((rows, tile), F32),
+            DMA((2, 10)), DMA((2, 10)), DMA((devices,)), DMA((devices,)), DMA((2, 2)), DMA((2, 2)),
+            DMA((3,)),
+        ],
+        compiler_params=remote_params(4),
+        name="scan_backward_plane",
+    )(
+        proj, step_w, dbias, decay, skip, u_act, gate_in, out_w, grad_mix, step_size, mixed, hist,
+        grad_mix, normed_low, gated, own_grads, left_rows, right_rows,
+    )
+
+
+def back_plane_kernel(
+    gradproj_ref, scanw_ref, gradu_ref, xin_ref, conv_ref, bias_ref, wx_ref, wg_ref, u_ref,
+    tokens_ref, gain_ref, gradmid_ref, widths_ref,
+    gate_hbm, scan_parts, normed_hbm, mix_hbm, gated_hbm, left_grads, right_grads,
+    gradtok_ref, gradin_ref, gradout_ref, scan_ref, back_ref, tail_ref, next_left, next_right,
+    total, send_in, got_in, normed_all, mix_all, gated_all, got_scan, send_back, got_back,
+    send_tail, got_tail, x_send, x_recv, l_send, l_recv, local_sems, load_sems,
+):
+    tile_id = pl.program_id(0)
+    devices, me = lax.axis_size("expert"), lax.axis_index("expert")
+    half = devices // 2
+    gates = send_in.shape[0] // 4
+    ways = [
+        Exchange(source, target, x_send.at[k], x_recv.at[k], local_sems.at[k])
+        for k, (source, target) in enumerate(
+            [
+                (send_in, got_in), (scan_parts, got_scan), (send_back, got_back),
+                (send_tail, got_tail),
+            ]
+        )
+    ]
+    line = Line(2, left_grads, right_grads, next_left, next_right, l_send, l_recv)
+    loads = [
+        pltpu.make_async_copy(source, target, load_sems.at[k])
+        for k, (source, target) in enumerate(
+            [
+                (gate_hbm, send_in.at[pl.ds(half, half)]), (normed_hbm, normed_all),
+                (mix_hbm, mix_all), (gated_hbm, gated_all),
+            ]
+        )
+    ]
+
+    def start_inputs(late):
+        for k, copy in enumerate(ways[0].copies):
+            peer = (me + k + 1) % devices
+            pl.when((peer < half) if late else (peer >= half))(lambda copy=copy: copy.start())
+        pl.when((me < half) if late else (me >= half))(lambda: ways[0].local.start())
+
+    @pl.when(tile_id == 0)
+    def _():
+        total[...] = jnp.zeros_like(total)
+        for load in loads:
+            load.start()
+        greet()
+        line.start()
+        ways[1].start()
+        loads[0].wait()
+        start_inputs(False)
+
+    grad_proj = gradproj_ref[...].astype(BF16)
+    grad_u = gradu_ref[...] + times_transpose(grad_proj, scanw_ref[...])
+    pieces = [contract_rows(grad_proj, u_ref[...].astype(BF16))]
+    x_inner = xin_ref[...]
+    taps = conv_ref.shape[0]
+    shifted = [shift_rows(x_inner, taps - 1 - tap) for tap in range(taps)]
+    summed = bias_ref[...]
+    for tap in range(taps):
+        summed = summed + conv_ref[tap : tap + 1, :] * shifted[tap]
+    sig = sigmoid(summed)
+    grad_sum = grad_u * (sig * (1.0 + summed * (1.0 - sig)))
+    grad_x = jnp.zeros_like(x_inner)
+    for tap in range(taps):
+        pieces.append(jnp.sum(grad_sum * shifted[tap], 0, keepdims=True))
+        grad_x = grad_x + conv_ref[tap : tap + 1, :] * shift_rows(grad_sum, tap + 1 - taps)
+    pieces.append(jnp.sum(grad_sum, 0, keepdims=True))
+    spare = send_back.shape[1] - grad_proj.shape[1] - taps - 1
+    pieces.append(jnp.zeros((spare, x_inner.shape[1]), F32))
+    packed = jnp.concatenate(pieces, 0).astype(BF16)
+    grad_x = grad_x.astype(BF16)
+    for turn in range(2):
+
+        @pl.when(tile_id == turn)
+        def _():
+            split_lanes(send_back.at[pl.ds(turn * half, half)], packed)
+            split_lanes(send_in.at[pl.ds(turn * gates, gates)], grad_x)
+
+    @pl.when(tile_id == 1)
+    def _():
+        start_inputs(True)
+        ways[2].start()
+
+    for turn in range(2):
+
+        @pl.when(tile_id == turn)
+        def _():
+            first = half + turn * gates
+            grad_gate = jnp.concatenate([send_in[first + k] for k in range(gates)], 1)
+            total[...] += product(grad_x, wx_ref[...]) + product(grad_gate, wg_ref[...])
+
+    @pl.when(tile_id == 1)
+    def _():
+        values = tokens_ref[...].astype(F32)
+        scale = lax.rsqrt(jnp.mean(values * values, -1, keepdims=True) + 1e-05)
+        unit = values * scale
+        grad = total[...]
+        widths = jnp.concatenate([widths_ref[...], jnp.sum(grad * unit, 0, keepdims=True)], 0)
+        widths = jnp.concatenate(
+            [widths, jnp.zeros((send_tail.shape[1] - widths.shape[0], widths.shape[1]), F32)], 0
+        )
+        split_lanes(send_tail, widths.astype(BF16))
+        ways[3].start()
+        inner = grad * gain_ref[...]
+        gradtok_ref[...] = gradmid_ref[...] + scale * (
+            inner - unit * jnp.mean(inner * unit, -1, keepdims=True)
+        )
+        for load in loads[1:]:
+            load.wait()
+        rows, part = gated_all.shape[1:]
+        width = mix_all.shape[2]
+        gradout_ref[...] = contract_rows(
+            gated_all[...].reshape(devices * rows, part), mix_all[...].reshape(devices * rows, width)
+        ).astype(BF16)
+        ways[0].wait()
+        gradin_ref[...] = contract_rows(
+            normed_all[...].reshape(devices * rows, width),
+            got_in[...].reshape(devices * rows, got_in.shape[2]),
+        ).astype(BF16)
+        for way, got, out in (
+            (ways[1], got_scan, scan_ref), (ways[2], got_back, back_ref), (ways[3], got_tail, tail_ref),
+        ):
+            way.wait()
+            out[...] = jnp.sum(got[...].astype(F32), 0).astype(BF16)
+        line.wait()
+
+
+def mixer_back_plane(
+    grad_proj, scan_w, grad_u, x_inner, conv, bias, in_t, u_act, tokens, gain, grad_mid,
+    grad_widths, grad_gate, scan_parts, normed_all, mix_all, gated_all, left_grads, right_grads,
+):
+    rows, channels = u_act.shape
+    width = tokens.shape[1]
+    cols = scan_w.shape[1]
+    taps = conv.shape[0]
+    devices = lax.axis_size("expert")
+    part = channels // devices
+    tile = channels // 2
+    pack_rows = cols + 8
+    tail_rows = grad_widths.shape[0] + 7
+    column = lambda i: (0, i)
+    fixed = lambda i: (0, 0)
+    slots = jax.ShapeDtypeStruct(left_grads.shape, BF16)
+    return pl.pallas_call(
+        back_plane_kernel,
+        grid=(2,),
+        in_specs=[
+            pl.BlockSpec((rows, cols), fixed),
+            pl.BlockSpec((tile, cols), lambda i: (i, 0)),
+            pl.BlockSpec((rows, tile), column),
+            pl.BlockSpec((rows, tile), column),
+            pl.BlockSpec((taps, tile), column),
+            pl.BlockSpec((1, tile), column),
+            pl.BlockSpec((tile, width), lambda i: (i, 0)),
+            pl.BlockSpec((tile, width), lambda i: (i + 2, 0)),
+            pl.BlockSpec((rows, tile), column),
+            pl.BlockSpec((rows, width), fixed),
+            pl.BlockSpec((1, width), fixed),
+            pl.BlockSpec((rows, width), fixed),
+            pl.BlockSpec(grad_widths.shape, fixed),
+        ] + [FAR] * 7,
+        out_specs=[
+            pl.BlockSpec((rows, width), fixed),
+            pl.BlockSpec((width, 2 * part), fixed),
+            pl.BlockSpec((part, width), fixed),
+            pl.BlockSpec(scan_parts.shape[1:], fixed),
+            pl.BlockSpec((pack_rows, part), fixed),
+            pl.BlockSpec((tail_rows, width // devices), fixed),
+            FAR,
+            FAR,
+        ],
+        out_shape=[
+            jax.ShapeDtypeStruct((rows, width), F32),
+            jax.ShapeDtypeStruct((width, 2 * part), BF16),
+            jax.ShapeDtypeStruct((part, width), BF16),
+            jax.ShapeDtypeStruct(scan_parts.shape[1:], BF16),
+            jax.ShapeDtypeStruct((pack_rows, part), BF16),
+            jax.ShapeDtypeStruct((tail_rows, width // devices), BF16),
+            slots,
+            slots,
+        ],
+        scratch_shapes=[
+            pltpu.VMEM((rows, width), F32),
+            pltpu.VMEM((devices, rows, 2 * part), BF16),
+            pltpu.VMEM((devices, rows, 2 * part), BF16),
+            pltpu.VMEM(normed_all.shape, BF16),
+            pltpu.VMEM(mix_all.shape, BF16),
+            pltpu.VMEM(gated_all.shape, BF16),
+            pltpu.VMEM(scan_parts.shape, BF16),
+            pltpu.VMEM((devices, pack_rows, part), BF16),
+            pltpu.VMEM((devices, pack_rows, part), BF16),
+            pltpu.VMEM((devices, tail_rows, width // devices), BF16),
+            pltpu.VMEM((devices, tail_rows, width // devices), BF16),
+            DMA((4, devices)), DMA((4, devices)), DMA((2,)), DMA((2,)), DMA((4,)), DMA((4,)),
+        ],
+        compiler_params=remote_params(5),
+        name="mixer_back_plane",
+    )(
+        grad_proj, scan_w, grad_u, x_inner, conv, bias, in_t, in_t, u_act, tokens, gain, grad_mid,
+        grad_widths, grad_gate, scan_parts, normed_all, mix_all, gated_all, left_grads, right_grads,
+    )
+
+
+def add_groups(rows, grads, rows_t, up_ref, down_ref):
+    activated, slope = gelu_parts(product(rows, up_ref[...]))
+    grad_pre = (times_transpose(grads, down_ref[...]) * slope).astype(BF16)
+    return product(rows_t, grad_pre), contract_rows(activated.astype(BF16), grads)
+
+
+def first_grads_kernel(
+    up_ref, down_ref, rows_0, grads_0, rows_l1, rows_r1, grads_l1, grads_r1, rows_l2, rows_r2,
+    grads_l2, grads_r2,
+    gup_ref, gdown_ref, rows_l3, rows_r3, grads_l3, grads_r3,
+    rows_ref, grads_ref, rows_t, l_send, l_recv, load_sems,
+):
+    step = pl.program_id(0)
+    place = lax.axis_index("dp")
+    count, width = rows_ref.shape[0] * rows_ref.shape[1] * rows_ref.shape[2], rows_ref.shape[3]
+    lines = [
+        Line(3, rows_l2, rows_r2, rows_l3, rows_r3, l_send.at[0], l_recv.at[0]),
+        Line(3, grads_l2, grads_r2, grads_l3, grads_r3, l_send.at[1], l_recv.at[1]),
+    ]
+
+    @pl.when(step == 0)
+    def _():
+        greet()
+        for line in lines:
+            line.start()
+        own = [
+            pltpu.make_async_copy(rows_0, rows_ref.at[0], load_sems.at[0]),
+            pltpu.make_async_copy(grads_0, grads_ref.at[0], load_sems.at[1]),
+        ]
+        for copy in own:
+            copy.start()
+        for condition, rows_1, grads_1 in (
+            (place >= 1, rows_l1, grads_l1), (place < 1, rows_r1, grads_r1),
+        ):
+
+            @pl.when(condition)
+            def _():
+                next_to = [
+                    pltpu.make_async_copy(rows_1, rows_ref.at[1], load_sems.at[2]),
+                    pltpu.make_async_copy(grads_1, grads_ref.at[1], load_sems.at[3]),
+                ]
+                for copy in next_to:
+                    copy.start()
+                for copy in next_to:
+                    copy.wait()
+
+        for copy in own:
+            copy.wait()
+        rows_t[...] = rows_ref[...].reshape(count, width).T
+
+    gup_ref[...], gdown_ref[...] = add_groups(
+        rows_ref[...].reshape(count, width), grads_ref[...].reshape(count, width), rows_t[...],
+        up_ref, down_ref,
+    )
+
+    @pl.when(step == pl.num_programs(0) - 1)
+    def _():
+        for line in lines:
+            line.wait()
+
+
+def last_grads_kernel(
+    up_ref, down_ref, gup_in, gdown_in, *refs
+):
+    choices, (gup_ref, gdown_ref, rows_ref, grads_ref, rows_t, load_sems) = refs[:10], refs[10:]
+    rows_l2, rows_l3, rows_r1, rows_r2, rows_r3 = choices[:5]
+    grads_l2, grads_l3, grads_r1, grads_r2, grads_r3 = choices[5:]
+    step = pl.program_id(0)
+    place = lax.axis_index("dp")
+    count, width = rows_ref.shape[0] * rows_ref.shape[1] * rows_ref.shape[2], rows_ref.shape[3]
+
+    @pl.when(step == 0)
+    def _():
+        for spot, pairs in enumerate(
+            (
+                ((rows_r2, grads_r2), (rows_r1, grads_r1), (rows_l2, grads_l2), (rows_l2, grads_l2)),
+                ((rows_r3, grads_r3), (rows_r2, grads_r2), (rows_r1, grads_r1), (rows_l3, grads_l3)),
+            )
+        ):
+            for where, (rows_1, grads_1) in enumerate(pairs):
+
+                @pl.when(place == where)
+                def _():
+                    copies = [
+                        pltpu.make_async_copy(rows_1, rows_ref.at[spot], load_sems.at[0]),
+                        pltpu.make_async_copy(grads_1, grads_ref.at[spot], load_sems.at[1]),
+                    ]
+                    for copy in copies:
+                        copy.start()
+                    for copy in copies:
+                        copy.wait()
+
+        rows_t[...] = rows_ref[...].reshape(count, width).T
+
+    grad_up, grad_down = add_groups(
+        rows_ref[...].reshape(count, width), grads_ref[...].reshape(count, width), rows_t[...],
+        up_ref, down_ref,
+    )
+    gup_ref[...] = gup_in[...] + grad_up
+    gdown_ref[...] = gdown_in[...] + grad_down
+
+
+def expert_grads_plane(up, down, rows, grads, tile):
+    width, hidden = up.shape
+    slots = jax.ShapeDtypeStruct(rows[0].shape, BF16)
+    pair = (2,) + rows[0].shape
+    count = pair[0] * pair[1] * pair[2]
+    across = pl.BlockSpec((width, tile), lambda i: (0, i))
+    along = pl.BlockSpec((tile, width), lambda i: (i, 0))
+    shapes = [
+        jax.ShapeDtypeStruct((width, hidden), F32), jax.ShapeDtypeStruct((hidden, width), F32)
+    ]
+    buffers = [pltpu.VMEM(pair, BF16), pltpu.VMEM(pair, BF16), pltpu.VMEM((width, count), BF16)]
+    grad_up, grad_down, rows_l3, rows_r3, grads_l3, grads_r3 = pl.pallas_call(
+        first_grads_kernel,
+        grid=(hidden // tile,),
+        in_specs=[across, along] + [FAR] * 10,
+        out_specs=[across, along] + [FAR] * 4,
+        out_shape=shapes + [slots] * 4,
+        scratch_shapes=buffers + [DMA((2, 2)), DMA((2, 2)), DMA((4,))],
+        compiler_params=remote_params(6),
+        name="expert_grads_first",
+    )(
+        up, down, rows[0], grads[0], rows[1], rows[2], grads[1], grads[2], rows[3], rows[4],
+        grads[3], grads[4],
+    )
+    return pl.pallas_call(
+        last_grads_kernel,
+        grid=(hidden // tile,),
+        in_specs=[across, along, across, along] + [FAR] * 10,
+        out_specs=[across, along],
+        out_shape=shapes,
+        scratch_shapes=buffers + [DMA((2,))],
+        compiler_params=pltpu.CompilerParams(vmem_limit_bytes=VMEM_LIMIT),
+        name="expert_grads_last",
+    )(
+        up, down, grad_up, grad_down, rows[3], rows_l3, rows[2], rows[4], rows_r3, grads[3],
+        grads_l3, grads[2], grads[4], grads_r3,
+    )
 
 
 def gather(value):
@@ -739,26 +1707,30 @@
     experts = router_weight.shape[1]
     split = devices // experts
     slice_w = width // devices
-    tile = 768
-
-    in_t = gather(in_weight.T)
+    tile = channels // 2
+
+    on_plane = devices == 8 and split == 1 and lax.axis_size("dp") == 4
     by_column = jnp.concatenate(
-        [step_weight, decay_log.T, conv_weight, conv_bias[None], step_bias[None], skip_gain[None]], 0
-    )
-    by_width = jnp.concatenate([mixer_norm[:, None], moe_norm[:, None], router_weight], 1)
-    small = jnp.concatenate(
-        [by_column.reshape(-1), scan_weight.reshape(-1), by_width.reshape(-1)]
-    )
-    small = gather(small[None])
-    first = by_column.size
-    second = first + scan_weight.size
-    columns = (
-        small[:, :first].reshape(devices, by_column.shape[0], part)
-        .transpose(1, 0, 2).reshape(by_column.shape[0], channels)
-    )
-    scan_full = small[:, first:second].reshape(channels, cols)
-    widths = small[:, second:].reshape(width, experts + 2)
-    out_full = gather(out_weight)
+        [
+            step_weight, decay_log.T, conv_weight, conv_bias[None], step_bias[None],
+            skip_gain[None], jnp.zeros_like(skip_gain)[None],
+        ],
+        0,
+    )
+    by_width = jnp.concatenate(
+        [router_weight.T, mixer_norm[None], moe_norm[None], jnp.zeros((6, slice_w), BF16)], 0
+    )
+    in_t = in_weight.T
+    if on_plane:
+        in_t, by_column, scan_full, by_width = gather_weights(in_t, by_column, scan_weight, by_width)
+    else:
+        in_t, by_column, scan_full, by_width = (
+            lax.all_gather(value, "expert") for value in (in_t, by_column, scan_weight, by_width)
+        )
+    in_t = in_t.reshape(2 * channels, width)
+    scan_full = scan_full.reshape(channels, cols)
+    columns = by_column.transpose(1, 0, 2).reshape(by_column.shape[1], channels)
+    widths = by_width.transpose(1, 0, 2).reshape(by_width.shape[1], width)
     step_full = columns[:rank]
     rest = columns[rank:].astype(F32)
     rate = -jnp.exp(rest[:state])
@@ -766,9 +1738,9 @@
     bias_full, dbias_full, skip_full = (
         rest[state + taps + k : state + taps + k + 1] for k in range(3)
     )
-    gain_first = widths[:, 0].astype(F32)[None]
-    gain_second = widths[:, 1].astype(F32)[None]
-    router = widths[:, 2:]
+    router = widths[:experts].T
+    gain_first = widths[experts : experts + 1].astype(F32)
+    gain_second = widths[experts + 1 : experts + 2].astype(F32)
     up, down = up_weight[0], down_weight[0]
     live = (jnp.arange(rows, dtype=jnp.int32) < lengths[0]).astype(F32)[:, None]
     routes_col, slots_col = routes[0][:, None], slot_index[0][:, None]
@@ -776,84 +1748,109 @@
     normed_low, x_inner, u_act, gate_in, proj = front(
         tokens[0], gain_first, in_t, conv_full, bias_full, scan_full, tile
     )
-    step_size, mixed, gated, hist, mid = scan_forward(
-        proj, step_full, dbias_full, rate, skip_full, u_act, gate_in, out_full, tokens[0], tile
-    )
-    send, normed_two, probs = router_step(
-        mid, gain_second, router, routes_col, routes, slot_index, live, cotangent[0]
-    )
-    wide = jnp.broadcast_to(send[:, None], (experts, split) + send.shape[1:])
-    got = exchange(wide.reshape(devices, 2 * CAP, width))
-    everyone = lax.all_gather(got, "dp")
-    pieces_back = exchange(expert_step(got, up, down, min(512, up.shape[1] // 3)))
-    pieces_back = pieces_back.reshape(experts, split, 2 * CAP, width)
-    back = pieces_back[:, 0]
-    if split > 1:
-        back = jnp.sum(pieces_back.astype(F32), 1).astype(BF16)
-    layer_out, grad_mid, grad_mix, grad_router, grad_gain_second = combine_step(
-        mid, gain_second, router, routes_col, slots_col, live, cotangent[0], probs, normed_two, back
-    )
-    grad_u, grad_gate, grad_step_w, grad_dbias, grad_skip, grad_log, grad_proj = scan_backward(
-        proj, step_full, dbias_full, rate, skip_full, u_act, gate_in, out_full, grad_mix, step_size,
-        mixed, hist, tile,
-    )
-    grad_x, grad_conv, grad_bias, grad_scan_w, tokens_grad, grad_gain_first = mixer_back(
-        grad_proj, scan_full, grad_u, x_inner, conv_full, bias_full, grad_gate, in_t, u_act,
-        tokens[0], gain_first, grad_mid, tile,
-    )
-
-    grad_in = jnp.concatenate([grad_x, grad_gate], 1)
-    grad_in_parts = exchange(grad_in.reshape(rows, devices, 2 * part).transpose(1, 0, 2))
-    normed_all = gather(normed_low)
-    grad_in_w = contract_rows(normed_all, grad_in_parts.reshape(devices * rows, 2 * part))
-    gated_parts = exchange(gated.reshape(rows, devices, part).transpose(1, 0, 2))
-    grad_mix_all = gather(grad_mix)
-    grad_out_w = contract_rows(gated_parts.reshape(devices * rows, part), grad_mix_all)
-
-    grad_columns = jnp.concatenate(
-        [grad_step_w, grad_log, grad_conv, grad_bias, grad_dbias, grad_skip], 0
-    ).astype(BF16)
-    count = grad_columns.shape[0]
-    grad_columns = grad_columns.reshape(count, devices, part).transpose(1, 0, 2)
-    grad_widths = jnp.concatenate([grad_gain_first.T, grad_gain_second.T, grad_router], 1)
-    grad_small = jnp.concatenate(
-        [
-            grad_columns.reshape(devices, -1),
-            grad_scan_w.astype(BF16).reshape(devices, -1),
-            grad_widths.astype(BF16).reshape(devices, -1),
-        ],
-        1,
-    )
-    grad_small = jnp.sum(exchange(grad_small).astype(F32), 0)
-    flat = jnp.concatenate(
-        [grad_in_w.astype(BF16).reshape(-1), grad_out_w.astype(BF16).reshape(-1), grad_small.astype(BF16)]
-    )
-    flat = lax.psum(flat, "dp").astype(F32)
-    grad_up, grad_down = expert_grads(everyone, up, down, min(256, up.shape[1]))
-
-    in_size = in_weight.size
-    out_size = in_size + out_weight.size
-    in_total = flat[:in_size].reshape(in_weight.shape)
-    out_total = flat[in_size:out_size].reshape(out_weight.shape)
-    tail = flat[out_size:]
-    columns_total = tail[:first].reshape(by_column.shape)
-    scan_total = tail[first:second].reshape(scan_weight.shape)
-    widths_total = tail[second:].reshape(slice_w, experts + 2)
+    hidden = up.shape[1]
+    if on_plane:
+        step_size, mixed, gated, hist, mid, out_full = scan_forward_plane(
+            proj, step_full, dbias_full, rate, skip_full, u_act, gate_in, out_weight, tokens[0]
+        )
+        out_full = out_full.reshape(channels, width)
+        (
+            layer_out, grad_mid, grad_mix, grad_widths, rows_0, grads_0, rows_l1, rows_r1
+        ) = expert_layer(
+            mid, gain_second, router, routes_col, routes, slots_col, slot_index, live, cotangent[0],
+            up, down,
+        )
+        (
+            grad_u, grad_gate, scan_parts, grad_proj, mix_all, normed_all, gated_all, grads_l1,
+            grads_r1, rows_l2, rows_r2,
+        ) = scan_backward_plane(
+            proj, step_full, dbias_full, rate, skip_full, u_act, gate_in, out_full, grad_mix,
+            step_size, mixed, hist, normed_low, gated, grads_0, rows_l1, rows_r1,
+        )
+        tokens_grad, *totals, grads_l2, grads_r2 = mixer_back_plane(
+            grad_proj, scan_full, grad_u, x_inner, conv_full, bias_full, in_t, u_act, tokens[0],
+            gain_first, grad_mid, grad_widths, grad_gate, scan_parts, normed_all, mix_all,
+            gated_all, grads_l1, grads_r1,
+        )
+        totals = lax.psum(tuple(totals), "dp")
+        grad_up, grad_down = expert_grads_plane(
+            up, down, (rows_0, rows_l1, rows_r1, rows_l2, rows_r2),
+            (grads_0, grads_l1, grads_r1, grads_l2, grads_r2), min(256, hidden),
+        )
+        in_total, out_total, scan_small, back_small, width_small = (t.astype(F32) for t in totals)
+    else:
+        out_full = gather(out_weight)
+        step_size, mixed, gated, hist, mid = scan_forward(
+            proj, step_full, dbias_full, rate, skip_full, u_act, gate_in, out_full, tokens[0], tile
+        )
+        send_rows, send_grads, normed_two, probs = router_step(
+            mid, gain_second, router, routes_col, routes, slot_index, live, cotangent[0]
+        )
+
+        def to_pieces(value):
+            wide = jnp.broadcast_to(value[:, None], (experts, split) + value.shape[1:])
+            return exchange(wide.reshape(devices, CAP, width))
+
+        def from_pieces(value):
+            value = exchange(value).reshape(experts, split, CAP, width)
+            if split == 1:
+                return value[:, 0]
+            return jnp.sum(value.astype(F32), 1).astype(BF16)
+
+        some = min(512, hidden // 3)
+        rows_in = to_pieces(send_rows)
+        grads_in = to_pieces(send_grads)
+        partial_out, slope = expert_out(rows_in, up, down, some)
+        back_rows = from_pieces(partial_out)
+        back_grads = from_pieces(expert_back(grads_in, up, down, slope, some))
+        all_rows = lax.all_gather(rows_in, "dp")
+        layer_out, grad_mid, grad_mix, grad_widths = combine_step(
+            mid, gain_second, router, routes_col, slots_col, live, cotangent[0], probs, normed_two,
+            back_rows, back_grads,
+        )
+        grad_mix, all_rows = lax.optimization_barrier((grad_mix, all_rows))
+        all_grads = lax.all_gather(grads_in, "dp")
+        out_parts = contract_rows(gated, grad_mix).astype(BF16).reshape(devices, part, width)
+        grad_out_w = jnp.sum(exchange(out_parts).astype(F32), 0).astype(BF16)
+        grad_u, grad_gate, scan_parts, grad_proj = scan_backward(
+            proj, step_full, dbias_full, rate, skip_full, u_act, gate_in, out_full, grad_mix, step_size,
+            mixed, hist, tile, devices,
+        )
+        scan_small = jnp.sum(exchange(scan_parts).astype(F32), 0).astype(BF16)
+        grad_x, back_parts, width_parts, tokens_grad = mixer_back(
+            grad_proj, scan_full, grad_u, x_inner, conv_full, bias_full, grad_gate, in_t, u_act,
+            tokens[0], gain_first, grad_mid, grad_widths, tile, devices,
+        )
+        back_small = jnp.sum(exchange(back_parts).astype(F32), 0).astype(BF16)
+        width_small = jnp.sum(exchange(width_parts).astype(F32), 0).astype(BF16)
+        normed_all = gather(normed_low)
+        grad_in_parts = exchange(jnp.concatenate([grad_x, grad_gate], 0))
+        grad_in_w = contract_rows(
+            grad_in_parts.reshape(devices * rows, 2 * part), normed_all
+        ).astype(BF16)
+        totals = (grad_in_w, grad_out_w, scan_small, back_small, width_small)
+        totals, all_grads = lax.optimization_barrier((totals, all_grads))
+        totals = lax.psum(totals, "dp")
+        in_total, out_total, scan_small, back_small, width_small = (
+            t.astype(F32) for t in totals
+        )
+        in_total = in_total.T
+        grad_up, grad_down = expert_grads(all_rows, all_grads, up, down, min(256, hidden))
     return (
         layer_out[None],
         tokens_grad[None],
-        widths_total[:, 0],
+        width_small[experts + 1],
         in_total,
-        columns_total[rank + state : rank + state + taps],
-        columns_total[rank + state + taps],
-        scan_total,
-        columns_total[:rank],
-        columns_total[rank + state + taps + 1],
-        columns_total[rank : rank + state].T,
-        columns_total[rank + state + taps + 2],
+        back_small[cols : cols + taps],
+        back_small[cols + taps],
+        back_small[:cols].T,
+        scan_small[:rank],
+        scan_small[rank + state],
+        scan_small[rank : rank + state].T,
+        scan_small[rank + state + 1],
         out_total,
-        widths_total[:, 1],
-        widths_total[:, 2:],
+        width_small[experts],
+        width_small[:experts].T,
         grad_up[None],
         grad_down[None],
     )

time: 812 us -> 520 us (0.64)
  waiting for transfers between devices: 343 us -> 0.73 us
  Pallas kernels: 243 us -> 456 us
  blocking collectives: 55.3 us -> 0 us
  local copies, waits for them, and re-layouts: 73.5 us -> 29.6 us
  starting transfers between devices: 34.9 us -> 0.08 us
  other arithmetic: 22.6 us -> 7.53 us
  matrix products: 10.6 us -> 0 us
    pallas_call x7, Pallas kernels: 232 us -> 446 us  [the longest x1 97.1 us: expert_grads_plane(): pl.pallas_call(first_grads_kernel, grid=(hidden // tile,), in_specs=[acro...]
    all_gather x5 -> x0, waiting for transfers between devices: 207 us -> none  [the longest x1 145 us: shards(): everyone = lax.all_gather(got, 'dp')]
    psum x1 -> x2, waiting for transfers between devices: 87.2 us -> 0.02 us  [shards(): totals = lax.psum(tuple(totals), 'dp')]
    all_to_all x4 -> x0, waiting for transfers between devices: 46.5 us -> none  [exchange(): lax.all_to_all(value, 'expert', split_axis=0, concat_axis=0, tiled=True)]
    all_to_all x4 -> x0, starting transfers between devices: 34.7 us -> none  [exchange(): lax.all_to_all(value, 'expert', split_axis=0, concat_axis=0, tiled=True)]
    all_to_all x1 -> x0, blocking collectives: 33 us -> none  [exchange(): lax.all_to_all(value, 'expert', split_axis=0, concat_axis=0, tiled=True)]
    all_gather x1 -> x0, blocking collectives: 22.3 us -> none  [gather(): return lax.all_gather(value, 'expert', axis=0, tiled=True)]
    unnamed x44 -> x14, local copies, waits for them, and re-layouts: 20.4 us -> 5.69 us
  transfers between devices with their start and end apart: 10 -> 2, of which waited for: 7 -> 0; matrix products, arithmetic and copies ran while one was open for 11% -> 2% of each run, Pallas kernels for 18% -> 29%
where the time goes in v2:
time: 520 us; the launch traced here: 510 us
  Pallas kernels  456 us (88%)
  local copies, waits for them, and re-layouts  29.6 us (6%)
  between operations  15.3 us (3%)
  other arithmetic  7.53 us (1%)
    pallas_call x1, Pallas kernels, expert_grads_plane(): pl.pallas_call(first_grads_kernel, grid=(hidden // tile,), in_specs=[acro...  97.1 us
    pallas_call x1, Pallas kernels, scan_backward_plane(): pl.pallas_call(scan_back_plane_kernel, grid=(2,), in_specs=[pl.BlockSpec(...  76.8 us
    pallas_call x1, Pallas kernels, gather_weights(): pl.pallas_call(gather_kernel, in_specs=[FAR] * (count + 1), out_specs=[FA...  64.7 us
    pallas_call x1, Pallas kernels, expert_layer(): pl.pallas_call(expert_layer_kernel, in_specs=[here] * 9 + [far] * 2, out_...  62.3 us
    pallas_call x1, Pallas kernels, mixer_back_plane(): pl.pallas_call(back_plane_kernel, grid=(2,), in_specs=[pl.BlockSpec((rows...  56.7 us
    pallas_call x1, Pallas kernels, expert_grads_plane(): pl.pallas_call(last_grads_kernel, grid=(hidden // tile,), in_specs=[acros...  49.9 us
    pallas_call x1, Pallas kernels, scan_forward_plane(): pl.pallas_call(scan_plane_kernel, grid=(2,), in_specs=[pl.BlockSpec((rows...  38.3 us
    pallas_call x1, Pallas kernels, front(): pl.pallas_call(front_kernel, grid=(steps,), in_specs=[pl.BlockSpec((rows,...  10.6 us
  transfers between devices with their start and end apart: 2, of which 0 were waited for; matrix products, arithmetic and copies ran while one was open for 2% of the time, Pallas kernels for 29%

profile of v2, /device:TPU:9, one launch (start us, length us, event | category | flops | bytes accessed | tf_op | source)
XLA Modules:
  0.0 509.7 jit_solution(300124644004196046)
XLA Ops:
  10.7 1.4 maximum_maximum_fusion.refs_2_
  12.0 4.0 concatenate.6.refs_0_
  16.1 64.7 %gather_weights.1 = (bf16[8,576,1152]{2,1,0:T(8,128)(2,1)}, bf16[8,96,288]{2,1,0:T(8,128)(2,1)}, bf16[8,288,104]{2,1,0:T(8,128)(2,1)}, bf16[8,16,144]{2,1,0:T(8,128)(2,1)}) custom-call(bf16[576,1152]{1,0:T(8,128)(2,1)} %bitcast.47, bf16[96,288]{1,0:T(8,128)(2,1)} %concatenate.6.refs_0_, bf16[288,104]{1,0:T(8,128)(2,1)} %refs_1_.1, ...), custom_call_target="tpu_custom_call" | custom-call | tf_op jit(solution)/shard_map/gather_weights/pallas_call | solution.py:1122
  80.8 0.9 fusion.2
  81.7 0.8 slice.117
  82.5 0.9 slice_convert_fusion
  83.4 1.1 slice.112
  86.0 0.8 copy.46.slots_col_ref
  86.8 0.8 copy.45.routes_col_ref
  88.9 0.9 copy.44
  89.9 1.1 slice.89.stepw_ref.refs_1_
  93.1 0.8 neg.6.decay_ref.refs_3_
  93.8 0.7 slice.85.conv_ref
  94.5 10.6 %mixer_front.1 = (bf16[256,1152]{1,0:T(8,128)(2,1)}, f32[256,2304]{1,0:T(8,128)}, f32[256,2304]{1,0:T(8,128)}, f32[256,2304]{1,0:T(8,128)}, f32[256,104]{1,0:T(8,128)}) custom-call(bf16[256,1152]{1,0:T(8,128)(2,1)} %bitcast.42, f32[1,1152]{1,0:T(1,128)} %reshape.97.gain_ref, bf16[4608,1152]{1,0:T(8,128)(2,1)} %bitcast.31, bf16[4608,1152]{1,0:T(8,128)(2,1)} %bitcast.32, ...), custom_call_target="tpu_custom_call" | custom-call | tf_op jit(solution)/shard_map/mixer_front/pallas_call | solution.py:122
  105.1 38.3 %scan_forward_plane.1 = (f32[256,2304]{1,0:T(8,128)}, f32[256,2304]{1,0:T(8,128)}, bf16[8,256,288]{2,1,0:T(8,128)(2,1)}, bf16[4112,2304]{1,0:T(8,128)(2,1)}, f32...) custom-call(f32[256,104]{1,0:T(8,128)} %get-tuple-element.70.proj_ref.refs_0_, bf16[72,2304]{1,0:T(8,128)(2,1)} %slice.89.stepw_ref.refs_1_, ...), custom_call_target="tpu_custom_call" | custom-call | tf_op jit(solution)/shard_map/scan_forward_plane/pallas_call | solution.py:1187
  143.5 62.3 %expert_layer.1 = (bf16[256,1152]{1,0:T(8,128)(2,1)}, f32[256,1152]{1,0:T(8,128)}, bf16[256,1152]{1,0:T(8,128)(2,1)}, f32[9,1152]{1,0:T(8,128)}, bf16[8,64,1152]...) custom-call(f32[256,1152]{1,0:T(8,128)} %get-tuple-element.73.mid_ref, ...), custom_call_target="tpu_custom_call" | custom-call | tf_op jit(solution)/shard_map/expert_layer/pallas_call | solution.py:1001
  205.8 76.8 %scan_backward_plane.1 = (f32[256,2304]{1,0:T(8,128)}, bf16[4,256,576]{2,1,0:T(8,128)(2,1)}, bf16[8,96,288]{2,1,0:T(8,128)(2,1)}, f32[256,104]{1,0:T(8,128)}, bf...) custom-call(f32[256,104]{1,0:T(8,128)} %get-tuple-element.70.proj_re, ...), custom_call_target="tpu_custom_call" | custom-call | tf_op jit(solution)/shard_map/scan_backward_plane/pallas_call | solution.py:1292
  282.6 56.7 %mixer_back_plane.1 = (f32[256,1152]{1,0:T(8,128)}, bf16[1152,576]{1,0:T(8,128)(2,1)}, bf16[288,1152]{1,0:T(8,128)(2,1)}, bf16[96,288]{1,0:T(8,128)(2,1)}, bf16[...) custom-call(f32[256,104]{1,0:T(8,128)} %get-tuple-element.85.gradpro, ...), custom_call_target="tpu_custom_call" | custom-call | tf_op jit(solution)/shard_map/mixer_back_plane/pallas_call | solution.py:1487
  339.5 0.7 all-reduce.7.cloned.1.call-update
  340.2 97.1 %expert_grads_first.1 = (f32[1152,3072]{1,0:T(8,128)}, f32[3072,1152]{1,0:T(8,128)}, bf16[8,64,1152]{2,1,0:T(8,128)(2,1)}, bf16[8,64,1152]{2,1,0:T(8,128)(2,1)},...) custom-call(bf16[1152,3072]{1,0:T(8,128)(2,1)} %bitcast.36, bf16[3072,1152]{1,0:T(8,128)(2,1)} %bitcast.39, ...), custom_call_target="tpu_custom_call" | custom-call | tf_op jit(solution)/shard_map/expert_grads_first/pallas_call | solution.py:1660
  437.3 49.9 %expert_grads_last.1 = (f32[1152,3072]{1,0:T(8,128)}, f32[3072,1152]{1,0:T(8,128)}) custom-call(bf16[1152,3072]{1,0:T(8,128)(2,1)} %bitcast.37, bf16[3072,1152]{1,0:T(8,128)(2,1)} %bitcast.40, f32[1152,3072]{1,0:T(8,128)} %get-tuple-element.108.gup_in, f32[3072,1152]{1,0:T(8,128)} %get-tuple-element.109.gdown_in, ...), custom_call_target="tpu_custom_call" | custom-call | tf_op jit(solution)/shard_map/expert_grads_last/pallas_call | solution.py:1673
  487.2 1.3 slice.119
  488.5 0.9 convert_element_type.47
  489.4 1.5 slice.122
  490.8 0.9 convert_element_type.48
  491.7 0.7 convert_element_type.45
  492.5 0.8 copy.48
  493.8 1.3 fusion.4
  496.4 3.0 copy.47
  499.4 1.1 convert_element_type.49
  500.6 0.8 copy.57
  501.4 1.0 copy.58
  (39 shorter events, 9.8 us)
Async XLA Ops:
  7.2 480.0 %all-reduce.5.cloned.1.call-start = ((), (), s32[]{:S(2)}) async-start(), calls=%async_computation | async-start | bytes 335872 | tf_op jit(solution)/shard_map/psum | solution.py:1775
  16.1 69.9 %copy-start.4 = (s32[1,256]{1,0:T(1,128)S(1)}, s32[1,256]{1,0:T(1,128)}, u32[]{:S(2)}) copy-start(s32[1,256]{1,0:T(1,128)} %slots_row_ref.1) | copy-start | bytes 3076
  80.8 6.0 %copy-start.3 = (s32[1,256]{1,0:T(1,128)S(1)}, s32[1,256]{1,0:T(1,128)}, u32[]{:S(2)}) copy-start(s32[1,256]{1,0:T(1,128)} %routes_row_ref.1) | copy-start | bytes 3076
  339.4 157.0 %all-reduce.7.cloned.1.call-start = ((), (), s32[]{:S(2)}) async-start(), calls=%async_computation.1 | async-start | bytes 4276224 | tf_op jit(solution)/shard_map/psum | solution.py:1775
  496.4 3.0 copy-start.1
  499.4 1.2 copy-start.2
  499.4 2.0 copy-start
Sparse Core Ops, SparseCore 0:
  339.5 32.3 all-reduce.4
  374.5 106.3 all-reduce.6

commit v3 on v2

--- a/solution.py
+++ b/solution.py
@@ -41,6 +41,24 @@
 
 def softplus(values):
     return jnp.maximum(values, 0.0) + jnp.log1p(jnp.exp(-jnp.abs(values)))
+
+
+class Rows:
+    def __init__(self, ref, first, count):
+        self.ref, self.first = ref, first
+        self.shape = (count, ref.shape[1])
+
+    def __getitem__(self, index):
+        low, high = (0, self.shape[0]) if index is Ellipsis else (index[0].start, index[0].stop)
+        return self.ref[self.first + low : self.first + high, :]
+
+
+def conv_rows(misc_ref):
+    return Rows(misc_ref, 0, 4), Rows(misc_ref, 4, 1)
+
+
+def scan_rows(misc_ref):
+    return Rows(misc_ref, 5, 1), Rows(misc_ref, 6, 1)
 
 
 def split_lanes(out_ref, value):
@@ -88,16 +106,17 @@
 
 
 def front_kernel(
-    tokens_ref, gain_ref, wx_ref, wg_ref, conv_ref, bias_ref, scanw_ref,
+    tokens_ref, gain_ref, wx_ref, wg_ref, misc_ref, scanw_ref,
     normed_ref, xin_ref, u_ref, gate_ref, proj_ref,
 ):
     step = pl.program_id(0)
+    conv_ref, bias_ref = conv_rows(misc_ref)
 
     @pl.when(step == 0)
     def _():
         values = tokens_ref[...].astype(F32)
         scale = lax.rsqrt(jnp.mean(values * values, -1, keepdims=True) + 1e-05)
-        normed_ref[...] = (values * scale * gain_ref[...]).astype(BF16)
+        normed_ref[...] = (values * scale * gain_ref[0:1, :]).astype(BF16)
         proj_ref[...] = jnp.zeros_like(proj_ref)
 
     normed = normed_ref[...]
@@ -114,7 +133,7 @@
     proj_ref[...] += product(u_act.astype(BF16), scanw_ref[...])
 
 
-def front(tokens, gain, in_t, conv, bias, scan_w, tile):
+def front(tokens, gains, in_t, vec, scan_w, tile):
     rows, width = tokens.shape
     channels = scan_w.shape[0]
     cols = scan_w.shape[1]
@@ -124,11 +143,10 @@
         grid=(steps,),
         in_specs=[
             pl.BlockSpec((rows, width), lambda i: (0, 0)),
-            pl.BlockSpec((1, width), lambda i: (0, 0)),
+            pl.BlockSpec(gains.shape, lambda i: (0, 0)),
             pl.BlockSpec((tile, width), lambda i: (i, 0)),
             pl.BlockSpec((tile, width), lambda i: (i + steps, 0)),
-            pl.BlockSpec((conv.shape[0], tile), lambda i: (0, i)),
-            pl.BlockSpec((1, tile), lambda i: (0, i)),
+            pl.BlockSpec((8, tile), lambda i: ((vec.shape[0] - 8) // 8, i)),
             pl.BlockSpec((tile, cols), lambda i: (i, 0)),
         ],
         out_specs=[
@@ -147,7 +165,7 @@
         ],
         compiler_params=pltpu.CompilerParams(vmem_limit_bytes=VMEM_LIMIT),
         name="mixer_front",
-    )(tokens, gain, in_t, in_t, conv, bias, scan_w)
+    )(tokens, gains, in_t, in_t, vec, scan_w)
 
 
 def scan_prepare(proj_ref, b_wide, c_blocks, b_first, c_first, state):
@@ -166,13 +184,14 @@
 
 
 def scan_tile(
-    proj_ref, stepw_ref, dbias_ref, decay_ref, skip_ref, u_ref, gate_ref, step_ref, mixed_ref,
-    hist_ref, b_wide, c_blocks, du, scanned, between,
+    proj_ref, stepw_ref, decay_ref, misc_ref, u_ref, gate_ref, step_ref, mixed_ref, hist_ref,
+    b_wide, c_blocks, du, scanned, between,
 ):
     rank, state = stepw_ref.shape[0], decay_ref.shape[0]
     rows, tile = u_ref.shape
     blocks = rows // BLOCK
     big = BLOCK * state
+    dbias_ref, skip_ref = scan_rows(misc_ref)
     u_act = u_ref[...]
     step_size = softplus(
         product(proj_ref[:, :rank].astype(BF16), stepw_ref[...]) + dbias_ref[...]
@@ -210,7 +229,7 @@
 
 
 def scan_kernel(
-    proj_ref, stepw_ref, dbias_ref, decay_ref, skip_ref, u_ref, gate_ref, outw_ref, tokens_ref,
+    proj_ref, stepw_ref, decay_ref, misc_ref, u_ref, gate_ref, outw_ref, tokens_ref,
     step_ref, mixed_ref, gated_ref, hist_ref, mid_ref,
     b_wide, c_blocks, du, scanned,
 ):
@@ -222,18 +241,18 @@
         scan_prepare(proj_ref, b_wide, c_blocks, rank, rank + state, state)
 
     gated = scan_tile(
-        proj_ref, stepw_ref, dbias_ref, decay_ref, skip_ref, u_ref, gate_ref, step_ref, mixed_ref,
-        hist_ref, b_wide, c_blocks, du, scanned, lambda half: None,
+        proj_ref, stepw_ref, decay_ref, misc_ref, u_ref, gate_ref, step_ref, mixed_ref, hist_ref,
+        b_wide, c_blocks, du, scanned, lambda half: None,
     )
     gated_ref[...] = gated
     mid_ref[...] += product(gated, outw_ref[...])
 
 
-def scan_forward(proj, step_w, dbias, decay, skip, u_act, gate_in, out_w, tokens, tile):
+def scan_forward(proj, step_w, vec, u_act, gate_in, out_w, tokens, tile):
     rows, channels = u_act.shape
     width = tokens.shape[1]
     cols = proj.shape[1]
-    rank, state = step_w.shape[0], decay.shape[0]
+    rank, state = step_w.shape[0], vec.shape[0] - 8
     steps = channels // tile
     hist_rows = (rows + 1) * state
     column = lambda i: (0, i)
@@ -244,9 +263,8 @@
         in_specs=[
             pl.BlockSpec((rows, cols), fixed),
             pl.BlockSpec((rank, tile), column),
-            pl.BlockSpec((1, tile), column),
             pl.BlockSpec((state, tile), column),
-            pl.BlockSpec((1, tile), column),
+            pl.BlockSpec((8, tile), lambda i: ((vec.shape[0] - 8) // 8, i)),
             pl.BlockSpec((rows, tile), column),
             pl.BlockSpec((rows, tile), column),
             pl.BlockSpec((tile, width), lambda i: (i, 0)),
@@ -274,15 +292,15 @@
         ],
         compiler_params=pltpu.CompilerParams(vmem_limit_bytes=VMEM_LIMIT),
         name="scan_forward",
-    )(proj, step_w, dbias, decay, skip, u_act, gate_in, out_w, tokens)
-
-
-def scan_back_kernel(*refs, between=lambda half: None):
-    scan_back_tile(between, *refs)
+    )(proj, step_w, vec, vec, u_act, gate_in, out_w, tokens)
+
+
+def scan_back_kernel(*refs):
+    scan_back_tile(lambda half: None, split_lanes, *refs)
 
 
 def scan_back_tile(
-    between, proj_ref, stepw_ref, dbias_ref, decay_ref, skip_ref, u_ref, gate_ref, outw_ref, gradmix_ref,
+    between, put_gate, proj_ref, stepw_ref, decay_ref, misc_ref, u_ref, gate_ref, outw_ref, gradmix_ref,
     step_ref, mixed_ref, hist_ref,
     gradu_ref, gradgate_ref, pack_ref, gradproj_ref,
     c_wide, b_blocks, b_sums, c_sums, gy, du, g_hist, w_hist, grad_du, grad_step,
@@ -301,11 +319,12 @@
         c_sums[...] = jnp.zeros_like(c_sums)
         scan_prepare(proj_ref, c_wide, b_blocks, rank + state, rank, state)
 
+    skip_ref = scan_rows(misc_ref)[1]
     grad_gated = times_transpose(gradmix_ref[...], outw_ref[...])
     gate_in = gate_ref[...]
     gate_sig = sigmoid(gate_in)
     grad_mixed = grad_gated * (gate_in * gate_sig)
-    split_lanes(
+    put_gate(
         gradgate_ref,
         (grad_gated * mixed_ref[...] * (gate_sig * (1.0 + gate_in * (1.0 - gate_sig)))).astype(BF16),
     )
@@ -380,16 +399,15 @@
 
 
 def scan_backward(
-    proj, step_w, dbias, decay, skip, u_act, gate_in, out_w, grad_mix, step_size, mixed, hist, tile,
-    devices,
+    proj, step_w, vec, u_act, gate_in, out_w, grad_mix, step_size, mixed, hist, tile, devices
 ):
     rows, channels = u_act.shape
     gate_parts = tile * devices // (2 * channels)
     pack_parts = tile * devices // channels
-    pack_rows = step_w.shape[0] + decay.shape[0] + 8
+    pack_rows = step_w.shape[0] + vec.shape[0]
     width = grad_mix.shape[1]
     cols = proj.shape[1]
-    rank, state = step_w.shape[0], decay.shape[0]
+    rank, state = step_w.shape[0], vec.shape[0] - 8
     steps = channels // tile
     big = BLOCK * state
     column = lambda i: (0, i)
@@ -400,9 +418,8 @@
         in_specs=[
             pl.BlockSpec((rows, cols), fixed),
             pl.BlockSpec((rank, tile), column),
-            pl.BlockSpec((1, tile), column),
             pl.BlockSpec((state, tile), column),
-            pl.BlockSpec((1, tile), column),
+            pl.BlockSpec((8, tile), lambda i: ((vec.shape[0] - 8) // 8, i)),
             pl.BlockSpec((rows, tile), column),
             pl.BlockSpec((rows, tile), column),
             pl.BlockSpec((tile, width), lambda i: (i, 0)),
@@ -437,11 +454,11 @@
         ],
         compiler_params=pltpu.CompilerParams(vmem_limit_bytes=VMEM_LIMIT),
         name="scan_backward",
-    )(proj, step_w, dbias, decay, skip, u_act, gate_in, out_w, grad_mix, step_size, mixed, hist)
+    )(proj, step_w, vec, vec, u_act, gate_in, out_w, grad_mix, step_size, mixed, hist)
 
 
 def back_kernel(
-    gradproj_ref, scanw_ref, gradu_ref, xin_ref, conv_ref, bias_ref, gradgate_ref, wx_ref, wg_ref,
+    gradproj_ref, scanw_ref, gradu_ref, xin_ref, misc_ref, gradgate_ref, wx_ref, wg_ref,
     u_ref, tokens_ref, gain_ref, gradmid_ref, widths_ref,
     gradx_ref, pack_ref, tail_ref, gradtok_ref,
     total,
@@ -452,6 +469,7 @@
     def _():
         total[...] = jnp.zeros_like(total)
 
+    conv_ref, bias_ref = conv_rows(misc_ref)
     grad_proj = gradproj_ref[...].astype(BF16)
     grad_u = gradu_ref[...] + times_transpose(grad_proj, scanw_ref[...])
     pieces = [contract_rows(grad_proj, u_ref[...].astype(BF16))]
@@ -486,14 +504,14 @@
             [widths, jnp.zeros((tail_ref.shape[1] - widths.shape[0], widths.shape[1]), F32)], 0
         )
         split_lanes(tail_ref, widths.astype(BF16))
-        inner = grad * gain_ref[...]
+        inner = grad * gain_ref[0:1, :]
         gradtok_ref[...] = gradmid_ref[...] + scale * (
             inner - unit * jnp.mean(inner * unit, -1, keepdims=True)
         )
 
 
 def mixer_back(
-    grad_proj, scan_w, grad_u, x_inner, conv, bias, grad_gate, in_t, u_act, tokens, gain, grad_mid,
+    grad_proj, scan_w, grad_u, x_inner, vec, grad_gate, in_t, u_act, tokens, gains, grad_mid,
     grad_widths, tile, devices,
 ):
     rows, channels = u_act.shape
@@ -503,7 +521,6 @@
     tail_rows = grad_widths.shape[0] + 7
     width = tokens.shape[1]
     cols = scan_w.shape[1]
-    taps = conv.shape[0]
     steps = channels // tile
     column = lambda i: (0, i)
     fixed = lambda i: (0, 0)
@@ -515,14 +532,13 @@
             pl.BlockSpec((tile, cols), lambda i: (i, 0)),
             pl.BlockSpec((rows, tile), column),
             pl.BlockSpec((rows, tile), column),
-            pl.BlockSpec((taps, tile), column),
-            pl.BlockSpec((1, tile), column),
+            pl.BlockSpec((8, tile), lambda i: ((vec.shape[0] - 8) // 8, i)),
             pl.BlockSpec((gate_parts, rows, tile // gate_parts), lambda i: (i, 0, 0)),
             pl.BlockSpec((tile, width), lambda i: (i, 0)),
             pl.BlockSpec((tile, width), lambda i: (i + steps, 0)),
             pl.BlockSpec((rows, tile), column),
             pl.BlockSpec((rows, width), fixed),
-            pl.BlockSpec((1, width), fixed),
+            pl.BlockSpec(gains.shape, fixed),
             pl.BlockSpec((rows, width), fixed),
             pl.BlockSpec(grad_widths.shape, fixed),
         ],
@@ -542,7 +558,7 @@
         compiler_params=pltpu.CompilerParams(vmem_limit_bytes=VMEM_LIMIT),
         name="mixer_back",
     )(
-        grad_proj, scan_w, grad_u, x_inner, conv, bias, grad_gate, in_t, in_t, u_act, tokens, gain,
+        grad_proj, scan_w, grad_u, x_inner, vec, grad_gate, in_t, in_t, u_act, tokens, gains,
         grad_mid, grad_widths,
     )
 
@@ -876,17 +892,26 @@
         pl.when(self.get_right)(lambda: self.left.wait_recv())
 
 
+def as_column(row):
+    return jnp.broadcast_to(row.astype(F32), (8, row.shape[1])).T[:, 0:1].astype(jnp.int32)
+
+
+def dispatch_matrix(goal, experts):
+    slot = iota((experts * CAP, goal.shape[1]), 0)
+    return (goal[0:1, :] == slot).astype(BF16)
+
+
 def expert_layer_kernel(
-    mid_ref, gain_ref, router_ref, routes_col_ref, routes_row_ref, slots_col_ref, slots_row_ref,
-    live_ref, cot_ref, up_hbm, down_hbm,
-    out_ref, gradmid_ref, gradmix_ref, widths_ref, rows_out, grads_out, left_rows, right_rows,
-    up_ref, down_ref, normed_ref, send_r, send_g, got_r, got_g, slope_ref, total, give_r, give_g,
-    back_r, back_g, probs_ref, weight_sems, send_sems, recv_sems, local_sems, line_send, line_recv,
-    out_sems,
+    length_ref, mid_ref, gains_ref, router_ref, routes_ref, slots_ref, cot_ref, up_hbm, down_hbm,
+    out_ref, gradmid_ref, gradmix_ref, widths_ref, rows_out, grads_out,
+    left_1, right_1, left_2, right_2, goal_l1, goal_r1, goal_l2, goal_r2, gup_hbm, gdown_hbm,
+    raw, goal, up_ref, down_ref, send_r, send_g, got_r, got_g, slope_ref, total, give_r, give_g,
+    back_r, back_g, probs_ref, act_ref, rows_t, gup_ref, gdown_ref,
+    weight_sems, send_sems, recv_sems, local_sems, line_send, line_recv, out_sems, grad_sems,
 ):
     tile = 512
     rows, width = mid_ref.shape
-    experts = router_ref.shape[1]
+    experts = router_ref.shape[0]
     hidden = up_ref.shape[1]
     load_up = pltpu.make_async_copy(up_hbm, up_ref, weight_sems.at[0])
     load_down = pltpu.make_async_copy(down_hbm, down_ref, weight_sems.at[1])
@@ -900,31 +925,51 @@
             [(send_r, got_r), (send_g, got_g), (give_r, back_r), (give_g, back_g)]
         )
     ]
+    lines = [
+        Line(stage, *buffers, line_send.at[k], line_recv.at[k])
+        for k, (stage, buffers) in enumerate(
+            [(1, (raw.at[part], raw.at[part], left_1.at[part], right_1.at[part])) for part in (0, 1)]
+            + [(1, (goal, goal, goal_l1, goal_r1))]
+            + [
+                (2, (left_1.at[part], right_1.at[part], left_2.at[part], right_2.at[part]))
+                for part in (0, 1)
+            ]
+            + [(2, (goal_l1, goal_r1, goal_l2, goal_r2))]
+        )
+    ]
+    gain = gains_ref[1:2, :]
+    live = (iota((rows, 1), 0) < length_ref[0]).astype(F32)
+    routes, slots = as_column(routes_ref[...]), as_column(slots_ref[...])
     mid = mid_ref[...]
     scale = lax.rsqrt(jnp.mean(mid * mid, -1, keepdims=True) + 1e-05)
-    normed = (mid * scale * gain_ref[...]).astype(BF16)
-    normed_ref[...] = normed
-    slot = iota((experts * CAP, rows), 0)
-    dispatch = (
-        (routes_row_ref[...] == slot // CAP) & (slots_row_ref[...] == slot % CAP)
-    ).astype(BF16)
+    normed = (mid * scale * gain).astype(BF16)
+    raw[0] = normed
+    slots_row = slots_ref[...]
+    target = jnp.where(slots_row < CAP, routes_ref[...] * CAP + slots_row, -1)
+    goal[...] = jnp.broadcast_to(target, goal.shape)
+    dispatch = dispatch_matrix(goal, experts)
     send_r[...] = product(dispatch, normed).astype(BF16).reshape(experts, CAP, width)
     ways[0].start()
-    logits = product(normed, router_ref[...])
+    for k in (0, 2):
+        lines[k].start()
+    logits = times_transpose(normed, router_ref[...])
     weights = jnp.exp(logits - jnp.max(logits, -1, keepdims=True))
     probs = weights / jnp.sum(weights, -1, keepdims=True)
     probs_ref[...] = probs
-    chosen = (routes_col_ref[...] == iota((rows, experts), 1)).astype(F32)
+    chosen = (routes == iota((rows, experts), 1)).astype(F32)
     gate = jnp.sum(probs * chosen, 1, keepdims=True)
-    grads = (gate * (cot_ref[...].astype(F32) * live_ref[...])).astype(BF16)
+    grads = (gate * (cot_ref[...].astype(F32) * live)).astype(BF16)
+    raw[1] = grads
     send_g[...] = product(dispatch, grads).astype(BF16).reshape(experts, CAP, width)
     ways[1].start()
+    lines[1].start()
 
     load_up.wait()
     load_down.wait()
     ways[0].wait()
-    line = Line(1, got_r, got_r, left_rows, right_rows, line_send, line_recv)
-    line.start()
+    for k in (0, 2):
+        lines[k].wait()
+        lines[k + 3].start()
     keep_rows = pltpu.make_async_copy(got_r, rows_out, out_sems.at[0])
     keep_rows.start()
     total[...] = jnp.zeros_like(total)
@@ -934,13 +979,17 @@
         inputs = got_r[...].reshape(experts * CAP, width)
         activated, slope = gelu_parts(product(inputs, up_ref[:, at]))
         slope_ref[:, at] = slope.astype(BF16)
-        total[...] += product(activated.astype(BF16), down_ref[at, :])
+        activated = activated.astype(BF16)
+        act_ref[:, at] = activated
+        total[...] += product(activated, down_ref[at, :])
         return carry
 
     lax.fori_loop(0, hidden // tile, forward, 0)
     give_r[...] = total[...].astype(BF16).reshape(experts, CAP, width)
     ways[2].start()
     ways[1].wait()
+    lines[1].wait()
+    lines[4].start()
     keep_grads = pltpu.make_async_copy(got_g, grads_out, out_sems.at[1])
     keep_grads.start()
     total[...] = jnp.zeros_like(total)
@@ -950,6 +999,7 @@
         outputs = got_g[...].reshape(experts * CAP, width)
         slope = slope_ref[:, at].astype(F32)
         grad_pre = (times_transpose(outputs, down_ref[at, :]) * slope).astype(BF16)
+        slope_ref[:, at] = grad_pre
         total[...] += times_transpose(grad_pre, up_ref[:, at])
         return carry
 
@@ -957,13 +1007,30 @@
     give_g[...] = total[...].astype(BF16).reshape(experts, CAP, width)
     ways[3].start()
 
-    routes = routes_col_ref[...]
+    rows_t[...] = got_r[...].reshape(experts * CAP, width).T
+    stores = []
+    for step in range(hidden // tile):
+        spot = step % 2
+        at = pl.ds(step * tile, tile)
+        if step >= 2:
+            for store in stores[2 * (step - 2) : 2 * (step - 1)]:
+                store.wait()
+        gup_ref[spot] = product(rows_t[...], slope_ref[:, at]).astype(BF16)
+        gdown_ref[spot] = contract_rows(
+            act_ref[:, at], got_g[...].reshape(experts * CAP, width)
+        ).astype(BF16)
+        stores += [
+            pltpu.make_async_copy(gup_ref.at[spot], gup_hbm.at[:, at], grad_sems.at[0, spot]),
+            pltpu.make_async_copy(gdown_ref.at[spot], gdown_hbm.at[at], grad_sems.at[1, spot]),
+        ]
+        for store in stores[-2:]:
+            store.start()
+
     chosen = (routes == iota((rows, experts), 1)).astype(F32)
     probs = probs_ref[...]
     gate = jnp.sum(probs * chosen, 1, keepdims=True)
-    live = live_ref[...]
     slot = iota((rows, experts * CAP), 1)
-    collect = ((routes == slot // CAP) & (slots_col_ref[...] == slot % CAP)).astype(BF16)
+    collect = ((routes == slot // CAP) & (slots == slot % CAP)).astype(BF16)
     ways[2].wait()
     expert_sum = product(collect, back_r[...].reshape(experts * CAP, width))
     mid = mid_ref[...]
@@ -971,60 +1038,71 @@
     grad_out = cot_ref[...].astype(F32) * live
     grad_gate = jnp.sum(grad_out * expert_sum, 1, keepdims=True)
     grad_logits = (probs * (chosen * grad_gate - gate * grad_gate)).astype(BF16)
-    grad_router = contract_rows(grad_logits, normed_ref[...])
-    from_logits = times_transpose(grad_logits, router_ref[...])
+    grad_router = contract_rows(grad_logits, raw[0])
+    from_logits = product(grad_logits, router_ref[...])
     scale = lax.rsqrt(jnp.mean(mid * mid, -1, keepdims=True) + 1e-05)
     unit = mid * scale
     ways[3].wait()
     grad = product(collect, back_g[...].reshape(experts * CAP, width)) + from_logits
     widths_ref[...] = jnp.concatenate([grad_router, jnp.sum(grad * unit, 0, keepdims=True)], 0)
-    inner = grad * gain_ref[...]
+    inner = grad * gain
     grad_mid = grad_out + scale * (inner - unit * jnp.mean(inner * unit, -1, keepdims=True))
     gradmid_ref[...] = grad_mid
     gradmix_ref[...] = grad_mid.astype(BF16)
+    for store in stores[-4:]:
+        store.wait()
     keep_rows.wait()
     keep_grads.wait()
-    line.wait()
-
-
-def expert_layer(
-    mid, gain, router, routes_col, routes_row, slots_col, slots_row, live, cotangent, up, down
-):
+    for k in (3, 4, 5):
+        lines[k].wait()
+
+
+def expert_layer(lengths, mid, gains, router, routes, slots, cotangent, up, down):
     rows, width = mid.shape
-    experts = router.shape[1]
+    experts = router.shape[0]
     hidden = up.shape[1]
     buffer = (experts, CAP, width)
     here = pl.BlockSpec(memory_space=pltpu.VMEM)
     far = pl.BlockSpec(memory_space=pl.ANY)
-    slots = jax.ShapeDtypeStruct(buffer, BF16)
+    blocks = jax.ShapeDtypeStruct(buffer, BF16)
+    raw = jax.ShapeDtypeStruct((2, rows, width), BF16)
+    goal = jax.ShapeDtypeStruct((8, rows), jnp.int32)
     dma = pltpu.SemaphoreType.DMA
     return pl.pallas_call(
         expert_layer_kernel,
-        in_specs=[here] * 9 + [far] * 2,
-        out_specs=[here] * 4 + [far] * 4,
+        in_specs=[pl.BlockSpec(memory_space=pltpu.SMEM)] + [here] * 6 + [far] * 2,
+        out_specs=[here] * 4 + [far] * 12,
         out_shape=[
             jax.ShapeDtypeStruct((rows, width), BF16),
             jax.ShapeDtypeStruct((rows, width), F32),
             jax.ShapeDtypeStruct((rows, width), BF16),
             jax.ShapeDtypeStruct((experts + 1, width), F32),
-        ] + [slots] * 4,
+        ] + [blocks] * 2 + [raw] * 4 + [goal] * 4 + [
+            jax.ShapeDtypeStruct(up.shape, BF16),
+            jax.ShapeDtypeStruct(down.shape, BF16),
+        ],
         scratch_shapes=[
+            pltpu.VMEM(raw.shape, BF16),
+            pltpu.VMEM(goal.shape, jnp.int32),
             pltpu.VMEM(up.shape, BF16),
             pltpu.VMEM(down.shape, BF16),
-            pltpu.VMEM((rows, width), BF16),
         ] + [pltpu.VMEM(buffer, BF16)] * 4 + [
             pltpu.VMEM((experts * CAP, hidden), BF16),
             pltpu.VMEM((experts * CAP, width), F32),
         ] + [pltpu.VMEM(buffer, BF16)] * 4 + [
             pltpu.VMEM((rows, experts), F32),
-            dma((2,)), dma((4, experts)), dma((4, experts)), dma((4,)), dma((2,)), dma((2,)),
-            dma((2,)),
+            pltpu.VMEM((experts * CAP, hidden), BF16),
+            pltpu.VMEM((width, experts * CAP), BF16),
+            pltpu.VMEM((2, width, 512), BF16),
+            pltpu.VMEM((2, 512, width), BF16),
+            dma((2,)), dma((4, experts)), dma((4, experts)), dma((4,)), dma((6, 2)), dma((6, 2)),
+            dma((2,)), dma((2, 2)),
         ],
         compiler_params=pltpu.CompilerParams(
             vmem_limit_bytes=VMEM_LIMIT, collective_id=1, has_side_effects=True
         ),
         name="expert_layer",
-    )(mid, gain, router, routes_col, routes_row, slots_col, slots_row, live, cotangent, up, down)
+    )(lengths, mid, gains, router, routes, slots, cotangent, up, down)
 
 
 class PlaneGather:
@@ -1085,6 +1163,30 @@
     start, wait = Exchange.start, Exchange.wait
 
 
+class Near:
+    def __init__(self, own, target, send_sems, recv_sems):
+        self.place = lax.axis_index("dp")
+        self.last = lax.axis_size("dp") - 1
+        self.right = pltpu.make_async_remote_copy(
+            own, target, send_sems.at[0], recv_sems.at[0],
+            device_id={"dp": jnp.minimum(self.place + 1, self.last)}, device_id_type=MESH,
+        )
+        self.left = pltpu.make_async_remote_copy(
+            own, target, send_sems.at[1], recv_sems.at[1],
+            device_id={"dp": jnp.maximum(self.place - 1, 0)}, device_id_type=MESH,
+        )
+
+    def start(self):
+        pl.when(self.place < self.last)(lambda: self.right.start())
+        pl.when(self.place == 1)(lambda: self.left.start())
+
+    def wait(self):
+        pl.when(self.place < self.last)(lambda: self.right.wait_send())
+        pl.when(self.place == 1)(lambda: self.left.wait_send())
+        pl.when(self.place > 0)(lambda: self.right.wait_recv())
+        pl.when(self.place == 0)(lambda: self.left.wait_recv())
+
+
 DMA = pltpu.SemaphoreType.DMA
 FAR = pl.BlockSpec(memory_space=pl.ANY)
 
@@ -1095,52 +1197,101 @@
     )
 
 
-def gather_kernel(in_ref, *refs):
-    small = len(refs) // 2 - 3
-    sources, targets = refs[:small], refs[small + 1 : 2 * small + 1]
-    in_full = refs[small]
-    big_send, big_recv, small_send, small_recv, local_sems = refs[2 * small + 1 :]
+def gather_kernel(
+    in_ref, scan_ref, step_ref, decay_ref, conv_ref, vectors_ref, norms_ref, router_ref,
+    in_full, scan_full, step_full, vec_ref, router_full, gains_ref,
+    columns, widths, columns_all, widths_all, send_sems, recv_sems, local_sems,
+):
+    devices, rank, part = columns_all.shape[0], step_ref.shape[0], step_ref.shape[1]
+    state, taps, experts = decay_ref.shape[0], conv_ref.shape[0], router_ref.shape[0]
+    slice_w = widths.shape[1]
     greet(line=False)
-    big = PlaneGather(in_ref, in_full, big_send, big_recv, local_sems.at[small])
-    spreads = [
-        Spread(sources[k], targets[k], small_send.at[k], small_recv.at[k], local_sems.at[k])
-        for k in range(small)
+    spare = columns.shape[0] - rank - state - taps - 3
+    columns[...] = jnp.concatenate(
+        [
+            step_ref[...].astype(F32), decay_ref[...].astype(F32), conv_ref[...].astype(F32),
+            vectors_ref[...].astype(F32), jnp.zeros((spare, part), F32),
+        ],
+        0,
+    ).astype(BF16)
+    widths[...] = jnp.concatenate(
+        [
+            router_ref[...].astype(F32), norms_ref[...].astype(F32),
+            jnp.zeros((widths.shape[0] - experts - 2, slice_w), F32),
+        ],
+        0,
+    ).astype(BF16)
+    small = [
+        PlaneGather(source, target, send_sems.at[k], recv_sems.at[k], local_sems.at[k])
+        for k, (source, target) in enumerate(
+            [(columns, columns_all), (widths, widths_all), (scan_ref, scan_full)]
+        )
     ]
-    big.step(0)
-    for spread in spreads:
-        spread.start()
-    for number in range(1, 5):
+    big = PlaneGather(in_ref, in_full, send_sems.at[3], recv_sems.at[3], local_sems.at[3])
+    for number in range(3):
+        for one in small:
+            one.step(number)
         big.step(number)
-    for spread in spreads:
-        spread.wait()
-
-
-def gather_weights(in_t, *small):
+    for number in (3, 4):
+        for one in small:
+            one.step(number)
+    table = jnp.concatenate([columns_all[k].astype(F32) for k in range(devices)], 1)
+    step_full[...] = table[:rank].astype(BF16)
+    rest = table[rank:]
+    vec_ref[0:state, :] = -jnp.exp(rest[:state])
+    vec_ref[state : state + 8, :] = rest[state : state + 8]
+    across = jnp.concatenate([widths_all[k].astype(F32) for k in range(devices)], 1)
+    router_full[...] = across[:experts].astype(BF16)
+    gains_ref[...] = across[experts : experts + 8]
+    for number in (3, 4):
+        big.step(number)
+
+
+def gather_weights(in_t, scan_w, step_w, decay_t, conv, vectors, norms, router_t):
     devices = lax.axis_size("expert")
-    count = len(small)
-    full = [jax.ShapeDtypeStruct((devices,) + v.shape, v.dtype) for v in (in_t,) + small]
+    rank, part = step_w.shape
+    state, experts, slice_w = decay_t.shape[0], router_t.shape[0], router_t.shape[1]
+    channels = devices * part
+    here = pl.BlockSpec(memory_space=pltpu.VMEM)
     return pl.pallas_call(
         gather_kernel,
-        in_specs=[FAR] * (count + 1),
-        out_specs=[FAR] * (count + 1),
-        out_shape=full,
+        in_specs=[here] * 8,
+        out_specs=[FAR] * 2 + [here] * 4,
+        out_shape=[
+            jax.ShapeDtypeStruct((devices,) + in_t.shape, BF16),
+            jax.ShapeDtypeStruct((devices,) + scan_w.shape, BF16),
+            jax.ShapeDtypeStruct((rank, channels), BF16),
+            jax.ShapeDtypeStruct((state + 8, channels), F32),
+            jax.ShapeDtypeStruct((experts, devices * slice_w), BF16),
+            jax.ShapeDtypeStruct((8, devices * slice_w), F32),
+        ],
         scratch_shapes=[
-            DMA((10,)), DMA((10,)), DMA((count, devices)), DMA((count, devices)), DMA((count + 1,)),
+            pltpu.VMEM((rank + state + 8, part), BF16),
+            pltpu.VMEM((32, slice_w), BF16),
+            pltpu.VMEM((devices, rank + state + 8, part), BF16),
+            pltpu.VMEM((devices, 32, slice_w), BF16),
+            DMA((4, 10)), DMA((4, 10)), DMA((4,)),
         ],
         compiler_params=remote_params(2),
         name="gather_weights",
-    )(in_t, *small)
+    )(in_t, scan_w, step_w, decay_t, conv, vectors, norms, router_t)
 
 
 def scan_plane_kernel(
-    proj_ref, stepw_ref, dbias_ref, decay_ref, skip_ref, u_ref, gate_ref, tokens_ref, outw_ref,
-    step_ref, mixed_ref, gated_ref, hist_ref, mid_ref, outw_all,
+    proj_ref, stepw_ref, decay_ref, misc_ref, u_ref, gate_ref, tokens_ref, normed_ref, outw_ref,
+    step_ref, mixed_ref, gated_ref, hist_ref, mid_ref, outw_all, normed_all,
     b_wide, c_blocks, du, scanned, gated_all, outw_here, send_sems, recv_sems, local_sems,
 ):
     tile_id = pl.program_id(0)
     rank, state = stepw_ref.shape[0], decay_ref.shape[0]
     tile = u_ref.shape[1]
-    gather = PlaneGather(outw_ref, outw_here, send_sems, recv_sems, local_sems.at[0])
+    gather = PlaneGather(
+        outw_ref, outw_here, send_sems.at[0], recv_sems.at[0], local_sems.at[0]
+    )
+    normed = PlaneGather(
+        normed_ref.at[pl.ds(0, normed_all.shape[1])], normed_all, send_sems.at[1],
+        recv_sems.at[1], local_sems.at[2],
+    )
     keep = pltpu.make_async_copy(outw_here, outw_all, local_sems.at[1])
 
     @pl.when(tile_id == 0)
@@ -1155,14 +1306,15 @@
             @pl.when(tile_id == turn)
             def _():
                 gather.step(2 * turn + half + 1)
+                normed.step(2 * turn + half)
                 if turn + half == 2:
                     keep.start()
 
     gated = scan_tile(
-        proj_ref, stepw_ref, dbias_ref, decay_ref, skip_ref, u_ref, gate_ref, step_ref, mixed_ref,
-        hist_ref, b_wide, c_blocks, du, scanned, between,
+        proj_ref, stepw_ref, decay_ref, misc_ref, u_ref, gate_ref, step_ref, mixed_ref, hist_ref,
+        b_wide, c_blocks, du, scanned, between,
     )
-    split_lanes(gated_ref, gated)
+    gated_ref[...] = gated.T.reshape(gated_ref.shape)
     gated_all[:, pl.ds(pl.multiple_of(tile_id * tile, tile), tile)] = gated
 
     @pl.when(tile_id == 1)
@@ -1171,13 +1323,14 @@
         weights = outw_here[...].reshape(devices * part, width)
         mid_ref[...] = tokens_ref[...].astype(F32) + product(gated_all[...], weights)
         keep.wait()
-
-
-def scan_forward_plane(proj, step_w, dbias, decay, skip, u_act, gate_in, out_w, tokens):
+        normed.step(4)
+
+
+def scan_forward_plane(proj, step_w, vec, u_act, gate_in, out_w, tokens, normed_low):
     rows, channels = u_act.shape
     width = tokens.shape[1]
     cols = proj.shape[1]
-    rank, state = step_w.shape[0], decay.shape[0]
+    rank, state = step_w.shape[0], vec.shape[0] - 8
     devices = lax.axis_size("expert")
     tile = channels // 2
     part = channels // devices
@@ -1190,29 +1343,31 @@
         in_specs=[
             pl.BlockSpec((rows, cols), fixed),
             pl.BlockSpec((rank, tile), column),
-            pl.BlockSpec((1, tile), column),
             pl.BlockSpec((state, tile), column),
-            pl.BlockSpec((1, tile), column),
-            pl.BlockSpec((rows, tile), column),
-            pl.BlockSpec((rows, tile), column),
+            pl.BlockSpec((8, tile), lambda i: (state // 8, i)),
+            pl.BlockSpec((rows, tile), column),
+            pl.BlockSpec((rows, tile), column),
+            pl.BlockSpec((rows, width), fixed),
             pl.BlockSpec((rows, width), fixed),
             FAR,
         ],
         out_specs=[
             pl.BlockSpec((rows, tile), column),
             pl.BlockSpec((rows, tile), column),
-            pl.BlockSpec((devices // 2, rows, part), lambda i: (i, 0, 0)),
+            pl.BlockSpec((devices // 2, part, rows), lambda i: (i, 0, 0)),
             pl.BlockSpec((hist_rows, tile), column),
             pl.BlockSpec((rows, width), fixed),
             FAR,
+            FAR,
         ],
         out_shape=[
             jax.ShapeDtypeStruct((rows, channels), F32),
             jax.ShapeDtypeStruct((rows, channels), F32),
-            jax.ShapeDtypeStruct((devices, rows, part), BF16),
+            jax.ShapeDtypeStruct((devices, part, rows), BF16),
             jax.ShapeDtypeStruct((hist_rows, channels), BF16),
             jax.ShapeDtypeStruct((rows, width), F32),
             jax.ShapeDtypeStruct((devices, part, width), BF16),
+            jax.ShapeDtypeStruct((devices, rows // 2, width), BF16),
         ],
         scratch_shapes=[
             pltpu.VMEM((rows * state, 128), F32),
@@ -1221,65 +1376,126 @@
             pltpu.VMEM((rows, tile), F32),
             pltpu.VMEM((rows, channels), BF16),
             pltpu.VMEM((devices, part, width), BF16),
-            DMA((10,)), DMA((10,)), DMA((2,)),
+            DMA((2, 10)), DMA((2, 10)), DMA((3,)),
         ],
         compiler_params=remote_params(3),
         name="scan_forward_plane",
-    )(proj, step_w, dbias, decay, skip, u_act, gate_in, tokens, out_w)
+    )(proj, step_w, vec, vec, u_act, gate_in, tokens, normed_low, out_w)
+
+
+class Dispatch:
+    def __init__(self, raw, goal, sends, targets, send_sems, recv_sems, local_sems):
+        self.raw, self.goal, self.sends = raw, goal, sends
+        self.ways = [
+            Exchange(sends.at[k], out, send_sems.at[k], recv_sems.at[k], local_sems.at[k])
+            for k, out in enumerate(targets)
+        ]
+
+    def prepare(self, parts):
+        experts, cap, width = self.sends.shape[1:]
+        matrix = dispatch_matrix(self.goal, experts)
+        for k, part in enumerate(parts):
+            values = product(matrix, self.raw[part]).astype(BF16)
+            self.sends[k] = values.reshape(experts, cap, width)
+
+    def start(self):
+        for way in self.ways:
+            way.start()
+
+    def wait(self):
+        for way in self.ways:
+            way.wait()
+
+
+def pick(choices, raw, goal, sems):
+    place = lax.axis_index("dp")
+    for where, (source, source_goal) in enumerate(choices):
+
+        @pl.when(place == where)
+        def _():
+            copies = [
+                pltpu.make_async_copy(source, raw, sems.at[0]),
+                pltpu.make_async_copy(source_goal, goal, sems.at[1]),
+            ]
+            for copy in copies:
+                copy.start()
+            for copy in copies:
+                copy.wait()
 
 
 def scan_back_plane_kernel(*refs):
-    inputs, refs = refs[:12], refs[12:]
-    (mix_ref, normed_ref, gated_ref, own_grads, left_rows, right_rows), refs = refs[:6], refs[6:]
+    inputs, refs = refs[:11], refs[11:]
+    (normed_ref, gated_ref, rows_0, left_2, right_2, goal_l2, goal_r2), refs = refs[:7], refs[7:]
     outputs, refs = refs[:4], refs[4:]
-    (mix_all, normed_all, gated_all, left_grads, right_grads, next_left, next_right), refs = (
-        refs[:7], refs[7:]
+    (parts_ref, mix_all, normed_all, gated_all, rows_1, left_3, right_3, goal_l3, goal_r3), refs = (
+        refs[:9], refs[9:]
     )
     scratch, refs = refs[:10], refs[10:]
     g_send, g_recv, x_send, x_recv, l_send, l_recv, local_sems = refs
+    mix_ref = inputs[7]
+    half_rows = normed_all.shape[1]
+    near_rows = rows_1.shape[0]
     tile_id = pl.program_id(0)
     mix = PlaneGather(mix_ref, mix_all, g_send.at[0], g_recv.at[0], local_sems.at[0])
-    normed = PlaneGather(normed_ref, normed_all, g_send.at[1], g_recv.at[1], local_sems.at[1])
+    normed = PlaneGather(
+        normed_ref.at[pl.ds(half_rows, half_rows)], normed_all, g_send.at[1], g_recv.at[1],
+        local_sems.at[1],
+    )
     gated = Exchange(gated_ref, gated_all, x_send, x_recv, local_sems.at[2])
-    line_g = Line(
-        1, own_grads, own_grads, left_grads, right_grads, l_send.at[0], l_recv.at[0]
-    )
-    line_r = Line(
-        2, left_rows, right_rows, next_left, next_right, l_send.at[1], l_recv.at[1]
-    )
+    lines = [
+        Line(3, left_2, right_2, left_3, right_3, l_send.at[0], l_recv.at[0]),
+        Line(3, goal_l2, goal_r2, goal_l3, goal_r3, l_send.at[1], l_recv.at[1]),
+        Near(rows_0.at[pl.ds(0, near_rows)], rows_1, l_send.at[2], l_recv.at[2]),
+    ]
 
     @pl.when(tile_id == 0)
     def _():
         greet()
-        line_g.start()
-        line_r.start()
+        for line in lines:
+            line.start()
         mix.step(0)
-        gated.start()
-        normed.step(0)
 
     def between(half):
-        for turn in range(2):
-
-            @pl.when(tile_id == turn)
-            def _():
-                mix.step(2 * turn + half + 1)
-                normed.step(2 * turn + half + 1)
-                if turn + half == 2:
-                    gated.wait()
-                    line_g.wait()
-                    line_r.wait()
-
-    scan_back_tile(between, *inputs, *outputs, *scratch)
+        @pl.when((tile_id == 0) & (half == 0))
+        def _():
+            mix.step(1)
+            gated.start()
+
+        @pl.when((tile_id == 0) & (half == 1))
+        def _():
+            mix.step(2)
+            normed.step(0)
+
+        @pl.when((tile_id == 1) & (half == 0))
+        def _():
+            mix.step(3)
+            normed.step(1)
+
+        @pl.when((tile_id == 1) & (half == 1))
+        def _():
+            mix.step(4)
+            normed.step(2)
+            for line in lines:
+                line.wait()
+            gated.wait()
+            normed.step(3)
+            normed.step(4)
+
+    def put_gate(out_ref, value):
+        out_ref[...] = value
+        parts_ref[...] = value.T.reshape(parts_ref.shape)
+
+    scan_back_tile(between, put_gate, *inputs, *outputs, *scratch)
 
 
 def scan_backward_plane(
-    proj, step_w, dbias, decay, skip, u_act, gate_in, out_w, grad_mix, step_size, mixed, hist,
-    normed_low, gated, own_grads, left_rows, right_rows,
+    proj, step_w, vec, u_act, gate_in, out_w, grad_mix, step_size, mixed, hist, normed_low, gated,
+    rows_0, raws, goals,
 ):
     rows, channels = u_act.shape
     width = grad_mix.shape[1]
     cols = proj.shape[1]
-    rank, state = step_w.shape[0], decay.shape[0]
+    rank, state = step_w.shape[0], vec.shape[0] - 8
     devices = lax.axis_size("expert")
     tile = channels // 2
     gate_parts, pack_parts = devices // 4, devices // 2
@@ -1287,17 +1503,17 @@
     big = BLOCK * state
     column = lambda i: (0, i)
     fixed = lambda i: (0, 0)
-    slots = jax.ShapeDtypeStruct(own_grads.shape, BF16)
-    everyone = jax.ShapeDtypeStruct((devices, rows, width), BF16)
+    slots = jax.ShapeDtypeStruct((devices // 2, CAP, width), BF16)
+    raw = jax.ShapeDtypeStruct(raws[0].shape, BF16)
+    goal = jax.ShapeDtypeStruct(goals[0].shape, jnp.int32)
     return pl.pallas_call(
         scan_back_plane_kernel,
         grid=(2,),
         in_specs=[
             pl.BlockSpec((rows, cols), fixed),
             pl.BlockSpec((rank, tile), column),
-            pl.BlockSpec((1, tile), column),
             pl.BlockSpec((state, tile), column),
-            pl.BlockSpec((1, tile), column),
+            pl.BlockSpec((8, tile), lambda i: (state // 8, i)),
             pl.BlockSpec((rows, tile), column),
             pl.BlockSpec((rows, tile), column),
             pl.BlockSpec((tile, width), lambda i: (i, 0)),
@@ -1305,22 +1521,27 @@
             pl.BlockSpec((rows, tile), column),
             pl.BlockSpec((rows, tile), column),
             pl.BlockSpec((hist.shape[0], tile), column),
-        ] + [FAR] * 6,
+            pl.BlockSpec((rows, width), fixed),
+            pl.BlockSpec(gated.shape, lambda i: (0, 0, 0)),
+        ] + [FAR] * 5,
         out_specs=[
             pl.BlockSpec((rows, tile), column),
-            pl.BlockSpec((gate_parts, rows, tile // gate_parts), lambda i: (i, 0, 0)),
+            pl.BlockSpec((rows, tile), column),
             pl.BlockSpec((pack_parts, pack_rows, tile // pack_parts), lambda i: (i, 0, 0)),
             pl.BlockSpec((rows, cols), fixed),
-        ] + [FAR] * 7,
+            pl.BlockSpec((gate_parts, tile // gate_parts, rows), lambda i: (i, 0, 0)),
+        ] + [FAR] * 8,
         out_shape=[
             jax.ShapeDtypeStruct((rows, channels), F32),
-            jax.ShapeDtypeStruct((devices // 2, rows, 2 * channels // devices), BF16),
+            jax.ShapeDtypeStruct((rows, channels), BF16),
             jax.ShapeDtypeStruct((devices, pack_rows, channels // devices), BF16),
             jax.ShapeDtypeStruct((rows, cols), F32),
-            everyone,
-            everyone,
+            jax.ShapeDtypeStruct((devices // 2, 2 * channels // devices, rows), BF16),
+            jax.ShapeDtypeStruct((devices, rows, width), BF16),
+            jax.ShapeDtypeStruct((devices, rows // 2, width), BF16),
             jax.ShapeDtypeStruct(gated.shape, BF16),
-        ] + [slots] * 4,
+            slots, raw, raw, goal, goal,
+        ],
         scratch_shapes=[
             pltpu.VMEM((rows * state, 128), F32),
             pltpu.VMEM((rows * 2, big), BF16),
@@ -1332,22 +1553,22 @@
             pltpu.VMEM((big, tile), BF16),
             pltpu.VMEM((rows, tile), F32),
             pltpu.VMEM((rows, tile), F32),
-            DMA((2, 10)), DMA((2, 10)), DMA((devices,)), DMA((devices,)), DMA((2, 2)), DMA((2, 2)),
+            DMA((2, 10)), DMA((2, 10)), DMA((devices,)), DMA((devices,)), DMA((3, 2)), DMA((3, 2)),
             DMA((3,)),
         ],
         compiler_params=remote_params(4),
         name="scan_backward_plane",
     )(
-        proj, step_w, dbias, decay, skip, u_act, gate_in, out_w, grad_mix, step_size, mixed, hist,
-        grad_mix, normed_low, gated, own_grads, left_rows, right_rows,
+        proj, step_w, vec, vec, u_act, gate_in, out_w, grad_mix, step_size, mixed, hist,
+        normed_low, gated, rows_0, raws[2], raws[3], goals[2], goals[3],
     )
 
 
 def back_plane_kernel(
-    gradproj_ref, scanw_ref, gradu_ref, xin_ref, conv_ref, bias_ref, wx_ref, wg_ref, u_ref,
-    tokens_ref, gain_ref, gradmid_ref, widths_ref,
-    gate_hbm, scan_parts, normed_hbm, mix_hbm, gated_hbm, left_grads, right_grads,
-    gradtok_ref, gradin_ref, gradout_ref, scan_ref, back_ref, tail_ref, next_left, next_right,
+    gradproj_ref, scanw_ref, gradu_ref, xin_ref, misc_ref, wx_ref, wg_ref, u_ref,
+    tokens_ref, gain_ref, gradmid_ref, widths_ref, gradgate_ref,
+    gate_hbm, scan_parts, normed_low, normed_high, mix_hbm, gated_hbm, rows_0, grads_0,
+    gradtok_ref, totals_ref, rows_1, grads_1,
     total, send_in, got_in, normed_all, mix_all, gated_all, got_scan, send_back, got_back,
     send_tail, got_tail, x_send, x_recv, l_send, l_recv, local_sems, load_sems,
 ):
@@ -1364,22 +1585,30 @@
             ]
         )
     ]
-    line = Line(2, left_grads, right_grads, next_left, next_right, l_send, l_recv)
+    conv_ref, bias_ref = conv_rows(misc_ref)
+    near_rows = rows_1.shape[0]
+    half_rows = normed_low.shape[1]
+    nears = [
+        Near(rows_0.at[pl.ds(near_rows, near_rows)], rows_1, l_send.at[0], l_recv.at[0]),
+        Near(grads_0, grads_1, l_send.at[1], l_recv.at[1]),
+    ]
     loads = [
         pltpu.make_async_copy(source, target, load_sems.at[k])
         for k, (source, target) in enumerate(
             [
-                (gate_hbm, send_in.at[pl.ds(half, half)]), (normed_hbm, normed_all),
+                (gate_hbm, send_in.at[pl.ds(half, half)]),
+                (normed_low, normed_all.at[:, pl.ds(0, half_rows)]),
+                (normed_high, normed_all.at[:, pl.ds(half_rows, half_rows)]),
                 (mix_hbm, mix_all), (gated_hbm, gated_all),
             ]
         )
     ]
 
-    def start_inputs(late):
+    def start_inputs(first, last):
         for k, copy in enumerate(ways[0].copies):
             peer = (me + k + 1) % devices
-            pl.when((peer < half) if late else (peer >= half))(lambda copy=copy: copy.start())
-        pl.when((me < half) if late else (me >= half))(lambda: ways[0].local.start())
+            pl.when((peer >= first) & (peer < last))(lambda copy=copy: copy.start())
+        pl.when((me >= first) & (me < last))(lambda: ways[0].local.start())
 
     @pl.when(tile_id == 0)
     def _():
@@ -1387,10 +1616,11 @@
         for load in loads:
             load.start()
         greet()
-        line.start()
+        for near in nears:
+            near.start()
+        loads[0].wait()
+        start_inputs(half, devices)
         ways[1].start()
-        loads[0].wait()
-        start_inputs(False)
 
     grad_proj = gradproj_ref[...].astype(BF16)
     grad_u = gradu_ref[...] + times_transpose(grad_proj, scanw_ref[...])
@@ -1417,20 +1647,16 @@
         @pl.when(tile_id == turn)
         def _():
             split_lanes(send_back.at[pl.ds(turn * half, half)], packed)
-            split_lanes(send_in.at[pl.ds(turn * gates, gates)], grad_x)
+            send_in[turn * gates : (turn + 1) * gates] = grad_x.T.reshape(
+                (gates,) + send_in.shape[1:]
+            )
+            start_inputs(turn * gates, (turn + 1) * gates)
 
     @pl.when(tile_id == 1)
     def _():
-        start_inputs(True)
         ways[2].start()
 
-    for turn in range(2):
-
-        @pl.when(tile_id == turn)
-        def _():
-            first = half + turn * gates
-            grad_gate = jnp.concatenate([send_in[first + k] for k in range(gates)], 1)
-            total[...] += product(grad_x, wx_ref[...]) + product(grad_gate, wg_ref[...])
+    total[...] += product(grad_x, wx_ref[...]) + product(gradgate_ref[...], wg_ref[...])
 
     @pl.when(tile_id == 1)
     def _():
@@ -1444,38 +1670,53 @@
         )
         split_lanes(send_tail, widths.astype(BF16))
         ways[3].start()
-        inner = grad * gain_ref[...]
+        inner = grad * gain_ref[0:1, :]
         gradtok_ref[...] = gradmid_ref[...] + scale * (
             inner - unit * jnp.mean(inner * unit, -1, keepdims=True)
         )
         for load in loads[1:]:
             load.wait()
-        rows, part = gated_all.shape[1:]
-        width = mix_all.shape[2]
-        gradout_ref[...] = contract_rows(
-            gated_all[...].reshape(devices * rows, part), mix_all[...].reshape(devices * rows, width)
+        rows, width = mix_all.shape[1:]
+
+        def side_by_side(ref):
+            return jnp.concatenate([ref[k] for k in range(devices)], 1)
+
+        in_rows, part = got_in.shape[1], gated_all.shape[1]
+        totals_ref[in_rows : in_rows + part, :] = product(
+            side_by_side(gated_all), mix_all[...].reshape(devices * rows, width)
         ).astype(BF16)
         ways[0].wait()
-        gradin_ref[...] = contract_rows(
-            normed_all[...].reshape(devices * rows, width),
-            got_in[...].reshape(devices * rows, got_in.shape[2]),
+        totals_ref[0:in_rows, :] = product(
+            side_by_side(got_in), normed_all[...].reshape(devices * rows, width)
         ).astype(BF16)
-        for way, got, out in (
-            (ways[1], got_scan, scan_ref), (ways[2], got_back, back_ref), (ways[3], got_tail, tail_ref),
-        ):
+        at = in_rows + part
+        for way, got in ((ways[1], got_scan), (ways[2], got_back)):
             way.wait()
-            out[...] = jnp.sum(got[...].astype(F32), 0).astype(BF16)
-        line.wait()
+            total_here = jnp.sum(got[...].astype(F32), 0)
+            quarter = total_here.shape[0] // 4
+            folded = jnp.concatenate(
+                [total_here[k * quarter : (k + 1) * quarter] for k in range(4)], 1
+            )
+            padding = jnp.zeros((32 - quarter, width), F32)
+            totals_ref[at : at + 32, :] = jnp.concatenate([folded, padding], 0).astype(BF16)
+            at += 32
+        ways[3].wait()
+        tail = jnp.sum(got_tail[...].astype(F32), 0)
+        tail = jnp.concatenate(
+            [tail, jnp.zeros((tail.shape[0], width - tail.shape[1]), F32)], 1
+        )
+        totals_ref[at : at + 16, :] = tail.astype(BF16)
+        for near in nears:
+            near.wait()
 
 
 def mixer_back_plane(
-    grad_proj, scan_w, grad_u, x_inner, conv, bias, in_t, u_act, tokens, gain, grad_mid,
-    grad_widths, grad_gate, scan_parts, normed_all, mix_all, gated_all, left_grads, right_grads,
+    grad_proj, scan_w, grad_u, x_inner, vec, in_t, u_act, tokens, gains, grad_mid, grad_widths,
+    grad_gate, gate_parts, scan_parts, normed_low, normed_high, mix_all, gated_all, rows_0, grads_0,
 ):
     rows, channels = u_act.shape
     width = tokens.shape[1]
     cols = scan_w.shape[1]
-    taps = conv.shape[0]
     devices = lax.axis_size("expert")
     part = channels // devices
     tile = channels // 2
@@ -1483,7 +1724,6 @@
     tail_rows = grad_widths.shape[0] + 7
     column = lambda i: (0, i)
     fixed = lambda i: (0, 0)
-    slots = jax.ShapeDtypeStruct(left_grads.shape, BF16)
     return pl.pallas_call(
         back_plane_kernel,
         grid=(2,),
@@ -1492,41 +1732,33 @@
             pl.BlockSpec((tile, cols), lambda i: (i, 0)),
             pl.BlockSpec((rows, tile), column),
             pl.BlockSpec((rows, tile), column),
-            pl.BlockSpec((taps, tile), column),
-            pl.BlockSpec((1, tile), column),
+            pl.BlockSpec((8, tile), lambda i: ((vec.shape[0] - 8) // 8, i)),
             pl.BlockSpec((tile, width), lambda i: (i, 0)),
             pl.BlockSpec((tile, width), lambda i: (i + 2, 0)),
             pl.BlockSpec((rows, tile), column),
             pl.BlockSpec((rows, width), fixed),
-            pl.BlockSpec((1, width), fixed),
+            pl.BlockSpec(gains.shape, fixed),
             pl.BlockSpec((rows, width), fixed),
             pl.BlockSpec(grad_widths.shape, fixed),
-        ] + [FAR] * 7,
+            pl.BlockSpec((rows, tile), column),
+        ] + [FAR] * 8,
         out_specs=[
             pl.BlockSpec((rows, width), fixed),
-            pl.BlockSpec((width, 2 * part), fixed),
-            pl.BlockSpec((part, width), fixed),
-            pl.BlockSpec(scan_parts.shape[1:], fixed),
-            pl.BlockSpec((pack_rows, part), fixed),
-            pl.BlockSpec((tail_rows, width // devices), fixed),
+            pl.BlockSpec((3 * part + 80, width), fixed),
             FAR,
             FAR,
         ],
         out_shape=[
             jax.ShapeDtypeStruct((rows, width), F32),
-            jax.ShapeDtypeStruct((width, 2 * part), BF16),
-            jax.ShapeDtypeStruct((part, width), BF16),
-            jax.ShapeDtypeStruct(scan_parts.shape[1:], BF16),
-            jax.ShapeDtypeStruct((pack_rows, part), BF16),
-            jax.ShapeDtypeStruct((tail_rows, width // devices), BF16),
-            slots,
-            slots,
+            jax.ShapeDtypeStruct((3 * part + 80, width), BF16),
+            jax.ShapeDtypeStruct((devices // 2,) + rows_0.shape[1:], BF16),
+            jax.ShapeDtypeStruct(grads_0.shape, BF16),
         ],
         scratch_shapes=[
             pltpu.VMEM((rows, width), F32),
-            pltpu.VMEM((devices, rows, 2 * part), BF16),
-            pltpu.VMEM((devices, rows, 2 * part), BF16),
-            pltpu.VMEM(normed_all.shape, BF16),
+            pltpu.VMEM((devices, 2 * part, rows), BF16),
+            pltpu.VMEM((devices, 2 * part, rows), BF16),
+            pltpu.VMEM((devices, rows, width), BF16),
             pltpu.VMEM(mix_all.shape, BF16),
             pltpu.VMEM(gated_all.shape, BF16),
             pltpu.VMEM(scan_parts.shape, BF16),
@@ -1534,13 +1766,14 @@
             pltpu.VMEM((devices, pack_rows, part), BF16),
             pltpu.VMEM((devices, tail_rows, width // devices), BF16),
             pltpu.VMEM((devices, tail_rows, width // devices), BF16),
-            DMA((4, devices)), DMA((4, devices)), DMA((2,)), DMA((2,)), DMA((4,)), DMA((4,)),
+            DMA((4, devices)), DMA((4, devices)), DMA((2, 2)), DMA((2, 2)), DMA((4,)), DMA((5,)),
         ],
         compiler_params=remote_params(5),
         name="mixer_back_plane",
     )(
-        grad_proj, scan_w, grad_u, x_inner, conv, bias, in_t, in_t, u_act, tokens, gain, grad_mid,
-        grad_widths, grad_gate, scan_parts, normed_all, mix_all, gated_all, left_grads, right_grads,
+        grad_proj, scan_w, grad_u, x_inner, vec, in_t, in_t, u_act, tokens, gains, grad_mid,
+        grad_widths, grad_gate, gate_parts, scan_parts, normed_low, normed_high, mix_all, gated_all,
+        rows_0, grads_0,
     )
 
 
@@ -1550,139 +1783,151 @@
     return product(rows_t, grad_pre), contract_rows(activated.astype(BF16), grads)
 
 
-def first_grads_kernel(
-    up_ref, down_ref, rows_0, grads_0, rows_l1, rows_r1, grads_l1, grads_r1, rows_l2, rows_r2,
-    grads_l2, grads_r2,
-    gup_ref, gdown_ref, rows_l3, rows_r3, grads_l3, grads_r3,
-    rows_ref, grads_ref, rows_t, l_send, l_recv, load_sems,
-):
+def flat_rows(refs):
+    experts, cap, width = refs[0].shape
+    values = [ref[...].reshape(ref.shape[0] * cap, width) for ref in refs]
+    return values[0] if len(values) == 1 else jnp.concatenate(values, 0)
+
+
+def next_grads_kernel(sizes, choices, up_ref, down_ref, gup_in, gdown_in, *refs):
+    row_parts, grad_parts, count = sizes
+    rows_in, refs = refs[:row_parts], refs[row_parts:]
+    grads_in, refs = refs[:grad_parts], refs[grad_parts:]
+    raws, goals, refs = refs[:count], refs[count : 2 * count], refs[2 * count :]
+    gup_ref, gdown_ref, rows_out, grads_out, refs = *refs[:4], refs[4:]
+    rows_t, raw, goal, sends, x_send, x_recv, local_sems, load_sems = refs
     step = pl.program_id(0)
-    place = lax.axis_index("dp")
-    count, width = rows_ref.shape[0] * rows_ref.shape[1] * rows_ref.shape[2], rows_ref.shape[3]
-    lines = [
-        Line(3, rows_l2, rows_r2, rows_l3, rows_r3, l_send.at[0], l_recv.at[0]),
-        Line(3, grads_l2, grads_r2, grads_l3, grads_r3, l_send.at[1], l_recv.at[1]),
-    ]
+    rows, grads = flat_rows(rows_in), flat_rows(grads_in)
+    group = Dispatch(raw, goal, sends, (rows_out, grads_out), x_send, x_recv, local_sems)
 
     @pl.when(step == 0)
     def _():
-        greet()
-        for line in lines:
-            line.start()
-        own = [
-            pltpu.make_async_copy(rows_0, rows_ref.at[0], load_sems.at[0]),
-            pltpu.make_async_copy(grads_0, grads_ref.at[0], load_sems.at[1]),
-        ]
-        for copy in own:
-            copy.start()
-        for condition, rows_1, grads_1 in (
-            (place >= 1, rows_l1, grads_l1), (place < 1, rows_r1, grads_r1),
-        ):
-
-            @pl.when(condition)
-            def _():
-                next_to = [
-                    pltpu.make_async_copy(rows_1, rows_ref.at[1], load_sems.at[2]),
-                    pltpu.make_async_copy(grads_1, grads_ref.at[1], load_sems.at[3]),
-                ]
-                for copy in next_to:
-                    copy.start()
-                for copy in next_to:
-                    copy.wait()
-
-        for copy in own:
-            copy.wait()
-        rows_t[...] = rows_ref[...].reshape(count, width).T
-
-    gup_ref[...], gdown_ref[...] = add_groups(
-        rows_ref[...].reshape(count, width), grads_ref[...].reshape(count, width), rows_t[...],
-        up_ref, down_ref,
-    )
+        greet(line=False)
+        pick([(raws[k], goals[k]) for k in choices], raw, goal, load_sems)
+        group.prepare((0, 1))
+        group.start()
+        rows_t[...] = rows.T
+
+    grad_up, grad_down = add_groups(rows, grads, rows_t[...], up_ref, down_ref)
+    gup_ref[...] = (gup_in[...].astype(F32) + grad_up).astype(BF16)
+    gdown_ref[...] = (gdown_in[...].astype(F32) + grad_down).astype(BF16)
 
     @pl.when(step == pl.num_programs(0) - 1)
     def _():
-        for line in lines:
-            line.wait()
+        group.wait()
 
 
 def last_grads_kernel(
-    up_ref, down_ref, gup_in, gdown_in, *refs
+    up_ref, down_ref, gup_in, gdown_in, rows_ref, grads_ref, gup_ref, gdown_ref, rows_t
 ):
-    choices, (gup_ref, gdown_ref, rows_ref, grads_ref, rows_t, load_sems) = refs[:10], refs[10:]
-    rows_l2, rows_l3, rows_r1, rows_r2, rows_r3 = choices[:5]
-    grads_l2, grads_l3, grads_r1, grads_r2, grads_r3 = choices[5:]
-    step = pl.program_id(0)
-    place = lax.axis_index("dp")
-    count, width = rows_ref.shape[0] * rows_ref.shape[1] * rows_ref.shape[2], rows_ref.shape[3]
-
-    @pl.when(step == 0)
+    rows, grads = flat_rows((rows_ref,)), flat_rows((grads_ref,))
+
+    @pl.when(pl.program_id(0) == 0)
     def _():
-        for spot, pairs in enumerate(
-            (
-                ((rows_r2, grads_r2), (rows_r1, grads_r1), (rows_l2, grads_l2), (rows_l2, grads_l2)),
-                ((rows_r3, grads_r3), (rows_r2, grads_r2), (rows_r1, grads_r1), (rows_l3, grads_l3)),
-            )
-        ):
-            for where, (rows_1, grads_1) in enumerate(pairs):
-
-                @pl.when(place == where)
-                def _():
-                    copies = [
-                        pltpu.make_async_copy(rows_1, rows_ref.at[spot], load_sems.at[0]),
-                        pltpu.make_async_copy(grads_1, grads_ref.at[spot], load_sems.at[1]),
-                    ]
-                    for copy in copies:
-                        copy.start()
-                    for copy in copies:
-                        copy.wait()
-
-        rows_t[...] = rows_ref[...].reshape(count, width).T
-
-    grad_up, grad_down = add_groups(
-        rows_ref[...].reshape(count, width), grads_ref[...].reshape(count, width), rows_t[...],
-        up_ref, down_ref,
-    )
-    gup_ref[...] = gup_in[...] + grad_up
-    gdown_ref[...] = gdown_in[...] + grad_down
-
-
-def expert_grads_plane(up, down, rows, grads, tile):
+        rows_t[...] = rows.T
+
+    grad_up, grad_down = add_groups(rows, grads, rows_t[...], up_ref, down_ref)
+    gup_ref[...] = gup_in[...].astype(F32) + grad_up
+    gdown_ref[...] = gdown_in[...].astype(F32) + grad_down
+
+
+def expert_grads_plane(up, down, grad_up, grad_down, rows_1, grads_1, raws, goals, tile):
     width, hidden = up.shape
-    slots = jax.ShapeDtypeStruct(rows[0].shape, BF16)
-    pair = (2,) + rows[0].shape
-    count = pair[0] * pair[1] * pair[2]
+    devices, cap = grads_1.shape[:2]
+    slots = jax.ShapeDtypeStruct(grads_1.shape, BF16)
     across = pl.BlockSpec((width, tile), lambda i: (0, i))
     along = pl.BlockSpec((tile, width), lambda i: (i, 0))
-    shapes = [
-        jax.ShapeDtypeStruct((width, hidden), F32), jax.ShapeDtypeStruct((hidden, width), F32)
-    ]
-    buffers = [pltpu.VMEM(pair, BF16), pltpu.VMEM(pair, BF16), pltpu.VMEM((width, count), BF16)]
-    grad_up, grad_down, rows_l3, rows_r3, grads_l3, grads_r3 = pl.pallas_call(
-        first_grads_kernel,
-        grid=(hidden // tile,),
-        in_specs=[across, along] + [FAR] * 10,
-        out_specs=[across, along] + [FAR] * 4,
-        out_shape=shapes + [slots] * 4,
-        scratch_shapes=buffers + [DMA((2, 2)), DMA((2, 2)), DMA((4,))],
-        compiler_params=remote_params(6),
-        name="expert_grads_first",
-    )(
-        up, down, rows[0], grads[0], rows[1], rows[2], grads[1], grads[2], rows[3], rows[4],
-        grads[3], grads[4],
-    )
+
+    def shapes(kind):
+        return [
+            jax.ShapeDtypeStruct((width, hidden), kind), jax.ShapeDtypeStruct((hidden, width), kind)
+        ]
+
+    def wholes(values):
+        return [pl.BlockSpec(value.shape, lambda i: (0, 0, 0)) for value in values]
+
+    left_2, left_3, right_1, right_2, right_3 = range(5)
+    rows, grads = rows_1, (grads_1,)
+    for turn, choices in enumerate(
+        ((right_2, right_1, right_1, left_2), (right_3, right_2, left_2, left_3))
+    ):
+        grad_up, grad_down, rows_next, grads_next = pl.pallas_call(
+            partial(next_grads_kernel, (len(rows), len(grads), len(raws)), choices),
+            grid=(hidden // tile,),
+            in_specs=[across, along] * 2 + wholes(rows + grads) + [FAR] * (2 * len(raws)),
+            out_specs=[across, along, FAR, FAR],
+            out_shape=shapes(BF16) + [slots] * 2,
+            scratch_shapes=[
+                pltpu.VMEM((width, devices * cap), BF16),
+                pltpu.VMEM(raws[0].shape, BF16),
+                pltpu.VMEM(goals[0].shape, jnp.int32),
+                pltpu.VMEM((2,) + slots.shape, BF16),
+                DMA((2, devices)), DMA((2, devices)), DMA((2,)), DMA((2,)),
+            ],
+            compiler_params=remote_params(6 + turn),
+            name="expert_grads_" + str(turn + 1),
+        )(up, down, grad_up, grad_down, *rows, *grads, *raws, *goals)
+        rows, grads = (rows_next,), (grads_next,)
     return pl.pallas_call(
         last_grads_kernel,
         grid=(hidden // tile,),
-        in_specs=[across, along, across, along] + [FAR] * 10,
+        in_specs=[across, along] * 2 + wholes(rows + grads),
         out_specs=[across, along],
-        out_shape=shapes,
-        scratch_shapes=buffers + [DMA((2,))],
+        out_shape=shapes(F32),
+        scratch_shapes=[pltpu.VMEM((width, devices * cap), BF16)],
         compiler_params=pltpu.CompilerParams(vmem_limit_bytes=VMEM_LIMIT),
-        name="expert_grads_last",
-    )(
-        up, down, grad_up, grad_down, rows[3], rows_l3, rows[2], rows[4], rows_r3, grads[3],
-        grads_l3, grads[2], grads[4], grads_r3,
+        name="expert_grads_3",
+    )(up, down, grad_up, grad_down, *rows, *grads)
+
+
+def finish_kernel(
+    totals_ref, in_ref, out_ref, scanw_ref, stepw_ref, decay_ref, conv_ref, vectors_ref, norms_ref,
+    router_ref,
+):
+    in_rows, part = in_ref.shape[0], out_ref.shape[0]
+    cols, rank, state, taps = (
+        scanw_ref.shape[1], stepw_ref.shape[0], decay_ref.shape[0], conv_ref.shape[0]
     )
+    experts, slice_w = router_ref.shape
+    in_ref[...] = totals_ref[0:in_rows, :].astype(F32)
+    out_ref[...] = totals_ref[in_rows : in_rows + part, :].astype(F32)
+    at = in_rows + part
+    unfolded = []
+    for quarter in ((rank + state + 8) // 4, (cols + 8) // 4):
+        block = totals_ref[at : at + 32, :].astype(F32)[:quarter]
+        unfolded.append(
+            jnp.concatenate([block[:, k * part : (k + 1) * part] for k in range(4)], 0)
+        )
+        at += 32
+    scan, back = unfolded
+    stepw_ref[...] = scan[:rank]
+    decay_ref[...] = scan[rank : rank + state]
+    scanw_ref[...] = back[:cols].T
+    conv_ref[...] = back[cols : cols + taps]
+    vectors_ref[...] = jnp.concatenate(
+        [back[cols + taps : cols + taps + 1], scan[rank + state : rank + state + 2]], 0
+    )
+    tail = totals_ref[at : at + 16, :].astype(F32)[:, :slice_w]
+    router_ref[...] = tail[:experts]
+    norms_ref[...] = tail[experts : experts + 2]
+
+
+def finish(totals, in_rows, part, cols, rank, state, taps, experts, slice_w):
+    here = pl.BlockSpec(memory_space=pltpu.VMEM)
+    return pl.pallas_call(
+        finish_kernel,
+        in_specs=[here],
+        out_specs=[here] * 9,
+        out_shape=[
+            jax.ShapeDtypeStruct(shape, F32)
+            for shape in (
+                (in_rows, totals.shape[1]), (part, totals.shape[1]), (part, cols), (rank, part),
+                (state, part), (taps, part), (3, part), (2, slice_w), (experts, slice_w),
+            )
+        ],
+        compiler_params=pltpu.CompilerParams(vmem_limit_bytes=VMEM_LIMIT),
+        name="finish",
+    )(totals)
 
 
 def gather(value):
@@ -1710,78 +1955,70 @@
     tile = channels // 2
 
     on_plane = devices == 8 and split == 1 and lax.axis_size("dp") == 4
-    by_column = jnp.concatenate(
-        [
-            step_weight, decay_log.T, conv_weight, conv_bias[None], step_bias[None],
-            skip_gain[None], jnp.zeros_like(skip_gain)[None],
-        ],
-        0,
-    )
-    by_width = jnp.concatenate(
-        [router_weight.T, mixer_norm[None], moe_norm[None], jnp.zeros((6, slice_w), BF16)], 0
-    )
-    in_t = in_weight.T
+    vectors = jnp.stack([conv_bias, step_bias, skip_gain])
+    norms = jnp.stack([mixer_norm, moe_norm])
+    in_t, decay_t, router_t = in_weight.T, decay_log.T, router_weight.T
     if on_plane:
-        in_t, by_column, scan_full, by_width = gather_weights(in_t, by_column, scan_weight, by_width)
+        in_t, scan_full, step_full, vec, router_t, gains = gather_weights(
+            in_t, scan_weight, step_weight, decay_t, conv_weight, vectors, norms, router_t
+        )
     else:
-        in_t, by_column, scan_full, by_width = (
-            lax.all_gather(value, "expert") for value in (in_t, by_column, scan_weight, by_width)
-        )
+        spare = jnp.zeros((8 - taps - 3, part), BF16)
+        columns = jnp.concatenate([step_weight, decay_t, conv_weight, vectors, spare], 0)
+        across = jnp.concatenate([router_t, norms, jnp.zeros((6, slice_w), BF16)], 0)
+        in_t, scan_full, columns, across = (
+            lax.all_gather(value, "expert") for value in (in_t, scan_weight, columns, across)
+        )
+        columns = columns.transpose(1, 0, 2).reshape(columns.shape[1], channels)
+        across = across.transpose(1, 0, 2).reshape(across.shape[1], width)
+        step_full, rest = columns[:rank], columns[rank:].astype(F32)
+        vec = jnp.concatenate([-jnp.exp(rest[:state]), rest[state:]], 0)
+        router_t, gains = across[:experts], across[experts:].astype(F32)
     in_t = in_t.reshape(2 * channels, width)
     scan_full = scan_full.reshape(channels, cols)
-    columns = by_column.transpose(1, 0, 2).reshape(by_column.shape[1], channels)
-    widths = by_width.transpose(1, 0, 2).reshape(by_width.shape[1], width)
-    step_full = columns[:rank]
-    rest = columns[rank:].astype(F32)
-    rate = -jnp.exp(rest[:state])
-    conv_full = rest[state : state + taps]
-    bias_full, dbias_full, skip_full = (
-        rest[state + taps + k : state + taps + k + 1] for k in range(3)
-    )
-    router = widths[:experts].T
-    gain_first = widths[experts : experts + 1].astype(F32)
-    gain_second = widths[experts + 1 : experts + 2].astype(F32)
     up, down = up_weight[0], down_weight[0]
-    live = (jnp.arange(rows, dtype=jnp.int32) < lengths[0]).astype(F32)[:, None]
-    routes_col, slots_col = routes[0][:, None], slot_index[0][:, None]
-
     normed_low, x_inner, u_act, gate_in, proj = front(
-        tokens[0], gain_first, in_t, conv_full, bias_full, scan_full, tile
+        tokens[0], gains, in_t, vec, scan_full, tile
     )
     hidden = up.shape[1]
     if on_plane:
-        step_size, mixed, gated, hist, mid, out_full = scan_forward_plane(
-            proj, step_full, dbias_full, rate, skip_full, u_act, gate_in, out_weight, tokens[0]
+        step_size, mixed, gated, hist, mid, out_full, normed_first = scan_forward_plane(
+            proj, step_full, vec, u_act, gate_in, out_weight, tokens[0], normed_low
         )
         out_full = out_full.reshape(channels, width)
+        layer_out, grad_mid, grad_mix, grad_widths, rows_0, grads_0, *line = expert_layer(
+            lengths, mid, gains, router_t, routes, slot_index, cotangent[0], up, down
+        )
+        raws, goals, grad_up, grad_down = line[:4], line[4:8], line[8], line[9]
         (
-            layer_out, grad_mid, grad_mix, grad_widths, rows_0, grads_0, rows_l1, rows_r1
-        ) = expert_layer(
-            mid, gain_second, router, routes_col, routes, slots_col, slot_index, live, cotangent[0],
-            up, down,
-        )
-        (
-            grad_u, grad_gate, scan_parts, grad_proj, mix_all, normed_all, gated_all, grads_l1,
-            grads_r1, rows_l2, rows_r2,
+            grad_u, grad_gate, scan_parts, grad_proj, gate_parts, mix_all, normed_last, gated_all,
+            rows_1a, left_3, right_3, goal_l3, goal_r3,
         ) = scan_backward_plane(
-            proj, step_full, dbias_full, rate, skip_full, u_act, gate_in, out_full, grad_mix,
-            step_size, mixed, hist, normed_low, gated, grads_0, rows_l1, rows_r1,
-        )
-        tokens_grad, *totals, grads_l2, grads_r2 = mixer_back_plane(
-            grad_proj, scan_full, grad_u, x_inner, conv_full, bias_full, in_t, u_act, tokens[0],
-            gain_first, grad_mid, grad_widths, grad_gate, scan_parts, normed_all, mix_all,
-            gated_all, grads_l1, grads_r1,
-        )
-        totals = lax.psum(tuple(totals), "dp")
+            proj, step_full, vec, u_act, gate_in, out_full, grad_mix, step_size, mixed, hist,
+            normed_low, gated, rows_0, raws, goals,
+        )
+        tokens_grad, totals, rows_1b, grads_1 = mixer_back_plane(
+            grad_proj, scan_full, grad_u, x_inner, vec, in_t, u_act, tokens[0], gains, grad_mid,
+            grad_widths, grad_gate, gate_parts, scan_parts, normed_first, normed_last, mix_all,
+            gated_all, rows_0, grads_0,
+        )
+        totals = lax.psum(totals, "dp")
         grad_up, grad_down = expert_grads_plane(
-            up, down, (rows_0, rows_l1, rows_r1, rows_l2, rows_r2),
-            (grads_0, grads_l1, grads_r1, grads_l2, grads_r2), min(256, hidden),
-        )
-        in_total, out_total, scan_small, back_small, width_small = (t.astype(F32) for t in totals)
+            up, down, grad_up, grad_down, (rows_1a, rows_1b), grads_1,
+            (raws[2], left_3, raws[1], raws[3], right_3),
+            (goals[2], goal_l3, goals[1], goals[3], goal_r3), 512,
+        )
+        in_total, out_total, scan_w_total, step_w_total, decay_total, conv_total, *rest = finish(
+            totals, 2 * part, part, cols, rank, state, taps, experts, slice_w
+        )
+        vector_totals, norm_totals, router_total = rest
     else:
+        live = (jnp.arange(rows, dtype=jnp.int32) < lengths[0]).astype(F32)[:, None]
+        routes_col, slots_col = routes[0][:, None], slot_index[0][:, None]
+        router, gain_second = router_t.T, gains[1:2]
         out_full = gather(out_weight)
         step_size, mixed, gated, hist, mid = scan_forward(
-            proj, step_full, dbias_full, rate, skip_full, u_act, gate_in, out_full, tokens[0], tile
+            proj, step_full, vec, u_act, gate_in, out_full, tokens[0], tile
         )
         send_rows, send_grads, normed_two, probs = router_step(
             mid, gain_second, router, routes_col, routes, slot_index, live, cotangent[0]
@@ -1813,13 +2050,13 @@
         out_parts = contract_rows(gated, grad_mix).astype(BF16).reshape(devices, part, width)
         grad_out_w = jnp.sum(exchange(out_parts).astype(F32), 0).astype(BF16)
         grad_u, grad_gate, scan_parts, grad_proj = scan_backward(
-            proj, step_full, dbias_full, rate, skip_full, u_act, gate_in, out_full, grad_mix, step_size,
-            mixed, hist, tile, devices,
+            proj, step_full, vec, u_act, gate_in, out_full, grad_mix, step_size, mixed, hist, tile,
+            devices,
         )
         scan_small = jnp.sum(exchange(scan_parts).astype(F32), 0).astype(BF16)
         grad_x, back_parts, width_parts, tokens_grad = mixer_back(
-            grad_proj, scan_full, grad_u, x_inner, conv_full, bias_full, grad_gate, in_t, u_act,
-            tokens[0], gain_first, grad_mid, grad_widths, tile, devices,
+            grad_proj, scan_full, grad_u, x_inner, vec, grad_gate, in_t, u_act, tokens[0], gains,
+            grad_mid, grad_widths, tile, devices,
         )
         back_small = jnp.sum(exchange(back_parts).astype(F32), 0).astype(BF16)
         width_small = jnp.sum(exchange(width_parts).astype(F32), 0).astype(BF16)
@@ -1834,23 +2071,29 @@
         in_total, out_total, scan_small, back_small, width_small = (
             t.astype(F32) for t in totals
         )
-        in_total = in_total.T
         grad_up, grad_down = expert_grads(all_rows, all_grads, up, down, min(256, hidden))
+        scan_w_total, conv_total = back_small[:cols].T, back_small[cols : cols + taps]
+        step_w_total, decay_total = scan_small[:rank], scan_small[rank : rank + state]
+        vector_totals = (
+            back_small[cols + taps], scan_small[rank + state], scan_small[rank + state + 1]
+        )
+        router_total = width_small[:experts]
+        norm_totals = (width_small[experts], width_small[experts + 1])
     return (
         layer_out[None],
         tokens_grad[None],
-        width_small[experts + 1],
-        in_total,
-        back_small[cols : cols + taps],
-        back_small[cols + taps],
-        back_small[:cols].T,
-        scan_small[:rank],
-        scan_small[rank + state],
-        scan_small[rank : rank + state].T,
-        scan_small[rank + state + 1],
+        norm_totals[1],
+        in_total.T,
+        conv_total,
+        vector_totals[0],
+        scan_w_total,
+        step_w_total,
+        vector_totals[1],
+        decay_total.T,
+        vector_totals[2],
         out_total,
-        width_small[experts],
-        width_small[:experts].T,
+        norm_totals[0],
+        router_total.T,
         grad_up[None],
         grad_down[None],
     )

time: 520 us -> 437 us (0.84)
  Pallas kernels: 456 us -> 406 us
  local copies, waits for them, and re-layouts: 29.6 us -> 7.93 us
  other arithmetic: 7.53 us -> 1.16 us
    pallas_call x1, Pallas kernels: 49.9 us -> 28.2 us  [expert_grads_plane(): pl.pallas_call(last_grads_kernel, grid=(hidden // tile,), in_specs=[acros...]
    pallas_call x3 -> x5, Pallas kernels: 224 us -> 204 us  [the longest x2 77.1 us: expert_grads_plane(): pl.pallas_call(partial(next_grads_kernel, (len(rows), len(grads), len(raw...]
    pallas_call x1, Pallas kernels: 76.8 us -> 63.8 us  [scan_backward_plane(): pl.pallas_call(scan_back_plane_kernel, grid=(2,), in_specs=[pl.BlockSpec(...]
    pallas_call x1, Pallas kernels: 38.3 us -> 48 us  [scan_forward_plane(): pl.pallas_call(scan_plane_kernel, grid=(2,), in_specs=[pl.BlockSpec((rows...]
    slice x16 -> x2, local copies, waits for them, and re-layouts: 11.4 us -> 2.73 us  [the longest x1 1.41 us: shards(): vector_totals[2]]
    convert_element_type x7 -> x0, other arithmetic: 6.13 us -> none  [the longest x4 3.64 us: shards(): t.astype(F32)]
  transfers between devices with their start and end apart: 2 -> 1, of which waited for: 0 -> 0; matrix products, arithmetic and copies ran while one was open for 2% -> 0% of each run, Pallas kernels for 29% -> 25%
where the time goes in v3:
time: 437 us; the launch traced here: 430 us
  Pallas kernels  406 us (93%)
  between operations  15 us (3%)
  local copies, waits for them, and re-layouts  7.93 us (2%)
    pallas_call x2, Pallas kernels, expert_grads_plane(): pl.pallas_call(partial(next_grads_kernel, (len(rows), len(grads), len(raw...  77.1 us
    pallas_call x1, Pallas kernels, expert_layer(): pl.pallas_call(expert_layer_kernel, in_specs=[pl.BlockSpec(memory_space=p...  64.1 us
    pallas_call x1, Pallas kernels, scan_backward_plane(): pl.pallas_call(scan_back_plane_kernel, grid=(2,), in_specs=[pl.BlockSpec(...  63.8 us
    pallas_call x1, Pallas kernels, gather_weights(): pl.pallas_call(gather_kernel, in_specs=[here] * 8, out_specs=[FAR] * 2 +...  58.6 us
    pallas_call x1, Pallas kernels, mixer_back_plane(): pl.pallas_call(back_plane_kernel, grid=(2,), in_specs=[pl.BlockSpec((rows...  52.2 us
    pallas_call x1, Pallas kernels, scan_forward_plane(): pl.pallas_call(scan_plane_kernel, grid=(2,), in_specs=[pl.BlockSpec((rows...  48 us
    pallas_call x1, Pallas kernels, expert_grads_plane(): pl.pallas_call(last_grads_kernel, grid=(hidden // tile,), in_specs=[acros...  28.2 us
    pallas_call x1, Pallas kernels, front(): pl.pallas_call(front_kernel, grid=(steps,), in_specs=[pl.BlockSpec((rows,...  9.83 us
  transfers between devices with their start and end apart: 1, of which 0 were waited for; matrix products, arithmetic and copies ran while one was open for 0% of the time, Pallas kernels for 25%

profile of v3, /device:TPU:9, one launch (start us, length us, event | category | flops | bytes accessed | tf_op | source)
XLA Modules:
  0.0 430.1 jit_solution(4772658042136760737)
XLA Ops:
  7.2 0.0 all-reduce.2.cloned.1.call-start
  7.9 0.7 stack.25
  8.5 0.7 stack.26
  9.2 0.7 stack.21
  9.9 0.7 stack.22
  10.6 0.7 stack.23
  11.2 0.6 pad_maximum_fusion.1.norms_ref
  11.8 0.6 pad_maximum_fusion.vectors_ref
  12.4 58.6 %gather_weights.1 = (bf16[8,576,1152]{2,1,0:T(8,128)(2,1)}, bf16[8,288,104]{2,1,0:T(8,128)(2,1)}, bf16[72,2304]{1,0:T(8,128)(2,1)}, f32[24,2304]{1,0:T(8,128)}, ...) custom-call(bf16[576,1152]{1,0:T(8,128)(2,1)} %bitcast.37, bf16[288,104]{1,0:T(8,128)(2,1)} %scan_ref.1, ...), custom_call_target="tpu_custom_call" | custom-call | tf_op jit(solution)/shard_map/gather_weights/pallas_call | solution.py:1256
  71.0 9.8 %mixer_front.1 = (bf16[256,1152]{1,0:T(8,128)(2,1)}, f32[256,2304]{1,0:T(8,128)}, f32[256,2304]{1,0:T(8,128)}, f32[256,2304]{1,0:T(8,128)}, f32[256,104]{1,0:T(8,128)}) custom-call(bf16[256,1152]{1,0:T(8,128)(2,1)} %bitcast.32, f32[8,1152]{1,0:T(8,128)} %get-tuple-element.84.gain_ref.gains_ref, bf16[4608,1152]{1,0:T(8,128)(2,1)} %bitcast.19, ...), custom_call_target="tpu_custom_call" | custom-call | tf_op jit(solution)/shard_map/mixer_front/pallas_call | solution.py:141
  80.9 48.0 %scan_forward_plane.1 = (f32[256,2304]{1,0:T(8,128)}, f32[256,2304]{1,0:T(8,128)}, bf16[8,288,256]{2,1,0:T(8,128)(2,1)}, bf16[4112,2304]{1,0:T(8,128)(2,1)}, f32...) custom-call(f32[256,104]{1,0:T(8,128)} %get-tuple-element.88.proj_ref.refs_0_, ...), custom_call_target="tpu_custom_call" | custom-call | tf_op jit(solution)/shard_map/scan_forward_plane/pallas_call | solution.py:1340
  128.9 64.1 %expert_layer.1 = (bf16[256,1152]{1,0:T(8,128)(2,1)}, f32[256,1152]{1,0:T(8,128)}, bf16[256,1152]{1,0:T(8,128)(2,1)}, f32[9,1152]{1,0:T(8,128)}, bf16[8,64,1152]...) custom-call(s32[1]{0:T(128)S(6)} %copy.38.length_ref, ...), custom_call_target="tpu_custom_call" | custom-call | tf_op jit(solution)/shard_map/expert_layer/pallas_call | solution.py:1071
  193.0 63.8 %scan_backward_plane.1 = (f32[256,2304]{1,0:T(8,128)}, bf16[256,2304]{1,0:T(8,128)(2,1)}, bf16[8,96,288]{2,1,0:T(8,128)(2,1)}, f32[256,104]{1,0:T(8,128)}, bf16[...) custom-call(f32[256,104]{1,0:T(8,128)} %get-tuple-element.88.proj_re, ...), custom_call_target="tpu_custom_call" | custom-call | tf_op jit(solution)/shard_map/scan_backward_plane/pallas_call | solution.py:1509
  256.9 52.2 %mixer_back_plane.1 = (f32[256,1152]{1,0:T(8,128)}, bf16[944,1152]{1,0:T(8,128)(2,1)}, bf16[4,64,1152]{2,1,0:T(8,128)(2,1)}, bf16[8,64,1152]{2,1,0:T(8,128)(2,1)}) custom-call(f32[256,104]{1,0:T(8,128)} %get-tuple-element.107.gradproj_ref, bf16[2304,104]{1,0:T(8,128)(2,1)} %bitcast.36, f32[256,2304]{1,0:T(8,128)} %get-tuple-element.108.gradu_ref, ...), custom_call_target="tpu_custom_call" | custom-call | tf_op jit(solution)/shard_map/mixer_back_plane/pallas_call | solution.py:1727
  309.1 0.0 all-reduce.2.cloned.1.call-update
  309.1 40.2 %expert_grads_1.1 = (bf16[1152,3072]{1,0:T(8,128)(2,1)}, bf16[3072,1152]{1,0:T(8,128)(2,1)}, bf16[8,64,1152]{2,1,0:T(8,128)(2,1)}, bf16[8,64,1152]{2,1,0:T(8,128)(2,1)}) custom-call(bf16[1152,3072]{1,0:T(8,128)(2,1)} %bitcast.24, bf16[3072,1152]{1,0:T(8,128)(2,1)} %bitcast.28, bf16[1152,3072]{1,0:T(8,128)(2,1)} %get-tuple-element.131.gup_in, ...), custom_call_target="tpu_custom_call" | custom-call | tf_op jit(solution)/shard_map/expert_grads_1/pallas_call | solution.py:1854
  349.3 36.9 %expert_grads_2.1 = (bf16[1152,3072]{1,0:T(8,128)(2,1)}, bf16[3072,1152]{1,0:T(8,128)(2,1)}, bf16[8,64,1152]{2,1,0:T(8,128)(2,1)}, bf16[8,64,1152]{2,1,0:T(8,128)(2,1)}) custom-call(bf16[1152,3072]{1,0:T(8,128)(2,1)} %bitcast.25, bf16[3072,1152]{1,0:T(8,128)(2,1)} %bitcast.29, bf16[1152,3072]{1,0:T(8,128)(2,1)} %get-tuple-element.142.gup_in, ...), custom_call_target="tpu_custom_call" | custom-call | tf_op jit(solution)/shard_map/expert_grads_2/pallas_call | solution.py:1854
  386.2 28.2 %expert_grads_3.1 = (f32[1152,3072]{1,0:T(8,128)}, f32[3072,1152]{1,0:T(8,128)}) custom-call(bf16[1152,3072]{1,0:T(8,128)(2,1)} %bitcast.26, bf16[3072,1152]{1,0:T(8,128)(2,1)} %bitcast.30, bf16[1152,3072]{1,0:T(8,128)(2,1)} %get-tuple-element.146.gup_in, bf16[3072,1152]{1,0:T(8,128)(2,1)} %get-tuple-element.147.gdown_in, ...), custom_call_target="tpu_custom_call" | custom-call | tf_op jit(solution)/shard_map/expert_grads_3/pallas_call | solution.py:1871
  414.5 0.0 copy-start.1
  414.5 0.0 copy-start
  414.5 0.0 all-reduce.2.cloned.1.call-done.totals_ref
  414.5 4.0 finish.1
  418.5 1.3 fusion
  419.8 1.4 slice_reduce_fusion
  421.2 0.0 copy-done.1
  421.2 0.8 copy.39
  422.1 0.0 copy-done
  422.1 1.0 copy.40
Async XLA Ops:
  7.2 407.3 %all-reduce.2.cloned.1.call-start = ((), (), s32[]{:S(2)}) async-start(), calls=%async_computation | async-start | bytes 4349952 | tf_op jit(solution)/shard_map/psum | solution.py:2005
  414.5 6.7 %copy-start.1 = (bf16[256,1152]{1,0:T(8,128)(2,1)S(1)}, bf16[256,1152]{1,0:T(8,128)(2,1)}, u32[]{:S(2)}) copy-start(bf16[256,1152]{1,0:T(8,128)(2,1)} %get-tuple-element.95) | copy-start | bytes 1769476
  414.5 7.6 %copy-start = (f32[256,1152]{1,0:T(8,128)S(1)}, f32[256,1152]{1,0:T(8,128)}, u32[]{:S(2)}) copy-start(f32[256,1152]{1,0:T(8,128)} %get-tuple-element.120) | copy-start | bytes 3538948
Sparse Core Ops, SparseCore 0:
  309.2 91.4 all-reduce.1

commit v4 on v3

--- a/solution.py
+++ b/solution.py
@@ -1148,19 +1148,62 @@
                 copy.wait_send()
 
 
-class Spread:
+class WideGather:
     def __init__(self, source, target, send_sems, recv_sems, local_sem):
-        devices, me = lax.axis_size("expert"), lax.axis_index("expert")
+        me, place = lax.axis_index("expert"), lax.axis_index("dp")
+        core, side, above = neighbour(1), neighbour(2), neighbour(4)
+        far = side + above - me
+        odd = place % 2
+        partner = place + 1 - 2 * odd
+        rows = target.shape[1]
+        unit = rows // 6
+
+        def part(start, count):
+            return pl.ds(pl.multiple_of(start * unit, unit), count * unit)
+
+        def send(k, block, owner, where, **device):
+            return pltpu.make_async_remote_copy(
+                block, target.at[owner, where], send_sems.at[k], recv_sems.at[k],
+                device_id=device, device_id_type=MESH,
+            )
+
+        def forward(k, owner, where, **device):
+            return send(k, target.at[owner, where], owner, where, **device)
+
+        outer, inner = part(4 * odd, 2), part(4 * (1 - odd), 2)
+        middle = part(2, 2)
         self.copies = [
-            pltpu.make_async_remote_copy(
-                source, target.at[me], send_sems.at[k], recv_sems.at[k],
-                device_id={"expert": (me + k) % devices}, device_id_type=MESH,
-            )
-            for k in range(1, devices)
+            send(0, source.at[outer], me, outer, expert=side),
+            send(1, source.at[middle], me, middle, expert=side),
+            send(2, source.at[inner], me, inner, expert=above),
+            send(3, source.at[middle], me, middle, expert=above),
+            forward(4, side, outer, expert=above),
+            forward(5, side, part(2 + odd, 1), expert=above),
+            forward(6, above, inner, expert=side),
+            forward(7, above, part(3 - odd, 1), expert=side),
+            forward(8, side, outer, dp=partner),
+            forward(9, above, inner, dp=partner),
+            send(10, source, me, part(0, 6), expert=core),
+            forward(11, side, part(2 * odd, 4), expert=core),
+            forward(12, above, part(2 - 2 * odd, 4), expert=core),
+            forward(13, side, inner, expert=core),
+            forward(14, above, outer, expert=core),
+            forward(15, far, part(0, 6), expert=core),
         ]
         self.local = pltpu.make_async_copy(source, target.at[me], local_sem)
 
-    start, wait = Exchange.start, Exchange.wait
+    def step(self, number):
+        copies = self.copies
+        for k in ((), (0, 2), (1, 3), (8, 9), (4, 5, 6, 7), (10, 11, 12, 13, 14, 15))[number]:
+            copies[k].wait_recv()
+        for k in ((0, 2, 1, 3, 10), (4, 6, 8, 9), (5, 7, 11, 12), (13, 14), (15,), ())[number]:
+            copies[k].start()
+        if number == 0:
+            self.local.start()
+        if number == 5:
+            self.local.wait()
+            for copy in copies:
+                copy.wait_send()
 
 
 class Near:
@@ -1197,214 +1240,315 @@
     )
 
 
-def gather_kernel(
-    in_ref, scan_ref, step_ref, decay_ref, conv_ref, vectors_ref, norms_ref, router_ref,
-    in_full, scan_full, step_full, vec_ref, router_full, gains_ref,
-    columns, widths, columns_all, widths_all, send_sems, recv_sems, local_sems,
+def columns_of(proj_ref, first, state, target):
+    turned = proj_ref[...].T[first : first + state]
+    for block in range(proj_ref.shape[0] // BLOCK):
+        target[block * state : (block + 1) * state, 0:BLOCK] = turned[
+            :, block * BLOCK : (block + 1) * BLOCK
+        ]
+
+
+def diagonals_of(proj_ref, first, state, high_ref, low_ref):
+    rows, width = proj_ref.shape
+    big = BLOCK * state
+    place = (iota((width, big), 0) == first + iota((width, big), 1) % state).astype(BF16)
+    own = iota((rows, big), 0) % BLOCK == iota((rows, big), 1) // state
+    for part, target in zip(two_parts(proj_ref[...]), (high_ref, low_ref)):
+        target[...] = jnp.where(own, product(part, place), 0.0).astype(BF16)
+
+
+def block_of(ref, block, size):
+    return ref[pl.ds(pl.multiple_of(block * size, size), size), :]
+
+
+def forward_kernel(
+    tokens_ref, in_ref, scan_ref, step_w_ref, decay_ref, conv_ref, vectors_ref, norms_ref,
+    router_ref, outw_ref,
+    normed_ref, xin_ref, u_out, gate_out, proj_ref, step_ref, mixed_ref, gated_ref, mid_ref,
+    step_full, vec_ref, router_full, gains_ref, scan_full, in_full, outw_all, normed_all, hist_hbm,
+    columns, widths, columns_all, widths_all, scan_here, in_here, u_all, gate_all, b_cols, c_high, c_low, du,
+    scanned, gated_all, outw_here, ring,
+    send_sems, recv_sems, local_sems, ring_sems,
 ):
-    devices, rank, part = columns_all.shape[0], step_ref.shape[0], step_ref.shape[1]
+    step = pl.program_id(0)
+    devices, rank, part = columns_all.shape[0], step_w_ref.shape[0], step_w_ref.shape[1]
     state, taps, experts = decay_ref.shape[0], conv_ref.shape[0], router_ref.shape[0]
     slice_w = widths.shape[1]
-    greet(line=False)
-    spare = columns.shape[0] - rank - state - taps - 3
-    columns[...] = jnp.concatenate(
-        [
-            step_ref[...].astype(F32), decay_ref[...].astype(F32), conv_ref[...].astype(F32),
-            vectors_ref[...].astype(F32), jnp.zeros((spare, part), F32),
-        ],
-        0,
-    ).astype(BF16)
-    widths[...] = jnp.concatenate(
-        [
-            router_ref[...].astype(F32), norms_ref[...].astype(F32),
-            jnp.zeros((widths.shape[0] - experts - 2, slice_w), F32),
-        ],
-        0,
-    ).astype(BF16)
+    rows, tile = xin_ref.shape
+    width = tokens_ref.shape[1]
+    big = BLOCK * state
+    turns = ring.shape[0]
+    last = rows // BLOCK - 1
     small = [
         PlaneGather(source, target, send_sems.at[k], recv_sems.at[k], local_sems.at[k])
         for k, (source, target) in enumerate(
-            [(columns, columns_all), (widths, widths_all), (scan_ref, scan_full)]
+            [(columns, columns_all), (widths, widths_all), (scan_ref, scan_here)]
         )
     ]
-    big = PlaneGather(in_ref, in_full, send_sems.at[3], recv_sems.at[3], local_sems.at[3])
-    for number in range(3):
-        for one in small:
-            one.step(number)
-        big.step(number)
-    for number in (3, 4):
-        for one in small:
-            one.step(number)
-    table = jnp.concatenate([columns_all[k].astype(F32) for k in range(devices)], 1)
-    step_full[...] = table[:rank].astype(BF16)
-    rest = table[rank:]
-    vec_ref[0:state, :] = -jnp.exp(rest[:state])
-    vec_ref[state : state + 8, :] = rest[state : state + 8]
-    across = jnp.concatenate([widths_all[k].astype(F32) for k in range(devices)], 1)
-    router_full[...] = across[:experts].astype(BF16)
-    gains_ref[...] = across[experts : experts + 8]
-    for number in (3, 4):
-        big.step(number)
-
-
-def gather_weights(in_t, scan_w, step_w, decay_t, conv, vectors, norms, router_t):
+    big_gather = WideGather(in_ref, in_here, send_sems.at[3], recv_sems.at[3], local_sems.at[3])
+    gather = WideGather(outw_ref, outw_here, send_sems.at[4], recv_sems.at[4], local_sems.at[4])
+    normed_gather = PlaneGather(
+        normed_ref, normed_all, send_sems.at[5], recv_sems.at[5], local_sems.at[5]
+    )
+    keep = pltpu.make_async_copy(outw_here, outw_all, local_sems.at[6])
+    keep_in = pltpu.make_async_copy(in_here, in_full, local_sems.at[7])
+    half = step % 2
+    lanes = pl.ds(pl.multiple_of(half * tile, tile), tile)
+
+    @pl.when(step == 0)
+    def _():
+        spare = columns.shape[0] - rank - state - taps - 3
+        columns[...] = jnp.concatenate(
+            [
+                step_w_ref[...].astype(F32), decay_ref[...].astype(F32), conv_ref[...].astype(F32),
+                vectors_ref[...].astype(F32), jnp.zeros((spare, part), F32),
+            ],
+            0,
+        ).astype(BF16)
+        widths[...] = jnp.concatenate(
+            [
+                router_ref[...].astype(F32), norms_ref[...].astype(F32),
+                jnp.zeros((widths.shape[0] - experts - 2, slice_w), F32),
+            ],
+            0,
+        ).astype(BF16)
+        greet()
+        for number in range(3):
+            for one in small:
+                one.step(number)
+            big_gather.step(number)
+        for number in (3, 4):
+            for one in small:
+                one.step(number)
+        big_gather.step(3)
+        table = jnp.concatenate([columns_all[k].astype(F32) for k in range(devices)], 1)
+        step_full[...] = table[:rank].astype(BF16)
+        scan_full[...] = scan_here[...]
+        rest = table[rank:]
+        vec_ref[0:state, :] = -jnp.exp(rest[:state])
+        vec_ref[state : state + 8, :] = rest[state : state + 8]
+        across = jnp.concatenate([widths_all[k].astype(F32) for k in range(devices)], 1)
+        router_full[...] = across[:experts].astype(BF16)
+        gains_ref[...] = across[experts : experts + 8]
+        values = tokens_ref[...].astype(F32)
+        scale = lax.rsqrt(jnp.mean(values * values, -1, keepdims=True) + 1e-05)
+        normed_ref[...] = (values * scale * gains_ref[0:1, :]).astype(BF16)
+        proj_ref[...] = jnp.zeros_like(proj_ref)
+        big_gather.step(4)
+        gather.step(0)
+        big_gather.step(5)
+        keep_in.start()
+
+    @pl.when(step < 2)
+    def _():
+        misc = vec_ref[state : state + 8, lanes]
+        normed = normed_ref[...]
+        own = devices // 4
+
+        def weights(first):
+            rows_here = in_here.shape[1]
+            return in_here[pl.ds(first + half * own, own)].reshape(own * rows_here, width)
+
+        x_inner = times_transpose(normed, weights(0))
+        gate_in = times_transpose(normed, weights(devices // 2))
+        gate_out[...] = gate_in
+        gate_all[:, lanes] = gate_in
+        xin_ref[...] = x_inner
+        summed = misc[taps : taps + 1] + misc[taps - 1 : taps] * x_inner
+        for back in range(1, taps):
+            tap = taps - 1 - back
+            summed = summed + misc[tap : tap + 1] * shift_rows(x_inner, back)
+        u_act = summed * sigmoid(summed)
+        u_out[...] = u_act
+        u_all[:, lanes] = u_act
+        parts = devices // 2
+        scan_rows_here = scan_here[pl.ds(half * parts, parts)].reshape(tile, scan_here.shape[2])
+        proj_ref[...] += product(u_act.astype(BF16), scan_rows_here)
+
+    @pl.when(step == 1)
+    def _():
+        gather.step(1)
+        gather.step(2)
+        normed_gather.step(0)
+        columns_of(proj_ref, rank, state, b_cols)
+        diagonals_of(proj_ref, rank + state, state, c_high, c_low)
+
+    def store(spot, block):
+        start = pl.multiple_of((block * BLOCK + 1) * state, state)
+        return pltpu.make_async_copy(
+            ring.at[spot], hist_hbm.at[pl.ds(start, big), lanes], ring_sems.at[spot]
+        )
+
+    def sum_states(spot, block):
+        high, low = block_of(c_high, block, BLOCK), block_of(c_low, block, BLOCK)
+        both = product(jnp.concatenate([high, low], 0), ring[spot])
+        return both[:BLOCK] + both[BLOCK:]
+
+    def between(position):
+        if position == 1:
+            gather.step(3)
+            gather.step(4)
+        if position == 4:
+            gather.step(5)
+            keep.start()
+            normed_gather.step(1)
+            normed_gather.step(2)
+        if position == 7:
+            normed_gather.step(3)
+
+    @pl.when(step >= 2)
+    def _():
+        misc = vec_ref[state : state + 8, lanes]
+        u_act = u_all[:, lanes]
+        step_size = softplus(
+            product(proj_ref[:, :rank].astype(BF16), step_full[:, lanes])
+            + misc[taps + 1 : taps + 2]
+        )
+        step_ref[...] = step_size
+        du[...] = step_size * u_act
+        decay = vec_ref[0:state, lanes] * LOG2E
+        ring[turns - 1] = jnp.zeros((big, tile), BF16)
+        zero_row = pltpu.make_async_copy(
+            ring.at[turns - 1, pl.ds(0, state)], hist_hbm.at[pl.ds(0, state), lanes],
+            ring_sems.at[turns],
+        )
+        zero_row.start()
+        zero_row.wait()
+
+        def run_blocks(quarter, held):
+            for spot in range(turns):
+                block = quarter * turns + spot
+                pl.when(quarter > 0)(lambda: store(spot, block).wait())
+                base = pl.multiple_of(block * BLOCK, BLOCK)
+                before = (spot - 1) % turns
+                scanned[pl.ds(base, BLOCK), :] = sum_states(before, jnp.maximum(block - 1, 0))
+                steps_now, du_now = block_of(step_ref, block, BLOCK), block_of(du, block, BLOCK)
+                b_now = block_of(b_cols, block, state)
+                for t in range(BLOCK):
+                    b_wide = jnp.broadcast_to(b_now[:, t : t + 1], (state, tile))
+                    fade = jnp.exp2(steps_now[t : t + 1, :] * decay)
+                    held = fade * held + du_now[t : t + 1, :] * b_wide
+                    ring[spot, t * state : (t + 1) * state, :] = held.astype(BF16)
+                store(spot, block).start()
+            for turn in range(2):
+                for count in range(rows // BLOCK // turns):
+
+                    @pl.when((step == turn + 2) & (quarter == count))
+                    def _():
+                        between(turn * 4 + count)
+
+            return held
+
+        quarters = rows // BLOCK // turns
+        lax.fori_loop(0, quarters, run_blocks, jnp.zeros((state, tile), F32))
+        scanned[pl.ds(rows, BLOCK), :] = sum_states(turns - 1, last)
+        mixed = scanned[pl.ds(BLOCK, rows), :] + misc[taps + 2 : taps + 3] * u_act
+        mixed_ref[...] = mixed
+        gate_in = gate_all[:, lanes]
+        gated = (mixed * (gate_in * sigmoid(gate_in))).astype(BF16)
+        gated_ref[...] = gated.T.reshape(gated_ref.shape)
+        gated_all[:, lanes] = gated
+        for spot in range(turns):
+            store(spot, last - turns + 1 + spot).wait()
+
+    @pl.when(step == 3)
+    def _():
+        weights = outw_here[...].reshape(devices * part, width)
+        mid_ref[...] = tokens_ref[...].astype(F32) + product(gated_all[...], weights)
+        keep.wait()
+        keep_in.wait()
+        normed_gather.step(4)
+
+
+def forward_plane(
+    tokens, in_t, scan_w, step_w, decay_t, conv, vectors, norms, router_t, out_w
+):
+    rows, width = tokens.shape
+    rank, part = step_w.shape
+    cols = scan_w.shape[1]
     devices = lax.axis_size("expert")
-    rank, part = step_w.shape
+    channels = devices * part
     state, experts, slice_w = decay_t.shape[0], router_t.shape[0], router_t.shape[1]
-    channels = devices * part
-    here = pl.BlockSpec(memory_space=pltpu.VMEM)
+    tile = channels // 2
+    hist_rows = (rows + 1) * state
+    first = lambda i: jnp.minimum(i, 1)
+    second = lambda i: jnp.maximum(i - 2, 0)
+
+    def whole(shape):
+        return pl.BlockSpec(shape, lambda i: (0,) * len(shape), pipeline_mode=pl.Buffered(1))
+
+    def kept(shape):
+        return pl.BlockSpec(shape, lambda i: (0,) * len(shape))
+
+    def halves(index):
+        return pl.BlockSpec((rows, tile), lambda i: (0, index(i)))
+
+    inputs = (tokens, in_t, scan_w, step_w, decay_t, conv, vectors, norms, router_t)
+    fixed = [
+        ((rank, channels), BF16), ((state + 8, channels), F32), ((experts, width), BF16),
+        ((8, width), F32), ((devices, part, cols), BF16),
+    ]
     return pl.pallas_call(
-        gather_kernel,
-        in_specs=[here] * 8,
-        out_specs=[FAR] * 2 + [here] * 4,
+        forward_kernel,
+        grid=(4,),
+        in_specs=[whole(value.shape) for value in inputs] + [FAR],
+        out_specs=[
+            kept((rows, width)),
+            halves(first),
+            halves(first),
+            halves(first),
+            kept((rows, cols)),
+            halves(second),
+            halves(second),
+            pl.BlockSpec((devices // 2, part, rows), lambda i: (second(i), 0, 0)),
+            kept((rows, width)),
+        ] + [kept(shape) for shape, _ in fixed] + [FAR] * 4,
         out_shape=[
+            jax.ShapeDtypeStruct((rows, width), BF16),
+            jax.ShapeDtypeStruct((rows, channels), F32),
+            jax.ShapeDtypeStruct((rows, channels), F32),
+            jax.ShapeDtypeStruct((rows, channels), F32),
+            jax.ShapeDtypeStruct((rows, cols), F32),
+            jax.ShapeDtypeStruct((rows, channels), F32),
+            jax.ShapeDtypeStruct((rows, channels), F32),
+            jax.ShapeDtypeStruct((devices, part, rows), BF16),
+            jax.ShapeDtypeStruct((rows, width), F32),
+        ] + [jax.ShapeDtypeStruct(shape, kind) for shape, kind in fixed] + [
             jax.ShapeDtypeStruct((devices,) + in_t.shape, BF16),
-            jax.ShapeDtypeStruct((devices,) + scan_w.shape, BF16),
-            jax.ShapeDtypeStruct((rank, channels), BF16),
-            jax.ShapeDtypeStruct((state + 8, channels), F32),
-            jax.ShapeDtypeStruct((experts, devices * slice_w), BF16),
-            jax.ShapeDtypeStruct((8, devices * slice_w), F32),
+            jax.ShapeDtypeStruct((devices, part, width), BF16),
+            jax.ShapeDtypeStruct((devices, rows, width), BF16),
+            jax.ShapeDtypeStruct((hist_rows, channels), BF16),
         ],
         scratch_shapes=[
             pltpu.VMEM((rank + state + 8, part), BF16),
             pltpu.VMEM((32, slice_w), BF16),
             pltpu.VMEM((devices, rank + state + 8, part), BF16),
             pltpu.VMEM((devices, 32, slice_w), BF16),
-            DMA((4, 10)), DMA((4, 10)), DMA((4,)),
-        ],
-        compiler_params=remote_params(2),
-        name="gather_weights",
-    )(in_t, scan_w, step_w, decay_t, conv, vectors, norms, router_t)
-
-
-def scan_plane_kernel(
-    proj_ref, stepw_ref, decay_ref, misc_ref, u_ref, gate_ref, tokens_ref, normed_ref, outw_ref,
-    step_ref, mixed_ref, gated_ref, hist_ref, mid_ref, outw_all, normed_all,
-    b_wide, c_blocks, du, scanned, gated_all, outw_here, send_sems, recv_sems, local_sems,
-):
-    tile_id = pl.program_id(0)
-    rank, state = stepw_ref.shape[0], decay_ref.shape[0]
-    tile = u_ref.shape[1]
-    gather = PlaneGather(
-        outw_ref, outw_here, send_sems.at[0], recv_sems.at[0], local_sems.at[0]
-    )
-    normed = PlaneGather(
-        normed_ref.at[pl.ds(0, normed_all.shape[1])], normed_all, send_sems.at[1],
-        recv_sems.at[1], local_sems.at[2],
-    )
-    keep = pltpu.make_async_copy(outw_here, outw_all, local_sems.at[1])
-
-    @pl.when(tile_id == 0)
-    def _():
-        greet(line=False)
-        gather.step(0)
-        scan_prepare(proj_ref, b_wide, c_blocks, rank, rank + state, state)
-
-    def between(half):
-        for turn in range(2):
-
-            @pl.when(tile_id == turn)
-            def _():
-                gather.step(2 * turn + half + 1)
-                normed.step(2 * turn + half)
-                if turn + half == 2:
-                    keep.start()
-
-    gated = scan_tile(
-        proj_ref, stepw_ref, decay_ref, misc_ref, u_ref, gate_ref, step_ref, mixed_ref, hist_ref,
-        b_wide, c_blocks, du, scanned, between,
-    )
-    gated_ref[...] = gated.T.reshape(gated_ref.shape)
-    gated_all[:, pl.ds(pl.multiple_of(tile_id * tile, tile), tile)] = gated
-
-    @pl.when(tile_id == 1)
-    def _():
-        devices, part, width = outw_here.shape
-        weights = outw_here[...].reshape(devices * part, width)
-        mid_ref[...] = tokens_ref[...].astype(F32) + product(gated_all[...], weights)
-        keep.wait()
-        normed.step(4)
-
-
-def scan_forward_plane(proj, step_w, vec, u_act, gate_in, out_w, tokens, normed_low):
-    rows, channels = u_act.shape
-    width = tokens.shape[1]
-    cols = proj.shape[1]
-    rank, state = step_w.shape[0], vec.shape[0] - 8
-    devices = lax.axis_size("expert")
-    tile = channels // 2
-    part = channels // devices
-    hist_rows = (rows + 1) * state
-    column = lambda i: (0, i)
-    fixed = lambda i: (0, 0)
-    return pl.pallas_call(
-        scan_plane_kernel,
-        grid=(2,),
-        in_specs=[
-            pl.BlockSpec((rows, cols), fixed),
-            pl.BlockSpec((rank, tile), column),
-            pl.BlockSpec((state, tile), column),
-            pl.BlockSpec((8, tile), lambda i: (state // 8, i)),
-            pl.BlockSpec((rows, tile), column),
-            pl.BlockSpec((rows, tile), column),
-            pl.BlockSpec((rows, width), fixed),
-            pl.BlockSpec((rows, width), fixed),
-            FAR,
-        ],
-        out_specs=[
-            pl.BlockSpec((rows, tile), column),
-            pl.BlockSpec((rows, tile), column),
-            pl.BlockSpec((devices // 2, part, rows), lambda i: (i, 0, 0)),
-            pl.BlockSpec((hist_rows, tile), column),
-            pl.BlockSpec((rows, width), fixed),
-            FAR,
-            FAR,
-        ],
-        out_shape=[
-            jax.ShapeDtypeStruct((rows, channels), F32),
-            jax.ShapeDtypeStruct((rows, channels), F32),
-            jax.ShapeDtypeStruct((devices, part, rows), BF16),
-            jax.ShapeDtypeStruct((hist_rows, channels), BF16),
-            jax.ShapeDtypeStruct((rows, width), F32),
-            jax.ShapeDtypeStruct((devices, part, width), BF16),
-            jax.ShapeDtypeStruct((devices, rows // 2, width), BF16),
-        ],
-        scratch_shapes=[
-            pltpu.VMEM((rows * state, 128), F32),
-            pltpu.VMEM((rows * 2, BLOCK * state), BF16),
+            pltpu.VMEM((devices, part, cols), BF16),
+            pltpu.VMEM((devices,) + in_t.shape, BF16),
+            pltpu.VMEM((rows, channels), F32),
+            pltpu.VMEM((rows, channels), F32),
+            pltpu.VMEM((rows // BLOCK * state, 128), F32),
+            pltpu.VMEM((rows, BLOCK * state), BF16),
+            pltpu.VMEM((rows, BLOCK * state), BF16),
             pltpu.VMEM((rows, tile), F32),
-            pltpu.VMEM((rows, tile), F32),
+            pltpu.VMEM((rows + BLOCK, tile), F32),
             pltpu.VMEM((rows, channels), BF16),
             pltpu.VMEM((devices, part, width), BF16),
-            DMA((2, 10)), DMA((2, 10)), DMA((3,)),
+            pltpu.VMEM((4, BLOCK * state, tile), BF16),
+            DMA((6, 16)), DMA((6, 16)), DMA((8,)), DMA((5,)),
         ],
         compiler_params=remote_params(3),
-        name="scan_forward_plane",
-    )(proj, step_w, vec, vec, u_act, gate_in, tokens, normed_low, out_w)
-
-
-class Dispatch:
-    def __init__(self, raw, goal, sends, targets, send_sems, recv_sems, local_sems):
-        self.raw, self.goal, self.sends = raw, goal, sends
-        self.ways = [
-            Exchange(sends.at[k], out, send_sems.at[k], recv_sems.at[k], local_sems.at[k])
-            for k, out in enumerate(targets)
-        ]
-
-    def prepare(self, parts):
-        experts, cap, width = self.sends.shape[1:]
-        matrix = dispatch_matrix(self.goal, experts)
-        for k, part in enumerate(parts):
-            values = product(matrix, self.raw[part]).astype(BF16)
-            self.sends[k] = values.reshape(experts, cap, width)
-
-    def start(self):
-        for way in self.ways:
-            way.start()
-
-    def wait(self):
-        for way in self.ways:
-            way.wait()
+        name="mixer_forward",
+    )(*inputs, out_w)
+
+
+def prepare_sends(raw, goal, sends):
+    experts, cap, width = sends.shape[1:]
+    matrix = dispatch_matrix(goal, experts)
+    for part in range(2):
+        values = product(matrix, raw[part]).astype(BF16)
+        sends[part] = values.reshape(experts, cap, width)
 
 
 def pick(choices, raw, goal, sems):
@@ -1423,357 +1567,432 @@
                 copy.wait()
 
 
-def scan_back_plane_kernel(*refs):
-    inputs, refs = refs[:11], refs[11:]
-    (normed_ref, gated_ref, rows_0, left_2, right_2, goal_l2, goal_r2), refs = refs[:7], refs[7:]
-    outputs, refs = refs[:4], refs[4:]
-    (parts_ref, mix_all, normed_all, gated_all, rows_1, left_3, right_3, goal_l3, goal_r3), refs = (
-        refs[:9], refs[9:]
-    )
-    scratch, refs = refs[:10], refs[10:]
-    g_send, g_recv, x_send, x_recv, l_send, l_recv, local_sems = refs
-    mix_ref = inputs[7]
-    half_rows = normed_all.shape[1]
-    near_rows = rows_1.shape[0]
-    tile_id = pl.program_id(0)
-    mix = PlaneGather(mix_ref, mix_all, g_send.at[0], g_recv.at[0], local_sems.at[0])
-    normed = PlaneGather(
-        normed_ref.at[pl.ds(half_rows, half_rows)], normed_all, g_send.at[1], g_recv.at[1],
-        local_sems.at[1],
-    )
-    gated = Exchange(gated_ref, gated_all, x_send, x_recv, local_sems.at[2])
+def fold_rows(got_ref, width):
+    total = jnp.sum(got_ref[...].astype(F32), 0)
+    quarter = total.shape[0] // 4
+    folded = jnp.concatenate([total[k * quarter : (k + 1) * quarter] for k in range(4)], 1)
+    return jnp.concatenate([folded, jnp.zeros((32 - quarter, width), F32)], 0).astype(BF16)
+
+
+def backward_kernel(
+    proj_ref, stepw_ref, decay_ref, misc_ref, u_ref, gate_ref, outw_ref, gradmix_ref, step_ref,
+    mixed_ref, scanw_ref, xin_ref, misc_x_ref, wx_ref, wg_ref, u_x_ref, tokens_ref, gains_ref,
+    widths_ref,
+    gradmid_hbm, gated_hbm, normed_hbm, hist_hbm, rows_0, grads_0, left_2, right_2, right_1,
+    goal_l2, goal_r2, goal_r1,
+    gradtok_hbm, totals_hbm, rows_1, grads_1, left_3, right_3, goal_l3, goal_r3, sends_hbm,
+    c_cols, b_high, b_low, b_sums, c_sums, gy, du, grad_du, grad_step, ring, g_ring, w_ring,
+    gradproj, gradu_all, gate_all, send_in, got_in, everyone, gated_all, send_scan, got_scan,
+    pack_back, send_back, got_back, send_tail, got_tail, totals, raw, goal,
+    g_send, g_recv, x_send, x_recv, l_send, l_recv, local_sems, ring_sems, load_sems,
+):
+    step = pl.program_id(0)
+    devices, me = lax.axis_size("expert"), lax.axis_index("expert")
+    half = devices // 2
+    rank, state = stepw_ref.shape[0], decay_ref.shape[0]
+    rows, cols = proj_ref.shape
+    tile, small_tile, width = u_ref.shape[1], xin_ref.shape[1], tokens_ref.shape[1]
+    blocks, big = rows // BLOCK, BLOCK * state
+    turns = ring.shape[0]
+    quarters = blocks // turns
+    in_part = send_in.shape[0] // devices
+    channels = half * in_part
+    steps_x = channels // small_tile
+    mix = PlaneGather(gradmix_ref, everyone, g_send, g_recv, local_sems.at[0])
+    ways = [
+        Exchange(source, target, x_send.at[k], x_recv.at[k], local_sems.at[k + 1])
+        for k, (source, target) in enumerate(
+            [
+                (gated_hbm, gated_all), (send_scan, got_scan), (send_back, got_back),
+                (send_tail, got_tail),
+            ]
+        )
+    ]
+
+    def input_part(device):
+        return send_in.at[pl.ds(pl.multiple_of(device * in_part, in_part), in_part)]
+
+    input_copies = [
+        pltpu.make_async_remote_copy(
+            input_part((me + k) % devices), got_in.at[me], x_send.at[4, k], x_recv.at[4, k],
+            device_id={"expert": (me + k) % devices}, device_id_type=MESH,
+        )
+        for k in range(1, devices)
+    ]
+    input_local = pltpu.make_async_copy(input_part(me), got_in.at[me], local_sems.at[5])
+
+    def start_inputs(first, last):
+        for k, copy in enumerate(input_copies):
+            peer = (me + k + 1) % devices
+            pl.when((peer >= first) & (peer < last))(lambda copy=copy: copy.start())
+        pl.when((me >= first) & (me < last))(lambda: input_local.start())
+
     lines = [
         Line(3, left_2, right_2, left_3, right_3, l_send.at[0], l_recv.at[0]),
         Line(3, goal_l2, goal_r2, goal_l3, goal_r3, l_send.at[1], l_recv.at[1]),
-        Near(rows_0.at[pl.ds(0, near_rows)], rows_1, l_send.at[2], l_recv.at[2]),
+        Near(rows_0, rows_1, l_send.at[2], l_recv.at[2]),
+        Near(grads_0, grads_1, l_send.at[3], l_recv.at[3]),
     ]
-
-    @pl.when(tile_id == 0)
+    load_normed = pltpu.make_async_copy(normed_hbm, everyone, load_sems.at[0])
+    load_mid = pltpu.make_async_copy(gradmid_hbm, gy, load_sems.at[1])
+    store_sends = [
+        pltpu.make_async_copy(source, sends_hbm.at[k], load_sems.at[6 + k])
+        for k, source in enumerate((g_ring, w_ring))
+    ]
+    x_spot = (jnp.maximum(step - 2, 0) % steps_x) // (steps_x // 2)
+    x_lanes = pl.ds(
+        pl.multiple_of((jnp.maximum(step - 2, 0) % (steps_x // 2)) * small_tile, small_tile),
+        small_tile,
+    )
+    lanes = pl.ds(pl.multiple_of(jnp.minimum(step, 1) * tile, tile), tile)
+
+    def load(spot, block):
+        start = pl.multiple_of(block * big, big)
+        return pltpu.make_async_copy(
+            hist_hbm.at[pl.ds(start, big + state), lanes], ring.at[spot], ring_sems.at[spot]
+        )
+
+    @pl.when(step < 2)
+    def _():
+        for spot in range(turns - 1):
+            load(spot, blocks - 1 - spot).start()
+
+    @pl.when(step == 0)
     def _():
         greet()
+        mix.step(0)
         for line in lines:
             line.start()
-        mix.step(0)
-
-    def between(half):
-        @pl.when((tile_id == 0) & (half == 0))
-        def _():
+        gradproj[...] = jnp.zeros_like(gradproj)
+        b_sums[...] = jnp.zeros_like(b_sums)
+        c_sums[...] = jnp.zeros_like(c_sums)
+        columns_of(proj_ref, rank + state, state, c_cols)
+        diagonals_of(proj_ref, rank, state, b_high, b_low)
+
+    def between(position):
+        if position == 2:
             mix.step(1)
-            gated.start()
-
-        @pl.when((tile_id == 0) & (half == 1))
-        def _():
             mix.step(2)
-            normed.step(0)
-
-        @pl.when((tile_id == 1) & (half == 0))
-        def _():
+            ways[0].start()
+        if position == 5:
             mix.step(3)
-            normed.step(1)
-
-        @pl.when((tile_id == 1) & (half == 1))
-        def _():
+        if position == 7:
             mix.step(4)
-            normed.step(2)
-            for line in lines:
-                line.wait()
-            gated.wait()
-            normed.step(3)
-            normed.step(4)
-
-    def put_gate(out_ref, value):
-        out_ref[...] = value
-        parts_ref[...] = value.T.reshape(parts_ref.shape)
-
-    scan_back_tile(between, put_gate, *inputs, *outputs, *scratch)
-
-
-def scan_backward_plane(
-    proj, step_w, vec, u_act, gate_in, out_w, grad_mix, step_size, mixed, hist, normed_low, gated,
-    rows_0, raws, goals,
+            ways[0].wait()
+
+    @pl.when(step < 2)
+    def _():
+        skip_ref = scan_rows(misc_ref)[1]
+        grad_gated = times_transpose(gradmix_ref[...], outw_ref[...])
+        gate_in = gate_ref[...]
+        gate_sig = sigmoid(gate_in)
+        grad_mixed = grad_gated * (gate_in * gate_sig)
+        grad_gate = (
+            grad_gated * mixed_ref[...] * (gate_sig * (1.0 + gate_in * (1.0 - gate_sig)))
+        ).astype(BF16)
+        gate_all[:, lanes] = grad_gate
+        start = pl.multiple_of(channels + step * tile, tile)
+        send_in[pl.ds(start, tile), :] = grad_gate.T
+        u_act = u_ref[...]
+        step_size = step_ref[...]
+        gy[...] = grad_mixed
+        du[0:rows, :] = step_size * u_act
+        du[rows:, :] = jnp.zeros((BLOCK, tile), F32)
+        grad_skip = jnp.sum(grad_mixed * u_act, 0, keepdims=True)
+        rate = decay_ref[...]
+        decay = rate * LOG2E
+        sums = (iota((BLOCK, big), 0) == iota((BLOCK, big), 1) // state).astype(BF16)
+        g_ring[1] = jnp.zeros((big, tile), BF16)
+        w_ring[1] = jnp.zeros((big, tile), BF16)
+
+        def reduce_block(spot, block):
+            grads = g_ring[spot]
+            source = jnp.minimum(block, blocks - 1)
+            high, low = block_of(b_high, source, BLOCK), block_of(b_low, source, BLOCK)
+            both = product(jnp.concatenate([high, low], 0), grads)
+            base = pl.ds(pl.multiple_of(block * BLOCK, BLOCK), BLOCK)
+            grad_du[base, :] = both[:BLOCK] + both[BLOCK:]
+            grad_step[base, :] = product(sums, w_ring[spot])
+            b_sums[base, :] += times_transpose(du[base, :].astype(BF16), grads)
+
+        def run_blocks(quarter, carry):
+            carried, log_sum = carry
+            for spot in range(turns):
+                turn = quarter * turns + spot
+                block = blocks - 1 - turn
+                later = (spot + turns - 1) % turns
+                if spot == 0:
+                    load(later, block - turns + 1).start()
+                else:
+                    pl.when(quarter < quarters - 1)(
+                        lambda: load(later, block - turns + 1).start()
+                    )
+                load(spot, block).wait()
+                here, before = spot % 2, (spot + 1) % 2
+                reduce_block(before, block + 1)
+                base = pl.ds(pl.multiple_of(block * BLOCK, BLOCK), BLOCK)
+                steps_now, gy_now = step_ref[base, :], gy[base, :]
+                c_now = block_of(c_cols, block, state)
+                c_sums[base, :] += times_transpose(gy_now.astype(BF16), ring[spot, state:, :])
+                for t in range(BLOCK - 1, -1, -1):
+                    at = slice(t * state, (t + 1) * state)
+                    c_wide = jnp.broadcast_to(c_now[:, t : t + 1], (state, tile))
+                    step_now = steps_now[t : t + 1, :]
+                    fade = jnp.exp2(step_now * decay)
+                    grad = gy_now[t : t + 1, :] * c_wide + carried
+                    g_ring[here, at, :] = grad.astype(BF16)
+                    carried = fade * grad
+                    weighted = carried * ring[spot, at, :].astype(F32) * rate
+                    w_ring[here, at, :] = weighted.astype(BF16)
+                    log_sum = log_sum + weighted * step_now
+            for turn in range(2):
+                for part in range(quarters):
+
+                    @pl.when((step == turn) & (quarter == part))
+                    def _():
+                        between(turn * 4 + part)
+
+            return carried, log_sum
+
+        zeros = jnp.zeros((state, tile), F32)
+        _, log_sum = lax.fori_loop(0, quarters, run_blocks, (zeros, zeros))
+        reduce_block(1, 0)
+        full_du = grad_du[0:rows, :]
+        gradu_all[:, lanes] = full_du * step_size + skip_ref[...] * gy[...]
+        grad_size = grad_step[0:rows, :] + full_du * u_act
+        grad_pre = grad_size * (1.0 - jnp.exp(-step_size))
+        grad_low = grad_pre.astype(BF16)
+        grad_step_w = contract_rows(proj_ref[:, :rank].astype(BF16), grad_low)
+        packed = jnp.concatenate(
+            [grad_step_w, log_sum, jnp.sum(grad_pre, 0, keepdims=True), grad_skip, zeros[:6]], 0
+        ).astype(BF16)
+        for turn in range(2):
+
+            @pl.when(step == turn)
+            def _():
+                split_lanes(send_scan.at[pl.ds(turn * half, half)], packed)
+                start_inputs(half + turn * half // 2, half + (turn + 1) * half // 2)
+
+        gradproj[:, :rank] += times_transpose(grad_low, stepw_ref[...])
+
+    @pl.when(step == 1)
+    def _():
+        ways[1].start()
+        own = iota((rows, big), 0) % BLOCK == iota((rows, big), 1) // state
+        lane = iota((big, cols), 1)
+        slot = iota((big, cols), 0) % state
+        total = gradproj[...]
+        for sums_here, first in ((b_sums[0:rows, :], rank), (c_sums[...], rank + state)):
+            place = (lane == first + slot).astype(F32)
+            total = total + exact_product(jnp.where(own, sums_here, 0.0), place)
+        gradproj[...] = total
+
+    @pl.when(step == 2)
+    def _():
+        load_mid.start()
+        grad_du[...] = jnp.zeros_like(grad_du)
+
+    @pl.when(step == steps_x + 2)
+    def _():
+        split_lanes(send_back, pack_back[...])
+        ways[2].start()
+        lhs = jnp.concatenate([gated_all[k] for k in range(devices)], 1)
+        totals[2 * gated_all.shape[1] : 3 * gated_all.shape[1], :] = product(
+            lhs, everyone[...].reshape(devices * rows, width)
+        ).astype(BF16)
+        load_normed.start()
+
+    here = pl.ds(
+        pl.multiple_of((jnp.maximum(step - 2, 0) % steps_x) * small_tile, small_tile), small_tile
+    )
+
+    @pl.when((step >= 2) & (step < steps_x + 2))
+    def _():
+        conv_ref, bias_ref = conv_rows(misc_x_ref)
+        grad_proj = gradproj[...].astype(BF16)
+        grad_u = gradu_all[:, here] + times_transpose(grad_proj, scanw_ref[...])
+        pieces = [contract_rows(grad_proj, u_x_ref[...].astype(BF16))]
+        x_inner = xin_ref[...]
+        taps = conv_ref.shape[0]
+        shifted = [shift_rows(x_inner, taps - 1 - tap) for tap in range(taps)]
+        summed = bias_ref[...]
+        for tap in range(taps):
+            summed = summed + conv_ref[tap : tap + 1, :] * shifted[tap]
+        sig = sigmoid(summed)
+        grad_sum = grad_u * (sig * (1.0 + summed * (1.0 - sig)))
+        grad_x = jnp.zeros_like(x_inner)
+        for tap in range(taps):
+            pieces.append(jnp.sum(grad_sum * shifted[tap], 0, keepdims=True))
+            grad_x = grad_x + conv_ref[tap : tap + 1, :] * shift_rows(grad_sum, tap + 1 - taps)
+        pieces.append(jnp.sum(grad_sum, 0, keepdims=True))
+        pieces.append(jnp.zeros((pack_back.shape[0] - cols - taps - 1, small_tile), F32))
+        pack_back[:, here] = jnp.concatenate(pieces, 0).astype(BF16)
+        grad_x = grad_x.astype(BF16)
+        send_in[here, :] = grad_x.T
+        ring[x_spot, 0:rows, x_lanes] = grad_x
+        for part in range(half):
+            done = -(-(part + 1) * in_part // small_tile) + 1
+            pl.when(step == done)(lambda: start_inputs(part, part + 1))
+
+    @pl.when(step >= steps_x + 2)
+    def _():
+        grad_du[0:rows, :] += product(ring[x_spot, 0:rows, x_lanes], wx_ref[...]) + product(
+            gate_all[:, here], wg_ref[...]
+        )
+
+    @pl.when(step == steps_x + 3)
+    def _():
+        next_to = [(left_2, goal_l2), (right_2, goal_r2), (right_1, goal_r1)]
+        pick(
+            (next_to[1], next_to[2], next_to[2], next_to[0]), raw, goal, load_sems.at[pl.ds(4, 2)]
+        )
+        matrix = dispatch_matrix(goal, devices)
+        for part, (target, store) in enumerate(zip((g_ring, w_ring), store_sends)):
+            target[...] = product(matrix, raw[part]).astype(BF16).reshape(target.shape)
+            store.start()
+
+    @pl.when(step == 2 * steps_x + 1)
+    def _():
+        values = tokens_ref[...].astype(F32)
+        scale = lax.rsqrt(jnp.mean(values * values, -1, keepdims=True) + 1e-05)
+        unit = values * scale
+        grad = grad_du[0:rows, :]
+        widths = jnp.concatenate([widths_ref[...], jnp.sum(grad * unit, 0, keepdims=True)], 0)
+        widths = jnp.concatenate(
+            [widths, jnp.zeros((send_tail.shape[1] - widths.shape[0], width), F32)], 0
+        )
+        split_lanes(send_tail, widths.astype(BF16))
+        ways[3].start()
+        inner = grad * gains_ref[0:1, :]
+        load_mid.wait()
+        gy[...] += scale * (inner - unit * jnp.mean(inner * unit, -1, keepdims=True))
+        store_tokens = pltpu.make_async_copy(gy, gradtok_hbm, load_sems.at[2])
+        store_tokens.start()
+        at = 3 * gated_all.shape[1]
+        for way, got in ((ways[1], got_scan), (ways[2], got_back)):
+            way.wait()
+            totals[at : at + 32, :] = fold_rows(got, width)
+            at += 32
+        ways[3].wait()
+        tail = jnp.sum(got_tail[...].astype(F32), 0)
+        tail = jnp.concatenate([tail, jnp.zeros((tail.shape[0], width - tail.shape[1]), F32)], 1)
+        totals[at : at + 16, :] = tail.astype(BF16)
+        load_normed.wait()
+        input_local.wait()
+        for copy in input_copies:
+            copy.wait()
+        lhs = jnp.concatenate([got_in[k] for k in range(devices)], 1)
+        totals[0:in_part, :] = product(
+            lhs, everyone[...].reshape(devices * rows, width)
+        ).astype(BF16)
+        store_totals = pltpu.make_async_copy(totals, totals_hbm, load_sems.at[3])
+        store_totals.start()
+        for line in lines:
+            line.wait()
+        store_tokens.wait()
+        store_totals.wait()
+        for store in store_sends:
+            store.wait()
+
+
+def backward_plane(
+    proj, step_w, vec, u_act, gate_in, out_w, grad_mix, step_size, mixed, scan_w, x_inner, in_t,
+    tokens, gains, grad_widths, grad_mid, gated, normed_all, hist, rows_0, grads_0, raws, goals,
 ):
     rows, channels = u_act.shape
     width = grad_mix.shape[1]
     cols = proj.shape[1]
     rank, state = step_w.shape[0], vec.shape[0] - 8
     devices = lax.axis_size("expert")
-    tile = channels // 2
-    gate_parts, pack_parts = devices // 4, devices // 2
-    pack_rows = rank + state + 8
+    part = channels // devices
+    tile, small = channels // 2, channels // 6
     big = BLOCK * state
-    column = lambda i: (0, i)
+    pack_rows, tail_rows = cols + 8, grad_widths.shape[0] + 7
     fixed = lambda i: (0, 0)
-    slots = jax.ShapeDtypeStruct((devices // 2, CAP, width), BF16)
+    first = lambda i: jnp.minimum(i, 1)
+    second = lambda i: jnp.clip(i - 2, 0, 5)
+    once = pl.Buffered(1)
+    slots = jax.ShapeDtypeStruct(rows_0.shape, BF16)
     raw = jax.ShapeDtypeStruct(raws[0].shape, BF16)
     goal = jax.ShapeDtypeStruct(goals[0].shape, jnp.int32)
+    total_rows = 3 * part + 80
+    pair = jax.ShapeDtypeStruct((2, 2, big, tile), BF16)
+    third = lambda i: jnp.maximum(i - 8, 0)
+    packs = [
+        pltpu.VMEM((devices, count, lanes), BF16)
+        for count, lanes in (
+            (rank + state + 8, part), (pack_rows, part), (tail_rows, width // devices)
+        )
+        for _ in range(2)
+    ]
     return pl.pallas_call(
-        scan_back_plane_kernel,
-        grid=(2,),
+        backward_kernel,
+        grid=(14,),
         in_specs=[
             pl.BlockSpec((rows, cols), fixed),
-            pl.BlockSpec((rank, tile), column),
-            pl.BlockSpec((state, tile), column),
-            pl.BlockSpec((8, tile), lambda i: (state // 8, i)),
-            pl.BlockSpec((rows, tile), column),
-            pl.BlockSpec((rows, tile), column),
-            pl.BlockSpec((tile, width), lambda i: (i, 0)),
-            pl.BlockSpec((rows, width), fixed),
-            pl.BlockSpec((rows, tile), column),
-            pl.BlockSpec((rows, tile), column),
-            pl.BlockSpec((hist.shape[0], tile), column),
-            pl.BlockSpec((rows, width), fixed),
-            pl.BlockSpec(gated.shape, lambda i: (0, 0, 0)),
-        ] + [FAR] * 5,
-        out_specs=[
-            pl.BlockSpec((rows, tile), column),
-            pl.BlockSpec((rows, tile), column),
-            pl.BlockSpec((pack_parts, pack_rows, tile // pack_parts), lambda i: (i, 0, 0)),
-            pl.BlockSpec((rows, cols), fixed),
-            pl.BlockSpec((gate_parts, tile // gate_parts, rows), lambda i: (i, 0, 0)),
-        ] + [FAR] * 8,
+            pl.BlockSpec((rank, tile), lambda i: (0, first(i))),
+            pl.BlockSpec((state, tile), lambda i: (0, first(i))),
+            pl.BlockSpec((8, tile), lambda i: (state // 8, first(i))),
+            pl.BlockSpec((rows, tile), lambda i: (0, first(i))),
+            pl.BlockSpec((rows, tile), lambda i: (0, first(i))),
+            pl.BlockSpec((tile, width), lambda i: (first(i), 0), pipeline_mode=once),
+            pl.BlockSpec((rows, width), fixed, pipeline_mode=once),
+            pl.BlockSpec((rows, tile), lambda i: (0, first(i))),
+            pl.BlockSpec((rows, tile), lambda i: (0, first(i))),
+            pl.BlockSpec((small, cols), lambda i: (second(i), 0)),
+            pl.BlockSpec((rows, small), lambda i: (0, second(i))),
+            pl.BlockSpec((8, small), lambda i: (state // 8, second(i))),
+            pl.BlockSpec((small, width), lambda i: (third(i), 0)),
+            pl.BlockSpec((small, width), lambda i: (third(i) + 6, 0)),
+            pl.BlockSpec((rows, small), lambda i: (0, second(i))),
+            pl.BlockSpec((rows, width), fixed, pipeline_mode=once),
+            pl.BlockSpec(gains.shape, fixed),
+            pl.BlockSpec(grad_widths.shape, fixed),
+        ] + [FAR] * 12,
+        out_specs=[FAR] * 9,
         out_shape=[
-            jax.ShapeDtypeStruct((rows, channels), F32),
-            jax.ShapeDtypeStruct((rows, channels), BF16),
-            jax.ShapeDtypeStruct((devices, pack_rows, channels // devices), BF16),
-            jax.ShapeDtypeStruct((rows, cols), F32),
-            jax.ShapeDtypeStruct((devices // 2, 2 * channels // devices, rows), BF16),
-            jax.ShapeDtypeStruct((devices, rows, width), BF16),
-            jax.ShapeDtypeStruct((devices, rows // 2, width), BF16),
-            jax.ShapeDtypeStruct(gated.shape, BF16),
-            slots, raw, raw, goal, goal,
+            jax.ShapeDtypeStruct((rows, width), F32),
+            jax.ShapeDtypeStruct((total_rows, width), BF16),
+            slots, slots, raw, raw, goal, goal, pair,
         ],
         scratch_shapes=[
-            pltpu.VMEM((rows * state, 128), F32),
-            pltpu.VMEM((rows * 2, big), BF16),
-            pltpu.VMEM((rows, big), F32),
+            pltpu.VMEM((rows // BLOCK * state, 128), F32),
+            pltpu.VMEM((rows, big), BF16),
+            pltpu.VMEM((rows, big), BF16),
+            pltpu.VMEM((rows + BLOCK, big), F32),
             pltpu.VMEM((rows, big), F32),
             pltpu.VMEM((rows, tile), F32),
-            pltpu.VMEM((rows, tile), F32),
-            pltpu.VMEM((big, tile), BF16),
-            pltpu.VMEM((big, tile), BF16),
-            pltpu.VMEM((rows, tile), F32),
-            pltpu.VMEM((rows, tile), F32),
-            DMA((2, 10)), DMA((2, 10)), DMA((devices,)), DMA((devices,)), DMA((3, 2)), DMA((3, 2)),
-            DMA((3,)),
-        ],
-        compiler_params=remote_params(4),
-        name="scan_backward_plane",
-    )(
-        proj, step_w, vec, vec, u_act, gate_in, out_w, grad_mix, step_size, mixed, hist,
-        normed_low, gated, rows_0, raws[2], raws[3], goals[2], goals[3],
-    )
-
-
-def back_plane_kernel(
-    gradproj_ref, scanw_ref, gradu_ref, xin_ref, misc_ref, wx_ref, wg_ref, u_ref,
-    tokens_ref, gain_ref, gradmid_ref, widths_ref, gradgate_ref,
-    gate_hbm, scan_parts, normed_low, normed_high, mix_hbm, gated_hbm, rows_0, grads_0,
-    gradtok_ref, totals_ref, rows_1, grads_1,
-    total, send_in, got_in, normed_all, mix_all, gated_all, got_scan, send_back, got_back,
-    send_tail, got_tail, x_send, x_recv, l_send, l_recv, local_sems, load_sems,
-):
-    tile_id = pl.program_id(0)
-    devices, me = lax.axis_size("expert"), lax.axis_index("expert")
-    half = devices // 2
-    gates = send_in.shape[0] // 4
-    ways = [
-        Exchange(source, target, x_send.at[k], x_recv.at[k], local_sems.at[k])
-        for k, (source, target) in enumerate(
-            [
-                (send_in, got_in), (scan_parts, got_scan), (send_back, got_back),
-                (send_tail, got_tail),
-            ]
-        )
-    ]
-    conv_ref, bias_ref = conv_rows(misc_ref)
-    near_rows = rows_1.shape[0]
-    half_rows = normed_low.shape[1]
-    nears = [
-        Near(rows_0.at[pl.ds(near_rows, near_rows)], rows_1, l_send.at[0], l_recv.at[0]),
-        Near(grads_0, grads_1, l_send.at[1], l_recv.at[1]),
-    ]
-    loads = [
-        pltpu.make_async_copy(source, target, load_sems.at[k])
-        for k, (source, target) in enumerate(
-            [
-                (gate_hbm, send_in.at[pl.ds(half, half)]),
-                (normed_low, normed_all.at[:, pl.ds(0, half_rows)]),
-                (normed_high, normed_all.at[:, pl.ds(half_rows, half_rows)]),
-                (mix_hbm, mix_all), (gated_hbm, gated_all),
-            ]
-        )
-    ]
-
-    def start_inputs(first, last):
-        for k, copy in enumerate(ways[0].copies):
-            peer = (me + k + 1) % devices
-            pl.when((peer >= first) & (peer < last))(lambda copy=copy: copy.start())
-        pl.when((me >= first) & (me < last))(lambda: ways[0].local.start())
-
-    @pl.when(tile_id == 0)
-    def _():
-        total[...] = jnp.zeros_like(total)
-        for load in loads:
-            load.start()
-        greet()
-        for near in nears:
-            near.start()
-        loads[0].wait()
-        start_inputs(half, devices)
-        ways[1].start()
-
-    grad_proj = gradproj_ref[...].astype(BF16)
-    grad_u = gradu_ref[...] + times_transpose(grad_proj, scanw_ref[...])
-    pieces = [contract_rows(grad_proj, u_ref[...].astype(BF16))]
-    x_inner = xin_ref[...]
-    taps = conv_ref.shape[0]
-    shifted = [shift_rows(x_inner, taps - 1 - tap) for tap in range(taps)]
-    summed = bias_ref[...]
-    for tap in range(taps):
-        summed = summed + conv_ref[tap : tap + 1, :] * shifted[tap]
-    sig = sigmoid(summed)
-    grad_sum = grad_u * (sig * (1.0 + summed * (1.0 - sig)))
-    grad_x = jnp.zeros_like(x_inner)
-    for tap in range(taps):
-        pieces.append(jnp.sum(grad_sum * shifted[tap], 0, keepdims=True))
-        grad_x = grad_x + conv_ref[tap : tap + 1, :] * shift_rows(grad_sum, tap + 1 - taps)
-    pieces.append(jnp.sum(grad_sum, 0, keepdims=True))
-    spare = send_back.shape[1] - grad_proj.shape[1] - taps - 1
-    pieces.append(jnp.zeros((spare, x_inner.shape[1]), F32))
-    packed = jnp.concatenate(pieces, 0).astype(BF16)
-    grad_x = grad_x.astype(BF16)
-    for turn in range(2):
-
-        @pl.when(tile_id == turn)
-        def _():
-            split_lanes(send_back.at[pl.ds(turn * half, half)], packed)
-            send_in[turn * gates : (turn + 1) * gates] = grad_x.T.reshape(
-                (gates,) + send_in.shape[1:]
-            )
-            start_inputs(turn * gates, (turn + 1) * gates)
-
-    @pl.when(tile_id == 1)
-    def _():
-        ways[2].start()
-
-    total[...] += product(grad_x, wx_ref[...]) + product(gradgate_ref[...], wg_ref[...])
-
-    @pl.when(tile_id == 1)
-    def _():
-        values = tokens_ref[...].astype(F32)
-        scale = lax.rsqrt(jnp.mean(values * values, -1, keepdims=True) + 1e-05)
-        unit = values * scale
-        grad = total[...]
-        widths = jnp.concatenate([widths_ref[...], jnp.sum(grad * unit, 0, keepdims=True)], 0)
-        widths = jnp.concatenate(
-            [widths, jnp.zeros((send_tail.shape[1] - widths.shape[0], widths.shape[1]), F32)], 0
-        )
-        split_lanes(send_tail, widths.astype(BF16))
-        ways[3].start()
-        inner = grad * gain_ref[0:1, :]
-        gradtok_ref[...] = gradmid_ref[...] + scale * (
-            inner - unit * jnp.mean(inner * unit, -1, keepdims=True)
-        )
-        for load in loads[1:]:
-            load.wait()
-        rows, width = mix_all.shape[1:]
-
-        def side_by_side(ref):
-            return jnp.concatenate([ref[k] for k in range(devices)], 1)
-
-        in_rows, part = got_in.shape[1], gated_all.shape[1]
-        totals_ref[in_rows : in_rows + part, :] = product(
-            side_by_side(gated_all), mix_all[...].reshape(devices * rows, width)
-        ).astype(BF16)
-        ways[0].wait()
-        totals_ref[0:in_rows, :] = product(
-            side_by_side(got_in), normed_all[...].reshape(devices * rows, width)
-        ).astype(BF16)
-        at = in_rows + part
-        for way, got in ((ways[1], got_scan), (ways[2], got_back)):
-            way.wait()
-            total_here = jnp.sum(got[...].astype(F32), 0)
-            quarter = total_here.shape[0] // 4
-            folded = jnp.concatenate(
-                [total_here[k * quarter : (k + 1) * quarter] for k in range(4)], 1
-            )
-            padding = jnp.zeros((32 - quarter, width), F32)
-            totals_ref[at : at + 32, :] = jnp.concatenate([folded, padding], 0).astype(BF16)
-            at += 32
-        ways[3].wait()
-        tail = jnp.sum(got_tail[...].astype(F32), 0)
-        tail = jnp.concatenate(
-            [tail, jnp.zeros((tail.shape[0], width - tail.shape[1]), F32)], 1
-        )
-        totals_ref[at : at + 16, :] = tail.astype(BF16)
-        for near in nears:
-            near.wait()
-
-
-def mixer_back_plane(
-    grad_proj, scan_w, grad_u, x_inner, vec, in_t, u_act, tokens, gains, grad_mid, grad_widths,
-    grad_gate, gate_parts, scan_parts, normed_low, normed_high, mix_all, gated_all, rows_0, grads_0,
-):
-    rows, channels = u_act.shape
-    width = tokens.shape[1]
-    cols = scan_w.shape[1]
-    devices = lax.axis_size("expert")
-    part = channels // devices
-    tile = channels // 2
-    pack_rows = cols + 8
-    tail_rows = grad_widths.shape[0] + 7
-    column = lambda i: (0, i)
-    fixed = lambda i: (0, 0)
-    return pl.pallas_call(
-        back_plane_kernel,
-        grid=(2,),
-        in_specs=[
-            pl.BlockSpec((rows, cols), fixed),
-            pl.BlockSpec((tile, cols), lambda i: (i, 0)),
-            pl.BlockSpec((rows, tile), column),
-            pl.BlockSpec((rows, tile), column),
-            pl.BlockSpec((8, tile), lambda i: ((vec.shape[0] - 8) // 8, i)),
-            pl.BlockSpec((tile, width), lambda i: (i, 0)),
-            pl.BlockSpec((tile, width), lambda i: (i + 2, 0)),
-            pl.BlockSpec((rows, tile), column),
-            pl.BlockSpec((rows, width), fixed),
-            pl.BlockSpec(gains.shape, fixed),
-            pl.BlockSpec((rows, width), fixed),
-            pl.BlockSpec(grad_widths.shape, fixed),
-            pl.BlockSpec((rows, tile), column),
-        ] + [FAR] * 8,
-        out_specs=[
-            pl.BlockSpec((rows, width), fixed),
-            pl.BlockSpec((3 * part + 80, width), fixed),
-            FAR,
-            FAR,
-        ],
-        out_shape=[
-            jax.ShapeDtypeStruct((rows, width), F32),
-            jax.ShapeDtypeStruct((3 * part + 80, width), BF16),
-            jax.ShapeDtypeStruct((devices // 2,) + rows_0.shape[1:], BF16),
-            jax.ShapeDtypeStruct(grads_0.shape, BF16),
-        ],
-        scratch_shapes=[
-            pltpu.VMEM((rows, width), F32),
-            pltpu.VMEM((devices, 2 * part, rows), BF16),
+            pltpu.VMEM((rows + BLOCK, tile), F32),
+            pltpu.VMEM((rows + BLOCK, tile), F32),
+            pltpu.VMEM((rows + BLOCK, tile), F32),
+            pltpu.VMEM((4, big + state, tile), BF16),
+            pltpu.VMEM((2, big, tile), BF16),
+            pltpu.VMEM((2, big, tile), BF16),
+            pltpu.VMEM((rows, cols), F32),
+            pltpu.VMEM((rows, channels), F32),
+            pltpu.VMEM((rows, channels), BF16),
+            pltpu.VMEM((2 * channels, rows), BF16),
             pltpu.VMEM((devices, 2 * part, rows), BF16),
             pltpu.VMEM((devices, rows, width), BF16),
-            pltpu.VMEM(mix_all.shape, BF16),
-            pltpu.VMEM(gated_all.shape, BF16),
-            pltpu.VMEM(scan_parts.shape, BF16),
-            pltpu.VMEM((devices, pack_rows, part), BF16),
-            pltpu.VMEM((devices, pack_rows, part), BF16),
-            pltpu.VMEM((devices, tail_rows, width // devices), BF16),
-            pltpu.VMEM((devices, tail_rows, width // devices), BF16),
-            DMA((4, devices)), DMA((4, devices)), DMA((2, 2)), DMA((2, 2)), DMA((4,)), DMA((5,)),
-        ],
-        compiler_params=remote_params(5),
-        name="mixer_back_plane",
+            pltpu.VMEM(gated.shape, BF16),
+            packs[0],
+            packs[1],
+            pltpu.VMEM((pack_rows, channels), BF16),
+            *packs[2:],
+            pltpu.VMEM((total_rows, width), BF16),
+            pltpu.VMEM(raw.shape, BF16),
+            pltpu.VMEM(goal.shape, jnp.int32),
+            DMA((10,)), DMA((10,)), DMA((5, devices)), DMA((5, devices)), DMA((4, 2)), DMA((4, 2)),
+            DMA((6,)), DMA((4,)), DMA((8,)),
+        ],
+        compiler_params=pltpu.CompilerParams(
+            vmem_limit_bytes=VMEM_LIMIT, collective_id=4, has_side_effects=True
+        ),
+        name="mixer_backward",
     )(
-        grad_proj, scan_w, grad_u, x_inner, vec, in_t, in_t, u_act, tokens, gains, grad_mid,
-        grad_widths, grad_gate, gate_parts, scan_parts, normed_low, normed_high, mix_all, gated_all,
-        rows_0, grads_0,
+        proj, step_w, vec, vec, u_act, gate_in, out_w, grad_mix, step_size, mixed, scan_w, x_inner,
+        vec, in_t, in_t, u_act, tokens, gains, grad_widths, grad_mid, gated, normed_all, hist,
+        rows_0, grads_0, raws[2], raws[3], raws[1], goals[2], goals[3], goals[1],
     )
 
 
@@ -1789,32 +2008,49 @@
     return values[0] if len(values) == 1 else jnp.concatenate(values, 0)
 
 
-def next_grads_kernel(sizes, choices, up_ref, down_ref, gup_in, gdown_in, *refs):
-    row_parts, grad_parts, count = sizes
-    rows_in, refs = refs[:row_parts], refs[row_parts:]
-    grads_in, refs = refs[:grad_parts], refs[grad_parts:]
-    raws, goals, refs = refs[:count], refs[count : 2 * count], refs[2 * count :]
+def next_grads_kernel(
+    last, up_ref, down_ref, gup_in, gdown_in, rows_ref, grads_ref, sends_in, *refs
+):
+    if not last:
+        raws, goals, refs = refs[:4], refs[4:8], refs[8:]
     gup_ref, gdown_ref, rows_out, grads_out, refs = *refs[:4], refs[4:]
-    rows_t, raw, goal, sends, x_send, x_recv, local_sems, load_sems = refs
+    if not last:
+        sends_out, refs = refs[0], refs[1:]
+    rows_t, x_send, x_recv, local_sems, refs = *refs[:4], refs[4:]
     step = pl.program_id(0)
-    rows, grads = flat_rows(rows_in), flat_rows(grads_in)
-    group = Dispatch(raw, goal, sends, (rows_out, grads_out), x_send, x_recv, local_sems)
+    rows, grads = flat_rows((rows_ref,)), flat_rows((grads_ref,))
+    ways = [
+        Exchange(sends_in.at[k], out, x_send.at[k], x_recv.at[k], local_sems.at[k])
+        for k, out in enumerate((rows_out, grads_out))
+    ]
 
     @pl.when(step == 0)
     def _():
         greet(line=False)
-        pick([(raws[k], goals[k]) for k in choices], raw, goal, load_sems)
-        group.prepare((0, 1))
-        group.start()
+        for way in ways:
+            way.start()
         rows_t[...] = rows.T
 
     grad_up, grad_down = add_groups(rows, grads, rows_t[...], up_ref, down_ref)
     gup_ref[...] = (gup_in[...].astype(F32) + grad_up).astype(BF16)
     gdown_ref[...] = (gdown_in[...].astype(F32) + grad_down).astype(BF16)
+    if not last:
+        raw, goal, sends, load_sems = refs
+        left_2, left_3, right_2, right_3 = zip(raws, goals)
+        store = pltpu.make_async_copy(sends, sends_out, load_sems.at[2])
+
+        @pl.when(step == 1)
+        def _():
+            pick((right_3, right_2, left_2, left_3), raw, goal, load_sems)
+            prepare_sends(raw, goal, sends)
+            store.start()
 
     @pl.when(step == pl.num_programs(0) - 1)
     def _():
-        group.wait()
+        for way in ways:
+            way.wait()
+        if not last:
+            store.wait()
 
 
 def last_grads_kernel(
@@ -1831,53 +2067,54 @@
     gdown_ref[...] = gdown_in[...].astype(F32) + grad_down
 
 
-def expert_grads_plane(up, down, grad_up, grad_down, rows_1, grads_1, raws, goals, tile):
+def expert_grads_plane(up, down, grad_up, grad_down, rows, grads, sends, raws, goals, tile):
     width, hidden = up.shape
-    devices, cap = grads_1.shape[:2]
-    slots = jax.ShapeDtypeStruct(grads_1.shape, BF16)
-    across = pl.BlockSpec((width, tile), lambda i: (0, i))
-    along = pl.BlockSpec((tile, width), lambda i: (i, 0))
+    devices, cap = grads.shape[:2]
+    slots = jax.ShapeDtypeStruct(grads.shape, BF16)
+    pair = jax.ShapeDtypeStruct(sends.shape, BF16)
+    whole = pl.BlockSpec(grads.shape, lambda i: (0, 0, 0))
+
+    def tiles(size):
+        return [
+            pl.BlockSpec((width, size), lambda i: (0, i)),
+            pl.BlockSpec((size, width), lambda i: (i, 0)),
+        ]
 
     def shapes(kind):
         return [
             jax.ShapeDtypeStruct((width, hidden), kind), jax.ShapeDtypeStruct((hidden, width), kind)
         ]
 
-    def wholes(values):
-        return [pl.BlockSpec(value.shape, lambda i: (0, 0, 0)) for value in values]
-
-    left_2, left_3, right_1, right_2, right_3 = range(5)
-    rows, grads = rows_1, (grads_1,)
-    for turn, choices in enumerate(
-        ((right_2, right_1, right_1, left_2), (right_3, right_2, left_2, left_3))
-    ):
-        grad_up, grad_down, rows_next, grads_next = pl.pallas_call(
-            partial(next_grads_kernel, (len(rows), len(grads), len(raws)), choices),
+    turned = pltpu.VMEM((width, devices * cap), BF16)
+    sems = [DMA((2, devices)), DMA((2, devices)), DMA((2,))]
+    for last in (False, True):
+        extra = () if last else (*raws, *goals)
+        grad_up, grad_down, rows, grads, *more = pl.pallas_call(
+            partial(next_grads_kernel, last),
             grid=(hidden // tile,),
-            in_specs=[across, along] * 2 + wholes(rows + grads) + [FAR] * (2 * len(raws)),
-            out_specs=[across, along, FAR, FAR],
-            out_shape=shapes(BF16) + [slots] * 2,
-            scratch_shapes=[
-                pltpu.VMEM((width, devices * cap), BF16),
-                pltpu.VMEM(raws[0].shape, BF16),
-                pltpu.VMEM(goals[0].shape, jnp.int32),
-                pltpu.VMEM((2,) + slots.shape, BF16),
-                DMA((2, devices)), DMA((2, devices)), DMA((2,)), DMA((2,)),
-            ],
-            compiler_params=remote_params(6 + turn),
-            name="expert_grads_" + str(turn + 1),
-        )(up, down, grad_up, grad_down, *rows, *grads, *raws, *goals)
-        rows, grads = (rows_next,), (grads_next,)
+            in_specs=tiles(tile) * 2 + [whole] * 2 + [FAR] * (1 + len(extra)),
+            out_specs=tiles(tile) + [FAR] * (2 if last else 3),
+            out_shape=shapes(BF16) + [slots] * 2 + ([] if last else [pair]),
+            scratch_shapes=[turned] + sems + (
+                [] if last else [
+                    pltpu.VMEM(raws[0].shape, BF16), pltpu.VMEM(goals[0].shape, jnp.int32),
+                    pltpu.VMEM(pair.shape, BF16), DMA((3,)),
+                ]
+            ),
+            compiler_params=remote_params(7 if last else 6),
+            name="expert_grads_2" if last else "expert_grads_1",
+        )(up, down, grad_up, grad_down, rows, grads, sends, *extra)
+        sends = more[0] if more else None
     return pl.pallas_call(
         last_grads_kernel,
-        grid=(hidden // tile,),
-        in_specs=[across, along] * 2 + wholes(rows + grads),
-        out_specs=[across, along],
+        grid=(hidden // 768,),
+        in_specs=tiles(768) * 2 + [whole] * 2,
+        out_specs=tiles(768),
         out_shape=shapes(F32),
-        scratch_shapes=[pltpu.VMEM((width, devices * cap), BF16)],
+        scratch_shapes=[turned],
         compiler_params=pltpu.CompilerParams(vmem_limit_bytes=VMEM_LIMIT),
         name="expert_grads_3",
-    )(up, down, grad_up, grad_down, *rows, *grads)
+    )(up, down, grad_up, grad_down, rows, grads)
 
 
 def finish_kernel(
@@ -1958,10 +2195,39 @@
     vectors = jnp.stack([conv_bias, step_bias, skip_gain])
     norms = jnp.stack([mixer_norm, moe_norm])
     in_t, decay_t, router_t = in_weight.T, decay_log.T, router_weight.T
+    up, down = up_weight[0], down_weight[0]
+    hidden = up.shape[1]
     if on_plane:
-        in_t, scan_full, step_full, vec, router_t, gains = gather_weights(
-            in_t, scan_weight, step_weight, decay_t, conv_weight, vectors, norms, router_t
-        )
+        (
+            normed_low, x_inner, u_act, gate_in, proj, step_size, mixed, gated, mid, step_full, vec,
+            router_t, gains, scan_full, in_t, out_full, normed_all, hist,
+        ) = forward_plane(
+            tokens[0], in_t, scan_weight, step_weight, decay_t, conv_weight, vectors, norms,
+            router_t, out_weight,
+        )
+        in_t = in_t.reshape(2 * channels, width)
+        scan_full = scan_full.reshape(channels, cols)
+        out_full = out_full.reshape(channels, width)
+        layer_out, grad_mid, grad_mix, grad_widths, rows_0, grads_0, *line = expert_layer(
+            lengths, mid, gains, router_t, routes, slot_index, cotangent[0], up, down
+        )
+        raws, goals, grad_up, grad_down = line[:4], line[4:8], line[8], line[9]
+        (
+            tokens_grad, totals, rows_1, grads_1, left_3, right_3, goal_l3, goal_r3, sends
+        ) = backward_plane(
+            proj, step_full, vec, u_act, gate_in, out_full, grad_mix, step_size, mixed, scan_full,
+            x_inner, in_t, tokens[0], gains, grad_widths, grad_mid, gated, normed_all, hist, rows_0,
+            grads_0, raws, goals,
+        )
+        totals = lax.psum(totals, "dp")
+        grad_up, grad_down = expert_grads_plane(
+            up, down, grad_up, grad_down, rows_1, grads_1,
+            sends.reshape((2,) + rows_1.shape), (raws[2], left_3, raws[3], right_3), (goals[2], goal_l3, goals[3], goal_r3), 512,
+        )
+        in_total, out_total, scan_w_total, step_w_total, decay_total, conv_total, *rest = finish(
+            totals, 2 * part, part, cols, rank, state, taps, experts, slice_w
+        )
+        vector_totals, norm_totals, router_total = rest
     else:
         spare = jnp.zeros((8 - taps - 3, part), BF16)
         columns = jnp.concatenate([step_weight, decay_t, conv_weight, vectors, spare], 0)
@@ -1974,45 +2240,11 @@
         step_full, rest = columns[:rank], columns[rank:].astype(F32)
         vec = jnp.concatenate([-jnp.exp(rest[:state]), rest[state:]], 0)
         router_t, gains = across[:experts], across[experts:].astype(F32)
-    in_t = in_t.reshape(2 * channels, width)
-    scan_full = scan_full.reshape(channels, cols)
-    up, down = up_weight[0], down_weight[0]
-    normed_low, x_inner, u_act, gate_in, proj = front(
-        tokens[0], gains, in_t, vec, scan_full, tile
-    )
-    hidden = up.shape[1]
-    if on_plane:
-        step_size, mixed, gated, hist, mid, out_full, normed_first = scan_forward_plane(
-            proj, step_full, vec, u_act, gate_in, out_weight, tokens[0], normed_low
-        )
-        out_full = out_full.reshape(channels, width)
-        layer_out, grad_mid, grad_mix, grad_widths, rows_0, grads_0, *line = expert_layer(
-            lengths, mid, gains, router_t, routes, slot_index, cotangent[0], up, down
-        )
-        raws, goals, grad_up, grad_down = line[:4], line[4:8], line[8], line[9]
-        (
-            grad_u, grad_gate, scan_parts, grad_proj, gate_parts, mix_all, normed_last, gated_all,
-            rows_1a, left_3, right_3, goal_l3, goal_r3,
-        ) = scan_backward_plane(
-            proj, step_full, vec, u_act, gate_in, out_full, grad_mix, step_size, mixed, hist,
-            normed_low, gated, rows_0, raws, goals,
-        )
-        tokens_grad, totals, rows_1b, grads_1 = mixer_back_plane(
-            grad_proj, scan_full, grad_u, x_inner, vec, in_t, u_act, tokens[0], gains, grad_mid,
-            grad_widths, grad_gate, gate_parts, scan_parts, normed_first, normed_last, mix_all,
-            gated_all, rows_0, grads_0,
-        )
-        totals = lax.psum(totals, "dp")
-        grad_up, grad_down = expert_grads_plane(
-            up, down, grad_up, grad_down, (rows_1a, rows_1b), grads_1,
-            (raws[2], left_3, raws[1], raws[3], right_3),
-            (goals[2], goal_l3, goals[1], goals[3], goal_r3), 512,
-        )
-        in_total, out_total, scan_w_total, step_w_total, decay_total, conv_total, *rest = finish(
-            totals, 2 * part, part, cols, rank, state, taps, experts, slice_w
-        )
-        vector_totals, norm_totals, router_total = rest
-    else:
+        in_t = in_t.reshape(2 * channels, width)
+        scan_full = scan_full.reshape(channels, cols)
+        normed_low, x_inner, u_act, gate_in, proj = front(
+            tokens[0], gains, in_t, vec, scan_full, tile
+        )
         live = (jnp.arange(rows, dtype=jnp.int32) < lengths[0]).astype(F32)[:, None]
         routes_col, slots_col = routes[0][:, None], slot_index[0][:, None]
         router, gain_second = router_t.T, gains[1:2]

time: 437 us -> 384 us (0.88)
  Pallas kernels: 406 us -> 352 us
    pallas_call x8 -> x5, Pallas kernels: 338 us -> 285 us  [the longest x1 94.4 us: backward_plane(): pl.pallas_call(backward_kernel, grid=(14,), in_specs=[pl.BlockSpec((rows,...]
  transfers between devices with their start and end apart: 1 -> 1, of which waited for: 0 -> 0; matrix products, arithmetic and copies ran while one was open for 0% -> 0% of each run, Pallas kernels for 25% -> 27%
where the time goes in v4:
time: 384 us; the launch traced here: 376 us
  Pallas kernels  352 us (92%)
  between operations  14.9 us (4%)
  local copies, waits for them, and re-layouts  7.93 us (2%)
    pallas_call x1, Pallas kernels, backward_plane(): pl.pallas_call(backward_kernel, grid=(14,), in_specs=[pl.BlockSpec((rows,...  94.4 us
    pallas_call x1, Pallas kernels, forward_plane(): pl.pallas_call(forward_kernel, grid=(4,), in_specs=[whole(value.shape) fo...  90 us
    pallas_call x2, Pallas kernels, expert_grads_plane(): pl.pallas_call(partial(next_grads_kernel, last), grid=(hidden // tile,),...  73.6 us
    pallas_call x1, Pallas kernels, expert_layer(): pl.pallas_call(expert_layer_kernel, in_specs=[pl.BlockSpec(memory_space=p...  63.6 us
    pallas_call x1, Pallas kernels, expert_grads_plane(): pl.pallas_call(last_grads_kernel, grid=(hidden // 768,), in_specs=tiles(7...  26.5 us
  transfers between devices with their start and end apart: 1, of which 0 were waited for; matrix products, arithmetic and copies ran while one was open for 0% of the time, Pallas kernels for 27%

profile of v4, /device:TPU:9, one launch (start us, length us, event | category | flops | bytes accessed | tf_op | source)
XLA Modules:
  0.0 376.2 jit_solution(11598935139035527141)
XLA Ops:
  7.2 0.0 all-reduce.2.cloned.1.call-start
  7.9 0.7 stack.25
  8.5 0.7 stack.26
  9.2 0.7 stack.21
  9.9 0.7 stack.22
  10.6 0.7 stack.23
  11.2 0.6 pad_maximum_fusion.1.norms_ref
  11.8 0.6 pad_maximum_fusion.vectors_ref
  12.4 90.0 %mixer_forward.1 = (bf16[256,1152]{1,0:T(8,128)(2,1)}, f32[256,2304]{1,0:T(8,128)}, f32[256,2304]{1,0:T(8,128)}, f32[256,2304]{1,0:T(8,128)}, f32[256,104]{1,0:T...) custom-call(bf16[256,1152]{1,0:T(8,128)(2,1)} %bitcast.32, ...), custom_call_target="tpu_custom_call" | custom-call | tf_op jit(solution)/shard_map/mixer_forward/pallas_call | solution.py:1491
  102.4 63.6 %expert_layer.1 = (bf16[256,1152]{1,0:T(8,128)(2,1)}, f32[256,1152]{1,0:T(8,128)}, bf16[256,1152]{1,0:T(8,128)(2,1)}, f32[9,1152]{1,0:T(8,128)}, bf16[8,64,1152]...) custom-call(s32[1]{0:T(128)S(6)} %copy.38.length_ref, ...), custom_call_target="tpu_custom_call" | custom-call | tf_op jit(solution)/shard_map/expert_layer/pallas_call | solution.py:1071
  166.0 94.4 %mixer_backward.1 = (f32[256,1152]{1,0:T(8,128)}, bf16[944,1152]{1,0:T(8,128)(2,1)}, bf16[8,64,1152]{2,1,0:T(8,128)(2,1)}, bf16[8,64,1152]{2,1,0:T(8,128)(2,1)},...) custom-call(f32[256,104]{1,0:T(8,128)} %get-tuple-element.80.proj_re, ...), custom_call_target="tpu_custom_call" | custom-call | tf_op jit(solution)/shard_map/mixer_backward/pallas_call | solution.py:1928
  260.4 0.0 all-reduce.2.cloned.1.call-update
  260.4 38.6 %expert_grads_1.1 = (bf16[1152,3072]{1,0:T(8,128)(2,1)}, bf16[3072,1152]{1,0:T(8,128)(2,1)}, bf16[8,64,1152]{2,1,0:T(8,128)(2,1)}, bf16[8,64,1152]{2,1,0:T(8,128)(2,1)}, bf16[2,8,64,1152]{3,2,1,0:T(8,128)(2,1)}) custom-call(bf16[1152,3072]{1,0:T(8,128)(2,1)} %bitcast.21, bf16[3072,1152]{1,0:T(8,128)(2,1)} %bitcast.25, ...), custom_call_target="tpu_custom_call" | custom-call | tf_op jit(solution)/shard_map/expert_grads_1/pallas_call | solution.py:2092
  299.0 35.1 %expert_grads_2.1 = (bf16[1152,3072]{1,0:T(8,128)(2,1)}, bf16[3072,1152]{1,0:T(8,128)(2,1)}, bf16[8,64,1152]{2,1,0:T(8,128)(2,1)}, bf16[8,64,1152]{2,1,0:T(8,128)(2,1)}) custom-call(bf16[1152,3072]{1,0:T(8,128)(2,1)} %bitcast.22, bf16[3072,1152]{1,0:T(8,128)(2,1)} %bitcast.26, bf16[1152,3072]{1,0:T(8,128)(2,1)} %get-tuple-element.125.gup_in, ...), custom_call_target="tpu_custom_call" | custom-call | tf_op jit(solution)/shard_map/expert_grads_2/pallas_call | solution.py:2092
  334.1 26.5 %expert_grads_3.1 = (f32[1152,3072]{1,0:T(8,128)}, f32[3072,1152]{1,0:T(8,128)}) custom-call(bf16[1152,3072]{1,0:T(8,128)(2,1)} %bitcast.23, bf16[3072,1152]{1,0:T(8,128)(2,1)} %bitcast.27, bf16[1152,3072]{1,0:T(8,128)(2,1)} %get-tuple-element.130.gup_in, bf16[3072,1152]{1,0:T(8,128)(2,1)} %get-tuple-element.131.gdown_in, ...), custom_call_target="tpu_custom_call" | custom-call | tf_op jit(solution)/shard_map/expert_grads_3/pallas_call | solution.py:2108
  360.6 0.0 copy-start.1
  360.6 0.0 copy-start
  360.6 0.0 all-reduce.2.cloned.1.call-done.totals_ref
  360.6 4.0 %finish.1 = (f32[576,1152]{1,0:T(8,128)}, f32[288,1152]{1,0:T(8,128)}, f32[288,104]{1,0:T(8,128)}, f32[72,288]{1,0:T(8,128)}, f32[16,288]{1,0:T(8,128)}, /*index...) custom-call(bf16[944,1152]{1,0:T(8,128)(2,1)} %all-reduce.2.cloned.1.call-done.totals_ref), custom_call_target="tpu_custom_call" | custom-call | tf_op jit(solution)/shard_map/finish/pallas_call | solution.py:2154
  364.6 1.3 fusion
  365.9 1.4 slice_reduce_fusion
  367.3 0.0 copy-done.1
  367.4 0.8 copy.39
  368.2 0.0 copy-done
  368.2 1.0 copy.40
Async XLA Ops:
  7.2 353.5 %all-reduce.2.cloned.1.call-start = ((), (), s32[]{:S(2)}) async-start(), calls=%async_computation | async-start | bytes 4349952 | tf_op jit(solution)/shard_map/psum | solution.py:2222
  360.6 6.7 %copy-start.1 = (bf16[256,1152]{1,0:T(8,128)(2,1)S(1)}, bf16[256,1152]{1,0:T(8,128)(2,1)}, u32[]{:S(2)}) copy-start(bf16[256,1152]{1,0:T(8,128)(2,1)} %get-tuple-element.79) | copy-start | bytes 1769476
  360.6 7.6 %copy-start = (f32[256,1152]{1,0:T(8,128)S(1)}, f32[256,1152]{1,0:T(8,128)}, u32[]{:S(2)}) copy-start(f32[256,1152]{1,0:T(8,128)} %get-tuple-element.105) | copy-start | bytes 3538948
Sparse Core Ops, SparseCore 0:
  260.5 90.9 all-reduce.1

commit v5 on v4

--- a/solution.py
+++ b/solution.py
@@ -1262,8 +1262,8 @@
 
 
 def forward_kernel(
-    tokens_ref, in_ref, scan_ref, step_w_ref, decay_ref, conv_ref, vectors_ref, norms_ref,
-    router_ref, outw_ref,
+    tokens_ref, in_ref, scan_ref, step_w_ref, decay_ref, conv_ref, bias_ref, dbias_ref, skip_ref,
+    norm_ref, norm_two_ref, router_ref, outw_ref,
     normed_ref, xin_ref, u_out, gate_out, proj_ref, step_ref, mixed_ref, gated_ref, mid_ref,
     step_full, vec_ref, router_full, gains_ref, scan_full, in_full, outw_all, normed_all, hist_hbm,
     columns, widths, columns_all, widths_all, scan_here, in_here, u_all, gate_all, b_cols, c_high, c_low, du,
@@ -1301,13 +1301,15 @@
         columns[...] = jnp.concatenate(
             [
                 step_w_ref[...].astype(F32), decay_ref[...].astype(F32), conv_ref[...].astype(F32),
-                vectors_ref[...].astype(F32), jnp.zeros((spare, part), F32),
+                *(ref[...].astype(F32)[None] for ref in (bias_ref, dbias_ref, skip_ref)),
+                jnp.zeros((spare, part), F32),
             ],
             0,
         ).astype(BF16)
         widths[...] = jnp.concatenate(
             [
-                router_ref[...].astype(F32), norms_ref[...].astype(F32),
+                router_ref[...].astype(F32),
+                *(ref[...].astype(F32)[None] for ref in (norm_ref, norm_two_ref)),
                 jnp.zeros((widths.shape[0] - experts - 2, slice_w), F32),
             ],
             0,
@@ -1461,7 +1463,7 @@
 
 
 def forward_plane(
-    tokens, in_t, scan_w, step_w, decay_t, conv, vectors, norms, router_t, out_w
+    tokens, in_t, scan_w, step_w, decay_t, conv, bias, dbias, skip, norm, norm_two, router_t, out_w
 ):
     rows, width = tokens.shape
     rank, part = step_w.shape
@@ -1483,7 +1485,9 @@
     def halves(index):
         return pl.BlockSpec((rows, tile), lambda i: (0, index(i)))
 
-    inputs = (tokens, in_t, scan_w, step_w, decay_t, conv, vectors, norms, router_t)
+    inputs = (
+        tokens, in_t, scan_w, step_w, decay_t, conv, bias, dbias, skip, norm, norm_two, router_t
+    )
     fixed = [
         ((rank, channels), BF16), ((state + 8, channels), F32), ((experts, width), BF16),
         ((8, width), F32), ((devices, part, cols), BF16),
@@ -2008,49 +2012,75 @@
     return values[0] if len(values) == 1 else jnp.concatenate(values, 0)
 
 
-def next_grads_kernel(
-    last, up_ref, down_ref, gup_in, gdown_in, rows_ref, grads_ref, sends_in, *refs
+def two_grads_kernel(
+    up_ref, down_ref, gup_in, gdown_in, rows_1, grads_1, sends_2, left_2, left_3, right_2, right_3,
+    goal_l2, goal_l3, goal_r2, goal_r3,
+    gup_ref, gdown_ref, rows_3, grads_3,
+    rows_t, gup_all, gdown_all, rows_2, grads_2, raw, goal, sends_3,
+    x_send, x_recv, local_sems, load_sems,
 ):
-    if not last:
-        raws, goals, refs = refs[:4], refs[4:8], refs[8:]
-    gup_ref, gdown_ref, rows_out, grads_out, refs = *refs[:4], refs[4:]
-    if not last:
-        sends_out, refs = refs[0], refs[1:]
-    rows_t, x_send, x_recv, local_sems, refs = *refs[:4], refs[4:]
     step = pl.program_id(0)
-    rows, grads = flat_rows((rows_ref,)), flat_rows((grads_ref,))
-    ways = [
-        Exchange(sends_in.at[k], out, x_send.at[k], x_recv.at[k], local_sems.at[k])
-        for k, out in enumerate((rows_out, grads_out))
-    ]
+    tiles = gup_all.shape[0]
+    spot = step % tiles
+    seconds, thirds = (
+        [
+            Exchange(
+                source.at[k], out, x_send.at[first + k], x_recv.at[first + k],
+                local_sems.at[first + k],
+            )
+            for k, out in enumerate(targets)
+        ]
+        for first, source, targets in (
+            (0, sends_2, (rows_2, grads_2)), (2, sends_3, (rows_3, grads_3))
+        )
+    )
 
     @pl.when(step == 0)
     def _():
         greet(line=False)
-        for way in ways:
+        for way in seconds:
             way.start()
-        rows_t[...] = rows.T
-
-    grad_up, grad_down = add_groups(rows, grads, rows_t[...], up_ref, down_ref)
-    gup_ref[...] = (gup_in[...].astype(F32) + grad_up).astype(BF16)
-    gdown_ref[...] = (gdown_in[...].astype(F32) + grad_down).astype(BF16)
-    if not last:
-        raw, goal, sends, load_sems = refs
-        left_2, left_3, right_2, right_3 = zip(raws, goals)
-        store = pltpu.make_async_copy(sends, sends_out, load_sems.at[2])
-
-        @pl.when(step == 1)
-        def _():
-            pick((right_3, right_2, left_2, left_3), raw, goal, load_sems)
-            prepare_sends(raw, goal, sends)
-            store.start()
-
-    @pl.when(step == pl.num_programs(0) - 1)
-    def _():
-        for way in ways:
+        rows_t[...] = flat_rows((rows_1,)).T
+
+    @pl.when(step == 1)
+    def _():
+        pick(
+            ((right_3, goal_r3), (right_2, goal_r2), (left_2, goal_l2), (left_3, goal_l3)), raw,
+            goal, load_sems,
+        )
+        prepare_sends(raw, goal, sends_3)
+
+    @pl.when(step == tiles - 2)
+    def _():
+        for way in thirds:
+            way.start()
+
+    @pl.when(step < tiles)
+    def _():
+        grad_up, grad_down = add_groups(
+            flat_rows((rows_1,)), flat_rows((grads_1,)), rows_t[...], up_ref, down_ref
+        )
+        gup_all[spot] = (gup_in[...].astype(F32) + grad_up).astype(BF16)
+        gdown_all[spot] = (gdown_in[...].astype(F32) + grad_down).astype(BF16)
+
+    @pl.when(step == tiles)
+    def _():
+        for way in seconds:
             way.wait()
-        if not last:
-            store.wait()
+        rows_t[...] = flat_rows((rows_2,)).T
+
+    @pl.when(step >= tiles)
+    def _():
+        grad_up, grad_down = add_groups(
+            flat_rows((rows_2,)), flat_rows((grads_2,)), rows_t[...], up_ref, down_ref
+        )
+        gup_ref[...] = (gup_all[spot].astype(F32) + grad_up).astype(BF16)
+        gdown_ref[...] = (gdown_all[spot].astype(F32) + grad_down).astype(BF16)
+
+    @pl.when(step == 2 * tiles - 1)
+    def _():
+        for way in thirds:
+            way.wait()
 
 
 def last_grads_kernel(
@@ -2086,25 +2116,39 @@
         ]
 
     turned = pltpu.VMEM((width, devices * cap), BF16)
-    sems = [DMA((2, devices)), DMA((2, devices)), DMA((2,))]
-    for last in (False, True):
-        extra = () if last else (*raws, *goals)
-        grad_up, grad_down, rows, grads, *more = pl.pallas_call(
-            partial(next_grads_kernel, last),
-            grid=(hidden // tile,),
-            in_specs=tiles(tile) * 2 + [whole] * 2 + [FAR] * (1 + len(extra)),
-            out_specs=tiles(tile) + [FAR] * (2 if last else 3),
-            out_shape=shapes(BF16) + [slots] * 2 + ([] if last else [pair]),
-            scratch_shapes=[turned] + sems + (
-                [] if last else [
-                    pltpu.VMEM(raws[0].shape, BF16), pltpu.VMEM(goals[0].shape, jnp.int32),
-                    pltpu.VMEM(pair.shape, BF16), DMA((3,)),
-                ]
-            ),
-            compiler_params=remote_params(7 if last else 6),
-            name="expert_grads_2" if last else "expert_grads_1",
-        )(up, down, grad_up, grad_down, rows, grads, sends, *extra)
-        sends = more[0] if more else None
+    count = hidden // tile
+    again = [
+        pl.BlockSpec((width, tile), lambda i: (0, i % count)),
+        pl.BlockSpec((tile, width), lambda i: (i % count, 0)),
+    ]
+    early = [
+        pl.BlockSpec((width, tile), lambda i: (0, jnp.minimum(i, count - 1))),
+        pl.BlockSpec((tile, width), lambda i: (jnp.minimum(i, count - 1), 0)),
+    ]
+    late = [
+        pl.BlockSpec((width, tile), lambda i: (0, jnp.maximum(i - count, 0))),
+        pl.BlockSpec((tile, width), lambda i: (jnp.maximum(i - count, 0), 0)),
+    ]
+    grad_up, grad_down, rows, grads = pl.pallas_call(
+        two_grads_kernel,
+        grid=(2 * count,),
+        in_specs=again + early + [whole] * 2 + [FAR] * 9,
+        out_specs=late + [FAR] * 2,
+        out_shape=shapes(BF16) + [slots] * 2,
+        scratch_shapes=[
+            turned,
+            pltpu.VMEM((count, width, tile), BF16),
+            pltpu.VMEM((count, tile, width), BF16),
+            pltpu.VMEM(slots.shape, BF16),
+            pltpu.VMEM(slots.shape, BF16),
+            pltpu.VMEM(raws[0].shape, BF16),
+            pltpu.VMEM(goals[0].shape, jnp.int32),
+            pltpu.VMEM(pair.shape, BF16),
+            DMA((4, devices)), DMA((4, devices)), DMA((4,)), DMA((2,)),
+        ],
+        compiler_params=remote_params(6),
+        name="expert_grads_12",
+    )(up, down, grad_up, grad_down, rows, grads, sends, *raws, *goals)
     return pl.pallas_call(
         last_grads_kernel,
         grid=(hidden // 768,),
@@ -2118,8 +2162,8 @@
 
 
 def finish_kernel(
-    totals_ref, in_ref, out_ref, scanw_ref, stepw_ref, decay_ref, conv_ref, vectors_ref, norms_ref,
-    router_ref,
+    totals_ref, in_ref, out_ref, scanw_ref, stepw_ref, decay_ref, conv_ref, router_ref, bias_ref,
+    dbias_ref, skip_ref, norm_two_ref, norm_ref,
 ):
     in_rows, part = in_ref.shape[0], out_ref.shape[0]
     cols, rank, state, taps = (
@@ -2141,12 +2185,13 @@
     decay_ref[...] = scan[rank : rank + state]
     scanw_ref[...] = back[:cols].T
     conv_ref[...] = back[cols : cols + taps]
-    vectors_ref[...] = jnp.concatenate(
-        [back[cols + taps : cols + taps + 1], scan[rank + state : rank + state + 2]], 0
-    )
+    bias_ref[...] = back[cols + taps]
+    dbias_ref[...] = scan[rank + state]
+    skip_ref[...] = scan[rank + state + 1]
     tail = totals_ref[at : at + 16, :].astype(F32)[:, :slice_w]
     router_ref[...] = tail[:experts]
-    norms_ref[...] = tail[experts : experts + 2]
+    norm_two_ref[...] = tail[experts]
+    norm_ref[...] = tail[experts + 1]
 
 
 def finish(totals, in_rows, part, cols, rank, state, taps, experts, slice_w):
@@ -2154,12 +2199,13 @@
     return pl.pallas_call(
         finish_kernel,
         in_specs=[here],
-        out_specs=[here] * 9,
+        out_specs=[here] * 12,
         out_shape=[
             jax.ShapeDtypeStruct(shape, F32)
             for shape in (
                 (in_rows, totals.shape[1]), (part, totals.shape[1]), (part, cols), (rank, part),
-                (state, part), (taps, part), (3, part), (2, slice_w), (experts, slice_w),
+                (state, part), (taps, part), (experts, slice_w), (part,), (part,), (part,),
+                (slice_w,), (slice_w,),
             )
         ],
         compiler_params=pltpu.CompilerParams(vmem_limit_bytes=VMEM_LIMIT),
@@ -2192,8 +2238,6 @@
     tile = channels // 2
 
     on_plane = devices == 8 and split == 1 and lax.axis_size("dp") == 4
-    vectors = jnp.stack([conv_bias, step_bias, skip_gain])
-    norms = jnp.stack([mixer_norm, moe_norm])
     in_t, decay_t, router_t = in_weight.T, decay_log.T, router_weight.T
     up, down = up_weight[0], down_weight[0]
     hidden = up.shape[1]
@@ -2202,8 +2246,8 @@
             normed_low, x_inner, u_act, gate_in, proj, step_size, mixed, gated, mid, step_full, vec,
             router_t, gains, scan_full, in_t, out_full, normed_all, hist,
         ) = forward_plane(
-            tokens[0], in_t, scan_weight, step_weight, decay_t, conv_weight, vectors, norms,
-            router_t, out_weight,
+            tokens[0], in_t, scan_weight, step_weight, decay_t, conv_weight, conv_bias, step_bias,
+            skip_gain, mixer_norm, moe_norm, router_t, out_weight,
         )
         in_t = in_t.reshape(2 * channels, width)
         scan_full = scan_full.reshape(channels, cols)
@@ -2227,8 +2271,10 @@
         in_total, out_total, scan_w_total, step_w_total, decay_total, conv_total, *rest = finish(
             totals, 2 * part, part, cols, rank, state, taps, experts, slice_w
         )
-        vector_totals, norm_totals, router_total = rest
+        router_total, vector_totals, norm_totals = rest[0], rest[1:4], rest[4:]
     else:
+        vectors = jnp.stack([conv_bias, step_bias, skip_gain])
+        norms = jnp.stack([mixer_norm, moe_norm])
         spare = jnp.zeros((8 - taps - 3, part), BF16)
         columns = jnp.concatenate([step_weight, decay_t, conv_weight, vectors, spare], 0)
         across = jnp.concatenate([router_t, norms, jnp.zeros((6, slice_w), BF16)], 0)

time: 384 us -> 369 us (0.961)
  the two profiles are of different devices: /device:TPU:9 before, /device:TPU:0 now
where the time goes in v5:
time: 369 us; the launch traced here: 363 us
  Pallas kernels  341 us (92%)
  between operations  14.9 us (4%)
  waiting for transfers between devices  4.7 us (1%)
    pallas_call x1, Pallas kernels, backward_plane(): pl.pallas_call(backward_kernel, grid=(14,), in_specs=[pl.BlockSpec((rows,...  95.7 us
    pallas_call x1, Pallas kernels, forward_plane(): pl.pallas_call(forward_kernel, grid=(4,), in_specs=[whole(value.shape) fo...  91.4 us
    pallas_call x1, Pallas kernels, expert_grads_plane(): pl.pallas_call(two_grads_kernel, grid=(2 * count,), in_specs=again + earl...  62 us
    pallas_call x1, Pallas kernels, expert_layer(): pl.pallas_call(expert_layer_kernel, in_specs=[pl.BlockSpec(memory_space=p...  61.9 us
    pallas_call x1, Pallas kernels, expert_grads_plane(): pl.pallas_call(last_grads_kernel, grid=(hidden // 768,), in_specs=tiles(7...  26.5 us
  transfers between devices with their start and end apart: 1, of which 1 were waited for; matrix products, arithmetic and copies ran while one was open for 0% of the time, Pallas kernels for 24%

profile of v5, /device:TPU:0, one launch (start us, length us, event | category | flops | bytes accessed | tf_op | source)
XLA Modules:
  0.0 362.9 jit_solution(3715238253290281856)
XLA Ops:
  7.2 0.0 all-reduce.2.cloned.1.call-start
  7.9 91.4 %mixer_forward.1 = (bf16[256,1152]{1,0:T(8,128)(2,1)}, f32[256,2304]{1,0:T(8,128)}, f32[256,2304]{1,0:T(8,128)}, f32[256,2304]{1,0:T(8,128)}, f32[256,104]{1,0:T...) custom-call(bf16[256,1152]{1,0:T(8,128)(2,1)} %bitcast.28, ...), custom_call_target="tpu_custom_call" | custom-call | tf_op jit(solution)/shard_map/mixer_forward/pallas_call | solution.py:1495
  99.3 61.9 %expert_layer.1 = (bf16[256,1152]{1,0:T(8,128)(2,1)}, f32[256,1152]{1,0:T(8,128)}, bf16[256,1152]{1,0:T(8,128)(2,1)}, f32[9,1152]{1,0:T(8,128)}, bf16[8,64,1152]...) custom-call(s32[1]{0:T(128)S(6)} %copy.38.length_ref, ...), custom_call_target="tpu_custom_call" | custom-call | tf_op jit(solution)/shard_map/expert_layer/pallas_call | solution.py:1071
  161.2 95.7 %mixer_backward.1 = (f32[256,1152]{1,0:T(8,128)}, bf16[944,1152]{1,0:T(8,128)(2,1)}, bf16[8,64,1152]{2,1,0:T(8,128)(2,1)}, bf16[8,64,1152]{2,1,0:T(8,128)(2,1)},...) custom-call(f32[256,104]{1,0:T(8,128)} %get-tuple-element.78.proj_re, ...), custom_call_target="tpu_custom_call" | custom-call | tf_op jit(solution)/shard_map/mixer_backward/pallas_call | solution.py:1932
  256.9 0.0 all-reduce.2.cloned.1.call-update
  257.0 62.0 %expert_grads_12.1 = (bf16[1152,3072]{1,0:T(8,128)(2,1)}, bf16[3072,1152]{1,0:T(8,128)(2,1)}, bf16[8,64,1152]{2,1,0:T(8,128)(2,1)}, bf16[8,64,1152]{2,1,0:T(8,128)(2,1)}) custom-call(bf16[1152,3072]{1,0:T(8,128)(2,1)} %bitcast.19, bf16[3072,1152]{1,0:T(8,128)(2,1)} %bitcast.22, bf16[1152,3072]{1,0:T(8,128)(2,1)} %get-tuple-element.117.gup_in, ...), custom_call_target="tpu_custom_call" | custom-call | tf_op jit(solution)/shard_map/expert_grads_12/pallas_call | solution.py:2132
  318.9 26.5 %expert_grads_3.1 = (f32[1152,3072]{1,0:T(8,128)}, f32[3072,1152]{1,0:T(8,128)}) custom-call(bf16[1152,3072]{1,0:T(8,128)(2,1)} %bitcast.20, bf16[3072,1152]{1,0:T(8,128)(2,1)} %bitcast.23, bf16[1152,3072]{1,0:T(8,128)(2,1)} %get-tuple-element.126.gup_in, bf16[3072,1152]{1,0:T(8,128)(2,1)} %get-tuple-element.127.gdown_in, ...), custom_call_target="tpu_custom_call" | custom-call | tf_op jit(solution)/shard_map/expert_grads_3/pallas_call | solution.py:2152
  345.5 0.0 copy-start.1
  345.5 0.0 copy-start
  345.5 4.7 %all-reduce.2.cloned.1.call-done.totals_ref = bf16[944,1152]{1,0:T(8,128)(2,1)} async-done(((bf16[944,1152]{1,0:T(8,128)(2,1)}), bf16[944,1152]{1,0:T(8,128)(2,1)}) %all-reduce.2.cloned.1.call-update) | async-done | bytes 2174992 | tf_op jit(solution)/shard_map/psum | solution.py:2266
  350.1 3.8 %finish.1 = (f32[576,1152]{1,0:T(8,128)}, f32[288,1152]{1,0:T(8,128)}, f32[288,104]{1,0:T(8,128)}, f32[72,288]{1,0:T(8,128)}, f32[16,288]{1,0:T(8,128)}, /*index...) custom-call(bf16[944,1152]{1,0:T(8,128)(2,1)} %all-reduce.2.cloned.1, ...), custom_call_target="tpu_custom_call" | custom-call | tf_op jit(solution)/shard_map/finish/pallas_call | solution.py:2199
  354.0 0.0 copy-done.1
  354.0 0.8 copy.39
  354.8 0.0 copy-done
  354.8 1.0 copy.40
Async XLA Ops:
  7.2 343.0 %all-reduce.2.cloned.1.call-start = ((), (), s32[]{:S(2)}) async-start(), calls=%async_computation | async-start | bytes 4349952 | tf_op jit(solution)/shard_map/psum | solution.py:2266
  345.5 8.5 %copy-start.1 = (bf16[256,1152]{1,0:T(8,128)(2,1)S(1)}, bf16[256,1152]{1,0:T(8,128)(2,1)}, u32[]{:S(2)}) copy-start(bf16[256,1152]{1,0:T(8,128)(2,1)} %get-tuple-element.77) | copy-start | bytes 1769476
  345.5 9.4 %copy-start = (f32[256,1152]{1,0:T(8,128)S(1)}, f32[256,1152]{1,0:T(8,128)}, u32[]{:S(2)}) copy-start(f32[256,1152]{1,0:T(8,128)} %get-tuple-element.103) | copy-start | bytes 3538948
Sparse Core Ops, SparseCore 0:
  257.1 93.0 all-reduce.1

commit v6 on v5

--- a/solution.py
+++ b/solution.py
@@ -813,7 +813,7 @@
     return me + (1 - 2 * ((me // bit) % 2)) * bit
 
 
-def greet(line=True):
+def greet_send(line=True):
     devices, copies = lax.axis_size("expert"), lax.axis_size("dp")
     me, place = lax.axis_index("expert"), lax.axis_index("dp")
     barrier = pltpu.get_barrier_semaphore()
@@ -831,12 +831,22 @@
         def _():
             pl.semaphore_signal(barrier, inc=1, device_id={"dp": place - 1}, device_id_type=MESH)
 
+
+def greet_wait(line=True):
+    devices, copies = lax.axis_size("expert"), lax.axis_size("dp")
+    place = lax.axis_index("dp")
+    barrier = pltpu.get_barrier_semaphore()
     ends = (place == 0) | (place == copies - 1)
     if line:
         pl.when(ends)(lambda: pl.semaphore_wait(barrier, devices))
         pl.when(jnp.logical_not(ends))(lambda: pl.semaphore_wait(barrier, devices + 1))
     else:
         pl.semaphore_wait(barrier, devices - 1)
+
+
+def greet(line=True):
+    greet_send(line)
+    greet_wait(line)
 
 
 class Exchange:
@@ -915,9 +925,9 @@
     hidden = up_ref.shape[1]
     load_up = pltpu.make_async_copy(up_hbm, up_ref, weight_sems.at[0])
     load_down = pltpu.make_async_copy(down_hbm, down_ref, weight_sems.at[1])
+    greet_send()
     load_up.start()
     load_down.start()
-    greet()
 
     ways = [
         Exchange(source, target, send_sems.at[k], recv_sems.at[k], local_sems.at[k])
@@ -949,6 +959,7 @@
     goal[...] = jnp.broadcast_to(target, goal.shape)
     dispatch = dispatch_matrix(goal, experts)
     send_r[...] = product(dispatch, normed).astype(BF16).reshape(experts, CAP, width)
+    greet_wait()
     ways[0].start()
     for k in (0, 2):
         lines[k].start()
@@ -1148,6 +1159,21 @@
                 copy.wait_send()
 
 
+def greet_all():
+    devices, copies = lax.axis_size("expert"), lax.axis_size("dp")
+    me, place = lax.axis_index("expert"), lax.axis_index("dp")
+    barrier = pltpu.get_barrier_semaphore()
+    for k in range(1, devices):
+        pl.semaphore_signal(
+            barrier, inc=1, device_id={"expert": (me + k) % devices}, device_id_type=MESH
+        )
+    for k in range(1, copies):
+        pl.semaphore_signal(
+            barrier, inc=1, device_id={"dp": (place + k) % copies}, device_id_type=MESH
+        )
+    pl.semaphore_wait(barrier, devices + copies - 2)
+
+
 class WideGather:
     def __init__(self, source, target, send_sems, recv_sems, local_sem):
         me, place = lax.axis_index("expert"), lax.axis_index("dp")
@@ -1323,6 +1349,7 @@
             for one in small:
                 one.step(number)
         big_gather.step(3)
+        gather.step(0)
         table = jnp.concatenate([columns_all[k].astype(F32) for k in range(devices)], 1)
         step_full[...] = table[:rank].astype(BF16)
         scan_full[...] = scan_here[...]
@@ -1337,9 +1364,9 @@
         normed_ref[...] = (values * scale * gains_ref[0:1, :]).astype(BF16)
         proj_ref[...] = jnp.zeros_like(proj_ref)
         big_gather.step(4)
-        gather.step(0)
         big_gather.step(5)
         keep_in.start()
+        gather.step(1)
 
     @pl.when(step < 2)
     def _():
@@ -1369,7 +1396,6 @@
 
     @pl.when(step == 1)
     def _():
-        gather.step(1)
         gather.step(2)
         normed_gather.step(0)
         columns_of(proj_ref, rank, state, b_cols)
@@ -1572,7 +1598,10 @@
 
 
 def fold_rows(got_ref, width):
-    total = jnp.sum(got_ref[...].astype(F32), 0)
+    return fold_value(jnp.sum(got_ref[...].astype(F32), 0), width)
+
+
+def fold_value(total, width):
     quarter = total.shape[0] // 4
     folded = jnp.concatenate([total[k * quarter : (k + 1) * quarter] for k in range(4)], 1)
     return jnp.concatenate([folded, jnp.zeros((32 - quarter, width), F32)], 0).astype(BF16)
@@ -1582,12 +1611,12 @@
     proj_ref, stepw_ref, decay_ref, misc_ref, u_ref, gate_ref, outw_ref, gradmix_ref, step_ref,
     mixed_ref, scanw_ref, xin_ref, misc_x_ref, wx_ref, wg_ref, u_x_ref, tokens_ref, gains_ref,
     widths_ref,
-    gradmid_hbm, gated_hbm, normed_hbm, hist_hbm, rows_0, grads_0, left_2, right_2, right_1,
-    goal_l2, goal_r2, goal_r1,
-    gradtok_hbm, totals_hbm, rows_1, grads_1, left_3, right_3, goal_l3, goal_r3, sends_hbm,
+    gradmid_hbm, gated_hbm, normed_hbm, hist_hbm, rows_0, grads_0, left_1, right_1, left_2, right_2, goal_l1,
+    goal_r1, goal_l2, goal_r2,
+    gradtok_hbm, totals_hbm, back_hbm, tail_hbm, rows_1, grads_1, left_3, right_3, goal_l3, goal_r3, sends_hbm,
     c_cols, b_high, b_low, b_sums, c_sums, gy, du, grad_du, grad_step, ring, g_ring, w_ring,
     gradproj, gradu_all, gate_all, send_in, got_in, everyone, gated_all, send_scan, got_scan,
-    pack_back, send_back, got_back, send_tail, got_tail, totals, raw, goal,
+    pack_back, send_back, send_tail, totals, raw, goal, send_grads,
     g_send, g_recv, x_send, x_recv, l_send, l_recv, local_sems, ring_sems, load_sems,
 ):
     step = pl.program_id(0)
@@ -1603,42 +1632,44 @@
     channels = half * in_part
     steps_x = channels // small_tile
     mix = PlaneGather(gradmix_ref, everyone, g_send, g_recv, local_sems.at[0])
-    ways = [
-        Exchange(source, target, x_send.at[k], x_recv.at[k], local_sems.at[k + 1])
-        for k, (source, target) in enumerate(
-            [
-                (gated_hbm, gated_all), (send_scan, got_scan), (send_back, got_back),
-                (send_tail, got_tail),
-            ]
-        )
-    ]
+    gated = Exchange(gated_hbm, gated_all, x_send.at[0], x_recv.at[0], local_sems.at[1])
+    scan = Exchange(send_scan, got_scan, x_send.at[1], x_recv.at[1], local_sems.at[2])
+    near_grads = Exchange(send_grads, grads_1, x_send.at[2], x_recv.at[2], local_sems.at[3])
 
     def input_part(device):
         return send_in.at[pl.ds(pl.multiple_of(device * in_part, in_part), in_part)]
 
     input_copies = [
         pltpu.make_async_remote_copy(
-            input_part((me + k) % devices), got_in.at[me], x_send.at[4, k], x_recv.at[4, k],
+            input_part((me + k) % devices), got_in.at[me], x_send.at[3, k], x_recv.at[3, k],
             device_id={"expert": (me + k) % devices}, device_id_type=MESH,
         )
         for k in range(1, devices)
     ]
-    input_local = pltpu.make_async_copy(input_part(me), got_in.at[me], local_sems.at[5])
-
-    def start_inputs(first, last):
-        for k, copy in enumerate(input_copies):
+    input_local = pltpu.make_async_copy(input_part(me), got_in.at[me], local_sems.at[4])
+
+    def start_some(copies, local, first, last):
+        for k, copy in enumerate(copies):
             peer = (me + k + 1) % devices
             pl.when((peer >= first) & (peer < last))(lambda copy=copy: copy.start())
-        pl.when((me >= first) & (me < last))(lambda: input_local.start())
+        pl.when((me >= first) & (me < last))(lambda: local.start())
+
+    def start_inputs(first, last):
+        start_some(input_copies, input_local, first, last)
 
     lines = [
         Line(3, left_2, right_2, left_3, right_3, l_send.at[0], l_recv.at[0]),
         Line(3, goal_l2, goal_r2, goal_l3, goal_r3, l_send.at[1], l_recv.at[1]),
         Near(rows_0, rows_1, l_send.at[2], l_recv.at[2]),
-        Near(grads_0, grads_1, l_send.at[3], l_recv.at[3]),
+        *(
+            Near(grads_0.at[k], grads_1.at[k], l_send.at[3 + k // 2], l_recv.at[3 + k // 2])
+            for k in range(1, devices, 2)
+        ),
     ]
     load_normed = pltpu.make_async_copy(normed_hbm, everyone, load_sems.at[0])
     load_mid = pltpu.make_async_copy(gradmid_hbm, gy, load_sems.at[1])
+    store_back = pltpu.make_async_copy(send_back, back_hbm, load_sems.at[8])
+    store_tail = pltpu.make_async_copy(send_tail, tail_hbm, load_sems.at[9])
     store_sends = [
         pltpu.make_async_copy(source, sends_hbm.at[k], load_sems.at[6 + k])
         for k, source in enumerate((g_ring, w_ring))
@@ -1667,6 +1698,10 @@
         mix.step(0)
         for line in lines:
             line.start()
+        near_l, near_r = (left_1, goal_l1), (right_1, goal_r1)
+        pick((near_r, near_l, near_l, near_l), raw, goal, load_sems.at[pl.ds(4, 2)])
+        matrix = dispatch_matrix(goal, devices)
+        send_grads[...] = product(matrix, raw[1]).astype(BF16).reshape(send_grads.shape)
         gradproj[...] = jnp.zeros_like(gradproj)
         b_sums[...] = jnp.zeros_like(b_sums)
         c_sums[...] = jnp.zeros_like(c_sums)
@@ -1674,15 +1709,17 @@
         diagonals_of(proj_ref, rank, state, b_high, b_low)
 
     def between(position):
+        if position == 1:
+            pl.when(me % 2 == 0)(lambda: near_grads.start())
         if position == 2:
             mix.step(1)
             mix.step(2)
-            ways[0].start()
+            gated.start()
         if position == 5:
             mix.step(3)
         if position == 7:
             mix.step(4)
-            ways[0].wait()
+            gated.wait()
 
     @pl.when(step < 2)
     def _():
@@ -1775,13 +1812,13 @@
             @pl.when(step == turn)
             def _():
                 split_lanes(send_scan.at[pl.ds(turn * half, half)], packed)
+                start_some(scan.copies, scan.local, turn * half, (turn + 1) * half)
                 start_inputs(half + turn * half // 2, half + (turn + 1) * half // 2)
 
         gradproj[:, :rank] += times_transpose(grad_low, stepw_ref[...])
 
     @pl.when(step == 1)
     def _():
-        ways[1].start()
         own = iota((rows, big), 0) % BLOCK == iota((rows, big), 1) // state
         lane = iota((big, cols), 1)
         slot = iota((big, cols), 0) % state
@@ -1799,7 +1836,7 @@
     @pl.when(step == steps_x + 2)
     def _():
         split_lanes(send_back, pack_back[...])
-        ways[2].start()
+        store_back.start()
         lhs = jnp.concatenate([gated_all[k] for k in range(devices)], 1)
         totals[2 * gated_all.shape[1] : 3 * gated_all.shape[1], :] = product(
             lhs, everyone[...].reshape(devices * rows, width)
@@ -1866,21 +1903,15 @@
             [widths, jnp.zeros((send_tail.shape[1] - widths.shape[0], width), F32)], 0
         )
         split_lanes(send_tail, widths.astype(BF16))
-        ways[3].start()
+        store_tail.start()
         inner = grad * gains_ref[0:1, :]
         load_mid.wait()
         gy[...] += scale * (inner - unit * jnp.mean(inner * unit, -1, keepdims=True))
         store_tokens = pltpu.make_async_copy(gy, gradtok_hbm, load_sems.at[2])
         store_tokens.start()
         at = 3 * gated_all.shape[1]
-        for way, got in ((ways[1], got_scan), (ways[2], got_back)):
-            way.wait()
-            totals[at : at + 32, :] = fold_rows(got, width)
-            at += 32
-        ways[3].wait()
-        tail = jnp.sum(got_tail[...].astype(F32), 0)
-        tail = jnp.concatenate([tail, jnp.zeros((tail.shape[0], width - tail.shape[1]), F32)], 1)
-        totals[at : at + 16, :] = tail.astype(BF16)
+        scan.wait()
+        totals[at : at + 32, :] = fold_rows(got_scan, width)
         load_normed.wait()
         input_local.wait()
         for copy in input_copies:
@@ -1893,6 +1924,13 @@
         store_totals.start()
         for line in lines:
             line.wait()
+        for k, copy in enumerate(near_grads.copies):
+            pl.when(me % 2 == 0)(lambda copy=copy: copy.wait_send())
+            source = (me + devices - k - 1) % devices
+            pl.when(source % 2 == 0)(lambda copy=copy: copy.wait_recv())
+        pl.when(me % 2 == 0)(lambda: near_grads.local.wait())
+        store_back.wait()
+        store_tail.wait()
         store_tokens.wait()
         store_totals.wait()
         for store in store_sends:
@@ -1901,7 +1939,8 @@
 
 def backward_plane(
     proj, step_w, vec, u_act, gate_in, out_w, grad_mix, step_size, mixed, scan_w, x_inner, in_t,
-    tokens, gains, grad_widths, grad_mid, gated, normed_all, hist, rows_0, grads_0, raws, goals,
+    tokens, gains, grad_widths, grad_mid, gated, normed_all, hist, rows_0, grads_0, raws,
+    goals,
 ):
     rows, channels = u_act.shape
     width = grad_mix.shape[1]
@@ -1919,16 +1958,12 @@
     slots = jax.ShapeDtypeStruct(rows_0.shape, BF16)
     raw = jax.ShapeDtypeStruct(raws[0].shape, BF16)
     goal = jax.ShapeDtypeStruct(goals[0].shape, jnp.int32)
-    total_rows = 3 * part + 80
+    total_rows = 3 * part + 32
     pair = jax.ShapeDtypeStruct((2, 2, big, tile), BF16)
     third = lambda i: jnp.maximum(i - 8, 0)
-    packs = [
-        pltpu.VMEM((devices, count, lanes), BF16)
-        for count, lanes in (
-            (rank + state + 8, part), (pack_rows, part), (tail_rows, width // devices)
-        )
-        for _ in range(2)
-    ]
+    scan_pack = (devices, rank + state + 8, part)
+    back_pack = (devices, pack_rows, part)
+    tail_pack = (devices, tail_rows, width // devices)
     return pl.pallas_call(
         backward_kernel,
         grid=(14,),
@@ -1952,11 +1987,13 @@
             pl.BlockSpec((rows, width), fixed, pipeline_mode=once),
             pl.BlockSpec(gains.shape, fixed),
             pl.BlockSpec(grad_widths.shape, fixed),
-        ] + [FAR] * 12,
-        out_specs=[FAR] * 9,
+        ] + [FAR] * 14,
+        out_specs=[FAR] * 11,
         out_shape=[
             jax.ShapeDtypeStruct((rows, width), F32),
             jax.ShapeDtypeStruct((total_rows, width), BF16),
+            jax.ShapeDtypeStruct(back_pack, BF16),
+            jax.ShapeDtypeStruct(tail_pack, BF16),
             slots, slots, raw, raw, goal, goal, pair,
         ],
         scratch_shapes=[
@@ -1979,15 +2016,17 @@
             pltpu.VMEM((devices, 2 * part, rows), BF16),
             pltpu.VMEM((devices, rows, width), BF16),
             pltpu.VMEM(gated.shape, BF16),
-            packs[0],
-            packs[1],
+            pltpu.VMEM(scan_pack, BF16),
+            pltpu.VMEM(scan_pack, BF16),
             pltpu.VMEM((pack_rows, channels), BF16),
-            *packs[2:],
+            pltpu.VMEM(back_pack, BF16),
+            pltpu.VMEM(tail_pack, BF16),
             pltpu.VMEM((total_rows, width), BF16),
             pltpu.VMEM(raw.shape, BF16),
             pltpu.VMEM(goal.shape, jnp.int32),
-            DMA((10,)), DMA((10,)), DMA((5, devices)), DMA((5, devices)), DMA((4, 2)), DMA((4, 2)),
-            DMA((6,)), DMA((4,)), DMA((8,)),
+            pltpu.VMEM(slots.shape, BF16),
+            DMA((10,)), DMA((10,)), DMA((4, devices)), DMA((4, devices)), DMA((7, 2)), DMA((7, 2)),
+            DMA((5,)), DMA((4,)), DMA((10,)),
         ],
         compiler_params=pltpu.CompilerParams(
             vmem_limit_bytes=VMEM_LIMIT, collective_id=4, has_side_effects=True
@@ -1996,7 +2035,7 @@
     )(
         proj, step_w, vec, vec, u_act, gate_in, out_w, grad_mix, step_size, mixed, scan_w, x_inner,
         vec, in_t, in_t, u_act, tokens, gains, grad_widths, grad_mid, gated, normed_all, hist,
-        rows_0, grads_0, raws[2], raws[3], raws[1], goals[2], goals[3], goals[1],
+        rows_0, grads_0, *raws, *goals,
     )
 
 
@@ -2014,10 +2053,11 @@
 
 def two_grads_kernel(
     up_ref, down_ref, gup_in, gdown_in, rows_1, grads_1, sends_2, left_2, left_3, right_2, right_3,
-    goal_l2, goal_l3, goal_r2, goal_r3,
-    gup_ref, gdown_ref, rows_3, grads_3,
-    rows_t, gup_all, gdown_all, rows_2, grads_2, raw, goal, sends_3,
-    x_send, x_recv, local_sems, load_sems,
+    goal_l2, goal_l3, goal_r2, goal_r3, back_hbm, tail_hbm,
+    gup_ref, gdown_ref, rows_3, grads_3, small_ref,
+    rows_t, gup_all, gdown_all, rows_2, grads_2, raw, goal, sends_3, own_back, pair_back, pair_sum,
+    far_back, got_tail, small_here, small_all, z_send, z_recv, b_send, b_recv, x_send, x_recv,
+    local_sems, load_sems, back_sems,
 ):
     step = pl.program_id(0)
     tiles = gup_all.shape[0]
@@ -2035,11 +2075,47 @@
         )
     )
 
+    small_tail = Exchange(
+        tail_hbm, got_tail, x_send.at[4], x_recv.at[4], local_sems.at[4]
+    )
+    me = lax.axis_index("expert")
+    core, chip = me % 2, me // 2
+    chips = pair_sum.shape[0]
+    to_core = [
+        pltpu.make_async_remote_copy(
+            back_hbm.at[2 * k + 1 - core], pair_back.at[k], b_send.at[k], b_recv.at[k],
+            device_id={"expert": neighbour(1)}, device_id_type=MESH,
+        )
+        for k in range(chips)
+    ]
+    own_loads = [
+        pltpu.make_async_copy(back_hbm.at[2 * k + core], own_back.at[k], back_sems.at[k])
+        for k in range(chips)
+    ]
+    to_chips = [
+        pltpu.make_async_remote_copy(
+            pair_sum.at[(chip + k) % chips], far_back.at[k - 1], b_send.at[chips + k - 1],
+            b_recv.at[chips + k - 1], device_id={"expert": 2 * ((chip + k) % chips) + core},
+            device_id_type=MESH,
+        )
+        for k in range(1, chips)
+    ]
+    place, copies = lax.axis_index("dp"), lax.axis_size("dp")
+    to_copies = [
+        pltpu.make_async_remote_copy(
+            small_here, small_all.at[k - 1], z_send.at[k - 1], z_recv.at[k - 1],
+            device_id={"dp": (place + k) % copies}, device_id_type=MESH,
+        )
+        for k in range(1, copies)
+    ]
+
     @pl.when(step == 0)
     def _():
-        greet(line=False)
+        greet_all()
         for way in seconds:
             way.start()
+        for copy in to_core + own_loads:
+            copy.start()
         rows_t[...] = flat_rows((rows_1,)).T
 
     @pl.when(step == 1)
@@ -2052,8 +2128,28 @@
 
     @pl.when(step == tiles - 2)
     def _():
+        for copy in to_core + own_loads:
+            copy.wait()
+        pair_sum[...] = (own_back[...].astype(F32) + pair_back[...].astype(F32)).astype(BF16)
+        for copy in to_chips:
+            copy.start()
+        small_tail.start()
         for way in thirds:
             way.start()
+
+    @pl.when(step == 2 * tiles - 3)
+    def _():
+        small_tail.wait()
+        for copy in to_chips:
+            copy.wait()
+        width = small_here.shape[1]
+        back = pair_sum[chip].astype(F32) + jnp.sum(far_back[...].astype(F32), 0)
+        small_here[0:32, :] = fold_value(back, width)
+        tail = jnp.sum(got_tail[...].astype(F32), 0)
+        tail = jnp.concatenate([tail, jnp.zeros((tail.shape[0], width - tail.shape[1]), F32)], 1)
+        small_here[32:48, :] = tail.astype(BF16)
+        for copy in to_copies:
+            copy.start()
 
     @pl.when(step < tiles)
     def _():
@@ -2079,6 +2175,9 @@
 
     @pl.when(step == 2 * tiles - 1)
     def _():
+        for copy in to_copies:
+            copy.wait()
+        small_ref[...] = small_here[...].astype(F32) + jnp.sum(small_all[...].astype(F32), 0)
         for way in thirds:
             way.wait()
 
@@ -2097,7 +2196,9 @@
     gdown_ref[...] = gdown_in[...].astype(F32) + grad_down
 
 
-def expert_grads_plane(up, down, grad_up, grad_down, rows, grads, sends, raws, goals, tile):
+def expert_grads_plane(
+    up, down, grad_up, grad_down, rows, grads, sends, raws, goals, back, tail, tile
+):
     width, hidden = up.shape
     devices, cap = grads.shape[:2]
     slots = jax.ShapeDtypeStruct(grads.shape, BF16)
@@ -2129,12 +2230,13 @@
         pl.BlockSpec((width, tile), lambda i: (0, jnp.maximum(i - count, 0))),
         pl.BlockSpec((tile, width), lambda i: (jnp.maximum(i - count, 0), 0)),
     ]
-    grad_up, grad_down, rows, grads = pl.pallas_call(
+    small = (48, width)
+    grad_up, grad_down, rows, grads, small_total = pl.pallas_call(
         two_grads_kernel,
         grid=(2 * count,),
-        in_specs=again + early + [whole] * 2 + [FAR] * 9,
-        out_specs=late + [FAR] * 2,
-        out_shape=shapes(BF16) + [slots] * 2,
+        in_specs=again + early + [whole] * 2 + [FAR] * 11,
+        out_specs=late + [FAR] * 2 + [pl.BlockSpec(small, lambda i: (0, 0))],
+        out_shape=shapes(BF16) + [slots] * 2 + [jax.ShapeDtypeStruct(small, F32)],
         scratch_shapes=[
             turned,
             pltpu.VMEM((count, width, tile), BF16),
@@ -2144,12 +2246,20 @@
             pltpu.VMEM(raws[0].shape, BF16),
             pltpu.VMEM(goals[0].shape, jnp.int32),
             pltpu.VMEM(pair.shape, BF16),
-            DMA((4, devices)), DMA((4, devices)), DMA((4,)), DMA((2,)),
+            pltpu.VMEM((devices // 2,) + back.shape[1:], BF16),
+            pltpu.VMEM((devices // 2,) + back.shape[1:], BF16),
+            pltpu.VMEM((devices // 2,) + back.shape[1:], BF16),
+            pltpu.VMEM((devices // 2 - 1,) + back.shape[1:], BF16),
+            pltpu.VMEM(tail.shape, BF16),
+            pltpu.VMEM(small, BF16),
+            pltpu.VMEM((3,) + small, BF16),
+            DMA((3,)), DMA((3,)), DMA((devices - 1,)), DMA((devices - 1,)), DMA((5, devices)),
+            DMA((5, devices)), DMA((5,)), DMA((2,)), DMA((devices // 2,)),
         ],
         compiler_params=remote_params(6),
         name="expert_grads_12",
-    )(up, down, grad_up, grad_down, rows, grads, sends, *raws, *goals)
-    return pl.pallas_call(
+    )(up, down, grad_up, grad_down, rows, grads, sends, *raws, *goals, back, tail)
+    grad_up, grad_down = pl.pallas_call(
         last_grads_kernel,
         grid=(hidden // 768,),
         in_specs=tiles(768) * 2 + [whole] * 2,
@@ -2159,10 +2269,11 @@
         compiler_params=pltpu.CompilerParams(vmem_limit_bytes=VMEM_LIMIT),
         name="expert_grads_3",
     )(up, down, grad_up, grad_down, rows, grads)
+    return grad_up, grad_down, small_total
 
 
 def finish_kernel(
-    totals_ref, in_ref, out_ref, scanw_ref, stepw_ref, decay_ref, conv_ref, router_ref, bias_ref,
+    totals_ref, small_ref, in_ref, out_ref, scanw_ref, stepw_ref, decay_ref, conv_ref, router_ref, bias_ref,
     dbias_ref, skip_ref, norm_two_ref, norm_ref,
 ):
     in_rows, part = in_ref.shape[0], out_ref.shape[0]
@@ -2174,12 +2285,15 @@
     out_ref[...] = totals_ref[in_rows : in_rows + part, :].astype(F32)
     at = in_rows + part
     unfolded = []
-    for quarter in ((rank + state + 8) // 4, (cols + 8) // 4):
-        block = totals_ref[at : at + 32, :].astype(F32)[:quarter]
+    for block, quarter in (
+        (totals_ref[at : at + 32, :].astype(F32), (rank + state + 8) // 4),
+        (small_ref[0:32, :], (cols + 8) // 4),
+    ):
         unfolded.append(
-            jnp.concatenate([block[:, k * part : (k + 1) * part] for k in range(4)], 0)
-        )
-        at += 32
+            jnp.concatenate(
+                [block[:quarter, k * part : (k + 1) * part] for k in range(4)], 0
+            )
+        )
     scan, back = unfolded
     stepw_ref[...] = scan[:rank]
     decay_ref[...] = scan[rank : rank + state]
@@ -2188,17 +2302,17 @@
     bias_ref[...] = back[cols + taps]
     dbias_ref[...] = scan[rank + state]
     skip_ref[...] = scan[rank + state + 1]
-    tail = totals_ref[at : at + 16, :].astype(F32)[:, :slice_w]
+    tail = small_ref[32:48, :][:, :slice_w]
     router_ref[...] = tail[:experts]
     norm_two_ref[...] = tail[experts]
     norm_ref[...] = tail[experts + 1]
 
 
-def finish(totals, in_rows, part, cols, rank, state, taps, experts, slice_w):
+def finish(totals, small, in_rows, part, cols, rank, state, taps, experts, slice_w):
     here = pl.BlockSpec(memory_space=pltpu.VMEM)
     return pl.pallas_call(
         finish_kernel,
-        in_specs=[here],
+        in_specs=[here] * 2,
         out_specs=[here] * 12,
         out_shape=[
             jax.ShapeDtypeStruct(shape, F32)
@@ -2210,7 +2324,7 @@
         ],
         compiler_params=pltpu.CompilerParams(vmem_limit_bytes=VMEM_LIMIT),
         name="finish",
-    )(totals)
+    )(totals, small)
 
 
 def gather(value):
@@ -2257,19 +2371,21 @@
         )
         raws, goals, grad_up, grad_down = line[:4], line[4:8], line[8], line[9]
         (
-            tokens_grad, totals, rows_1, grads_1, left_3, right_3, goal_l3, goal_r3, sends
+            tokens_grad, totals, back_parts, tail_parts, rows_1, grads_1, left_3, right_3, goal_l3,
+            goal_r3, sends,
         ) = backward_plane(
             proj, step_full, vec, u_act, gate_in, out_full, grad_mix, step_size, mixed, scan_full,
             x_inner, in_t, tokens[0], gains, grad_widths, grad_mid, gated, normed_all, hist, rows_0,
             grads_0, raws, goals,
         )
         totals = lax.psum(totals, "dp")
-        grad_up, grad_down = expert_grads_plane(
+        grad_up, grad_down, small_total = expert_grads_plane(
             up, down, grad_up, grad_down, rows_1, grads_1,
-            sends.reshape((2,) + rows_1.shape), (raws[2], left_3, raws[3], right_3), (goals[2], goal_l3, goals[3], goal_r3), 512,
+            sends.reshape((2,) + rows_1.shape), (raws[2], left_3, raws[3], right_3),
+            (goals[2], goal_l3, goals[3], goal_r3), back_parts, tail_parts, 512,
         )
         in_total, out_total, scan_w_total, step_w_total, decay_total, conv_total, *rest = finish(
-            totals, 2 * part, part, cols, rank, state, taps, experts, slice_w
+            totals, small_total, 2 * part, part, cols, rank, state, taps, experts, slice_w
         )
         router_total, vector_totals, norm_totals = rest[0], rest[1:4], rest[4:]
     else:

time: 369 us -> 374 us (1.014)
  the two profiles are of different devices: /device:TPU:0 before, /device:TPU:9 now
where the time goes in v6:
time: 374 us; the launch traced here: 367 us
  Pallas kernels  350 us (94%)
  between operations  15.2 us (4%)
    pallas_call x1, Pallas kernels, backward_plane(): pl.pallas_call(backward_kernel, grid=(14,), in_specs=[pl.BlockSpec((rows,...  97.1 us
    pallas_call x1, Pallas kernels, forward_plane(): pl.pallas_call(forward_kernel, grid=(4,), in_specs=[whole(value.shape) fo...  88.1 us
    pallas_call x1, Pallas kernels, expert_grads_plane(): pl.pallas_call(two_grads_kernel, grid=(2 * count,), in_specs=again + earl...  70.7 us
    pallas_call x1, Pallas kernels, expert_layer(): pl.pallas_call(expert_layer_kernel, in_specs=[pl.BlockSpec(memory_space=p...  63.4 us
    pallas_call x1, Pallas kernels, expert_grads_plane(): pl.pallas_call(last_grads_kernel, grid=(hidden // 768,), in_specs=tiles(7...  26.6 us
  transfers between devices with their start and end apart: 1, of which 0 were waited for; matrix products, arithmetic and copies ran while one was open for 0% of the time, Pallas kernels for 27%

profile of v6, /device:TPU:9, one launch (start us, length us, event | category | flops | bytes accessed | tf_op | source)
XLA Modules:
  0.0 366.9 jit_solution(9721700666006116057)
XLA Ops:
  7.2 0.0 all-reduce.2.cloned.1.call-start
  7.9 88.1 %mixer_forward.1 = (bf16[256,1152]{1,0:T(8,128)(2,1)}, f32[256,2304]{1,0:T(8,128)}, f32[256,2304]{1,0:T(8,128)}, f32[256,2304]{1,0:T(8,128)}, f32[256,104]{1,0:T...) custom-call(bf16[256,1152]{1,0:T(8,128)(2,1)} %bitcast.28, ...), custom_call_target="tpu_custom_call" | custom-call | tf_op jit(solution)/shard_map/mixer_forward/pallas_call | solution.py:1521
  95.9 63.4 %expert_layer.1 = (bf16[256,1152]{1,0:T(8,128)(2,1)}, f32[256,1152]{1,0:T(8,128)}, bf16[256,1152]{1,0:T(8,128)(2,1)}, f32[9,1152]{1,0:T(8,128)}, bf16[8,64,1152]...) custom-call(s32[1]{0:T(128)S(6)} %copy.38.length_ref, ...), custom_call_target="tpu_custom_call" | custom-call | tf_op jit(solution)/shard_map/expert_layer/pallas_call | solution.py:1082
  159.3 97.1 %mixer_backward.1 = (f32[256,1152]{1,0:T(8,128)}, bf16[896,1152]{1,0:T(8,128)(2,1)}, bf16[8,112,288]{2,1,0:T(8,128)(2,1)}, bf16[8,16,144]{2,1,0:T(8,128)(2,1)}, ...) custom-call(f32[256,104]{1,0:T(8,128)} %get-tuple-element.83.proj_re, ...), custom_call_target="tpu_custom_call" | custom-call | tf_op jit(solution)/shard_map/mixer_backward/pallas_call | solution.py:1967
  256.4 0.0 all-reduce.2.cloned.1.call-update
  256.5 70.7 %expert_grads_12.1 = (bf16[1152,3072]{1,0:T(8,128)(2,1)}, bf16[3072,1152]{1,0:T(8,128)(2,1)}, bf16[8,64,1152]{2,1,0:T(8,128)(2,1)}, bf16[8,64,1152]{2,1,0:T(8,128)(2,1)}, f32[48,1152]{1,0:T(8,128)}) custom-call(bf16[1152,3072]{1,0:T(8,128)(2,1)} %bitcast.19, bf16[3072,1152]{1,0:T(8,128)(2,1)} %bitcast.22, bf16[1152,3072]{1,0:T(8,128)(2,1)} %get-tuple-element.112.gup_in, ...), custom_call_target="tpu_custom_call" | custom-call | tf_op jit(solution)/shard_map/expert_grads_12/pallas_call | solution.py:2234
  327.2 26.6 %expert_grads_3.1 = (f32[1152,3072]{1,0:T(8,128)}, f32[3072,1152]{1,0:T(8,128)}) custom-call(bf16[1152,3072]{1,0:T(8,128)(2,1)} %bitcast.20, bf16[3072,1152]{1,0:T(8,128)(2,1)} %bitcast.23, bf16[1152,3072]{1,0:T(8,128)(2,1)} %get-tuple-element.136.gup_in, bf16[3072,1152]{1,0:T(8,128)(2,1)} %get-tuple-element.137.gdown_in, ...), custom_call_target="tpu_custom_call" | custom-call | tf_op jit(solution)/shard_map/expert_grads_3/pallas_call | solution.py:2262
  353.8 0.0 copy-start.1
  353.8 0.0 copy-start
  353.8 0.0 all-reduce.2.cloned.1.call-done.totals_ref
  353.8 4.0 %finish.1 = (f32[576,1152]{1,0:T(8,128)}, f32[288,1152]{1,0:T(8,128)}, f32[288,104]{1,0:T(8,128)}, f32[72,288]{1,0:T(8,128)}, f32[16,288]{1,0:T(8,128)}, /*index...) custom-call(bf16[896,1152]{1,0:T(8,128)(2,1)} %all-reduce.2.cloned.1, ...), custom_call_target="tpu_custom_call" | custom-call | tf_op jit(solution)/shard_map/finish/pallas_call | solution.py:2313
  357.8 0.0 copy-done.1
  357.8 0.8 copy.39
  358.6 0.0 copy-done
  358.6 1.0 copy.40
Async XLA Ops:
  7.2 346.7 %all-reduce.2.cloned.1.call-start = ((), (), s32[]{:S(2)}) async-start(), calls=%async_computation | async-start | bytes 4128768 | tf_op jit(solution)/shard_map/psum | solution.py:2381
  353.8 4.0 %copy-start.1 = (bf16[256,1152]{1,0:T(8,128)(2,1)S(1)}, bf16[256,1152]{1,0:T(8,128)(2,1)}, u32[]{:S(2)}) copy-start(bf16[256,1152]{1,0:T(8,128)(2,1)} %get-tuple-element.82) | copy-start | bytes 1769476
  353.8 4.8 %copy-start = (f32[256,1152]{1,0:T(8,128)S(1)}, f32[256,1152]{1,0:T(8,128)}, u32[]{:S(2)}) copy-start(f32[256,1152]{1,0:T(8,128)} %get-tuple-element.110) | copy-start | bytes 3538948
Sparse Core Ops, SparseCore 0:
  256.6 88.8 all-reduce.1

commit v7 on v6

--- a/solution.py
+++ b/solution.py
@@ -1661,9 +1661,8 @@
         Line(3, left_2, right_2, left_3, right_3, l_send.at[0], l_recv.at[0]),
         Line(3, goal_l2, goal_r2, goal_l3, goal_r3, l_send.at[1], l_recv.at[1]),
         Near(rows_0, rows_1, l_send.at[2], l_recv.at[2]),
-        *(
-            Near(grads_0.at[k], grads_1.at[k], l_send.at[3 + k // 2], l_recv.at[3 + k // 2])
-            for k in range(1, devices, 2)
+        Near(
+            grads_0.at[pl.ds(half, half)], grads_1.at[pl.ds(half, half)], l_send.at[3], l_recv.at[3]
         ),
     ]
     load_normed = pltpu.make_async_copy(normed_hbm, everyone, load_sems.at[0])
@@ -1710,7 +1709,7 @@
 
     def between(position):
         if position == 1:
-            pl.when(me % 2 == 0)(lambda: near_grads.start())
+            pl.when(me < half)(lambda: near_grads.start())
         if position == 2:
             mix.step(1)
             mix.step(2)
@@ -1925,10 +1924,10 @@
         for line in lines:
             line.wait()
         for k, copy in enumerate(near_grads.copies):
-            pl.when(me % 2 == 0)(lambda copy=copy: copy.wait_send())
+            pl.when(me < half)(lambda copy=copy: copy.wait_send())
             source = (me + devices - k - 1) % devices
-            pl.when(source % 2 == 0)(lambda copy=copy: copy.wait_recv())
-        pl.when(me % 2 == 0)(lambda: near_grads.local.wait())
+            pl.when(source < half)(lambda copy=copy: copy.wait_recv())
+        pl.when(me < half)(lambda: near_grads.local.wait())
         store_back.wait()
         store_tail.wait()
         store_tokens.wait()
@@ -2025,7 +2024,7 @@
             pltpu.VMEM(raw.shape, BF16),
             pltpu.VMEM(goal.shape, jnp.int32),
             pltpu.VMEM(slots.shape, BF16),
-            DMA((10,)), DMA((10,)), DMA((4, devices)), DMA((4, devices)), DMA((7, 2)), DMA((7, 2)),
+            DMA((10,)), DMA((10,)), DMA((4, devices)), DMA((4, devices)), DMA((4, 2)), DMA((4, 2)),
             DMA((5,)), DMA((4,)), DMA((10,)),
         ],
         compiler_params=pltpu.CompilerParams(

time: 374 us -> 367 us (0.981)
  Pallas kernels: 350 us -> 343 us
    pallas_call x1, Pallas kernels: 97.1 us -> 90.5 us  [backward_plane(): pl.pallas_call(backward_kernel, grid=(14,), in_specs=[pl.BlockSpec((rows,...]
where the time goes in v7:
time: 367 us; the launch traced here: 360 us
  Pallas kernels  343 us (93%)
  between operations  15 us (4%)
    pallas_call x1, Pallas kernels, backward_plane(): pl.pallas_call(backward_kernel, grid=(14,), in_specs=[pl.BlockSpec((rows,...  90.5 us
    pallas_call x1, Pallas kernels, forward_plane(): pl.pallas_call(forward_kernel, grid=(4,), in_specs=[whole(value.shape) fo...  88.1 us
    pallas_call x1, Pallas kernels, expert_grads_plane(): pl.pallas_call(two_grads_kernel, grid=(2 * count,), in_specs=again + earl...  70.6 us
    pallas_call x1, Pallas kernels, expert_layer(): pl.pallas_call(expert_layer_kernel, in_specs=[pl.BlockSpec(memory_space=p...  63.6 us
    pallas_call x1, Pallas kernels, expert_grads_plane(): pl.pallas_call(last_grads_kernel, grid=(hidden // 768,), in_specs=tiles(7...  26.6 us
  transfers between devices with their start and end apart: 1, of which 0 were waited for; matrix products, arithmetic and copies ran while one was open for 0% of the time, Pallas kernels for 27%

profile of v7, /device:TPU:9, one launch (start us, length us, event | category | flops | bytes accessed | tf_op | source)
XLA Modules:
  0.0 360.2 jit_solution(3304243039736058326)
XLA Ops:
  7.2 0.0 all-reduce.2.cloned.1.call-start
  7.9 88.1 %mixer_forward.1 = (bf16[256,1152]{1,0:T(8,128)(2,1)}, f32[256,2304]{1,0:T(8,128)}, f32[256,2304]{1,0:T(8,128)}, f32[256,2304]{1,0:T(8,128)}, f32[256,104]{1,0:T...) custom-call(bf16[256,1152]{1,0:T(8,128)(2,1)} %bitcast.28, ...), custom_call_target="tpu_custom_call" | custom-call | tf_op jit(solution)/shard_map/mixer_forward/pallas_call | solution.py:1521
  95.9 63.6 %expert_layer.1 = (bf16[256,1152]{1,0:T(8,128)(2,1)}, f32[256,1152]{1,0:T(8,128)}, bf16[256,1152]{1,0:T(8,128)(2,1)}, f32[9,1152]{1,0:T(8,128)}, bf16[8,64,1152]...) custom-call(s32[1]{0:T(128)S(6)} %copy.38.length_ref, ...), custom_call_target="tpu_custom_call" | custom-call | tf_op jit(solution)/shard_map/expert_layer/pallas_call | solution.py:1082
  159.5 90.5 %mixer_backward.1 = (f32[256,1152]{1,0:T(8,128)}, bf16[896,1152]{1,0:T(8,128)(2,1)}, bf16[8,112,288]{2,1,0:T(8,128)(2,1)}, bf16[8,16,144]{2,1,0:T(8,128)(2,1)}, ...) custom-call(f32[256,104]{1,0:T(8,128)} %get-tuple-element.83.proj_re, ...), custom_call_target="tpu_custom_call" | custom-call | tf_op jit(solution)/shard_map/mixer_backward/pallas_call | solution.py:1966
  250.0 0.0 all-reduce.2.cloned.1.call-update
  250.0 70.6 %expert_grads_12.1 = (bf16[1152,3072]{1,0:T(8,128)(2,1)}, bf16[3072,1152]{1,0:T(8,128)(2,1)}, bf16[8,64,1152]{2,1,0:T(8,128)(2,1)}, bf16[8,64,1152]{2,1,0:T(8,128)(2,1)}, f32[48,1152]{1,0:T(8,128)}) custom-call(bf16[1152,3072]{1,0:T(8,128)(2,1)} %bitcast.19, bf16[3072,1152]{1,0:T(8,128)(2,1)} %bitcast.22, bf16[1152,3072]{1,0:T(8,128)(2,1)} %get-tuple-element.112.gup_in, ...), custom_call_target="tpu_custom_call" | custom-call | tf_op jit(solution)/shard_map/expert_grads_12/pallas_call | solution.py:2233
  320.6 26.6 %expert_grads_3.1 = (f32[1152,3072]{1,0:T(8,128)}, f32[3072,1152]{1,0:T(8,128)}) custom-call(bf16[1152,3072]{1,0:T(8,128)(2,1)} %bitcast.20, bf16[3072,1152]{1,0:T(8,128)(2,1)} %bitcast.23, bf16[1152,3072]{1,0:T(8,128)(2,1)} %get-tuple-element.136.gup_in, bf16[3072,1152]{1,0:T(8,128)(2,1)} %get-tuple-element.137.gdown_in, ...), custom_call_target="tpu_custom_call" | custom-call | tf_op jit(solution)/shard_map/expert_grads_3/pallas_call | solution.py:2261
  347.2 0.0 copy-start.1
  347.2 0.0 copy-start
  347.2 0.0 all-reduce.2.cloned.1.call-done.totals_ref
  347.2 4.0 %finish.1 = (f32[576,1152]{1,0:T(8,128)}, f32[288,1152]{1,0:T(8,128)}, f32[288,104]{1,0:T(8,128)}, f32[72,288]{1,0:T(8,128)}, f32[16,288]{1,0:T(8,128)}, /*index...) custom-call(bf16[896,1152]{1,0:T(8,128)(2,1)} %all-reduce.2.cloned.1, ...), custom_call_target="tpu_custom_call" | custom-call | tf_op jit(solution)/shard_map/finish/pallas_call | solution.py:2312
  351.2 0.0 copy-done.1
  351.2 0.8 copy.39
  352.0 0.0 copy-done
  352.0 1.0 copy.40
Async XLA Ops:
  7.2 340.0 %all-reduce.2.cloned.1.call-start = ((), (), s32[]{:S(2)}) async-start(), calls=%async_computation | async-start | bytes 4128768 | tf_op jit(solution)/shard_map/psum | solution.py:2380
  347.2 4.0 %copy-start.1 = (bf16[256,1152]{1,0:T(8,128)(2,1)S(1)}, bf16[256,1152]{1,0:T(8,128)(2,1)}, u32[]{:S(2)}) copy-start(bf16[256,1152]{1,0:T(8,128)(2,1)} %get-tuple-element.82) | copy-start | bytes 1769476
  347.2 4.8 %copy-start = (f32[256,1152]{1,0:T(8,128)S(1)}, f32[256,1152]{1,0:T(8,128)}, u32[]{:S(2)}) copy-start(f32[256,1152]{1,0:T(8,128)} %get-tuple-element.110) | copy-start | bytes 3538948
Sparse Core Ops, SparseCore 0:
  250.1 88.5 all-reduce.1

commit v8 on v7

--- a/solution.py
+++ b/solution.py
@@ -1323,6 +1323,7 @@
 
     @pl.when(step == 0)
     def _():
+        greet_send()
         spare = columns.shape[0] - rank - state - taps - 3
         columns[...] = jnp.concatenate(
             [
@@ -1340,7 +1341,7 @@
             ],
             0,
         ).astype(BF16)
-        greet()
+        greet_wait()
         for number in range(3):
             for one in small:
                 one.step(number)

time: 367 us -> 367 us (level)
  no operation moved by 1% of the time
where the time goes in v8:
time: 367 us; the launch traced here: 360 us
  Pallas kernels  343 us (93%)
  between operations  15 us (4%)
    pallas_call x1, Pallas kernels, backward_plane(): pl.pallas_call(backward_kernel, grid=(14,), in_specs=[pl.BlockSpec((rows,...  90.5 us
    pallas_call x1, Pallas kernels, forward_plane(): pl.pallas_call(forward_kernel, grid=(4,), in_specs=[whole(value.shape) fo...  88 us
    pallas_call x1, Pallas kernels, expert_grads_plane(): pl.pallas_call(two_grads_kernel, grid=(2 * count,), in_specs=again + earl...  70.6 us
    pallas_call x1, Pallas kernels, expert_layer(): pl.pallas_call(expert_layer_kernel, in_specs=[pl.BlockSpec(memory_space=p...  63.6 us
    pallas_call x1, Pallas kernels, expert_grads_plane(): pl.pallas_call(last_grads_kernel, grid=(hidden // 768,), in_specs=tiles(7...  26.6 us
  transfers between devices with their start and end apart: 1, of which 0 were waited for; matrix products, arithmetic and copies ran while one was open for 0% of the time, Pallas kernels for 27%

profile of v8, /device:TPU:9, one launch (start us, length us, event | category | flops | bytes accessed | tf_op | source)
XLA Modules:
  0.0 360.1 jit_solution(13619025879948327878)
XLA Ops:
  7.2 0.0 all-reduce.2.cloned.1.call-start
  7.9 88.0 %mixer_forward.1 = (bf16[256,1152]{1,0:T(8,128)(2,1)}, f32[256,2304]{1,0:T(8,128)}, f32[256,2304]{1,0:T(8,128)}, f32[256,2304]{1,0:T(8,128)}, f32[256,104]{1,0:T...) custom-call(bf16[256,1152]{1,0:T(8,128)(2,1)} %bitcast.28, ...), custom_call_target="tpu_custom_call" | custom-call | tf_op jit(solution)/shard_map/mixer_forward/pallas_call | solution.py:1522
  95.9 63.6 %expert_layer.1 = (bf16[256,1152]{1,0:T(8,128)(2,1)}, f32[256,1152]{1,0:T(8,128)}, bf16[256,1152]{1,0:T(8,128)(2,1)}, f32[9,1152]{1,0:T(8,128)}, bf16[8,64,1152]...) custom-call(s32[1]{0:T(128)S(6)} %copy.38.length_ref, ...), custom_call_target="tpu_custom_call" | custom-call | tf_op jit(solution)/shard_map/expert_layer/pallas_call | solution.py:1082
  159.5 90.5 %mixer_backward.1 = (f32[256,1152]{1,0:T(8,128)}, bf16[896,1152]{1,0:T(8,128)(2,1)}, bf16[8,112,288]{2,1,0:T(8,128)(2,1)}, bf16[8,16,144]{2,1,0:T(8,128)(2,1)}, ...) custom-call(f32[256,104]{1,0:T(8,128)} %get-tuple-element.83.proj_re, ...), custom_call_target="tpu_custom_call" | custom-call | tf_op jit(solution)/shard_map/mixer_backward/pallas_call | solution.py:1967
  250.0 0.0 all-reduce.2.cloned.1.call-update
  250.0 70.6 %expert_grads_12.1 = (bf16[1152,3072]{1,0:T(8,128)(2,1)}, bf16[3072,1152]{1,0:T(8,128)(2,1)}, bf16[8,64,1152]{2,1,0:T(8,128)(2,1)}, bf16[8,64,1152]{2,1,0:T(8,128)(2,1)}, f32[48,1152]{1,0:T(8,128)}) custom-call(bf16[1152,3072]{1,0:T(8,128)(2,1)} %bitcast.19, bf16[3072,1152]{1,0:T(8,128)(2,1)} %bitcast.22, bf16[1152,3072]{1,0:T(8,128)(2,1)} %get-tuple-element.112.gup_in, ...), custom_call_target="tpu_custom_call" | custom-call | tf_op jit(solution)/shard_map/expert_grads_12/pallas_call | solution.py:2234
  320.6 26.6 %expert_grads_3.1 = (f32[1152,3072]{1,0:T(8,128)}, f32[3072,1152]{1,0:T(8,128)}) custom-call(bf16[1152,3072]{1,0:T(8,128)(2,1)} %bitcast.20, bf16[3072,1152]{1,0:T(8,128)(2,1)} %bitcast.23, bf16[1152,3072]{1,0:T(8,128)(2,1)} %get-tuple-element.136.gup_in, bf16[3072,1152]{1,0:T(8,128)(2,1)} %get-tuple-element.137.gdown_in, ...), custom_call_target="tpu_custom_call" | custom-call | tf_op jit(solution)/shard_map/expert_grads_3/pallas_call | solution.py:2262
  347.2 0.0 copy-start.1
  347.2 0.0 copy-start
  347.2 0.0 all-reduce.2.cloned.1.call-done.totals_ref
  347.2 4.0 %finish.1 = (f32[576,1152]{1,0:T(8,128)}, f32[288,1152]{1,0:T(8,128)}, f32[288,104]{1,0:T(8,128)}, f32[72,288]{1,0:T(8,128)}, f32[16,288]{1,0:T(8,128)}, /*index...) custom-call(bf16[896,1152]{1,0:T(8,128)(2,1)} %all-reduce.2.cloned.1, ...), custom_call_target="tpu_custom_call" | custom-call | tf_op jit(solution)/shard_map/finish/pallas_call | solution.py:2313
  351.2 0.0 copy-done.1
  351.2 0.8 copy.39
  352.0 0.0 copy-done
  352.0 1.0 copy.40
Async XLA Ops:
  7.2 340.0 %all-reduce.2.cloned.1.call-start = ((), (), s32[]{:S(2)}) async-start(), calls=%async_computation | async-start | bytes 4128768 | tf_op jit(solution)/shard_map/psum | solution.py:2381
  347.2 4.0 %copy-start.1 = (bf16[256,1152]{1,0:T(8,128)(2,1)S(1)}, bf16[256,1152]{1,0:T(8,128)(2,1)}, u32[]{:S(2)}) copy-start(bf16[256,1152]{1,0:T(8,128)(2,1)} %get-tuple-element.82) | copy-start | bytes 1769476
  347.2 4.8 %copy-start = (f32[256,1152]{1,0:T(8,128)S(1)}, f32[256,1152]{1,0:T(8,128)}, u32[]{:S(2)}) copy-start(f32[256,1152]{1,0:T(8,128)} %get-tuple-element.110) | copy-start | bytes 3538948
Sparse Core Ops, SparseCore 0:
  250.1 88.5 all-reduce.1
